TPU v7x, 32 devices: a whole 2x2x4 slice. The times are simulated.
32 devices in a mesh: pose: 2 (over y), aux: 4 (over z), orb: 2 (over x), ao: 2 (over core).
Axes of the slice: x: 2, y: 2, z: 4, core: 2. Of those that a mesh axis runs over, the one named last changes fastest.
Arguments:
- blocks: bfloat16 [32, 512, 512], P(('pose', 'aux', 'orb'), None, 'ao'), parts along dimension 0, may hold values from -6 to 6
- pattern: int32 [16, 4, 4], P(('pose', 'aux', 'orb'), None, 'ao'), parts along dimension 0, may hold values 0 or 1
- occupied: bfloat16 [512, 1024], P(None, 'orb'), may hold values from -0.25 to 0.25
- ligand: bfloat16 [512, 256], P(None, 'pose'), parts along dimension 1, may hold values from -0.25 to 0.25
Outputs:
- density: float32 [32], P(('pose', 'aux', 'orb')), parts along dimension 0
- cross_terms: float32 [2048, 512, 128], P(('pose', 'aux', 'orb'), 'ao'), parts along dimension 0
There are 2 independent parts, one for each index of `pose`. A program takes and returns all parts, laid end to end along the dimension named above; an argument that names none is the same for every part. Nothing has to cross between parts.
All inputs are finite; a program needn't handle non-finite values. No bound on the sum of `pattern` on one device may be relied on, other than what follows from the above.
Results may differ from a plain program's by a relative error of at most 0.0049.
Values may be sent and summed in bfloat16 or wider, within the bound.
No kernel may reach another device: no remote copies, remote signals or barrier semaphores. Data moves between devices by JAX's collectives and lax.ppermute only.
A program may use at most 64 MiB of HBM per device.

v0:
```python
import math

import jax
import jax.numpy as jnp
from jax import lax
from jax.sharding import PartitionSpec as P

NOCC = 1024
BLK = 128
NBLK = 4
NB = 512


def body(blocks, pattern, occupied, ligand):
    panels = lax.all_gather(occupied, "orb", axis=1, tiled=True)
    aux_rows = blocks.shape[0]
    nu_width = blocks.shape[2]
    nu_blocks = pattern.shape[2]
    opened = pattern[0].astype(jnp.bfloat16)
    masked = blocks.reshape(aux_rows, NBLK, BLK, nu_blocks, BLK) * opened[None, :, None, :, None]
    masked = masked.reshape(aux_rows, NB, nu_width)
    transformed = jnp.einsum(
        "qmn,mi->qin", masked, panels, preferred_element_type=jnp.float32
    ).astype(jnp.bfloat16)
    nu_start = lax.axis_index("ao") * nu_width
    own_rows = lax.dynamic_slice_in_dim(panels, nu_start, nu_width, 0)
    partial_value = jnp.einsum(
        "qin,ni->q", transformed, own_rows, preferred_element_type=jnp.float32
    )
    density = lax.psum(partial_value, "ao") / math.sqrt(NOCC)
    arrived = lax.all_to_all(transformed, ("aux", "orb"), split_axis=1, concat_axis=0, tiled=True)
    own_ligand = lax.dynamic_slice_in_dim(ligand, nu_start, nu_width, 0)
    pair_part = jnp.einsum("qin,nj->qij", arrived, own_ligand, preferred_element_type=jnp.float32)
    mixed_pairs = lax.psum(pair_part, "ao").astype(jnp.bfloat16)
    crossed = jnp.einsum("qin,qij->inj", arrived, mixed_pairs, preferred_element_type=jnp.float32)
    cross_terms = crossed / math.sqrt(arrived.shape[0])
    return (density, cross_terms)


def solution(mesh):
    return jax.shard_map(
        body,
        mesh=mesh,
        in_specs=(
            P(("pose", "aux", "orb"), None, "ao"),
            P(("pose", "aux", "orb"), None, "ao"),
            P(None, "orb"),
            P(None, "pose"),
        ),
        out_specs=(P(("pose", "aux", "orb")), P(("pose", "aux", "orb"), "ao", None)),
        check_vma=False,
    )
```

profile of v0, /device:TPU:0, one launch (start us, length us, event | category | flops | bytes accessed | tf_op | source)
XLA Modules:
  0.0 90.8 jit_solution(9417237269828517178)
XLA Ops:
  7.2 0.0 copy-start
  7.2 0.0 all-gather.2.cloned.1.call-start
  7.2 0.7 all-gather.2.cloned.1.call-update
  7.9 0.7 convert_bitcast_fusion
  8.6 0.1 copy.9
  8.7 0.2 mul.16
  9.0 24.6 %all-gather.2.cloned.1.call-done = bf16[512,1024]{1,0:T(8,128)(2,1)} async-done(((bf16[512,512]{1,0:T(8,128)(2,1)}), bf16[512,1024]{1,0:T(8,128)(2,1)}) %all-gather.2.cloned.1.call-update) | async-done | bytes 1048592 | tf_op jit(solution)/shard_map/all_gather | solution.py:15
  33.6 2.1 %fusion = bf16[2,1024,256]{1,2,0:T(8,128)(2,1)S(1)} fusion(bf16[512,1024]{1,0:T(8,128)(2,1)} %all-gather.2.cloned.1.call-done, bf16[2,512,256]{2,1,0:T(8,128)(2,1)} %param.4, bf16[512,256]{1,0:T(8,128)(2,1)S(1)} %bitcast.33), kind=kOutput, calls=%fused_computation.2 | convolution fusion | flops 537657344 | bytes 2883584 | tf_op jit(solution)/shard_map/qmn,mi->qin/dot_general | solution.py:22
  35.7 2.0 %copy.11 = bf16[2,1024,256]{2,0,1:T(2,128)(2,1)} copy(bf16[2,1024,256]{1,2,0:T(8,128)(2,1)S(1)} %fusion) | data formatting | bytes 2097152 | tf_op jit(solution)/shard_map/convert_element_type | solution.py:24
  37.8 4.6 %all-to-all-start = ((bf16[2,1024,256]{2,0,1:T(2,128)(2,1)}), bf16[2,1024,256]{2,0,1:T(2,128)(2,1)S(1)}, u32[]{:S(2)}, u32[]{:S(2)}) async-start(bf16[2,1024,256]{2,0,1:T(2,128)(2,1)} %copy.11), calls=%async_computation | async-start | bytes 2097152 | tf_op jit(solution)/shard_map/all_to_all | solution.py:31
  42.4 1.1 %dynamic-slice_bitcast_fusion = bf16[256,1024,1]{1,0,2:T(8,128)(2,1)S(1)} fusion(bf16[512,1024]{1,0:T(8,128)(2,1)} %all-gather.2.cloned.1.call-done, s32[]{:T(128)S(6)} %select_n.4), kind=kLoop, calls=%fused_computation.7 | loop fusion | bytes 1048580 | tf_op jit(solution)/shard_map/dynamic_slice | solution.py:26
  43.4 0.9 copy.14
  44.3 4.0 %convolution_bitcast_fusion = f32[2]{0:T(128)S(1)} fusion(bf16[2,1024,256]{2,0,1:T(2,128)(2,1)} %copy.11, bf16[256,1024,1]{0,2,1:T(2,128)(2,1)S(1)} %copy.14), kind=kOutput, calls=%fused_computation.3 | convolution fusion | flops 1048576 | bytes 1572872 | tf_op jit(solution)/shard_map/qin,ni->q/dot_general | solution.py:27
  48.3 19.8 %all-to-all-done = bf16[2,1024,256]{2,0,1:T(2,128)(2,1)S(1)} async-done(((bf16[2,1024,256]{2,0,1:T(2,128)(2,1)}), bf16[2,1024,256]{2,0,1:T(2,128)(2,1)S(1)}, u32[]{:S(2)}, u32[]{:S(2)}) %all-to-all-start) | async-done | bytes 1048608 | tf_op jit(solution)/shard_map/all_to_all | solution.py:31
  68.1 0.7 copy.18
  68.9 0.4 all_to_all.16
  69.3 0.0 copy-done
  69.3 0.4 fusion.5
  69.8 6.3 %all-reduce.2 = (f32[2]{0:T(128)S(1)}, bf16[16,128,128]{2,0,1:T(8,128)(2,1)S(1)}) all-reduce(f32[2]{0:T(128)S(1)} %convolution_bitcast_fusion, f32[16,128,128]{2,0,1:T(8,128)S(1)} %fusion.5), channel_id=1, replica_groups=mesh['pose'=2,'aux'=4,'orb'=2,'ao'=2] {'ao'}, use_global_device_ids=true, to_apply=%region_0.0 | all-reduce | flops 262146 | bytes 1572880 | tf_op jit(solution)/shard_map/psum | solution.py:30
  76.0 0.5 broadcast_multiply_fusion
  76.5 7.5 %convolution_multiply_fusion = f32[128,256,128]{2,1,0:T(8,128)} fusion(bf16[16,128,256]{2,0,1:T(8,128)(2,1)S(1)} %all_to_all.16, bf16[16,128,128]{2,0,1:T(8,128)(2,1)S(1)} %get-tuple-element.3), kind=kOutput, calls=%fused_computation | convolution fusion | flops 138412032 | bytes 18350080 | tf_op jit(solution)/shard_map/qin,qij->inj/dot_general | solution.py:35
  (1 shorter events, 0.0 us)
Async XLA Ops:
  7.2 62.1 %copy-start = (bf16[512,128]{1,0:T(8,128)(2,1)S(1)}, bf16[512,128]{1,0:T(8,128)(2,1)}, u32[]{:S(2)}) copy-start(bf16[512,128]{1,0:T(8,128)(2,1)} %param.7) | copy-start | bytes 393220
  7.2 26.4 %all-gather.2.cloned.1.call-start = ((), (), s32[]{:S(2)}) async-start(), calls=%async_computation.1 | async-start | bytes 1572864 | tf_op jit(solution)/shard_map/all_gather | solution.py:15
  37.8 30.4 %all-to-all-start = ((bf16[2,1024,256]{2,0,1:T(2,128)(2,1)}), bf16[2,1024,256]{2,0,1:T(2,128)(2,1)S(1)}, u32[]{:S(2)}, u32[]{:S(2)}) async-start(bf16[2,1024,256]{2,0,1:T(2,128)(2,1)} %copy.11), calls=%async_computation | async-start | bytes 2097152 | tf_op jit(solution)/shard_map/all_to_all | solution.py:31
Sparse Core Ops, SparseCore 0:
  9.6 23.9 all-gather.1
where the time goes:
time: 91.2 us; the launch traced here: 90.8 us
  waiting for transfers between devices  45.1 us (49%)
  between operations  14.1 us (15%)
  matrix products  14 us (15%)
  blocking collectives  6.26 us (7%)
  local copies, waits for them, and re-layouts  5.49 us (6%)
  starting transfers between devices  4.64 us (5%)
  other arithmetic  1.2 us (1%)
    all_gather x1, waiting for transfers between devices, body(): panels = lax.all_gather(occupied, 'orb', axis=1, tiled=True)  24.6 us
    all_to_all x1, waiting for transfers between devices, body(): lax.all_to_all(transformed, ('aux', 'orb'), split_axis=1, concat_axis=0,...  19.8 us
    dot_general x1, matrix products, body(): jnp.einsum('qin,qij->inj', arrived, mixed_pairs, preferred_element_type=j...  7.46 us
    psum x1, blocking collectives, body(): density = lax.psum(partial_value, 'ao') / math.sqrt(NOCC)  6.26 us
    all_to_all x1, starting transfers between devices, body(): lax.all_to_all(transformed, ('aux', 'orb'), split_axis=1, concat_axis=0,...  4.61 us
    dot_general x1, matrix products, body(): jnp.einsum('qin,ni->q', transformed, own_rows, preferred_element_type=jnp...  4.02 us
    dot_general x1, matrix products, body(): jnp.einsum('qmn,mi->qin', masked, panels, preferred_element_type=jnp.floa...  2.12 us
    convert_element_type x1, local copies, waits for them, and re-layouts, body(): transformed = jnp.einsum('qmn,mi->qin', masked, panels, preferred_element...  2.04 us
  transfers between devices with their start and end apart: 2, of which 2 were waited for; matrix products, arithmetic and copies ran while one was open for 8% of the time, Pallas kernels for 0%

commit v1 on v0

--- a/solution.py
+++ b/solution.py
@@ -1,17 +1,180 @@
+import functools
 import math
 
 import jax
 import jax.numpy as jnp
 from jax import lax
+from jax.experimental import pallas as pl
+from jax.experimental.pallas import tpu as pltpu
 from jax.sharding import PartitionSpec as P
 
 NOCC = 1024
 BLK = 128
 NBLK = 4
 NB = 512
-
-
-def body(blocks, pattern, occupied, ligand):
+GROUP = 16
+VMEM_LIMIT = 48 * 1024 * 1024
+
+
+def half_kernel(place, pattern, blocks, *refs):
+    panels, (out, masked) = refs[:-2], refs[-2:]
+    aux_rows, _, nu_width = blocks.shape
+    ni = out.shape[2]
+    per_panel = panels[0].shape[1] // ni
+    for q in range(aux_rows):
+        for m in range(NBLK):
+            for n in range(nu_width // BLK):
+                rows, columns = pl.ds(m * BLK, BLK), pl.ds(n * BLK, BLK)
+                tile = blocks[q, rows, columns]
+                keep = pattern[0, m, n] != 0
+                masked[rows, pl.ds(q * nu_width + n * BLK, BLK)] = jnp.where(keep, tile, jnp.zeros_like(tile))
+    for k, panel in enumerate(panels):
+        first = lax.rem(place[0] + k, len(panels)) * per_panel
+        for s in range(per_panel):
+            turned = panel[:, s * ni : (s + 1) * ni].T
+            result = jnp.dot(turned, masked[...], preferred_element_type=jnp.float32).astype(jnp.bfloat16)
+            for q in range(aux_rows):
+                out[first + s, q] = result[:, q * nu_width : (q + 1) * nu_width]
+
+
+def density_kernel(place, half, *refs):
+    panels, out = refs[:-1], refs[-1]
+    _, aux_rows, ni, nu_width = half.shape
+    per_panel = panels[0].shape[1] // ni
+    eye = lax.broadcasted_iota(jnp.int32, (nu_width, nu_width), 0) == lax.broadcasted_iota(
+        jnp.int32, (nu_width, nu_width), 1
+    )
+    for q in range(aux_rows):
+        total = jnp.zeros((nu_width, nu_width), jnp.float32)
+        for k, panel in enumerate(panels):
+            first = lax.rem(place[0] + k, len(panels)) * per_panel
+            for s in range(per_panel):
+                total += jnp.dot(
+                    panel[:, s * ni : (s + 1) * ni], half[first + s, q], preferred_element_type=jnp.float32
+                )
+        value = jnp.sum(jnp.where(eye, total, 0.0))
+        out[q] = jnp.full(out.shape[1:], value, jnp.float32)
+
+
+def pair_kernel(place, arrived, ligand, out, sent):
+    rows = arrived.shape[0] * arrived.shape[1]
+    part = jnp.dot(
+        arrived[...].reshape(rows, arrived.shape[2]), ligand[...], preferred_element_type=jnp.float32
+    )
+    part = part.reshape(out.shape)
+    out[...] = part
+    sent[...] = part.astype(jnp.bfloat16)
+
+
+def cross_kernel(scale, arrived, own, other, out):
+    q_total, group, nu_width = arrived.shape
+    width = own.shape[2]
+    depth = q_total * group
+    turned = arrived[...].reshape(depth, nu_width).T
+    pairs = (own[...] + other[...].astype(jnp.float32)).astype(jnp.bfloat16).reshape(depth, width)
+    row = lax.broadcasted_iota(jnp.int32, (depth, width), 0) % group
+    zero = jnp.zeros_like(pairs)
+    for i in range(0, group, 2):
+        both = jnp.concatenate([jnp.where(row == i, pairs, zero), jnp.where(row == i + 1, pairs, zero)], axis=1)
+        result = jnp.dot(turned, both, preferred_element_type=jnp.float32) * scale
+        out[i] = result[:, :width]
+        out[i + 1] = result[:, width:]
+
+
+def params():
+    return pltpu.CompilerParams(vmem_limit_bytes=VMEM_LIMIT)
+
+
+def whole(shape):
+    return pl.BlockSpec(shape, lambda step, place: (0,) * len(shape))
+
+
+def body(sizes, blocks, pattern, occupied, ligand):
+    n_aux, n_orb, n_ao = sizes
+    aux_rows, _, nu_width = blocks.shape
+    owners = n_aux * n_orb
+    ni = NOCC // owners
+    q_total = aux_rows * owners
+    panel_width = occupied.shape[1]
+    width = ligand.shape[1]
+    orb = lax.axis_index("orb")
+    ao = lax.axis_index("ao")
+    place = jnp.stack([orb, ao]).astype(jnp.int32)
+
+    panels = [occupied]
+    for k in range(1, n_orb):
+        panels.append(lax.ppermute(occupied, "orb", [((o + k) % n_orb, o) for o in range(n_orb)]))
+
+    half = pl.pallas_call(
+        half_kernel,
+        grid_spec=pltpu.PrefetchScalarGridSpec(
+            num_scalar_prefetch=1,
+            grid=(1,),
+            in_specs=[pl.BlockSpec(memory_space=pltpu.SMEM), whole(blocks.shape)] + [whole(occupied.shape)] * n_orb,
+            out_specs=whole((owners, aux_rows, ni, nu_width)),
+            scratch_shapes=[pltpu.VMEM((NB, aux_rows * nu_width), jnp.bfloat16)],
+        ),
+        out_shape=jax.ShapeDtypeStruct((owners, aux_rows, ni, nu_width), jnp.bfloat16),
+        compiler_params=params(),
+        name="half_transform",
+    )(place, pattern, blocks, *panels)
+
+    arrived = lax.all_to_all(half, ("aux", "orb"), split_axis=0, concat_axis=0, tiled=True)
+    arrived = arrived.reshape(q_total, ni, nu_width)
+
+    own_rows = pl.BlockSpec((nu_width, panel_width), lambda step, place: (place[1], 0))
+    value = pl.pallas_call(
+        density_kernel,
+        grid_spec=pltpu.PrefetchScalarGridSpec(
+            num_scalar_prefetch=1,
+            grid=(1,),
+            in_specs=[whole(half.shape)] + [own_rows] * n_orb,
+            out_specs=whole((aux_rows, 8, 128)),
+        ),
+        out_shape=jax.ShapeDtypeStruct((aux_rows, 8, 128), jnp.float32),
+        compiler_params=params(),
+        name="density_terms",
+    )(place, half, *panels)[:, 0, 0]
+    swap = [(c, (c + 1) % n_ao) for c in range(n_ao)]
+    density = (value + lax.ppermute(value, "ao", swap)) / math.sqrt(NOCC)
+
+    own, sent = pl.pallas_call(
+        pair_kernel,
+        grid_spec=pltpu.PrefetchScalarGridSpec(
+            num_scalar_prefetch=1,
+            grid=(1,),
+            in_specs=[
+                whole(arrived.shape),
+                pl.BlockSpec((nu_width, width), lambda step, place: (place[1], 0)),
+            ],
+            out_specs=[whole((q_total, ni, width))] * 2,
+        ),
+        out_shape=[
+            jax.ShapeDtypeStruct((q_total, ni, width), jnp.float32),
+            jax.ShapeDtypeStruct((q_total, ni, width), jnp.bfloat16),
+        ],
+        compiler_params=params(),
+        name="pair_terms",
+    )(place, arrived, ligand)
+    other = lax.ppermute(sent, "ao", swap)
+
+    cross_terms = pl.pallas_call(
+        functools.partial(cross_kernel, 1.0 / math.sqrt(q_total)),
+        grid=(ni // GROUP,),
+        in_specs=[
+            pl.BlockSpec((q_total, GROUP, nu_width), lambda g: (0, g, 0)),
+            pl.BlockSpec((q_total, GROUP, width), lambda g: (0, g, 0)),
+            pl.BlockSpec((q_total, GROUP, width), lambda g: (0, g, 0)),
+        ],
+        out_specs=pl.BlockSpec((GROUP, nu_width, width), lambda g: (g, 0, 0)),
+        out_shape=jax.ShapeDtypeStruct((ni, nu_width, width), jnp.float32),
+        compiler_params=params(),
+        name="cross_terms",
+    )(arrived, own, other)
+    return (density, cross_terms)
+
+
+def plain_body(blocks, pattern, occupied, ligand):
     panels = lax.all_gather(occupied, "orb", axis=1, tiled=True)
     aux_rows = blocks.shape[0]
     nu_width = blocks.shape[2]
@@ -38,8 +201,10 @@
 
 
 def solution(mesh):
+    sizes = (mesh.shape["aux"], mesh.shape["orb"], mesh.shape["ao"])
+    kernels = NOCC % (sizes[0] * sizes[1] * BLK) == 0 and sizes[2] == 2
     return jax.shard_map(
-        body,
+        functools.partial(body, sizes) if kernels else plain_body,
         mesh=mesh,
         in_specs=(
             P(("pose", "aux", "orb"), None, "ao"),

time: 91.2 us -> 65.2 us (0.71)
  waiting for transfers between devices: 45.1 us -> 12.1 us
  blocking collectives: 6.26 us -> 30.8 us
  matrix products: 14 us -> 0 us
  between operations: 14.1 us -> 0.67 us
  Pallas kernels: 0 us -> 12.3 us
  starting transfers between devices: 4.64 us -> 3.57 us
    all_to_all x0 -> x1, blocking collectives: none -> 30.8 us  [body(): lax.all_to_all(half, ('aux', 'orb'), split_axis=0, concat_axis=0, tiled=T...]
    all_gather x1 -> x0, waiting for transfers between devices: 24.6 us -> none  [body(): panels = lax.all_gather(occupied, 'orb', axis=1, tiled=True)]
    all_to_all x1 -> x0, waiting for transfers between devices: 19.8 us -> none  [body(): lax.all_to_all(transformed, ('aux', 'orb'), split_axis=1, concat_axis=0,...]
    dot_general x4 -> x0, matrix products: 14 us -> none  [the longest x1 7.46 us: body(): jnp.einsum('qin,qij->inj', arrived, mixed_pairs, preferred_element_type=j...]
    pallas_call x0 -> x4, Pallas kernels: none -> 12.3 us  [the longest x1 7.98 us: body(): pl.pallas_call(functools.partial(cross_kernel, 1.0 / math.sqrt(q_total)),...]
    ppermute x0 -> x3, waiting for transfers between devices: none -> 12.1 us  [the longest x1 11.3 us: body(): lax.ppermute(occupied, 'orb', [((o + k) % n_orb, o) for o in range(n_orb)])]
    psum x1 -> x0, blocking collectives: 6.26 us -> none  [body(): density = lax.psum(partial_value, 'ao') / math.sqrt(NOCC)]
    unnamed x3 -> x9, local copies, waits for them, and re-layouts: 0.05 us -> 4.79 us
  transfers between devices with their start and end apart: 2 -> 3, of which waited for: 2 -> 2; matrix products, arithmetic and copies ran while one was open for 8% -> 2% of each run, Pallas kernels for 0% -> 2%
where the time goes in v1:
time: 65.2 us; the launch traced here: 64.9 us
  blocking collectives  30.8 us (47%)
  Pallas kernels  12.3 us (19%)
  waiting for transfers between devices  12.1 us (19%)
  local copies, waits for them, and re-layouts  4.89 us (7%)
  starting transfers between devices  3.57 us (5%)
  between operations  0.67 us (1%)
    all_to_all x1, blocking collectives, body(): lax.all_to_all(half, ('aux', 'orb'), split_axis=0, concat_axis=0, tiled=T...  30.8 us
    ppermute x1, waiting for transfers between devices, body(): lax.ppermute(occupied, 'orb', [((o + k) % n_orb, o) for o in range(n_orb)])  11.3 us
    pallas_call x1, Pallas kernels, body(): pl.pallas_call(functools.partial(cross_kernel, 1.0 / math.sqrt(q_total)),...  7.98 us
    unnamed x9, local copies, waits for them, and re-layouts  4.79 us
    ppermute x1, starting transfers between devices, body(): lax.ppermute(occupied, 'orb', [((o + k) % n_orb, o) for o in range(n_orb)])  3 us
    pallas_call x1, Pallas kernels, body(): pl.pallas_call(half_kernel, grid_spec=pltpu.PrefetchScalarGridSpec(num_sc...  1.96 us
    pallas_call x1, Pallas kernels, body(): pl.pallas_call(density_kernel, grid_spec=pltpu.PrefetchScalarGridSpec(num...  1.35 us
  transfers between devices with their start and end apart: 3, of which 2 were waited for; matrix products, arithmetic and copies ran while one was open for 2% of the time, Pallas kernels for 2%

profile of v1, /device:TPU:0, one launch (start us, length us, event | category | flops | bytes accessed | tf_op | source)
XLA Modules:
  0.0 64.9 jit_solution(5268945257881556306)
XLA Ops:
  0.6 3.0 %collective-permute-start = (bf16[512,512]{1,0:T(8,128)(2,1)}, bf16[512,512]{1,0:T(8,128)(2,1)S(1)}, u32[]{:S(2)}, u32[]{:S(2)}) collective-permute-start(bf16[512,512]{1,0:T(8,128)(2,1)} %refs_0_.3), channel_id=1, source_target_pairs={{2,0},{0,2},{3,1},{1,3},{6,4},{4,6},{7,5},{5,7},{10,8},{8,10},{11,... | collective-permute-start | bytes 1572872 | tf_op jit(solution)/shard_map/ppermute | solution.py:106
  3.6 0.8 %copy.7.pattern = s32[1,4,2]{2,1,0:T(4,128)S(1)} copy(s32[1,4,2]{1,2,0:T(2,128)} %param.5) | data formatting | bytes 64 | tf_op args[1]
  4.4 0.1 pad_add_fusion.place
  4.5 11.3 %collective-permute-done.refs_1_ = bf16[512,512]{1,0:T(8,128)(2,1)S(1)} collective-permute-done((bf16[512,512]{1,0:T(8,128)(2,1)}, bf16[512,512]{1,0:T(8,128)(2,1)S(1)}, u32[]{:S(2)}, u32[]{:S(2)}) %collective-permute-start) | collective-permute-done | bytes 524320 | tf_op jit(solution)/shard_map/ppermute | solution.py:106
  15.8 0.0 copy-start
  15.8 1.0 %copy-done = bf16[512,512]{1,0:T(8,128)(2,1)S(1)} copy-done((bf16[512,512]{1,0:T(8,128)(2,1)S(1)}, bf16[512,512]{1,0:T(8,128)(2,1)}, u32[]{:S(2)}) %copy-start) | copy-done | bytes 524312
  16.8 0.0 copy-start.2
  16.8 1.0 %copy-done.2 = bf16[2,512,256]{2,1,0:T(8,128)(2,1)S(1)} copy-done((bf16[2,512,256]{2,1,0:T(8,128)(2,1)S(1)}, bf16[2,512,256]{2,1,0:T(8,128)(2,1)}, u32[]{:S(2)}) %copy-start.2) | copy-done | bytes 524312
  17.9 2.0 %half_transform.1.half = bf16[8,2,128,256]{3,2,1,0:T(8,128)(2,1)S(1)} custom-call(s32[2]{0:T(128)S(1)} %pad_add_fusion.place, s32[1,4,2]{2,1,0:T(4,128)S(1)} %copy.7.pattern, bf16[2,512,256]{2,1,0:T(8,128)(2,1)S(1)} %copy-done.2, bf16[512,512]{1,0:T(8,128)(2,1)S(1)} %copy-done, bf16[512,512]{1,0:T(8,128)(2,1)S(1)} %collective-permute-done.refs_1_), custom_call_target="tpu_custom_call" | custom-call | tf_op jit(solution)/shard_map/half_transform/pallas_call | solution.py:108
  19.8 30.8 %all_to_all.5 = bf16[8,2,128,256]{3,2,1,0:T(8,128)(2,1)S(1)} all-to-all(bf16[8,2,128,256]{3,2,1,0:T(8,128)(2,1)S(1)} %half_transform.1.half), channel_id=1, replica_groups=mesh['pose'=2,'aux'=4,'orb'=2,'ao'=2] {'aux','orb'}, dimensions={0} | all-to-all | bytes 2097152 | tf_op jit(solution)/shard_map/all_to_all | solution.py:122
  50.6 0.0 copy-start.3
  50.6 0.9 %copy-done.3 = bf16[512,128]{1,0:T(8,128)(2,1)S(1)} copy-done((bf16[512,128]{1,0:T(8,128)(2,1)S(1)}, bf16[512,128]{1,0:T(8,128)(2,1)}, u32[]{:S(2)}) %copy-start.3) | copy-done | bytes 131096
  51.5 1.0 %pair_terms.1 = (f32[16,128,128]{2,1,0:T(8,128)S(1)}, bf16[16,128,128]{2,1,0:T(8,128)(2,1)S(1)}) custom-call(s32[2]{0:T(128)S(1)} %pad_add_fusion.place, bf16[16,128,256]{2,1,0:T(8,128)(2,1)S(1)} %bitcast.3, bf16[512,128]{1,0:T(8,128)(2,1)S(1)} %copy-done.3), custom_call_target="tpu_custom_call" | custom-call | tf_op jit(solution)/shard_map/pair_terms/pallas_call | solution.py:141
  52.5 0.1 collective-permute-start.2
  52.6 0.0 copy-start.1
  52.6 1.0 %copy-done.1 = bf16[512,512]{1,0:T(8,128)(2,1)S(1)} copy-done((bf16[512,512]{1,0:T(8,128)(2,1)S(1)}, bf16[512,512]{1,0:T(8,128)(2,1)}, u32[]{:S(2)}) %copy-start.1) | copy-done | bytes 524312
  53.6 1.4 %density_terms.1 = f32[2,8,128]{2,1,0:T(8,128)S(1)} custom-call(s32[2]{0:T(128)S(1)} %pad_add_fusion.place, bf16[8,2,128,256]{3,2,1,0:T(8,128)(2,1)S(1)} %half_transform.1.half, bf16[512,512]{1,0:T(8,128)(2,1)S(1)} %copy-done.1, bf16[512,512]{1,0:T(8,128)(2,1)S(1)} %collective-permute-done.refs_1_), custom_call_target="tpu_custom_call" | custom-call | tf_op jit(solution)/shard_map/density_terms/pallas_call | solution.py:126
  55.0 0.1 slice_reduce_fusion
  55.1 0.5 collective-permute-start.1
  55.6 0.8 %collective-permute-done.1 = f32[2]{0:T(128)S(1)} collective-permute-done((f32[2]{0:T(128)S(1)}, f32[2]{0:T(128)S(1)}, u32[]{:S(2)}, u32[]{:S(2)}) %collective-permute-start.1) | collective-permute-done | bytes 40 | tf_op jit(solution)/shard_map/ppermute | solution.py:139
  56.4 0.5 add_multiply_fusion
  56.9 0.0 collective-permute-done.2.other
  56.9 8.0 %cross_terms.1 = f32[128,256,128]{2,1,0:T(8,128)} custom-call(bf16[16,128,256]{2,1,0:T(8,128)(2,1)S(1)} %bitcast.4, f32[16,128,128]{2,1,0:T(8,128)S(1)} %get-tuple-element.4.own, bf16[16,128,128]{2,1,0:T(8,128)(2,1)S(1)} %collective-permute-done.2.other), custom_call_target="tpu_custom_call" | custom-call | tf_op jit(solution)/shard_map/cross_terms/pallas_call | solution.py:161
Async XLA Ops:
  0.6 15.1 %collective-permute-start = (bf16[512,512]{1,0:T(8,128)(2,1)}, bf16[512,512]{1,0:T(8,128)(2,1)S(1)}, u32[]{:S(2)}, u32[]{:S(2)}) collective-permute-start(bf16[512,512]{1,0:T(8,128)(2,1)} %refs_0_.3), channel_id=1, source_target_pairs={{2,0},{0,2},{3,1},{1,3},{6,4},{4,6},{7,5},{5,7},{10,8},{8,10},{11,... | collective-permute-start | bytes 1572872 | tf_op jit(solution)/shard_map/ppermute | solution.py:106
  15.8 1.0 %copy-start = (bf16[512,512]{1,0:T(8,128)(2,1)S(1)}, bf16[512,512]{1,0:T(8,128)(2,1)}, u32[]{:S(2)}) copy-start(bf16[512,512]{1,0:T(8,128)(2,1)} %refs_0_.3) | copy-start | bytes 1572868
  16.8 1.0 %copy-start.2 = (bf16[2,512,256]{2,1,0:T(8,128)(2,1)S(1)}, bf16[2,512,256]{2,1,0:T(8,128)(2,1)}, u32[]{:S(2)}) copy-start(bf16[2,512,256]{2,1,0:T(8,128)(2,1)} %blocks.1) | copy-start | bytes 1572868
  50.6 0.9 %copy-start.3 = (bf16[512,128]{1,0:T(8,128)(2,1)S(1)}, bf16[512,128]{1,0:T(8,128)(2,1)}, u32[]{:S(2)}) copy-start(bf16[512,128]{1,0:T(8,128)(2,1)} %ligand.1) | copy-start | bytes 393220
  52.5 4.4 %collective-permute-start.2 = (bf16[16,128,128]{2,1,0:T(8,128)(2,1)S(1)}, bf16[16,128,128]{2,1,0:T(8,128)(2,1)S(1)}, u32[]{:S(2)}, u32[]{:S(2)}) collective-permute-start(bf16[16,128,128]{2,1,0:T(8,128)(2,1)S(1)} %get-tuple-element.5), channel_id=1, source_target_pairs={{0,1},{1,0},{2,3},{3,2},{4,5},{5,4},{6,7},{7,6},{8,9},{9,8},{10,11... | collective-permute-start | bytes 1572872 | tf_op jit(solution)/shard_map/ppermute | solution.py:159
  52.6 1.0 %copy-start.1 = (bf16[512,512]{1,0:T(8,128)(2,1)S(1)}, bf16[512,512]{1,0:T(8,128)(2,1)}, u32[]{:S(2)}) copy-start(bf16[512,512]{1,0:T(8,128)(2,1)} %refs_0_.3) | copy-start | bytes 1572868
  55.1 1.3 %collective-permute-start.1 = (f32[2]{0:T(128)S(1)}, f32[2]{0:T(128)S(1)}, u32[]{:S(2)}, u32[]{:S(2)}) collective-permute-start(f32[2]{0:T(128)S(1)} %slice_reduce_fusion), channel_id=1, source_target_pairs={{0,1},{1,0},{2,3},{3,2},{4,5},{5,4},{6,7},{7,6},{8,9},{9,8},{10,11... | collective-permute-start | bytes 32 | tf_op jit(solution)/shard_map/ppermute | solution.py:139

commit v2 on v0

--- a/solution.py
+++ b/solution.py
@@ -1,17 +1,259 @@
+import functools
 import math
 
 import jax
 import jax.numpy as jnp
 from jax import lax
+from jax.experimental import pallas as pl
+from jax.experimental.pallas import tpu as pltpu
 from jax.sharding import PartitionSpec as P
 
 NOCC = 1024
 BLK = 128
 NBLK = 4
 NB = 512
-
-
-def body(blocks, pattern, occupied, ligand):
+GROUP = 16
+VMEM_LIMIT = 48 * 1024 * 1024
+
+
+def own_half_kernel(place, pattern, blocks, occupied, *refs):
+    outs, masked, (held, panel, turned, sems) = refs[:-5], refs[-5], refs[-4:]
+    aux_rows, _, nu_width = blocks.shape
+    ni = outs[0].shape[1]
+    get_blocks = pltpu.make_async_copy(blocks, held, sems.at[0])
+    get_panel = pltpu.make_async_copy(occupied, panel, sems.at[1])
+    get_blocks.start()
+    get_panel.start()
+    get_blocks.wait()
+    for q in range(aux_rows):
+        for m in range(NBLK):
+            for n in range(nu_width // BLK):
+                rows, columns = pl.ds(m * BLK, BLK), pl.ds(n * BLK, BLK)
+                tile = held[q, rows, columns]
+                keep = pattern[0, m, n] != 0
+                masked[rows, pl.ds(q * nu_width + n * BLK, BLK)] = jnp.where(keep, tile, jnp.zeros_like(tile))
+    get_panel.wait()
+    for s in range(len(outs)):
+        turned[s] = panel[:, s * ni : (s + 1) * ni].T
+    for k, out in enumerate(outs):
+        result = jnp.dot(turned[place[0] ^ k], masked[...], preferred_element_type=jnp.float32).astype(jnp.bfloat16)
+        for q in range(aux_rows):
+            out[q] = result[:, q * nu_width : (q + 1) * nu_width]
+
+
+def other_half_kernel(place, piece, mine, theirs, *refs):
+    outs, turned = refs[:-1], refs[-1]
+    aux_rows, ni, nu_width = outs[0].shape
+    for t in range(piece.shape[1] // ni):
+        turned[t] = piece[:, t * ni : (t + 1) * ni].T
+
+    def emit(out, t, masked):
+        result = jnp.dot(turned[t], masked[...], preferred_element_type=jnp.float32).astype(jnp.bfloat16)
+        for q in range(aux_rows):
+            out[q] = result[:, q * nu_width : (q + 1) * nu_width]
+
+    for k, out in enumerate(outs):
+        m = place[0] ^ k
+        pl.when((m & 1) == place[2])(functools.partial(emit, out, m >> 1, mine))
+        pl.when((m & 1) != place[2])(functools.partial(emit, out, m >> 1, theirs))
+
+
+def density_kernel(place, occupied, piece, *refs):
+    near, far, out = refs[: (len(refs) - 1) // 2], refs[(len(refs) - 1) // 2 : -1], refs[-1]
+    aux_rows, ni, nu_width = near[0].shape
+    eye = lax.broadcasted_iota(jnp.int32, (nu_width, nu_width), 0) == lax.broadcasted_iota(
+        jnp.int32, (nu_width, nu_width), 1
+    )
+    for q in range(aux_rows):
+        total = jnp.zeros((nu_width, nu_width), jnp.float32)
+        for k, message in enumerate(near):
+            s = pl.multiple_of((place[0] ^ k) * ni, ni)
+            total += jnp.dot(occupied[:, pl.ds(s, ni)], message[q], preferred_element_type=jnp.float32)
+        for k, message in enumerate(far):
+            m = place[0] ^ k
+            t, h = pl.multiple_of((m >> 1) * ni, ni), pl.multiple_of((m & 1) * nu_width, nu_width)
+            total += jnp.dot(
+                piece[pl.ds(h, nu_width), pl.ds(t, ni)], message[q], preferred_element_type=jnp.float32
+            )
+        value = jnp.sum(jnp.where(eye, total, 0.0))
+        out[q] = jnp.full(out.shape[1:], value, jnp.float32)
+
+
+def pair_kernel(flip, place, ligand, *refs):
+    arrived, own, sent = refs[:-2], refs[-2], refs[-1]
+    aux_rows, ni, nu_width = arrived[0].shape
+    width = ligand.shape[1]
+    for k, message in enumerate(arrived):
+        part = jnp.dot(
+            message[...].reshape(aux_rows * ni, nu_width), ligand[...], preferred_element_type=jnp.float32
+        ).reshape(aux_rows, ni, width)
+        own[k] = part
+        sent[k ^ flip] = part.astype(jnp.bfloat16)
+
+
+def cross_kernel(scale, *refs):
+    messages, pairs, out = refs[:-5], refs[-5:-1], refs[-1]
+    aux_rows, group, nu_width = messages[0].shape
+    width = out.shape[2]
+    depth = len(messages) * aux_rows * group
+    turned = jnp.concatenate([x[...].reshape(aux_rows * group, nu_width) for x in messages], axis=0).T
+    summed = [pairs[j][...] + pairs[j + 1][...].astype(jnp.float32) for j in (0, 2)]
+    summed = jnp.concatenate([(x * scale).astype(jnp.bfloat16).reshape(-1, group, width) for x in summed], axis=0)
+    row = lax.broadcasted_iota(jnp.int32, (1, group, width), 1)
+    zero = jnp.zeros_like(summed)
+    for i in range(0, group, 2):
+        both = [jnp.where(row == i + e, summed, zero).reshape(depth, width) for e in (0, 1)]
+        result = jnp.dot(turned, jnp.concatenate(both, axis=1), preferred_element_type=jnp.float32)
+        out[i] = result[:, :width]
+        out[i + 1] = result[:, width:]
+
+
+def params():
+    return pltpu.CompilerParams(vmem_limit_bytes=VMEM_LIMIT)
+
+
+def cost(flops, bytes_accessed):
+    return pl.CostEstimate(flops=flops, bytes_accessed=bytes_accessed, transcendentals=0)
+
+
+def whole(shape):
+    return pl.BlockSpec(shape, lambda step, place: (0,) * len(shape))
+
+
+def body(sizes, blocks, pattern, occupied, ligand):
+    n_aux, n_orb, n_ao = sizes
+    aux_rows, _, nu_width = blocks.shape
+    owners = n_aux * n_orb
+    ni = NOCC // owners
+    q_total = aux_rows * owners
+    panel_width = occupied.shape[1]
+    width = ligand.shape[1]
+    aux, orb, ao = (lax.axis_index(name) for name in ("aux", "orb", "ao"))
+    place = jnp.stack([aux, orb, ao]).astype(jnp.int32)
+    axes = ("aux", "orb", "ao")
+
+    def number(a, o, c):
+        return (a * n_orb + o) * n_ao + c
+
+    everyone = [(a, o, c) for a in range(n_aux) for o in range(n_orb) for c in range(n_ao)]
+    swap = [(c, 1 - c) for c in range(n_ao)]
+    half_panel = panel_width // n_ao
+    message = jax.ShapeDtypeStruct((aux_rows, ni, nu_width), jnp.bfloat16)
+    masked_shape = (NB, aux_rows * nu_width)
+
+    piece = lax.ppermute(
+        lax.dynamic_slice_in_dim(occupied, ao * half_panel, half_panel, 1), "orb", [(0, 1), (1, 0)]
+    )
+
+    *near, masked = pl.pallas_call(
+        own_half_kernel,
+        grid_spec=pltpu.PrefetchScalarGridSpec(
+            num_scalar_prefetch=1,
+            grid=(1,),
+            in_specs=[pl.BlockSpec(memory_space=pltpu.SMEM)] + [pl.BlockSpec(memory_space=pltpu.HBM)] * 2,
+            out_specs=[whole(message.shape)] * n_aux + [whole(masked_shape)],
+            scratch_shapes=[
+                pltpu.VMEM(blocks.shape, jnp.bfloat16),
+                pltpu.VMEM(occupied.shape, jnp.bfloat16),
+                pltpu.VMEM((n_aux, ni, NB), jnp.bfloat16),
+                pltpu.SemaphoreType.DMA((2,)),
+            ],
+        ),
+        out_shape=[message] * n_aux + [jax.ShapeDtypeStruct(masked_shape, jnp.bfloat16)],
+        compiler_params=params(),
+        cost_estimate=cost(2 * NB * panel_width * aux_rows * nu_width, 2 << 20),
+        name="own_half",
+    )(place, pattern, blocks, occupied)
+
+    near_here = []
+    for k in range(n_aux):
+        moves = []
+        for a, o, c in everyone:
+            slot = o * n_aux + (a ^ k)
+            moves.append((number(a, o, c), number(slot // n_orb, slot % n_orb, c)))
+        near_here.append(lax.ppermute(near[k], axes, moves))
+    theirs = lax.ppermute(masked, "ao", swap)
+
+    far = pl.pallas_call(
+        other_half_kernel,
+        grid_spec=pltpu.PrefetchScalarGridSpec(
+            num_scalar_prefetch=1,
+            grid=(1,),
+            in_specs=[whole((NB, half_panel)), whole(masked_shape), whole(masked_shape)],
+            out_specs=[whole(message.shape)] * n_aux,
+            scratch_shapes=[pltpu.VMEM((half_panel // ni, ni, NB), jnp.bfloat16)],
+        ),
+        out_shape=[message] * n_aux,
+        compiler_params=params(),
+        cost_estimate=cost(2 * NB * panel_width * aux_rows * nu_width, 2 << 20),
+        name="other_half",
+    )(place, piece, masked, theirs)
+
+    far_here = []
+    for k in range(n_aux):
+        moves = []
+        for a, o, c in everyone:
+            m = a ^ k
+            slot = (1 - o) * n_aux + c * (n_aux // n_ao) + (m >> 1)
+            moves.append((number(a, o, c), number(slot // n_orb, slot % n_orb, m & 1)))
+        far_here.append(lax.ppermute(far[k], axes, moves))
+
+    def pairs_of(flip, arrived, name):
+        shape = (n_aux, aux_rows, ni, width)
+        own, sent = pl.pallas_call(
+            functools.partial(pair_kernel, flip),
+            grid_spec=pltpu.PrefetchScalarGridSpec(
+                num_scalar_prefetch=1,
+                grid=(1,),
+                in_specs=[pl.BlockSpec((nu_width, width), lambda step, place: (place[2], 0))]
+                + [whole(message.shape)] * n_aux,
+                out_specs=[whole(shape)] * 2,
+            ),
+            out_shape=[jax.ShapeDtypeStruct(shape, jnp.float32), jax.ShapeDtypeStruct(shape, jnp.bfloat16)],
+            compiler_params=params(),
+            cost_estimate=cost(q_total * ni * nu_width * width, 2 << 20),
+            name=name,
+        )(place, ligand, *arrived)
+        other = lax.ppermute(sent, "ao", swap)
+        return [x.reshape(n_aux * aux_rows, ni, width) for x in (own, other)]
+
+    near_pairs = pairs_of(0, near_here, "near_pairs")
+    far_pairs = pairs_of(1, far_here, "far_pairs")
+
+    value = pl.pallas_call(
+        density_kernel,
+        grid_spec=pltpu.PrefetchScalarGridSpec(
+            num_scalar_prefetch=1,
+            grid=(1,),
+            in_specs=[
+                pl.BlockSpec((nu_width, panel_width), lambda step, place: (place[2], 0)),
+                whole((NB, half_panel)),
+            ]
+            + [whole(message.shape)] * (2 * n_aux),
+            out_specs=whole((aux_rows, 8, 128)),
+        ),
+        out_shape=jax.ShapeDtypeStruct((aux_rows, 8, 128), jnp.float32),
+        compiler_params=params(),
+        cost_estimate=cost(4 * nu_width * nu_width * aux_rows * NOCC, 2 << 20),
+        name="density_terms",
+    )(place, occupied, piece, *near, *far)[:, 0, 0]
+    density = (value + lax.ppermute(value, "ao", swap)) / math.sqrt(NOCC)
+
+    cross_terms = pl.pallas_call(
+        functools.partial(cross_kernel, 1.0 / math.sqrt(q_total)),
+        grid=(ni // GROUP,),
+        in_specs=[pl.BlockSpec((aux_rows, GROUP, nu_width), lambda g: (0, g, 0))] * owners
+        + [pl.BlockSpec((n_aux * aux_rows, GROUP, width), lambda g: (0, g, 0))] * 4,
+        out_specs=pl.BlockSpec((GROUP, nu_width, width), lambda g: (g, 0, 0)),
+        out_shape=jax.ShapeDtypeStruct((ni, nu_width, width), jnp.float32),
+        compiler_params=params(),
+        cost_estimate=cost(32 * q_total * ni * nu_width * width, 18 << 20),
+        name="cross_terms",
+    )(*near_here, *far_here, *near_pairs, *far_pairs)
+    return (density, cross_terms)
+
+
+def plain_body(blocks, pattern, occupied, ligand):
     panels = lax.all_gather(occupied, "orb", axis=1, tiled=True)
     aux_rows = blocks.shape[0]
     nu_width = blocks.shape[2]
@@ -38,8 +280,10 @@
 
 
 def solution(mesh):
+    sizes = (mesh.shape["aux"], mesh.shape["orb"], mesh.shape["ao"])
+    kernels = sizes == (4, 2, 2)
     return jax.shard_map(
-        body,
+        functools.partial(body, sizes) if kernels else plain_body,
         mesh=mesh,
         in_specs=(
             P(("pose", "aux", "orb"), None, "ao"),

time: 91.2 us -> 63.3 us (0.69)
  waiting for transfers between devices: 45.1 us -> 15.8 us
  starting transfers between devices: 4.64 us -> 25.4 us
  Pallas kernels: 0 us -> 14.5 us
  matrix products: 14 us -> 0 us
  between operations: 14.1 us -> 0.74 us
  blocking collectives: 6.26 us -> 0 us
    ppermute x0 -> x13, starting transfers between devices: none -> 25.4 us  [the longest x4 11.4 us: body(): near_here.append(lax.ppermute(near[k], axes, moves))]
    all_gather x1 -> x0, waiting for transfers between devices: 24.6 us -> none  [body(): panels = lax.all_gather(occupied, 'orb', axis=1, tiled=True)]
    all_to_all x1 -> x0, waiting for transfers between devices: 19.8 us -> none  [body(): lax.all_to_all(transformed, ('aux', 'orb'), split_axis=1, concat_axis=0,...]
    ppermute x0 -> x13, waiting for transfers between devices: none -> 15.8 us  [the longest x4 8.99 us: body(): far_here.append(lax.ppermute(far[k], axes, moves))]
    pallas_call x0 -> x6, Pallas kernels: none -> 14.5 us  [the longest x1 8.01 us: body(): pl.pallas_call(functools.partial(cross_kernel, 1.0 / math.sqrt(q_total)),...]
    dot_general x4 -> x0, matrix products: 14 us -> none  [the longest x1 7.46 us: body(): jnp.einsum('qin,qij->inj', arrived, mixed_pairs, preferred_element_type=j...]
    psum x1 -> x0, blocking collectives: 6.26 us -> none  [body(): density = lax.psum(partial_value, 'ao') / math.sqrt(NOCC)]
    unnamed x3 -> x9, local copies, waits for them, and re-layouts: 0.05 us -> 4.79 us
  transfers between devices with their start and end apart: 2 -> 13, of which waited for: 2 -> 4; matrix products, arithmetic and copies ran while one was open for 8% -> 3% of each run, Pallas kernels for 0% -> 7%
where the time goes in v2:
time: 63.3 us; the launch traced here: 62.9 us
  starting transfers between devices  25.4 us (40%)
  waiting for transfers between devices  15.8 us (25%)
  Pallas kernels  14.5 us (23%)
  local copies, waits for them, and re-layouts  5.86 us (9%)
  between operations  0.74 us (1%)
    ppermute x4, starting transfers between devices, body(): near_here.append(lax.ppermute(near[k], axes, moves))  11.4 us
    ppermute x4, waiting for transfers between devices, body(): far_here.append(lax.ppermute(far[k], axes, moves))  8.99 us
    pallas_call x1, Pallas kernels, body(): pl.pallas_call(functools.partial(cross_kernel, 1.0 / math.sqrt(q_total)),...  8.01 us
    ppermute x4, starting transfers between devices, body(): far_here.append(lax.ppermute(far[k], axes, moves))  7.34 us
    unnamed x9, local copies, waits for them, and re-layouts  4.79 us
    ppermute x2, starting transfers between devices, pairs_of(): other = lax.ppermute(sent, 'ao', swap)  3.57 us
    ppermute x1, waiting for transfers between devices, body(): lax.ppermute(lax.dynamic_slice_in_dim(occupied, ao * half_panel, half_pan...  3.41 us
    ppermute x1, starting transfers between devices, body(): lax.ppermute(lax.dynamic_slice_in_dim(occupied, ao * half_panel, half_pan...  2.57 us
  transfers between devices with their start and end apart: 13, of which 4 were waited for; matrix products, arithmetic and copies ran while one was open for 3% of the time, Pallas kernels for 7%

profile of v2, /device:TPU:0, one launch (start us, length us, event | category | flops | bytes accessed | tf_op | source)
XLA Modules:
  0.0 62.9 jit_solution(849382256724350236)
XLA Ops:
  0.6 0.8 %copy.7.pattern = s32[1,4,2]{2,1,0:T(4,128)S(1)} copy(s32[1,4,2]{1,2,0:T(2,128)} %param.5) | data formatting | bytes 64 | tf_op args[1]
  1.4 0.1 pad_add_fusion.place
  1.5 0.0 copy-start
  1.5 1.0 %copy-done = bf16[512,512]{1,0:T(8,128)(2,1)S(1)} copy-done((bf16[512,512]{1,0:T(8,128)(2,1)S(1)}, bf16[512,512]{1,0:T(8,128)(2,1)}, u32[]{:S(2)}) %copy-start) | copy-done | bytes 524312
  2.5 0.0 copy-start.2
  2.5 1.0 %copy-done.2 = bf16[2,512,256]{2,1,0:T(8,128)(2,1)S(1)} copy-done((bf16[2,512,256]{2,1,0:T(8,128)(2,1)S(1)}, bf16[2,512,256]{2,1,0:T(8,128)(2,1)}, u32[]{:S(2)}) %copy-start.2) | copy-done | bytes 524312
  3.6 1.9 %own_half.1 = (bf16[2,128,256]{2,1,0:T(8,128)(2,1)S(1)}, bf16[2,128,256]{2,1,0:T(8,128)(2,1)S(1)}, bf16[2,128,256]{2,1,0:T(8,128)(2,1)S(1)}, bf16[2,128,256]{2,1,0:T(8,128)(2,1)S(1)}, bf16[512,512]{1,0:T(8,128)(2,1)S(1)}) custom-call(s32[3]{0:T(128)S(1)} %pad_add_fusion.place, s32[1,4,2]{2,1,0:T(4,128)S(1)} %copy.7.pattern, ...), custom_call_target="tpu_custom_call" | custom-call | flops 268435456 | bytes 2097152 | tf_op jit(solution)/shard_map/own_half/pallas_call | solution.py:148
  5.5 0.5 collective-permute-start.1
  6.0 1.0 %constant_dynamic-slice_fusion = bf16[512,256]{1,0:T(8,128)(2,1)S(1)} fusion(bf16[512,512]{1,0:T(8,128)(2,1)} %occupied.3, s32[]{:T(128)S(6)} %select_n.3), kind=kLoop, calls=%fused_computation.3 | loop fusion | bytes 524292 | tf_op jit(solution)/shard_map/dynamic_slice | solution.py:145
  7.0 2.6 %collective-permute-start = (bf16[512,256]{1,0:T(8,128)(2,1)S(1)}, bf16[512,256]{1,0:T(8,128)(2,1)S(1)}, u32[]{:S(2)}, u32[]{:S(2)}) collective-permute-start(bf16[512,256]{1,0:T(8,128)(2,1)S(1)} %constant_dynamic-slice_fusion), channel_id=1, source_target_pairs={{0,2},{2,0},{1,3},{3,1},{4,6},{6,4},{5,7},{7,5},{8,10},{10,8},{9,1... | collective-permute-start | bytes 786440 | tf_op jit(solution)/shard_map/ppermute | solution.py:144
  9.5 0.7 %collective-permute-start.3 = (bf16[2,128,256]{2,1,0:T(8,128)(2,1)S(1)}, bf16[2,128,256]{2,1,0:T(8,128)(2,1)S(1)}, u32[]{:S(2)}, u32[]{:S(2)}) collective-permute-start(bf16[2,128,256]{2,1,0:T(8,128)(2,1)S(1)} %get-tuple-element.15.refs_0_), channel_id=1, source_target_pairs={{0,0},{1,1},{2,8},{3,9},{4,2},{5,3},{6,10},{7,11},{8,4},{9,5},{10,... | collective-permute-start | bytes 393224 | tf_op jit(solution)/shard_map/ppermute | solution.py:174
  10.2 5.3 %collective-permute-start.4 = (bf16[2,128,256]{2,1,0:T(8,128)(2,1)S(1)}, bf16[2,128,256]{2,1,0:T(8,128)(2,1)S(1)}, u32[]{:S(2)}, u32[]{:S(2)}) collective-permute-start(bf16[2,128,256]{2,1,0:T(8,128)(2,1)S(1)} %get-tuple-element.16.refs_1_), channel_id=1, source_target_pairs={{0,2},{1,3},{2,10},{3,11},{4,0},{5,1},{6,8},{7,9},{8,6},{9,7},{10,... | collective-permute-start | bytes 393224 | tf_op jit(solution)/shard_map/ppermute | solution.py:174
  15.6 0.0 collective-permute-start.5
  15.6 3.4 %collective-permute-done.piece = bf16[512,256]{1,0:T(8,128)(2,1)S(1)} collective-permute-done((bf16[512,256]{1,0:T(8,128)(2,1)S(1)}, bf16[512,256]{1,0:T(8,128)(2,1)S(1)}, u32[]{:S(2)}, u32[]{:S(2)}) %collective-permute-start) | collective-permute-done | bytes 262176 | tf_op jit(solution)/shard_map/ppermute | solution.py:144
  19.0 5.4 %collective-permute-start.6 = (bf16[2,128,256]{2,1,0:T(8,128)(2,1)S(1)}, bf16[2,128,256]{2,1,0:T(8,128)(2,1)S(1)}, u32[]{:S(2)}, u32[]{:S(2)}) collective-permute-start(bf16[2,128,256]{2,1,0:T(8,128)(2,1)S(1)} %get-tuple-element.18.refs_3_), channel_id=1, source_target_pairs={{0,6},{1,7},{2,14},{3,15},{4,4},{5,5},{6,12},{7,13},{8,2},{9,3},{1... | collective-permute-start | bytes 393224 | tf_op jit(solution)/shard_map/ppermute | solution.py:174
  24.4 0.0 collective-permute-done.1.theirs
  24.4 1.6 %other_half.1 = (bf16[2,128,256]{2,1,0:T(8,128)(2,1)S(1)}, bf16[2,128,256]{2,1,0:T(8,128)(2,1)S(1)}, bf16[2,128,256]{2,1,0:T(8,128)(2,1)S(1)}, bf16[2,128,256]{2,1,0:T(8,128)(2,1)S(1)}) custom-call(s32[3]{0:T(128)S(1)} %pad_add_fusion.place, bf16[512,256]{1,0:T(8,128)(2,1)S(1)} %collective-permute-done.piece, bf16[512,512]{1,0:T(8,128)(2,1)S(1)} %get-tuple-element.19.mine, ...), custom_call_target="tpu_custom_call" | custom-call | flops 268435456 | bytes 2097152 | tf_op jit(solution)/shard_map/other_half/pallas_call | solution.py:177
  26.0 1.4 %collective-permute-start.7 = (bf16[2,128,256]{2,1,0:T(8,128)(2,1)S(1)}, bf16[2,128,256]{2,1,0:T(8,128)(2,1)S(1)}, u32[]{:S(2)}, u32[]{:S(2)}) collective-permute-start(bf16[2,128,256]{2,1,0:T(8,128)(2,1)S(1)} %get-tuple-element.20.refs_4_), channel_id=1, source_target_pairs={{0,8},{1,12},{2,0},{3,4},{4,9},{5,13},{6,1},{7,5},{8,10},{9,14},{1... | collective-permute-start | bytes 393224 | tf_op jit(solution)/shard_map/ppermute | solution.py:199
  27.4 0.0 collective-permute-done.3.refs_0_
  27.4 1.4 %collective-permute-start.8 = (bf16[2,128,256]{2,1,0:T(8,128)(2,1)S(1)}, bf16[2,128,256]{2,1,0:T(8,128)(2,1)S(1)}, u32[]{:S(2)}, u32[]{:S(2)}) collective-permute-start(bf16[2,128,256]{2,1,0:T(8,128)(2,1)S(1)} %get-tuple-element.21.refs_5_), channel_id=1, source_target_pairs={{0,9},{1,13},{2,1},{3,5},{4,8},{5,12},{6,0},{7,4},{8,11},{9,15},{1... | collective-permute-start | bytes 393224 | tf_op jit(solution)/shard_map/ppermute | solution.py:199
  28.8 0.0 collective-permute-done.4.refs_1_
  28.8 4.5 %collective-permute-start.9 = (bf16[2,128,256]{2,1,0:T(8,128)(2,1)S(1)}, bf16[2,128,256]{2,1,0:T(8,128)(2,1)S(1)}, u32[]{:S(2)}, u32[]{:S(2)}) collective-permute-start(bf16[2,128,256]{2,1,0:T(8,128)(2,1)S(1)} %get-tuple-element.22.refs_6_), channel_id=1, source_target_pairs={{0,10},{1,14},{2,2},{3,6},{4,11},{5,15},{6,3},{7,7},{8,8},{9,12},{... | collective-permute-start | bytes 393224 | tf_op jit(solution)/shard_map/ppermute | solution.py:199
  33.3 2.3 %collective-permute-done.5.refs_2_ = bf16[2,128,256]{2,1,0:T(8,128)(2,1)S(1)} collective-permute-done((bf16[2,128,256]{2,1,0:T(8,128)(2,1)S(1)}, bf16[2,128,256]{2,1,0:T(8,128)(2,1)S(1)}, u32[]{:S(2)}, u32[]{:S(2)}) %collective-permute-start.5) | collective-permute-done | bytes 131104 | tf_op jit(solution)/shard_map/ppermute | solution.py:174
  35.6 0.0 collective-permute-start.10
  35.6 0.0 collective-permute-done.6.refs_3_
  35.6 0.0 copy-start.3
  35.6 0.9 %copy-done.3 = bf16[512,128]{1,0:T(8,128)(2,1)S(1)} copy-done((bf16[512,128]{1,0:T(8,128)(2,1)S(1)}, bf16[512,128]{1,0:T(8,128)(2,1)}, u32[]{:S(2)}) %copy-start.3) | copy-done | bytes 131096
  36.6 0.8 %near_pairs.1 = (f32[4,2,128,128]{3,2,1,0:T(8,128)S(1)}, bf16[4,2,128,128]{3,2,1,0:T(8,128)(2,1)S(1)}) custom-call(s32[3]{0:T(128)S(1)} %pad_add_fusion.place, bf16[512,128]{1,0:T(8,128)(2,1)S(1)} %copy-done.3, bf16[2,128,256]{2,1,0:T(8,128)(2,1)S(1)} %collective-permute-done.3.refs_0_, bf16[2,128,256]{2,1,0:T(8,128)(2,1)S(1)} %collective-permute-done.4.refs_1_, ...), custom_call_target="tpu_custom_call" | custom-call | flops 67108864 | bytes 2097152 | tf_op jit(solution)/shard_map/near_pairs/pallas_call | solution.py:203
  37.4 0.9 %collective-permute-start.11 = (bf16[4,2,128,128]{3,2,1,0:T(8,128)(2,1)S(1)}, bf16[4,2,128,128]{3,2,1,0:T(8,128)(2,1)S(1)}, u32[]{:S(2)}, u32[]{:S(2)}) collective-permute-start(bf16[4,2,128,128]{3,2,1,0:T(8,128)(2,1)S(1)} %get-tuple-element.25), channel_id=1, source_target_pairs={{0,1},{1,0},{2,3},{3,2},{4,5},{5,4},{6,7},{7,6},{8,9},{9,8},{10,11... | collective-permute-start | bytes 786440 | tf_op jit(solution)/shard_map/ppermute | solution.py:217
  38.3 0.0 copy-start.1
  38.3 1.0 %copy-done.1 = bf16[512,512]{1,0:T(8,128)(2,1)S(1)} copy-done((bf16[512,512]{1,0:T(8,128)(2,1)S(1)}, bf16[512,512]{1,0:T(8,128)(2,1)}, u32[]{:S(2)}) %copy-start.1) | copy-done | bytes 524312
  39.3 1.4 %density_terms.1 = f32[2,8,128]{2,1,0:T(8,128)S(1)} custom-call(s32[3]{0:T(128)S(1)} %pad_add_fusion.place, bf16[512,512]{1,0:T(8,128)(2,1)S(1)} %copy-done.1, bf16[512,256]{1,0:T(8,128)(2,1)S(1)} %collective-permute-done.piece, bf16[2,128,256]{2,1,0:T(8,128)(2,1)S(1)} %get-tuple-element.15.refs_0_, bf16[2,128,256]{2,1,0:T(8,128)(2,1)S(1)} %get-tuple-element.16.refs_1_, ...), custom_call_target="tpu_custom_call" | custom-call | flops 536870912 | bytes 2097152 | tf_op jit(solution)/shard_map/density_terms/pallas_call | solution.py:223
  40.7 0.0 collective-permute-done.7.refs_0_.refs_4_
  40.7 0.0 collective-permute-done.8.refs_1_.refs_5_
  40.7 9.0 %collective-permute-done.9.refs_2_.refs_6_ = bf16[2,128,256]{2,1,0:T(8,128)(2,1)S(1)} collective-permute-done((bf16[2,128,256]{2,1,0:T(8,128)(2,1)S(1)}, bf16[2,128,256]{2,1,0:T(8,128)(2,1)S(1)}, u32[]{:S(2)}, u32[]{:S(2)}) %collective-permute-start.9) | collective-permute-done | bytes 131104 | tf_op jit(solution)/shard_map/ppermute | solution.py:199
  49.7 0.0 collective-permute-done.10.refs_3_.refs_7_
  49.7 0.8 %far_pairs.1 = (f32[4,2,128,128]{3,2,1,0:T(8,128)S(1)}, bf16[4,2,128,128]{3,2,1,0:T(8,128)(2,1)S(1)}) custom-call(s32[3]{0:T(128)S(1)} %pad_add_fusion.place, bf16[512,128]{1,0:T(8,128)(2,1)S(1)} %copy-done.3, bf16[2,128,256]{2,1,0:T(8,128)(2,1)S(1)} %collective-permute-done.7.refs_0_.refs_4_, ...), custom_call_target="tpu_custom_call" | custom-call | flops 67108864 | bytes 2097152 | tf_op jit(solution)/shard_map/far_pairs/pallas_call | solution.py:203
  50.5 2.7 %collective-permute-start.12 = (bf16[4,2,128,128]{3,2,1,0:T(8,128)(2,1)S(1)}, bf16[4,2,128,128]{3,2,1,0:T(8,128)(2,1)S(1)}, u32[]{:S(2)}, u32[]{:S(2)}) collective-permute-start(bf16[4,2,128,128]{3,2,1,0:T(8,128)(2,1)S(1)} %get-tuple-element.27), channel_id=1, source_target_pairs={{0,1},{1,0},{2,3},{3,2},{4,5},{5,4},{6,7},{7,6},{8,9},{9,8},{10,11... | collective-permute-start | bytes 786440 | tf_op jit(solution)/shard_map/ppermute | solution.py:217
  53.2 0.1 slice_reduce_fusion
  53.3 0.0 collective-permute-start.2
  53.3 1.1 %collective-permute-done.2 = f32[2]{0:T(128)S(1)} collective-permute-done((f32[2]{0:T(128)S(1)}, f32[2]{0:T(128)S(1)}, u32[]{:S(2)}, u32[]{:S(2)}) %collective-permute-start.2) | collective-permute-done | bytes 40 | tf_op jit(solution)/shard_map/ppermute | solution.py:240
  54.4 0.5 add_multiply_fusion
  54.9 0.0 collective-permute-done.11
  54.9 0.0 collective-permute-done.12
  54.9 8.0 %cross_terms.1 = f32[128,256,128]{2,1,0:T(8,128)} custom-call(bf16[2,128,256]{2,1,0:T(8,128)(2,1)S(1)} %collective-permute-done.3.refs_0_, bf16[2,128,256]{2,1,0:T(8,128)(2,1)S(1)} %collective-permute-done.4.refs_1_, bf16[2,128,256]{2,1,0:T(8,128)(2,1)S(1)} %collective-permute-done.5.refs_2_, bf16[2,128,256]{2,1,0:T(8,128)(2,1)S(1)} %collective-permute-done.6.refs_3_, ...), custom_call_target="tpu_custom_call" | custom-call | flops 2147483648 | bytes 18874368 | tf_op jit(solution)/shard_map/cross_terms/pallas_call | solution.py:242
Async XLA Ops:
  1.5 1.0 %copy-start = (bf16[512,512]{1,0:T(8,128)(2,1)S(1)}, bf16[512,512]{1,0:T(8,128)(2,1)}, u32[]{:S(2)}) copy-start(bf16[512,512]{1,0:T(8,128)(2,1)} %occupied.3) | copy-start | bytes 1572868
  2.5 1.0 %copy-start.2 = (bf16[2,512,256]{2,1,0:T(8,128)(2,1)S(1)}, bf16[2,512,256]{2,1,0:T(8,128)(2,1)}, u32[]{:S(2)}) copy-start(bf16[2,512,256]{2,1,0:T(8,128)(2,1)} %blocks.1) | copy-start | bytes 1572868
  5.5 18.9 %collective-permute-start.1 = (bf16[512,512]{1,0:T(8,128)(2,1)S(1)}, bf16[512,512]{1,0:T(8,128)(2,1)S(1)}, u32[]{:S(2)}, u32[]{:S(2)}) collective-permute-start(bf16[512,512]{1,0:T(8,128)(2,1)S(1)} %get-tuple-element.19.mine), channel_id=1, source_target_pairs={{0,1},{1,0},{2,3},{3,2},{4,5},{5,4},{6,7},{7,6},{8,9},{9,8},{10,11... | collective-permute-start | bytes 1572872 | tf_op jit(solution)/shard_map/ppermute | solution.py:175
  7.0 12.0 %collective-permute-start = (bf16[512,256]{1,0:T(8,128)(2,1)S(1)}, bf16[512,256]{1,0:T(8,128)(2,1)S(1)}, u32[]{:S(2)}, u32[]{:S(2)}) collective-permute-start(bf16[512,256]{1,0:T(8,128)(2,1)S(1)} %constant_dynamic-slice_fusion), channel_id=1, source_target_pairs={{0,2},{2,0},{1,3},{3,1},{4,6},{6,4},{5,7},{7,5},{8,10},{10,8},{9,1... | collective-permute-start | bytes 786440 | tf_op jit(solution)/shard_map/ppermute | solution.py:144
  9.5 17.8 %collective-permute-start.3 = (bf16[2,128,256]{2,1,0:T(8,128)(2,1)S(1)}, bf16[2,128,256]{2,1,0:T(8,128)(2,1)S(1)}, u32[]{:S(2)}, u32[]{:S(2)}) collective-permute-start(bf16[2,128,256]{2,1,0:T(8,128)(2,1)S(1)} %get-tuple-element.15.refs_0_), channel_id=1, source_target_pairs={{0,0},{1,1},{2,8},{3,9},{4,2},{5,3},{6,10},{7,11},{8,4},{9,5},{10,... | collective-permute-start | bytes 393224 | tf_op jit(solution)/shard_map/ppermute | solution.py:174
  10.2 18.6 %collective-permute-start.4 = (bf16[2,128,256]{2,1,0:T(8,128)(2,1)S(1)}, bf16[2,128,256]{2,1,0:T(8,128)(2,1)S(1)}, u32[]{:S(2)}, u32[]{:S(2)}) collective-permute-start(bf16[2,128,256]{2,1,0:T(8,128)(2,1)S(1)} %get-tuple-element.16.refs_1_), channel_id=1, source_target_pairs={{0,2},{1,3},{2,10},{3,11},{4,0},{5,1},{6,8},{7,9},{8,6},{9,7},{10,... | collective-permute-start | bytes 393224 | tf_op jit(solution)/shard_map/ppermute | solution.py:174
  15.6 20.1 %collective-permute-start.5 = (bf16[2,128,256]{2,1,0:T(8,128)(2,1)S(1)}, bf16[2,128,256]{2,1,0:T(8,128)(2,1)S(1)}, u32[]{:S(2)}, u32[]{:S(2)}) collective-permute-start(bf16[2,128,256]{2,1,0:T(8,128)(2,1)S(1)} %get-tuple-element.17.refs_2_), channel_id=1, source_target_pairs={{0,4},{1,5},{2,12},{3,13},{4,6},{5,7},{6,14},{7,15},{8,0},{9,1},{1... | collective-permute-start | bytes 393224 | tf_op jit(solution)/shard_map/ppermute | solution.py:174
  19.0 16.7 %collective-permute-start.6 = (bf16[2,128,256]{2,1,0:T(8,128)(2,1)S(1)}, bf16[2,128,256]{2,1,0:T(8,128)(2,1)S(1)}, u32[]{:S(2)}, u32[]{:S(2)}) collective-permute-start(bf16[2,128,256]{2,1,0:T(8,128)(2,1)S(1)} %get-tuple-element.18.refs_3_), channel_id=1, source_target_pairs={{0,6},{1,7},{2,14},{3,15},{4,4},{5,5},{6,12},{7,13},{8,2},{9,3},{1... | collective-permute-start | bytes 393224 | tf_op jit(solution)/shard_map/ppermute | solution.py:174
  26.0 14.7 %collective-permute-start.7 = (bf16[2,128,256]{2,1,0:T(8,128)(2,1)S(1)}, bf16[2,128,256]{2,1,0:T(8,128)(2,1)S(1)}, u32[]{:S(2)}, u32[]{:S(2)}) collective-permute-start(bf16[2,128,256]{2,1,0:T(8,128)(2,1)S(1)} %get-tuple-element.20.refs_4_), channel_id=1, source_target_pairs={{0,8},{1,12},{2,0},{3,4},{4,9},{5,13},{6,1},{7,5},{8,10},{9,14},{1... | collective-permute-start | bytes 393224 | tf_op jit(solution)/shard_map/ppermute | solution.py:199
  27.4 13.3 %collective-permute-start.8 = (bf16[2,128,256]{2,1,0:T(8,128)(2,1)S(1)}, bf16[2,128,256]{2,1,0:T(8,128)(2,1)S(1)}, u32[]{:S(2)}, u32[]{:S(2)}) collective-permute-start(bf16[2,128,256]{2,1,0:T(8,128)(2,1)S(1)} %get-tuple-element.21.refs_5_), channel_id=1, source_target_pairs={{0,9},{1,13},{2,1},{3,5},{4,8},{5,12},{6,0},{7,4},{8,11},{9,15},{1... | collective-permute-start | bytes 393224 | tf_op jit(solution)/shard_map/ppermute | solution.py:199
  28.8 20.9 %collective-permute-start.9 = (bf16[2,128,256]{2,1,0:T(8,128)(2,1)S(1)}, bf16[2,128,256]{2,1,0:T(8,128)(2,1)S(1)}, u32[]{:S(2)}, u32[]{:S(2)}) collective-permute-start(bf16[2,128,256]{2,1,0:T(8,128)(2,1)S(1)} %get-tuple-element.22.refs_6_), channel_id=1, source_target_pairs={{0,10},{1,14},{2,2},{3,6},{4,11},{5,15},{6,3},{7,7},{8,8},{9,12},{... | collective-permute-start | bytes 393224 | tf_op jit(solution)/shard_map/ppermute | solution.py:199
  35.6 14.0 %collective-permute-start.10 = (bf16[2,128,256]{2,1,0:T(8,128)(2,1)S(1)}, bf16[2,128,256]{2,1,0:T(8,128)(2,1)S(1)}, u32[]{:S(2)}, u32[]{:S(2)}) collective-permute-start(bf16[2,128,256]{2,1,0:T(8,128)(2,1)S(1)} %get-tuple-element.23.refs_7_), channel_id=1, source_target_pairs={{0,11},{1,15},{2,3},{3,7},{4,10},{5,14},{6,2},{7,6},{8,9},{9,13},{... | collective-permute-start | bytes 393224 | tf_op jit(solution)/shard_map/ppermute | solution.py:199
  35.6 0.9 %copy-start.3 = (bf16[512,128]{1,0:T(8,128)(2,1)S(1)}, bf16[512,128]{1,0:T(8,128)(2,1)}, u32[]{:S(2)}) copy-start(bf16[512,128]{1,0:T(8,128)(2,1)} %ligand.3) | copy-start | bytes 393220
  37.4 17.6 %collective-permute-start.11 = (bf16[4,2,128,128]{3,2,1,0:T(8,128)(2,1)S(1)}, bf16[4,2,128,128]{3,2,1,0:T(8,128)(2,1)S(1)}, u32[]{:S(2)}, u32[]{:S(2)}) collective-permute-start(bf16[4,2,128,128]{3,2,1,0:T(8,128)(2,1)S(1)} %get-tuple-element.25), channel_id=1, source_target_pairs={{0,1},{1,0},{2,3},{3,2},{4,5},{5,4},{6,7},{7,6},{8,9},{9,8},{10,11... | collective-permute-start | bytes 786440 | tf_op jit(solution)/shard_map/ppermute | solution.py:217
  38.3 1.0 %copy-start.1 = (bf16[512,512]{1,0:T(8,128)(2,1)S(1)}, bf16[512,512]{1,0:T(8,128)(2,1)}, u32[]{:S(2)}) copy-start(bf16[512,512]{1,0:T(8,128)(2,1)} %occupied.3) | copy-start | bytes 1572868
  50.5 4.4 %collective-permute-start.12 = (bf16[4,2,128,128]{3,2,1,0:T(8,128)(2,1)S(1)}, bf16[4,2,128,128]{3,2,1,0:T(8,128)(2,1)S(1)}, u32[]{:S(2)}, u32[]{:S(2)}) collective-permute-start(bf16[4,2,128,128]{3,2,1,0:T(8,128)(2,1)S(1)} %get-tuple-element.27), channel_id=1, source_target_pairs={{0,1},{1,0},{2,3},{3,2},{4,5},{5,4},{6,7},{7,6},{8,9},{9,8},{10,11... | collective-permute-start | bytes 786440 | tf_op jit(solution)/shard_map/ppermute | solution.py:217
  53.3 1.1 %collective-permute-start.2 = (f32[2]{0:T(128)S(1)}, f32[2]{0:T(128)S(1)}, u32[]{:S(2)}, u32[]{:S(2)}) collective-permute-start(f32[2]{0:T(128)S(1)} %slice_reduce_fusion), channel_id=1, source_target_pairs={{0,1},{1,0},{2,3},{3,2},{4,5},{5,4},{6,7},{7,6},{8,9},{9,8},{10,11... | collective-permute-start | bytes 32 | tf_op jit(solution)/shard_map/ppermute | solution.py:240

commit v3 on v0

--- a/solution.py
+++ b/solution.py
@@ -1,17 +1,244 @@
+import functools
 import math
 
 import jax
 import jax.numpy as jnp
 from jax import lax
+from jax.experimental import pallas as pl
+from jax.experimental.pallas import tpu as pltpu
 from jax.sharding import PartitionSpec as P
 
 NOCC = 1024
 BLK = 128
 NBLK = 4
 NB = 512
-
-
-def body(blocks, pattern, occupied, ligand):
+GROUP = 16
+MIB = 1024 * 1024
+SMEM = pl.BlockSpec(memory_space=pltpu.SMEM)
+VMEM = pl.BlockSpec(memory_space=pltpu.VMEM)
+
+
+def spread_kernel(pattern, blocks, occupied, ligand, *refs):
+    parts, (panel, orbitals, held, opened, sems) = refs[:-5], refs[-5:]
+    nu_width = blocks.shape[2]
+    moves = ((blocks, held), (pattern, opened), (occupied, panel), (ligand, orbitals))
+    copies = [pltpu.make_async_copy(source, target, sems.at[k]) for k, (source, target) in enumerate(moves)]
+    for copy in copies:
+        copy.start()
+    copies[0].wait()
+    copies[1].wait()
+    for q, part in enumerate(parts):
+        for m in range(NBLK):
+            for n in range(nu_width // BLK):
+                rows, columns = pl.ds(m * BLK, BLK), pl.ds(n * BLK, BLK)
+                tile = held[q, rows, columns]
+                part[0, rows, columns] = jnp.where(opened[0, n, m] != 0, tile, jnp.zeros_like(tile))
+    for copy in copies[2:]:
+        copy.wait()
+
+
+def slot_of(place, d):
+    return (2 * (place[0] & 1) + place[1]) ^ d
+
+
+def half_into(outs, place, turned, parts):
+    for d, out in enumerate(outs):
+        rows = turned[slot_of(place, d)]
+        for q, masked in enumerate(parts):
+            out[q] = jnp.dot(rows, masked[0], preferred_element_type=jnp.float32).astype(jnp.bfloat16)
+
+
+def own_kernel(place, occupied, other, *refs):
+    parts, turned, outs = refs[:-5], refs[-5], refs[-4:]
+    ni = turned.shape[1]
+    near = place[1] == place[0] // 2
+
+    def turn(panel):
+        for s in range(turned.shape[0]):
+            turned[s] = panel[:, s * ni : (s + 1) * ni].T
+
+    pl.when(near)(functools.partial(turn, occupied))
+    pl.when(jnp.logical_not(near))(functools.partial(turn, other))
+    half_into(outs, place, turned, parts)
+
+
+def part_kernel(place, masked, turned, *outs):
+    half_into(outs, place, turned, [masked])
+
+
+def density_kernel(place, turned, *refs):
+    messages, out = refs[:-1], refs[-1]
+    nu_width = messages[0].shape[2]
+    first = pl.multiple_of(place[2] * nu_width, nu_width)
+    row = 0
+    for group in range(0, len(messages), 4):
+        for q in range(messages[group].shape[0]):
+            total = 0.0
+            for d in range(4):
+                rows = turned[slot_of(place, d), :, pl.ds(first, nu_width)].astype(jnp.float32)
+                total += jnp.sum(rows * messages[group + d][q].astype(jnp.float32))
+            out[row : row + 1, :] = jnp.full((1, out.shape[1]), total, jnp.float32)
+            row += 1
+
+
+def pair_kernel(place, ligand, *refs):
+    arrived, own, sent = refs[:-2], refs[-2], refs[-1]
+    aux_rows, ni, nu_width = arrived[0].shape
+    width = ligand.shape[1]
+    rows = ligand[pl.ds(pl.multiple_of(place[2] * nu_width, nu_width), nu_width), :]
+    for k, message in enumerate(arrived):
+        part = jnp.dot(
+            message[...].reshape(aux_rows * ni, nu_width), rows, preferred_element_type=jnp.float32
+        ).reshape(aux_rows, ni, width)
+        own[k * aux_rows : (k + 1) * aux_rows] = part
+        sent[k * aux_rows : (k + 1) * aux_rows] = part.astype(jnp.bfloat16)
+
+
+def cross_kernel(scale, *refs):
+    messages, pairs, (out, held, sem) = refs[:12], refs[12:18], refs[18:]
+    nu_width = messages[0].shape[2]
+    ni, _, width = out.shape
+
+    def step(g, carry):
+        here = pl.ds(pl.multiple_of(g * GROUP, GROUP), GROUP)
+        rows = [x[:, here, :].reshape(-1, nu_width) for x in messages]
+        turned = jnp.concatenate(rows, axis=0).T
+        summed = [pairs[j][:, here, :] + pairs[j + 1][:, here, :].astype(jnp.float32) for j in (0, 2, 4)]
+        summed = jnp.concatenate([(x * scale).astype(jnp.bfloat16) for x in summed], axis=0)
+        row = lax.broadcasted_iota(jnp.int32, (1, GROUP, width), 1)
+        zero = jnp.zeros_like(summed)
+        for i in range(0, GROUP, 2):
+            both = [jnp.where(row == i + e, summed, zero).reshape(-1, width) for e in (0, 1)]
+            result = jnp.dot(turned, jnp.concatenate(both, axis=1), preferred_element_type=jnp.float32)
+            held[g * GROUP + i] = result[:, :width]
+            held[g * GROUP + i + 1] = result[:, width:]
+            if i % 4 == 2:
+                done = pl.ds(g * GROUP + i - 2, 4)
+                pltpu.make_async_copy(held.at[done], out.at[done], sem).start()
+        return carry
+
+    lax.fori_loop(0, ni // GROUP, step, 0)
+    pltpu.make_async_copy(held, out, sem).wait()
+
+
+def call(kernel, name, inputs, outputs, scratch=(), limit=16, scalars=1, flops=0, moved=1 << 20, in_spec=VMEM, out_spec=VMEM):
+    inputs = list(inputs)
+    results = pl.pallas_call(
+        kernel,
+        in_specs=[SMEM] * scalars + [in_spec] * (len(inputs) - scalars),
+        out_specs=[out_spec] * len(outputs),
+        out_shape=outputs,
+        scratch_shapes=list(scratch),
+        compiler_params=pltpu.CompilerParams(vmem_limit_bytes=limit * MIB),
+        cost_estimate=pl.CostEstimate(flops=flops, bytes_accessed=moved, transcendentals=0),
+        name=name,
+    )(*inputs)
+    return list(results)
+
+
+def body(sizes, blocks, pattern, occupied, ligand):
+    n_aux, n_orb, n_ao = sizes
+    aux_rows, _, nu_width = blocks.shape
+    owners = n_aux * n_orb
+    ni = NOCC // owners
+    q_total = aux_rows * owners
+    panel_width = occupied.shape[1]
+    width = ligand.shape[1]
+    place = jnp.stack([lax.axis_index(name) for name in ("aux", "orb", "ao")]).astype(jnp.int32)
+    bf16 = functools.partial(jax.ShapeDtypeStruct, dtype=jnp.bfloat16)
+    f32 = functools.partial(jax.ShapeDtypeStruct, dtype=jnp.float32)
+
+    across = [(a, a ^ 2) for a in range(n_aux)]
+    swap = [(c, 1 - c) for c in range(n_ao)]
+    pattern = jnp.swapaxes(pattern, 1, 2)
+    *parts, panel, orbitals = call(
+        spread_kernel,
+        "masked_blocks",
+        (pltpu.with_memory_space_constraint(x, pltpu.HBM) for x in (pattern, blocks, occupied, ligand)),
+        [bf16((1, NB, nu_width))] * aux_rows + [bf16(occupied.shape), bf16(ligand.shape)],
+        [
+            pltpu.VMEM(blocks.shape, jnp.bfloat16),
+            pltpu.SMEM(pattern.shape, pattern.dtype),
+            pltpu.SemaphoreType.DMA((4,)),
+        ],
+        scalars=0,
+        in_spec=pl.BlockSpec(memory_space=pltpu.HBM),
+    )
+    far = [lax.ppermute(x, "aux", across) for x in parts]
+    fetch = [(a * n_orb + a // 2, a * n_orb + 1 - a // 2) for a in range(n_aux)]
+    other = lax.ppermute(panel, ("aux", "orb"), fetch)
+
+    def square(messages):
+        arrived = [messages[0]] + [None] * 3
+        for d in (3, 2, 1):
+            moves = [
+                (a * n_orb + o, (a ^ (d >> 1)) * n_orb + (o ^ (d & 1))) for a in range(n_aux) for o in range(n_orb)
+            ]
+            arrived[d] = lax.ppermute(messages[d], ("aux", "orb"), moves)
+        return arrived
+
+    work = 2 * NB * panel_width * nu_width
+    turned, *own = call(
+        own_kernel,
+        "own_half",
+        (place, panel, other, *parts),
+        [bf16((4, ni, NB))] + [bf16((aux_rows, ni, nu_width))] * 4,
+        flops=work * aux_rows,
+    )
+    sent = [own]
+    arrived = [square(own)]
+    for q in range(aux_rows):
+        messages = call(
+            part_kernel,
+            f"part_half_{q}",
+            (place, far[q], turned),
+            [bf16((1, ni, nu_width))] * 4,
+            flops=work,
+        )
+        sent.append(messages)
+        arrived.append(square(messages))
+
+    value = call(
+        density_kernel,
+        "density_terms",
+        (place, turned, *sum(sent, [])),
+        [f32((2 * aux_rows, 128))],
+        flops=8 * panel_width * nu_width * aux_rows,
+    )[0]
+    near = value[:aux_rows, 0] + lax.ppermute(value, "ao", swap)[:aux_rows, 0]
+    crossing = [(a * n_ao + c, (a ^ 2) * n_ao + 1 - c) for a in range(n_aux) for c in range(n_ao)]
+    back = lax.ppermute(value, "aux", across)[aux_rows:, 0] + lax.ppermute(value, ("aux", "ao"), crossing)[aux_rows:, 0]
+    density = (near + back) / math.sqrt(NOCC)
+
+    pairs = []
+    for k, group in enumerate(arrived):
+        shape = (4 * group[0].shape[0], ni, width)
+        kept, given = call(
+            pair_kernel,
+            f"pair_terms_{k}",
+            (place, orbitals, *group),
+            [f32(shape), bf16(shape)],
+            flops=2 * shape[0] * ni * nu_width * width,
+        )
+        pairs += [kept, lax.ppermute(given, "ao", swap)]
+
+    result = (ni, nu_width, width)
+    cross_terms = call(
+        functools.partial(cross_kernel, 1.0 / math.sqrt(q_total)),
+        "cross_terms",
+        (*sum(arrived, []), *pairs),
+        [f32(result)],
+        [pltpu.VMEM(result, jnp.float32), pltpu.SemaphoreType.DMA],
+        limit=32,
+        scalars=0,
+        flops=32 * q_total * ni * nu_width * width,
+        moved=18 * MIB,
+        out_spec=pl.BlockSpec(memory_space=pltpu.HBM),
+    )[0]
+    return (density, cross_terms)
+
+
+def plain_body(blocks, pattern, occupied, ligand):
     panels = lax.all_gather(occupied, "orb", axis=1, tiled=True)
     aux_rows = blocks.shape[0]
     nu_width = blocks.shape[2]
@@ -38,8 +265,10 @@
 
 
 def solution(mesh):
+    sizes = (mesh.shape["aux"], mesh.shape["orb"], mesh.shape["ao"])
+    kernels = sizes == (4, 2, 2)
     return jax.shard_map(
-        body,
+        functools.partial(body, sizes) if kernels else plain_body,
         mesh=mesh,
         in_specs=(
             P(("pose", "aux", "orb"), None, "ao"),

time: 91.2 us -> 64 us (0.70)
  waiting for transfers between devices: 45.1 us -> 28 us
  starting transfers between devices: 4.64 us -> 20.9 us
  matrix products: 14 us -> 0 us
  Pallas kernels: 0 us -> 13.5 us
  between operations: 14.1 us -> 0.76 us
  blocking collectives: 6.26 us -> 0 us
  local copies, waits for them, and re-layouts: 5.49 us -> 0 us
    ppermute x0 -> x18, waiting for transfers between devices: none -> 28 us  [the longest x9 11.9 us: square(): arrived[d] = lax.ppermute(messages[d], ('aux', 'orb'), moves)]
    all_gather x1 -> x0, waiting for transfers between devices: 24.6 us -> none  [body(): panels = lax.all_gather(occupied, 'orb', axis=1, tiled=True)]
    ppermute x0 -> x18, starting transfers between devices: none -> 20.9 us  [the longest x9 9.29 us: square(): arrived[d] = lax.ppermute(messages[d], ('aux', 'orb'), moves)]
    all_to_all x1 -> x0, waiting for transfers between devices: 19.8 us -> none  [body(): lax.all_to_all(transformed, ('aux', 'orb'), split_axis=1, concat_axis=0,...]
    dot_general x4 -> x0, matrix products: 14 us -> none  [the longest x1 7.46 us: body(): jnp.einsum('qin,qij->inj', arrived, mixed_pairs, preferred_element_type=j...]
    pallas_call x0 -> x9, Pallas kernels: none -> 13.5 us  [call(): pl.pallas_call(kernel, in_specs=[SMEM] * scalars + [in_spec] * (len(input...]
    psum x1 -> x0, blocking collectives: 6.26 us -> none  [body(): density = lax.psum(partial_value, 'ao') / math.sqrt(NOCC)]
    all_to_all x1 -> x0, starting transfers between devices: 4.61 us -> none  [body(): lax.all_to_all(transformed, ('aux', 'orb'), split_axis=1, concat_axis=0,...]
  transfers between devices with their start and end apart: 2 -> 18, of which waited for: 2 -> 9; matrix products, arithmetic and copies ran while one was open for 8% -> 1% of each run, Pallas kernels for 0% -> 10%
where the time goes in v3:
time: 64 us; the launch traced here: 63.9 us
  waiting for transfers between devices  28 us (44%)
  starting transfers between devices  20.9 us (33%)
  Pallas kernels  13.5 us (21%)
  between operations  0.76 us (1%)
  other arithmetic  0.71 us (1%)
    pallas_call x9, Pallas kernels, call(): pl.pallas_call(kernel, in_specs=[SMEM] * scalars + [in_spec] * (len(input...  13.5 us
    ppermute x9, waiting for transfers between devices, square(): arrived[d] = lax.ppermute(messages[d], ('aux', 'orb'), moves)  11.9 us
    ppermute x9, starting transfers between devices, square(): arrived[d] = lax.ppermute(messages[d], ('aux', 'orb'), moves)  9.29 us
    ppermute x1, waiting for transfers between devices, body(): other = lax.ppermute(panel, ('aux', 'orb'), fetch)  8.06 us
    ppermute x1, starting transfers between devices, body(): other = lax.ppermute(panel, ('aux', 'orb'), fetch)  4.88 us
    ppermute x2, waiting for transfers between devices, body(): far = [lax.ppermute(x, 'aux', across) for x in parts]  4.78 us
    ppermute x2, starting transfers between devices, body(): far = [lax.ppermute(x, 'aux', across) for x in parts]  2.99 us
    ppermute x1, waiting for transfers between devices, body(): lax.ppermute(value, 'aux', across)[aux_rows:, 0]  2.32 us
  transfers between devices with their start and end apart: 18, of which 9 were waited for; matrix products, arithmetic and copies ran while one was open for 1% of the time, Pallas kernels for 10%

profile of v3, /device:TPU:0, one launch (start us, length us, event | category | flops | bytes accessed | tf_op | source)
XLA Modules:
  0.0 63.9 jit_solution(6631592165127976454)
XLA Ops:
  0.6 1.3 %masked_blocks.1 = (bf16[1,512,256]{2,1,0:T(8,128)(2,1)S(1)}, bf16[1,512,256]{2,1,0:T(8,128)(2,1)S(1)}, bf16[512,512]{1,0:T(8,128)(2,1)S(1)}, bf16[512,128]{1,0:T(8,128)(2,1)S(1)}) custom-call(s32[1,2,4]{2,1,0:T(2,128)} %bitcast.4, bf16[2,512,256]{2,1,0:T(8,128)(2,1)} %blocks.1, bf16[512,512]{1,0:T(8,128)(2,1)} %occupied.1, bf16[512,128]{1,0:T(8,128)(2,1)} %ligand.1), custom_call_target="tpu_custom_call" | custom-call | bytes 1048576 | tf_op jit(solution)/shard_map/masked_blocks/pallas_call | solution.py:126
  1.9 4.9 %collective-permute-start = (bf16[512,512]{1,0:T(8,128)(2,1)S(1)}, bf16[512,512]{1,0:T(8,128)(2,1)S(1)}, u32[]{:S(2)}, u32[]{:S(2)}) collective-permute-start(bf16[512,512]{1,0:T(8,128)(2,1)S(1)} %get-tuple-element.25.occupied), channel_id=1, source_target_pairs={{0,2},{4,6},{10,8},{14,12},{1,3},{5,7},{11,9},{15,13},{16,18},{20,... | collective-permute-start | bytes 1572872 | tf_op jit(solution)/shard_map/ppermute | solution.py:169
  6.8 0.5 collective-permute-start.2
  7.3 2.5 %collective-permute-start.1 = (bf16[1,512,256]{2,1,0:T(8,128)(2,1)S(1)}, bf16[1,512,256]{2,1,0:T(8,128)(2,1)S(1)}, u32[]{:S(2)}, u32[]{:S(2)}) collective-permute-start(bf16[1,512,256]{2,1,0:T(8,128)(2,1)S(1)} %get-tuple-element.26.refs_0_), channel_id=1, source_target_pairs={{0,8},{4,12},{8,0},{12,4},{1,9},{5,13},{9,1},{13,5},{2,10},{6,14},... | collective-permute-start | bytes 786440 | tf_op jit(solution)/shard_map/ppermute | solution.py:167
  9.8 0.1 pad_add_fusion.place
  9.8 8.1 %collective-permute-done.other = bf16[512,512]{1,0:T(8,128)(2,1)S(1)} collective-permute-done((bf16[512,512]{1,0:T(8,128)(2,1)S(1)}, bf16[512,512]{1,0:T(8,128)(2,1)S(1)}, u32[]{:S(2)}, u32[]{:S(2)}) %collective-permute-start) | collective-permute-done | bytes 524320 | tf_op jit(solution)/shard_map/ppermute | solution.py:169
  17.9 1.2 %own_half.1 = (bf16[4,128,512]{2,1,0:T(8,128)(2,1)S(1)}, bf16[2,128,256]{2,1,0:T(8,128)(2,1)S(1)}, bf16[2,128,256]{2,1,0:T(8,128)(2,1)S(1)}, bf16[2,128,256]{2,1,0:T(8,128)(2,1)S(1)}, bf16[2,128,256]{2,1,0:T(8,128)(2,1)S(1)}) custom-call(s32[3]{0:T(128)S(1)} %pad_add_fusion.place, bf16[512,512]{1,0:T(8,128)(2,1)S(1)} %get-tuple-element.25.occupied, ...), custom_call_target="tpu_custom_call" | custom-call | flops 268435456 | bytes 1048576 | tf_op jit(solution)/shard_map/own_half/pallas_call | solution.py:126
  19.1 2.5 %collective-permute-start.6 = (bf16[2,128,256]{2,1,0:T(8,128)(2,1)S(1)}, bf16[2,128,256]{2,1,0:T(8,128)(2,1)S(1)}, u32[]{:S(2)}, u32[]{:S(2)}) collective-permute-start(bf16[2,128,256]{2,1,0:T(8,128)(2,1)S(1)} %get-tuple-element.30.refs_1_), channel_id=1, source_target_pairs={{0,2},{2,0},{4,6},{6,4},{8,10},{10,8},{12,14},{14,12},{1,3},{3,1},... | collective-permute-start | bytes 393224 | tf_op jit(solution)/shard_map/ppermute | solution.py:177
  21.6 1.6 %collective-permute-start.7 = (bf16[2,128,256]{2,1,0:T(8,128)(2,1)S(1)}, bf16[2,128,256]{2,1,0:T(8,128)(2,1)S(1)}, u32[]{:S(2)}, u32[]{:S(2)}) collective-permute-start(bf16[2,128,256]{2,1,0:T(8,128)(2,1)S(1)} %get-tuple-element.31.refs_2_), channel_id=1, source_target_pairs={{0,4},{2,6},{4,0},{6,2},{8,12},{10,14},{12,8},{14,10},{1,5},{3,7},... | collective-permute-start | bytes 393224 | tf_op jit(solution)/shard_map/ppermute | solution.py:177
  23.2 0.0 collective-permute-start.8
  23.2 4.8 %collective-permute-done.2.masked = bf16[1,512,256]{2,1,0:T(8,128)(2,1)S(1)} collective-permute-done((bf16[1,512,256]{2,1,0:T(8,128)(2,1)S(1)}, bf16[1,512,256]{2,1,0:T(8,128)(2,1)S(1)}, u32[]{:S(2)}, u32[]{:S(2)}) %collective-permute-start.2) | collective-permute-done | bytes 262176 | tf_op jit(solution)/shard_map/ppermute | solution.py:167
  28.0 0.8 %part_half_1.1 = (bf16[1,128,256]{2,1,0:T(8,128)(2,1)S(1)}, bf16[1,128,256]{2,1,0:T(8,128)(2,1)S(1)}, bf16[1,128,256]{2,1,0:T(8,128)(2,1)S(1)}, bf16[1,128,256]{2,1,0:T(8,128)(2,1)S(1)}) custom-call(s32[3]{0:T(128)S(1)} %pad_add_fusion.place, bf16[1,512,256]{2,1,0:T(8,128)(2,1)S(1)} %collective-permute-done.2.masked, ...), custom_call_target="tpu_custom_call" | custom-call | flops 134217728 | bytes 1048576 | tf_op jit(solution)/shard_map/part_half_1/pallas_call | solution.py:126
  28.9 0.5 collective-permute-start.12
  29.4 0.0 collective-permute-done.6.refs_1_
  29.4 0.0 collective-permute-start.13
  29.4 5.9 %collective-permute-done.7.refs_2_ = bf16[2,128,256]{2,1,0:T(8,128)(2,1)S(1)} collective-permute-done((bf16[2,128,256]{2,1,0:T(8,128)(2,1)S(1)}, bf16[2,128,256]{2,1,0:T(8,128)(2,1)S(1)}, u32[]{:S(2)}, u32[]{:S(2)}) %collective-permute-start.7) | collective-permute-done | bytes 131104 | tf_op jit(solution)/shard_map/ppermute | solution.py:177
  35.3 2.7 %collective-permute-done.8.refs_3_ = bf16[2,128,256]{2,1,0:T(8,128)(2,1)S(1)} collective-permute-done((bf16[2,128,256]{2,1,0:T(8,128)(2,1)S(1)}, bf16[2,128,256]{2,1,0:T(8,128)(2,1)S(1)}, u32[]{:S(2)}, u32[]{:S(2)}) %collective-permute-start.8) | collective-permute-done | bytes 131104 | tf_op jit(solution)/shard_map/ppermute | solution.py:177
  38.0 0.8 %pair_terms_0.1 = (f32[8,128,128]{2,1,0:T(8,128)S(1)}, bf16[8,128,128]{2,1,0:T(8,128)(2,1)S(1)}) custom-call(s32[3]{0:T(128)S(1)} %pad_add_fusion.place, bf16[512,128]{1,0:T(8,128)(2,1)S(1)} %get-tuple-element.41.ligand, bf16[2,128,256]{2,1,0:T(8,128)(2,1)S(1)} %get-tuple-element.29.refs_0_, bf16[2,128,256]{2,1,0:T(8,128)(2,1)S(1)} %collective-permute-done.6.refs_1_, ...), custom_call_target="tpu_custom_call" | custom-call | flops 67108864 | bytes 1048576 | tf_op jit(solution)/shard_map/pair_terms_0/pallas_call | solution.py:126
  38.8 0.1 collective-permute-start.15
  38.9 0.1 collective-permute-start.14
  39.0 0.0 collective-permute-done.1.masked
  39.0 0.8 %part_half_0.1 = (bf16[1,128,256]{2,1,0:T(8,128)(2,1)S(1)}, bf16[1,128,256]{2,1,0:T(8,128)(2,1)S(1)}, bf16[1,128,256]{2,1,0:T(8,128)(2,1)S(1)}, bf16[1,128,256]{2,1,0:T(8,128)(2,1)S(1)}) custom-call(s32[3]{0:T(128)S(1)} %pad_add_fusion.place, bf16[1,512,256]{2,1,0:T(8,128)(2,1)S(1)} %collective-permute-done.1.masked, ...), custom_call_target="tpu_custom_call" | custom-call | flops 134217728 | bytes 1048576 | tf_op jit(solution)/shard_map/part_half_0/pallas_call | solution.py:126
  39.8 1.6 %collective-permute-start.9 = (bf16[1,128,256]{2,1,0:T(8,128)(2,1)S(1)}, bf16[1,128,256]{2,1,0:T(8,128)(2,1)S(1)}, u32[]{:S(2)}, u32[]{:S(2)}) collective-permute-start(bf16[1,128,256]{2,1,0:T(8,128)(2,1)S(1)} %get-tuple-element.34.refs_5_), channel_id=1, source_target_pairs={{0,2},{2,0},{4,6},{6,4},{8,10},{10,8},{12,14},{14,12},{1,3},{3,1},... | collective-permute-start | bytes 196616 | tf_op jit(solution)/shard_map/ppermute | solution.py:177
  41.5 0.0 collective-permute-done.12.refs_1_.refs_9_
  41.5 1.9 %collective-permute-start.10 = (bf16[1,128,256]{2,1,0:T(8,128)(2,1)S(1)}, bf16[1,128,256]{2,1,0:T(8,128)(2,1)S(1)}, u32[]{:S(2)}, u32[]{:S(2)}) collective-permute-start(bf16[1,128,256]{2,1,0:T(8,128)(2,1)S(1)} %get-tuple-element.35.refs_6_), channel_id=1, source_target_pairs={{0,4},{2,6},{4,0},{6,2},{8,12},{10,14},{12,8},{14,10},{1,5},{3,7},... | collective-permute-start | bytes 196616 | tf_op jit(solution)/shard_map/ppermute | solution.py:177
  43.4 0.0 collective-permute-done.13.refs_2_.refs_10_
  43.4 1.0 %collective-permute-start.11 = (bf16[1,128,256]{2,1,0:T(8,128)(2,1)S(1)}, bf16[1,128,256]{2,1,0:T(8,128)(2,1)S(1)}, u32[]{:S(2)}, u32[]{:S(2)}) collective-permute-start(bf16[1,128,256]{2,1,0:T(8,128)(2,1)S(1)} %get-tuple-element.36.refs_7_), channel_id=1, source_target_pairs={{0,6},{2,4},{4,2},{6,0},{8,14},{10,12},{12,10},{14,8},{1,7},{3,5},... | collective-permute-start | bytes 196616 | tf_op jit(solution)/shard_map/ppermute | solution.py:177
  44.4 0.0 collective-permute-done.14.refs_3_.refs_11_
  44.4 0.8 %pair_terms_2.1 = (f32[4,128,128]{2,1,0:T(8,128)S(1)}, bf16[4,128,128]{2,1,0:T(8,128)(2,1)S(1)}) custom-call(s32[3]{0:T(128)S(1)} %pad_add_fusion.place, bf16[512,128]{1,0:T(8,128)(2,1)S(1)} %get-tuple-element.41.ligand, bf16[1,128,256]{2,1,0:T(8,128)(2,1)S(1)} %get-tuple-element.37.refs_8_.refs_0_, ...), custom_call_target="tpu_custom_call" | custom-call | flops 33554432 | bytes 1048576 | tf_op jit(solution)/shard_map/pair_terms_2/pallas_call | solution.py:126
  45.2 0.1 collective-permute-start.17
  45.3 0.4 collective-permute-done.9.refs_1_.refs_5_
  45.7 0.1 collective-permute-done.10.refs_2_.refs_6_
  45.9 2.7 %collective-permute-done.11.refs_3_.refs_7_ = bf16[1,128,256]{2,1,0:T(8,128)(2,1)S(1)} collective-permute-done((bf16[1,128,256]{2,1,0:T(8,128)(2,1)S(1)}, bf16[1,128,256]{2,1,0:T(8,128)(2,1)S(1)}, u32[]{:S(2)}, u32[]{:S(2)}) %collective-permute-start.11) | collective-permute-done | bytes 65568 | tf_op jit(solution)/shard_map/ppermute | solution.py:177
  48.5 0.8 %pair_terms_1.1 = (f32[4,128,128]{2,1,0:T(8,128)S(1)}, bf16[4,128,128]{2,1,0:T(8,128)(2,1)S(1)}) custom-call(s32[3]{0:T(128)S(1)} %pad_add_fusion.place, bf16[512,128]{1,0:T(8,128)(2,1)S(1)} %get-tuple-element.41.ligand, bf16[1,128,256]{2,1,0:T(8,128)(2,1)S(1)} %get-tuple-element.33.refs_4_.refs_0_, ...), custom_call_target="tpu_custom_call" | custom-call | flops 33554432 | bytes 1048576 | tf_op jit(solution)/shard_map/pair_terms_1/pallas_call | solution.py:126
  49.3 0.1 collective-permute-start.16
  49.4 1.0 %density_terms.1 = f32[4,128]{1,0:T(4,128)S(1)} custom-call(s32[3]{0:T(128)S(1)} %pad_add_fusion.place, bf16[4,128,512]{2,1,0:T(8,128)(2,1)S(1)} %get-tuple-element.28.turned, bf16[2,128,256]{2,1,0:T(8,128)(2,1)S(1)} %get-tuple-element.29.refs_0_, bf16[2,128,256]{2,1,0:T(8,128)(2,1)S(1)} %get-tuple-element.30.refs_1_, ...), custom_call_target="tpu_custom_call" | custom-call | flops 2097152 | bytes 1048576 | tf_op jit(solution)/shard_map/density_terms/pallas_call | solution.py:126
  50.4 2.3 %collective-permute-start.5 = (f32[4,128]{1,0:T(4,128)S(1)}, f32[4,128]{1,0:T(4,128)S(1)}, u32[]{:S(2)}, u32[]{:S(2)}) collective-permute-start(f32[4,128]{1,0:T(4,128)S(1)} %density_terms.1), channel_id=1, source_target_pairs={{0,9},{1,8},{4,13},{5,12},{8,1},{9,0},{12,5},{13,4},{2,11},{3,10},... | collective-permute-start | bytes 6152 | tf_op jit(solution)/shard_map/ppermute | solution.py:210
  52.7 0.8 %collective-permute-start.4 = (f32[4,128]{1,0:T(4,128)S(1)}, f32[4,128]{1,0:T(4,128)S(1)}, u32[]{:S(2)}, u32[]{:S(2)}) collective-permute-start(f32[4,128]{1,0:T(4,128)S(1)} %density_terms.1), channel_id=1, source_target_pairs={{0,8},{4,12},{8,0},{12,4},{1,9},{5,13},{9,1},{13,5},{2,10},{6,14},... | collective-permute-start | bytes 6152 | tf_op jit(solution)/shard_map/ppermute | solution.py:210
  53.4 0.9 %collective-permute-done.5 = f32[4,128]{1,0:T(4,128)S(1)} collective-permute-done((f32[4,128]{1,0:T(4,128)S(1)}, f32[4,128]{1,0:T(4,128)S(1)}, u32[]{:S(2)}, u32[]{:S(2)}) %collective-permute-start.5) | collective-permute-done | bytes 2080 | tf_op jit(solution)/shard_map/ppermute | solution.py:210
  54.3 0.5 collective-permute-start.3
  54.8 2.3 %collective-permute-done.4 = f32[4,128]{1,0:T(4,128)S(1)} collective-permute-done((f32[4,128]{1,0:T(4,128)S(1)}, f32[4,128]{1,0:T(4,128)S(1)}, u32[]{:S(2)}, u32[]{:S(2)}) %collective-permute-start.4) | collective-permute-done | bytes 2080 | tf_op jit(solution)/shard_map/ppermute | solution.py:210
  57.1 0.0 collective-permute-done.3
  57.2 0.6 multiply_reduce_fusion
  57.8 0.0 collective-permute-done.17.refs_17_
  57.8 0.0 collective-permute-done.16.refs_15_
  57.8 0.0 collective-permute-done.15.refs_13_
  57.8 6.1 %cross_terms.1 = f32[128,256,128]{2,1,0:T(8,128)} custom-call(bf16[2,128,256]{2,1,0:T(8,128)(2,1)S(1)} %get-tuple-element.29.refs_0_, bf16[2,128,256]{2,1,0:T(8,128)(2,1)S(1)} %collective-permute-done.6.refs_1_, bf16[2,128,256]{2,1,0:T(8,128)(2,1)S(1)} %collective-permute-done.7.refs_2_, bf16[2,128,256]{2,1,0:T(8,128)(2,1)S(1)} %collective-permute-done.8.refs_3_, ...), custom_call_target="tpu_custom_call" | custom-call | flops 2147483648 | bytes 18874368 | tf_op jit(solution)/shard_map/cross_terms/pallas_call | solution.py:126
Async XLA Ops:
  1.9 16.0 %collective-permute-start = (bf16[512,512]{1,0:T(8,128)(2,1)S(1)}, bf16[512,512]{1,0:T(8,128)(2,1)S(1)}, u32[]{:S(2)}, u32[]{:S(2)}) collective-permute-start(bf16[512,512]{1,0:T(8,128)(2,1)S(1)} %get-tuple-element.25.occupied), channel_id=1, source_target_pairs={{0,2},{4,6},{10,8},{14,12},{1,3},{5,7},{11,9},{15,13},{16,18},{20,... | collective-permute-start | bytes 1572872 | tf_op jit(solution)/shard_map/ppermute | solution.py:169
  6.8 21.2 %collective-permute-start.2 = (bf16[1,512,256]{2,1,0:T(8,128)(2,1)S(1)}, bf16[1,512,256]{2,1,0:T(8,128)(2,1)S(1)}, u32[]{:S(2)}, u32[]{:S(2)}) collective-permute-start(bf16[1,512,256]{2,1,0:T(8,128)(2,1)S(1)} %get-tuple-element.27.refs_1_), channel_id=1, source_target_pairs={{0,8},{4,12},{8,0},{12,4},{1,9},{5,13},{9,1},{13,5},{2,10},{6,14},... | collective-permute-start | bytes 786440 | tf_op jit(solution)/shard_map/ppermute | solution.py:167
  7.3 31.7 %collective-permute-start.1 = (bf16[1,512,256]{2,1,0:T(8,128)(2,1)S(1)}, bf16[1,512,256]{2,1,0:T(8,128)(2,1)S(1)}, u32[]{:S(2)}, u32[]{:S(2)}) collective-permute-start(bf16[1,512,256]{2,1,0:T(8,128)(2,1)S(1)} %get-tuple-element.26.refs_0_), channel_id=1, source_target_pairs={{0,8},{4,12},{8,0},{12,4},{1,9},{5,13},{9,1},{13,5},{2,10},{6,14},... | collective-permute-start | bytes 786440 | tf_op jit(solution)/shard_map/ppermute | solution.py:167
  19.1 10.3 %collective-permute-start.6 = (bf16[2,128,256]{2,1,0:T(8,128)(2,1)S(1)}, bf16[2,128,256]{2,1,0:T(8,128)(2,1)S(1)}, u32[]{:S(2)}, u32[]{:S(2)}) collective-permute-start(bf16[2,128,256]{2,1,0:T(8,128)(2,1)S(1)} %get-tuple-element.30.refs_1_), channel_id=1, source_target_pairs={{0,2},{2,0},{4,6},{6,4},{8,10},{10,8},{12,14},{14,12},{1,3},{3,1},... | collective-permute-start | bytes 393224 | tf_op jit(solution)/shard_map/ppermute | solution.py:177
  21.6 13.6 %collective-permute-start.7 = (bf16[2,128,256]{2,1,0:T(8,128)(2,1)S(1)}, bf16[2,128,256]{2,1,0:T(8,128)(2,1)S(1)}, u32[]{:S(2)}, u32[]{:S(2)}) collective-permute-start(bf16[2,128,256]{2,1,0:T(8,128)(2,1)S(1)} %get-tuple-element.31.refs_2_), channel_id=1, source_target_pairs={{0,4},{2,6},{4,0},{6,2},{8,12},{10,14},{12,8},{14,10},{1,5},{3,7},... | collective-permute-start | bytes 393224 | tf_op jit(solution)/shard_map/ppermute | solution.py:177
  23.2 14.8 %collective-permute-start.8 = (bf16[2,128,256]{2,1,0:T(8,128)(2,1)S(1)}, bf16[2,128,256]{2,1,0:T(8,128)(2,1)S(1)}, u32[]{:S(2)}, u32[]{:S(2)}) collective-permute-start(bf16[2,128,256]{2,1,0:T(8,128)(2,1)S(1)} %get-tuple-element.32.refs_3_), channel_id=1, source_target_pairs={{0,6},{2,4},{4,2},{6,0},{8,14},{10,12},{12,10},{14,8},{1,7},{3,5},... | collective-permute-start | bytes 393224 | tf_op jit(solution)/shard_map/ppermute | solution.py:177
  28.9 12.6 %collective-permute-start.12 = (bf16[1,128,256]{2,1,0:T(8,128)(2,1)S(1)}, bf16[1,128,256]{2,1,0:T(8,128)(2,1)S(1)}, u32[]{:S(2)}, u32[]{:S(2)}) collective-permute-start(bf16[1,128,256]{2,1,0:T(8,128)(2,1)S(1)} %get-tuple-element.38.refs_9_), channel_id=1, source_target_pairs={{0,2},{2,0},{4,6},{6,4},{8,10},{10,8},{12,14},{14,12},{1,3},{3,1},... | collective-permute-start | bytes 196616 | tf_op jit(solution)/shard_map/ppermute | solution.py:177
  29.4 14.0 %collective-permute-start.13 = (bf16[1,128,256]{2,1,0:T(8,128)(2,1)S(1)}, bf16[1,128,256]{2,1,0:T(8,128)(2,1)S(1)}, u32[]{:S(2)}, u32[]{:S(2)}) collective-permute-start(bf16[1,128,256]{2,1,0:T(8,128)(2,1)S(1)} %get-tuple-element.39.refs_10_), channel_id=1, source_target_pairs={{0,4},{2,6},{4,0},{6,2},{8,12},{10,14},{12,8},{14,10},{1,5},{3,7},... | collective-permute-start | bytes 196616 | tf_op jit(solution)/shard_map/ppermute | solution.py:177
  38.8 19.0 %collective-permute-start.15 = (bf16[8,128,128]{2,1,0:T(8,128)(2,1)S(1)}, bf16[8,128,128]{2,1,0:T(8,128)(2,1)S(1)}, u32[]{:S(2)}, u32[]{:S(2)}) collective-permute-start(bf16[8,128,128]{2,1,0:T(8,128)(2,1)S(1)} %get-tuple-element.43), channel_id=1, source_target_pairs={{0,1},{1,0},{2,3},{3,2},{4,5},{5,4},{6,7},{7,6},{8,9},{9,8},{10,11... | collective-permute-start | bytes 786440 | tf_op jit(solution)/shard_map/ppermute | solution.py:223
  38.9 5.5 %collective-permute-start.14 = (bf16[1,128,256]{2,1,0:T(8,128)(2,1)S(1)}, bf16[1,128,256]{2,1,0:T(8,128)(2,1)S(1)}, u32[]{:S(2)}, u32[]{:S(2)}) collective-permute-start(bf16[1,128,256]{2,1,0:T(8,128)(2,1)S(1)} %get-tuple-element.40.refs_11_), channel_id=1, source_target_pairs={{0,6},{2,4},{4,2},{6,0},{8,14},{10,12},{12,10},{14,8},{1,7},{3,5},... | collective-permute-start | bytes 196616 | tf_op jit(solution)/shard_map/ppermute | solution.py:177
  39.8 5.9 %collective-permute-start.9 = (bf16[1,128,256]{2,1,0:T(8,128)(2,1)S(1)}, bf16[1,128,256]{2,1,0:T(8,128)(2,1)S(1)}, u32[]{:S(2)}, u32[]{:S(2)}) collective-permute-start(bf16[1,128,256]{2,1,0:T(8,128)(2,1)S(1)} %get-tuple-element.34.refs_5_), channel_id=1, source_target_pairs={{0,2},{2,0},{4,6},{6,4},{8,10},{10,8},{12,14},{14,12},{1,3},{3,1},... | collective-permute-start | bytes 196616 | tf_op jit(solution)/shard_map/ppermute | solution.py:177
  41.5 4.4 %collective-permute-start.10 = (bf16[1,128,256]{2,1,0:T(8,128)(2,1)S(1)}, bf16[1,128,256]{2,1,0:T(8,128)(2,1)S(1)}, u32[]{:S(2)}, u32[]{:S(2)}) collective-permute-start(bf16[1,128,256]{2,1,0:T(8,128)(2,1)S(1)} %get-tuple-element.35.refs_6_), channel_id=1, source_target_pairs={{0,4},{2,6},{4,0},{6,2},{8,12},{10,14},{12,8},{14,10},{1,5},{3,7},... | collective-permute-start | bytes 196616 | tf_op jit(solution)/shard_map/ppermute | solution.py:177
  43.4 5.2 %collective-permute-start.11 = (bf16[1,128,256]{2,1,0:T(8,128)(2,1)S(1)}, bf16[1,128,256]{2,1,0:T(8,128)(2,1)S(1)}, u32[]{:S(2)}, u32[]{:S(2)}) collective-permute-start(bf16[1,128,256]{2,1,0:T(8,128)(2,1)S(1)} %get-tuple-element.36.refs_7_), channel_id=1, source_target_pairs={{0,6},{2,4},{4,2},{6,0},{8,14},{10,12},{12,10},{14,8},{1,7},{3,5},... | collective-permute-start | bytes 196616 | tf_op jit(solution)/shard_map/ppermute | solution.py:177
  45.2 12.6 %collective-permute-start.17 = (bf16[4,128,128]{2,1,0:T(8,128)(2,1)S(1)}, bf16[4,128,128]{2,1,0:T(8,128)(2,1)S(1)}, u32[]{:S(2)}, u32[]{:S(2)}) collective-permute-start(bf16[4,128,128]{2,1,0:T(8,128)(2,1)S(1)} %get-tuple-element.47), channel_id=1, source_target_pairs={{0,1},{1,0},{2,3},{3,2},{4,5},{5,4},{6,7},{7,6},{8,9},{9,8},{10,11... | collective-permute-start | bytes 393224 | tf_op jit(solution)/shard_map/ppermute | solution.py:223
  49.3 8.5 %collective-permute-start.16 = (bf16[4,128,128]{2,1,0:T(8,128)(2,1)S(1)}, bf16[4,128,128]{2,1,0:T(8,128)(2,1)S(1)}, u32[]{:S(2)}, u32[]{:S(2)}) collective-permute-start(bf16[4,128,128]{2,1,0:T(8,128)(2,1)S(1)} %get-tuple-element.45), channel_id=1, source_target_pairs={{0,1},{1,0},{2,3},{3,2},{4,5},{5,4},{6,7},{7,6},{8,9},{9,8},{10,11... | collective-permute-start | bytes 393224 | tf_op jit(solution)/shard_map/ppermute | solution.py:223
  50.4 4.0 %collective-permute-start.5 = (f32[4,128]{1,0:T(4,128)S(1)}, f32[4,128]{1,0:T(4,128)S(1)}, u32[]{:S(2)}, u32[]{:S(2)}) collective-permute-start(f32[4,128]{1,0:T(4,128)S(1)} %density_terms.1), channel_id=1, source_target_pairs={{0,9},{1,8},{4,13},{5,12},{8,1},{9,0},{12,5},{13,4},{2,11},{3,10},... | collective-permute-start | bytes 6152 | tf_op jit(solution)/shard_map/ppermute | solution.py:210
  52.7 4.5 %collective-permute-start.4 = (f32[4,128]{1,0:T(4,128)S(1)}, f32[4,128]{1,0:T(4,128)S(1)}, u32[]{:S(2)}, u32[]{:S(2)}) collective-permute-start(f32[4,128]{1,0:T(4,128)S(1)} %density_terms.1), channel_id=1, source_target_pairs={{0,8},{4,12},{8,0},{12,4},{1,9},{5,13},{9,1},{13,5},{2,10},{6,14},... | collective-permute-start | bytes 6152 | tf_op jit(solution)/shard_map/ppermute | solution.py:210
  54.3 2.8 %collective-permute-start.3 = (f32[4,128]{1,0:T(4,128)S(1)}, f32[4,128]{1,0:T(4,128)S(1)}, u32[]{:S(2)}, u32[]{:S(2)}) collective-permute-start(f32[4,128]{1,0:T(4,128)S(1)} %density_terms.1), channel_id=1, source_target_pairs={{0,1},{1,0},{2,3},{3,2},{4,5},{5,4},{6,7},{7,6},{8,9},{9,8},{10,11... | collective-permute-start | bytes 6152 | tf_op jit(solution)/shard_map/ppermute | solution.py:208

commit v4 on v3

--- a/solution.py
+++ b/solution.py
@@ -18,21 +18,20 @@
 VMEM = pl.BlockSpec(memory_space=pltpu.VMEM)
 
 
-def spread_kernel(pattern, blocks, occupied, ligand, *refs):
-    parts, (panel, orbitals, held, opened, sems) = refs[:-5], refs[-5:]
-    nu_width = blocks.shape[2]
+def masked_kernel(pattern, blocks, occupied, ligand, masked, panel, orbitals, held, opened, sems):
+    aux_rows, _, nu_width = blocks.shape
     moves = ((blocks, held), (pattern, opened), (occupied, panel), (ligand, orbitals))
     copies = [pltpu.make_async_copy(source, target, sems.at[k]) for k, (source, target) in enumerate(moves)]
     for copy in copies:
         copy.start()
     copies[0].wait()
     copies[1].wait()
-    for q, part in enumerate(parts):
+    for q in range(aux_rows):
         for m in range(NBLK):
             for n in range(nu_width // BLK):
                 rows, columns = pl.ds(m * BLK, BLK), pl.ds(n * BLK, BLK)
                 tile = held[q, rows, columns]
-                part[0, rows, columns] = jnp.where(opened[0, n, m] != 0, tile, jnp.zeros_like(tile))
+                masked[q, rows, columns] = jnp.where(opened[0, n, m] != 0, tile, jnp.zeros_like(tile))
     for copy in copies[2:]:
         copy.wait()
 
@@ -41,15 +40,14 @@
     return (2 * (place[0] & 1) + place[1]) ^ d
 
 
-def half_into(outs, place, turned, parts):
+def half_into(outs, place, turned, masked):
     for d, out in enumerate(outs):
         rows = turned[slot_of(place, d)]
-        for q, masked in enumerate(parts):
-            out[q] = jnp.dot(rows, masked[0], preferred_element_type=jnp.float32).astype(jnp.bfloat16)
-
-
-def own_kernel(place, occupied, other, *refs):
-    parts, turned, outs = refs[:-5], refs[-5], refs[-4:]
+        for q in range(out.shape[0]):
+            out[q] = jnp.dot(rows, masked[q], preferred_element_type=jnp.float32).astype(jnp.bfloat16)
+
+
+def own_kernel(place, occupied, other, masked, turned, *outs):
     ni = turned.shape[1]
     near = place[1] == place[0] // 2
 
@@ -59,29 +57,43 @@
 
     pl.when(near)(functools.partial(turn, occupied))
     pl.when(jnp.logical_not(near))(functools.partial(turn, other))
-    half_into(outs, place, turned, parts)
-
-
-def part_kernel(place, masked, turned, *outs):
-    half_into(outs, place, turned, [masked])
-
-
-def density_kernel(place, turned, *refs):
+    half_into(outs, place, turned, masked)
+
+
+def density_kernel(place, occupied, other, masked, turned, *refs):
     messages, out = refs[:-1], refs[-1]
-    nu_width = messages[0].shape[2]
-    first = pl.multiple_of(place[2] * nu_width, nu_width)
-    row = 0
-    for group in range(0, len(messages), 4):
-        for q in range(messages[group].shape[0]):
-            total = 0.0
-            for d in range(4):
-                rows = turned[slot_of(place, d), :, pl.ds(first, nu_width)].astype(jnp.float32)
-                total += jnp.sum(rows * messages[group + d][q].astype(jnp.float32))
-            out[row : row + 1, :] = jnp.full((1, out.shape[1]), total, jnp.float32)
-            row += 1
-
-
-def pair_kernel(place, ligand, *refs):
+    aux_rows, ni, nu_width = messages[0].shape
+    own = pl.ds(pl.multiple_of(place[2] * nu_width, nu_width), nu_width)
+    near = place[1] == place[0] // 2
+
+    def near_terms(q):
+        total = 0.0
+        for d in range(4):
+            rows = turned[slot_of(place, d), :, own].astype(jnp.float32)
+            total += jnp.sum(rows * messages[d][q].astype(jnp.float32))
+        return total
+
+    def far_terms(panel):
+        totals = [near_terms(q) for q in range(aux_rows)]
+        for s in range(4):
+            rows = panel[:, s * ni : (s + 1) * ni].T
+            weights = panel[own, s * ni : (s + 1) * ni].T.astype(jnp.float32)
+            for q in range(aux_rows):
+                result = jnp.dot(rows, masked[q], preferred_element_type=jnp.float32).astype(jnp.bfloat16)
+                totals[q] += jnp.sum(weights * result.astype(jnp.float32))
+        for q in range(aux_rows):
+            out[q : q + 1, :] = jnp.full((1, out.shape[1]), totals[q], jnp.float32)
+
+    pl.when(near)(functools.partial(far_terms, other))
+    pl.when(jnp.logical_not(near))(functools.partial(far_terms, occupied))
+
+
+def far_kernel(place, value, value_there, masked, turned, density, *outs):
+    density[...] = (value[...] + value_there[...]) / math.sqrt(NOCC)
+    half_into(outs, place, turned, masked)
+
+
+def pair_kernel(place, after, ligand, *refs):
     arrived, own, sent = refs[:-2], refs[-2], refs[-1]
     aux_rows, ni, nu_width = arrived[0].shape
     width = ligand.shape[1]
@@ -94,16 +106,27 @@
         sent[k * aux_rows : (k + 1) * aux_rows] = part.astype(jnp.bfloat16)
 
 
-def cross_kernel(scale, *refs):
-    messages, pairs, (out, held, sem) = refs[:12], refs[12:18], refs[18:]
+def turn_kernel(*refs):
+    messages, out = refs[:-1], refs[-1]
     nu_width = messages[0].shape[2]
+    for g in range(out.shape[0]):
+        here = pl.ds(g * GROUP, GROUP)
+        out[g] = jnp.concatenate([x[:, here, :].reshape(-1, nu_width) for x in messages], axis=0).T
+
+
+def pair_and_turn_kernel(place, after, ligand, *refs):
+    pair_kernel(place, after, ligand, *refs[:-1])
+    turn_kernel(*refs[:-3], refs[-1])
+
+
+def cross_kernel(scale, near, far, *refs):
+    pairs, (out, held, sem) = refs[:4], refs[4:]
     ni, _, width = out.shape
 
     def step(g, carry):
         here = pl.ds(pl.multiple_of(g * GROUP, GROUP), GROUP)
-        rows = [x[:, here, :].reshape(-1, nu_width) for x in messages]
-        turned = jnp.concatenate(rows, axis=0).T
-        summed = [pairs[j][:, here, :] + pairs[j + 1][:, here, :].astype(jnp.float32) for j in (0, 2, 4)]
+        turned = jnp.concatenate([near[g], far[g]], axis=1)
+        summed = [pairs[j][:, here, :] + pairs[j + 1][:, here, :].astype(jnp.float32) for j in (0, 2)]
         summed = jnp.concatenate([(x * scale).astype(jnp.bfloat16) for x in summed], axis=0)
         row = lax.broadcasted_iota(jnp.int32, (1, GROUP, width), 1)
         zero = jnp.zeros_like(summed)
@@ -151,11 +174,11 @@
     across = [(a, a ^ 2) for a in range(n_aux)]
     swap = [(c, 1 - c) for c in range(n_ao)]
     pattern = jnp.swapaxes(pattern, 1, 2)
-    *parts, panel, orbitals = call(
-        spread_kernel,
+    masked, panel, orbitals = call(
+        masked_kernel,
         "masked_blocks",
         (pltpu.with_memory_space_constraint(x, pltpu.HBM) for x in (pattern, blocks, occupied, ligand)),
-        [bf16((1, NB, nu_width))] * aux_rows + [bf16(occupied.shape), bf16(ligand.shape)],
+        [bf16(blocks.shape), bf16(occupied.shape), bf16(ligand.shape)],
         [
             pltpu.VMEM(blocks.shape, jnp.bfloat16),
             pltpu.SMEM(pattern.shape, pattern.dtype),
@@ -164,9 +187,8 @@
         scalars=0,
         in_spec=pl.BlockSpec(memory_space=pltpu.HBM),
     )
-    far = [lax.ppermute(x, "aux", across) for x in parts]
-    fetch = [(a * n_orb + a // 2, a * n_orb + 1 - a // 2) for a in range(n_aux)]
-    other = lax.ppermute(panel, ("aux", "orb"), fetch)
+    far_masked = lax.ppermute(masked, "aux", across)
+    other = lax.ppermute(panel, "orb", swap)
 
     def square(messages):
         arrived = [messages[0]] + [None] * 3
@@ -177,56 +199,51 @@
             arrived[d] = lax.ppermute(messages[d], ("aux", "orb"), moves)
         return arrived
 
-    work = 2 * NB * panel_width * nu_width
+    work = 2 * NB * panel_width * nu_width * aux_rows
+    messages = [bf16((aux_rows, ni, nu_width))] * 4
     turned, *own = call(
-        own_kernel,
-        "own_half",
-        (place, panel, other, *parts),
-        [bf16((4, ni, NB))] + [bf16((aux_rows, ni, nu_width))] * 4,
-        flops=work * aux_rows,
-    )
-    sent = [own]
-    arrived = [square(own)]
-    for q in range(aux_rows):
-        messages = call(
-            part_kernel,
-            f"part_half_{q}",
-            (place, far[q], turned),
-            [bf16((1, ni, nu_width))] * 4,
-            flops=work,
-        )
-        sent.append(messages)
-        arrived.append(square(messages))
-
+        own_kernel, "own_half", (place, panel, other, masked), [bf16((4, ni, NB))] + messages, flops=work
+    )
+    own_here = square(own)
     value = call(
         density_kernel,
         "density_terms",
-        (place, turned, *sum(sent, [])),
-        [f32((2 * aux_rows, 128))],
-        flops=8 * panel_width * nu_width * aux_rows,
+        (place, panel, other, masked, turned, *own),
+        [f32((aux_rows, 128))],
+        flops=work,
     )[0]
-    near = value[:aux_rows, 0] + lax.ppermute(value, "ao", swap)[:aux_rows, 0]
-    crossing = [(a * n_ao + c, (a ^ 2) * n_ao + 1 - c) for a in range(n_aux) for c in range(n_ao)]
-    back = lax.ppermute(value, "aux", across)[aux_rows:, 0] + lax.ppermute(value, ("aux", "ao"), crossing)[aux_rows:, 0]
-    density = (near + back) / math.sqrt(NOCC)
-
-    pairs = []
-    for k, group in enumerate(arrived):
-        shape = (4 * group[0].shape[0], ni, width)
-        kept, given = call(
-            pair_kernel,
-            f"pair_terms_{k}",
-            (place, orbitals, *group),
-            [f32(shape), bf16(shape)],
-            flops=2 * shape[0] * ni * nu_width * width,
-        )
-        pairs += [kept, lax.ppermute(given, "ao", swap)]
+    density, *far = call(
+        far_kernel,
+        "far_half",
+        (place, value, lax.ppermute(value, "ao", swap), far_masked, turned),
+        [f32((aux_rows, 128))] + messages,
+        flops=work,
+    )
+    far_here = square(far)
+
+    shape = (4 * aux_rows, ni, width)
+    kept_and_given = [f32(shape), bf16(shape)]
+    side = [bf16((ni // GROUP, nu_width, 4 * aux_rows * GROUP))]
+    pair_work = 2 * shape[0] * ni * nu_width * width
+    own_kept, own_given, own_rows = call(
+        pair_and_turn_kernel,
+        "own_pairs",
+        (place, density, orbitals, *own_here),
+        kept_and_given + side,
+        flops=pair_work,
+    )
+    own_pairs = (own_kept, lax.ppermute(own_given, "ao", swap))
+    far_kept, far_given = call(
+        pair_kernel, "far_pairs", (place, density, orbitals, *far_here), kept_and_given, flops=pair_work
+    )
+    far_pairs = (far_kept, lax.ppermute(far_given, "ao", swap))
+    far_rows = call(turn_kernel, "far_turned", far_here, side, scalars=0)[0]
 
     result = (ni, nu_width, width)
     cross_terms = call(
         functools.partial(cross_kernel, 1.0 / math.sqrt(q_total)),
         "cross_terms",
-        (*sum(arrived, []), *pairs),
+        (own_rows, far_rows, *own_pairs, *far_pairs),
         [f32(result)],
         [pltpu.VMEM(result, jnp.float32), pltpu.SemaphoreType.DMA],
         limit=32,
@@ -235,7 +252,7 @@
         moved=18 * MIB,
         out_spec=pl.BlockSpec(memory_space=pltpu.HBM),
     )[0]
-    return (density, cross_terms)
+    return (density[:, 0], cross_terms)
 
 
 def plain_body(blocks, pattern, occupied, ligand):

time: 64 us -> 50.2 us (0.78)
  starting transfers between devices: 20.9 us -> 13 us
  waiting for transfers between devices: 28 us -> 23.1 us
  Pallas kernels: 13.5 us -> 12.6 us
    ppermute x9 -> x6, waiting for transfers between devices: 11.9 us -> 5.61 us  [square(): arrived[d] = lax.ppermute(messages[d], ('aux', 'orb'), moves)]
    ppermute x9 -> x5, starting transfers between devices: 11.7 us -> 5.81 us  [the longest x1 3 us: body(): other = lax.ppermute(panel, 'orb', swap)]
    ppermute x9 -> x6, starting transfers between devices: 9.29 us -> 7.17 us  [square(): arrived[d] = lax.ppermute(messages[d], ('aux', 'orb'), moves)]
    ppermute x9 -> x5, waiting for transfers between devices: 16.1 us -> 17.5 us  [the longest x1 9.26 us: body(): other = lax.ppermute(panel, 'orb', swap)]
    pallas_call x9 -> x8, Pallas kernels: 13.5 us -> 12.6 us  [call(): pl.pallas_call(kernel, in_specs=[SMEM] * scalars + [in_spec] * (len(input...]
  transfers between devices with their start and end apart: 18 -> 11, of which waited for: 9 -> 6; matrix products, arithmetic and copies ran while one was open for 1% -> 1% of each run, Pallas kernels for 10% -> 11%
where the time goes in v4:
time: 50.2 us; the launch traced here: 50.1 us
  waiting for transfers between devices  23.1 us (46%)
  starting transfers between devices  13 us (26%)
  Pallas kernels  12.6 us (25%)
  between operations  0.72 us (1%)
  local copies, waits for them, and re-layouts  0.63 us (1%)
    pallas_call x8, Pallas kernels, call(): pl.pallas_call(kernel, in_specs=[SMEM] * scalars + [in_spec] * (len(input...  12.6 us
    ppermute x1, waiting for transfers between devices, body(): other = lax.ppermute(panel, 'orb', swap)  9.26 us
    ppermute x1, waiting for transfers between devices, body(): far_masked = lax.ppermute(masked, 'aux', across)  7.53 us
    ppermute x6, starting transfers between devices, square(): arrived[d] = lax.ppermute(messages[d], ('aux', 'orb'), moves)  7.17 us
    ppermute x6, waiting for transfers between devices, square(): arrived[d] = lax.ppermute(messages[d], ('aux', 'orb'), moves)  5.61 us
    ppermute x1, starting transfers between devices, body(): other = lax.ppermute(panel, 'orb', swap)  3 us
    ppermute x1, starting transfers between devices, body(): far_masked = lax.ppermute(masked, 'aux', across)  2.59 us
  transfers between devices with their start and end apart: 11, of which 6 were waited for; matrix products, arithmetic and copies ran while one was open for 1% of the time, Pallas kernels for 11%

profile of v4, /device:TPU:0, one launch (start us, length us, event | category | flops | bytes accessed | tf_op | source)
XLA Modules:
  0.0 50.1 jit_solution(12832009112211223269)
XLA Ops:
  0.6 1.3 %masked_blocks.1 = (bf16[2,512,256]{2,1,0:T(8,128)(2,1)S(1)}, bf16[512,512]{1,0:T(8,128)(2,1)S(1)}, bf16[512,128]{1,0:T(8,128)(2,1)S(1)}) custom-call(s32[1,2,4]{2,1,0:T(2,128)} %bitcast.4, bf16[2,512,256]{2,1,0:T(8,128)(2,1)} %blocks.1, bf16[512,512]{1,0:T(8,128)(2,1)} %occupied.1, bf16[512,128]{1,0:T(8,128)(2,1)} %ligand.1), custom_call_target="tpu_custom_call" | custom-call | bytes 1048576 | tf_op jit(solution)/shard_map/masked_blocks/pallas_call | solution.py:149
  1.9 3.0 %collective-permute-start = (bf16[512,512]{1,0:T(8,128)(2,1)S(1)}, bf16[512,512]{1,0:T(8,128)(2,1)S(1)}, u32[]{:S(2)}, u32[]{:S(2)}) collective-permute-start(bf16[512,512]{1,0:T(8,128)(2,1)S(1)} %get-tuple-element.20.occupied), channel_id=1, source_target_pairs={{0,2},{2,0},{1,3},{3,1},{4,6},{6,4},{5,7},{7,5},{8,10},{10,8},{9,1... | collective-permute-start | bytes 1572872 | tf_op jit(solution)/shard_map/ppermute | solution.py:191
  4.9 2.6 %collective-permute-start.2 = (bf16[2,512,256]{2,1,0:T(8,128)(2,1)S(1)}, bf16[2,512,256]{2,1,0:T(8,128)(2,1)S(1)}, u32[]{:S(2)}, u32[]{:S(2)}) collective-permute-start(bf16[2,512,256]{2,1,0:T(8,128)(2,1)S(1)} %get-tuple-element.21.masked), channel_id=1, source_target_pairs={{0,8},{4,12},{8,0},{12,4},{1,9},{5,13},{9,1},{13,5},{2,10},{6,14},... | collective-permute-start | bytes 1572872 | tf_op jit(solution)/shard_map/ppermute | solution.py:190
  7.5 0.1 pad_add_fusion.place
  7.6 9.3 %collective-permute-done.other = bf16[512,512]{1,0:T(8,128)(2,1)S(1)} collective-permute-done((bf16[512,512]{1,0:T(8,128)(2,1)S(1)}, bf16[512,512]{1,0:T(8,128)(2,1)S(1)}, u32[]{:S(2)}, u32[]{:S(2)}) %collective-permute-start) | collective-permute-done | bytes 524320 | tf_op jit(solution)/shard_map/ppermute | solution.py:191
  16.8 1.2 %own_half.1 = (bf16[4,128,512]{2,1,0:T(8,128)(2,1)S(1)}, bf16[2,128,256]{2,1,0:T(8,128)(2,1)S(1)}, bf16[2,128,256]{2,1,0:T(8,128)(2,1)S(1)}, bf16[2,128,256]{2,1,0:T(8,128)(2,1)S(1)}, bf16[2,128,256]{2,1,0:T(8,128)(2,1)S(1)}) custom-call(s32[3]{0:T(128)S(1)} %pad_add_fusion.place, bf16[512,512]{1,0:T(8,128)(2,1)S(1)} %get-tuple-element.20.occupied, ...), custom_call_target="tpu_custom_call" | custom-call | flops 268435456 | bytes 1048576 | tf_op jit(solution)/shard_map/own_half/pallas_call | solution.py:149
  18.0 1.8 %collective-permute-start.3 = (bf16[2,128,256]{2,1,0:T(8,128)(2,1)S(1)}, bf16[2,128,256]{2,1,0:T(8,128)(2,1)S(1)}, u32[]{:S(2)}, u32[]{:S(2)}) collective-permute-start(bf16[2,128,256]{2,1,0:T(8,128)(2,1)S(1)} %get-tuple-element.24.refs_1_), channel_id=1, source_target_pairs={{0,2},{2,0},{4,6},{6,4},{8,10},{10,8},{12,14},{14,12},{1,3},{3,1},... | collective-permute-start | bytes 393224 | tf_op jit(solution)/shard_map/ppermute | solution.py:199
  19.8 1.3 %density_terms.1.value = f32[2,128]{1,0:T(2,128)S(1)} custom-call(s32[3]{0:T(128)S(1)} %pad_add_fusion.place, bf16[512,512]{1,0:T(8,128)(2,1)S(1)} %get-tuple-element.20.occupied, bf16[512,512]{1,0:T(8,128)(2,1)S(1)} %collective-permute-done.other, bf16[2,512,256]{2,1,0:T(8,128)(2,1)S(1)} %get-tuple-element.21.masked, ...), custom_call_target="tpu_custom_call" | custom-call | flops 268435456 | bytes 1048576 | tf_op jit(solution)/shard_map/density_terms/pallas_call | solution.py:149
  21.1 0.1 collective-permute-start.1
  21.2 1.6 %collective-permute-start.4 = (bf16[2,128,256]{2,1,0:T(8,128)(2,1)S(1)}, bf16[2,128,256]{2,1,0:T(8,128)(2,1)S(1)}, u32[]{:S(2)}, u32[]{:S(2)}) collective-permute-start(bf16[2,128,256]{2,1,0:T(8,128)(2,1)S(1)} %get-tuple-element.25.refs_2_), channel_id=1, source_target_pairs={{0,4},{2,6},{4,0},{6,2},{8,12},{10,14},{12,8},{14,10},{1,5},{3,7},... | collective-permute-start | bytes 393224 | tf_op jit(solution)/shard_map/ppermute | solution.py:199
  22.8 0.2 collective-permute-start.5
  23.0 7.5 %collective-permute-done.2.masked = bf16[2,512,256]{2,1,0:T(8,128)(2,1)S(1)} collective-permute-done((bf16[2,512,256]{2,1,0:T(8,128)(2,1)S(1)}, bf16[2,512,256]{2,1,0:T(8,128)(2,1)S(1)}, u32[]{:S(2)}, u32[]{:S(2)}) %collective-permute-start.2) | collective-permute-done | bytes 524320 | tf_op jit(solution)/shard_map/ppermute | solution.py:190
  30.5 0.0 collective-permute-done.1.value_there
  30.5 1.0 %far_half.1 = (f32[2,128]{1,0:T(2,128)S(1)}, bf16[2,128,256]{2,1,0:T(8,128)(2,1)S(1)}, bf16[2,128,256]{2,1,0:T(8,128)(2,1)S(1)}, bf16[2,128,256]{2,1,0:T(8,128)(2,1)S(1)}, bf16[2,128,256]{2,1,0:T(8,128)(2,1)S(1)}) custom-call(s32[3]{0:T(128)S(1)} %pad_add_fusion.place, f32[2,128]{1,0:T(2,128)S(1)} %density_terms.1.value, ...), custom_call_target="tpu_custom_call" | custom-call | flops 268435456 | bytes 1048576 | tf_op jit(solution)/shard_map/far_half/pallas_call | solution.py:149
  31.5 0.5 %collective-permute-start.6 = (bf16[2,128,256]{2,1,0:T(8,128)(2,1)S(1)}, bf16[2,128,256]{2,1,0:T(8,128)(2,1)S(1)}, u32[]{:S(2)}, u32[]{:S(2)}) collective-permute-start(bf16[2,128,256]{2,1,0:T(8,128)(2,1)S(1)} %get-tuple-element.31), channel_id=1, source_target_pairs={{0,2},{2,0},{4,6},{6,4},{8,10},{10,8},{12,14},{14,12},{1,3},{3,1},... | collective-permute-start | bytes 393224 | tf_op jit(solution)/shard_map/ppermute | solution.py:199
  32.1 0.7 %collective-permute-start.7 = (bf16[2,128,256]{2,1,0:T(8,128)(2,1)S(1)}, bf16[2,128,256]{2,1,0:T(8,128)(2,1)S(1)}, u32[]{:S(2)}, u32[]{:S(2)}) collective-permute-start(bf16[2,128,256]{2,1,0:T(8,128)(2,1)S(1)} %get-tuple-element.32), channel_id=1, source_target_pairs={{0,4},{2,6},{4,0},{6,2},{8,12},{10,14},{12,8},{14,10},{1,5},{3,7},... | collective-permute-start | bytes 393224 | tf_op jit(solution)/shard_map/ppermute | solution.py:199
  32.7 0.0 collective-permute-done.3.refs_1_
  32.7 2.3 %collective-permute-start.8 = (bf16[2,128,256]{2,1,0:T(8,128)(2,1)S(1)}, bf16[2,128,256]{2,1,0:T(8,128)(2,1)S(1)}, u32[]{:S(2)}, u32[]{:S(2)}) collective-permute-start(bf16[2,128,256]{2,1,0:T(8,128)(2,1)S(1)} %get-tuple-element.33), channel_id=1, source_target_pairs={{0,6},{2,4},{4,2},{6,0},{8,14},{10,12},{12,10},{14,8},{1,7},{3,5},... | collective-permute-start | bytes 393224 | tf_op jit(solution)/shard_map/ppermute | solution.py:199
  35.1 0.0 collective-permute-done.4.refs_2_
  35.1 1.0 %collective-permute-done.5.refs_3_ = bf16[2,128,256]{2,1,0:T(8,128)(2,1)S(1)} collective-permute-done((bf16[2,128,256]{2,1,0:T(8,128)(2,1)S(1)}, bf16[2,128,256]{2,1,0:T(8,128)(2,1)S(1)}, u32[]{:S(2)}, u32[]{:S(2)}) %collective-permute-start.5) | collective-permute-done | bytes 131104 | tf_op jit(solution)/shard_map/ppermute | solution.py:199
  36.1 0.8 %own_pairs.1 = (f32[8,128,128]{2,1,0:T(8,128)S(1)}, bf16[8,128,128]{2,1,0:T(8,128)(2,1)S(1)}, bf16[8,256,128]{2,1,0:T(8,128)(2,1)S(1)}) custom-call(s32[3]{0:T(128)S(1)} %pad_add_fusion.place, f32[2,128]{1,0:T(2,128)S(1)} %get-tuple-element.27.after, bf16[512,128]{1,0:T(8,128)(2,1)S(1)} %get-tuple-element.28.ligand, ...), custom_call_target="tpu_custom_call" | custom-call | flops 67108864 | bytes 1048576 | tf_op jit(solution)/shard_map/own_pairs/pallas_call | solution.py:149
  36.9 0.1 collective-permute-start.9
  37.0 2.2 %collective-permute-done.6.refs_1_ = bf16[2,128,256]{2,1,0:T(8,128)(2,1)S(1)} collective-permute-done((bf16[2,128,256]{2,1,0:T(8,128)(2,1)S(1)}, bf16[2,128,256]{2,1,0:T(8,128)(2,1)S(1)}, u32[]{:S(2)}, u32[]{:S(2)}) %collective-permute-start.6) | collective-permute-done | bytes 131104 | tf_op jit(solution)/shard_map/ppermute | solution.py:199
  39.2 0.0 collective-permute-done.7.refs_2_
  39.2 2.4 %collective-permute-done.8.refs_3_ = bf16[2,128,256]{2,1,0:T(8,128)(2,1)S(1)} collective-permute-done((bf16[2,128,256]{2,1,0:T(8,128)(2,1)S(1)}, bf16[2,128,256]{2,1,0:T(8,128)(2,1)S(1)}, u32[]{:S(2)}, u32[]{:S(2)}) %collective-permute-start.8) | collective-permute-done | bytes 131104 | tf_op jit(solution)/shard_map/ppermute | solution.py:199
  41.6 0.8 %far_pairs.1 = (f32[8,128,128]{2,1,0:T(8,128)S(1)}, bf16[8,128,128]{2,1,0:T(8,128)(2,1)S(1)}) custom-call(s32[3]{0:T(128)S(1)} %pad_add_fusion.place, f32[2,128]{1,0:T(2,128)S(1)} %get-tuple-element.27.after, bf16[512,128]{1,0:T(8,128)(2,1)S(1)} %get-tuple-element.28.ligand, bf16[2,128,256]{2,1,0:T(8,128)(2,1)S(1)} %get-tuple-element.30.refs_0_, ...), custom_call_target="tpu_custom_call" | custom-call | flops 67108864 | bytes 1048576 | tf_op jit(solution)/shard_map/far_pairs/pallas_call | solution.py:149
  42.4 0.1 collective-permute-start.10
  42.5 0.6 %slice_reduce_fusion = f32[2]{0:T(128)} fusion(f32[2,128]{1,0:T(2,128)S(1)} %get-tuple-element.27.after), kind=kLoop, calls=%fused_computation | loop fusion | bytes 16 | tf_op jit(solution)/shard_map/slice | solution.py:255
  43.1 0.2 far_turned.1.far
  43.3 0.0 collective-permute-done.9.refs_1_
  43.4 0.7 %collective-permute-done.10.refs_3_ = bf16[8,128,128]{2,1,0:T(8,128)(2,1)S(1)} collective-permute-done((bf16[8,128,128]{2,1,0:T(8,128)(2,1)S(1)}, bf16[8,128,128]{2,1,0:T(8,128)(2,1)S(1)}, u32[]{:S(2)}, u32[]{:S(2)}) %collective-permute-start.10) | collective-permute-done | bytes 262176 | tf_op jit(solution)/shard_map/ppermute | solution.py:239
  44.0 6.0 %cross_terms.1 = f32[128,256,128]{2,1,0:T(8,128)} custom-call(bf16[8,256,128]{2,1,0:T(8,128)(2,1)S(1)} %get-tuple-element.29.near, bf16[8,256,128]{2,1,0:T(8,128)(2,1)S(1)} %far_turned.1.far, f32[8,128,128]{2,1,0:T(8,128)S(1)} %get-tuple-element.34.refs_0_, bf16[8,128,128]{2,1,0:T(8,128)(2,1)S(1)} %collective-permute-done.9.refs_1_, ...), custom_call_target="tpu_custom_call" | custom-call | flops 2147483648 | bytes 18874368 | tf_op jit(solution)/shard_map/cross_terms/pallas_call | solution.py:149
Async XLA Ops:
  1.9 14.9 %collective-permute-start = (bf16[512,512]{1,0:T(8,128)(2,1)S(1)}, bf16[512,512]{1,0:T(8,128)(2,1)S(1)}, u32[]{:S(2)}, u32[]{:S(2)}) collective-permute-start(bf16[512,512]{1,0:T(8,128)(2,1)S(1)} %get-tuple-element.20.occupied), channel_id=1, source_target_pairs={{0,2},{2,0},{1,3},{3,1},{4,6},{6,4},{5,7},{7,5},{8,10},{10,8},{9,1... | collective-permute-start | bytes 1572872 | tf_op jit(solution)/shard_map/ppermute | solution.py:191
  4.9 25.6 %collective-permute-start.2 = (bf16[2,512,256]{2,1,0:T(8,128)(2,1)S(1)}, bf16[2,512,256]{2,1,0:T(8,128)(2,1)S(1)}, u32[]{:S(2)}, u32[]{:S(2)}) collective-permute-start(bf16[2,512,256]{2,1,0:T(8,128)(2,1)S(1)} %get-tuple-element.21.masked), channel_id=1, source_target_pairs={{0,8},{4,12},{8,0},{12,4},{1,9},{5,13},{9,1},{13,5},{2,10},{6,14},... | collective-permute-start | bytes 1572872 | tf_op jit(solution)/shard_map/ppermute | solution.py:190
  18.0 14.7 %collective-permute-start.3 = (bf16[2,128,256]{2,1,0:T(8,128)(2,1)S(1)}, bf16[2,128,256]{2,1,0:T(8,128)(2,1)S(1)}, u32[]{:S(2)}, u32[]{:S(2)}) collective-permute-start(bf16[2,128,256]{2,1,0:T(8,128)(2,1)S(1)} %get-tuple-element.24.refs_1_), channel_id=1, source_target_pairs={{0,2},{2,0},{4,6},{6,4},{8,10},{10,8},{12,14},{14,12},{1,3},{3,1},... | collective-permute-start | bytes 393224 | tf_op jit(solution)/shard_map/ppermute | solution.py:199
  21.1 9.4 %collective-permute-start.1 = (f32[2,128]{1,0:T(2,128)S(1)}, f32[2,128]{1,0:T(2,128)S(1)}, u32[]{:S(2)}, u32[]{:S(2)}) collective-permute-start(f32[2,128]{1,0:T(2,128)S(1)} %density_terms.1.value), channel_id=1, source_target_pairs={{0,1},{1,0},{2,3},{3,2},{4,5},{5,4},{6,7},{7,6},{8,9},{9,8},{10,11... | collective-permute-start | bytes 3080 | tf_op jit(solution)/shard_map/ppermute | solution.py:218
  21.2 13.9 %collective-permute-start.4 = (bf16[2,128,256]{2,1,0:T(8,128)(2,1)S(1)}, bf16[2,128,256]{2,1,0:T(8,128)(2,1)S(1)}, u32[]{:S(2)}, u32[]{:S(2)}) collective-permute-start(bf16[2,128,256]{2,1,0:T(8,128)(2,1)S(1)} %get-tuple-element.25.refs_2_), channel_id=1, source_target_pairs={{0,4},{2,6},{4,0},{6,2},{8,12},{10,14},{12,8},{14,10},{1,5},{3,7},... | collective-permute-start | bytes 393224 | tf_op jit(solution)/shard_map/ppermute | solution.py:199
  22.8 13.2 %collective-permute-start.5 = (bf16[2,128,256]{2,1,0:T(8,128)(2,1)S(1)}, bf16[2,128,256]{2,1,0:T(8,128)(2,1)S(1)}, u32[]{:S(2)}, u32[]{:S(2)}) collective-permute-start(bf16[2,128,256]{2,1,0:T(8,128)(2,1)S(1)} %get-tuple-element.26.refs_3_), channel_id=1, source_target_pairs={{0,6},{2,4},{4,2},{6,0},{8,14},{10,12},{12,10},{14,8},{1,7},{3,5},... | collective-permute-start | bytes 393224 | tf_op jit(solution)/shard_map/ppermute | solution.py:199
  31.5 7.7 %collective-permute-start.6 = (bf16[2,128,256]{2,1,0:T(8,128)(2,1)S(1)}, bf16[2,128,256]{2,1,0:T(8,128)(2,1)S(1)}, u32[]{:S(2)}, u32[]{:S(2)}) collective-permute-start(bf16[2,128,256]{2,1,0:T(8,128)(2,1)S(1)} %get-tuple-element.31), channel_id=1, source_target_pairs={{0,2},{2,0},{4,6},{6,4},{8,10},{10,8},{12,14},{14,12},{1,3},{3,1},... | collective-permute-start | bytes 393224 | tf_op jit(solution)/shard_map/ppermute | solution.py:199
  32.1 7.2 %collective-permute-start.7 = (bf16[2,128,256]{2,1,0:T(8,128)(2,1)S(1)}, bf16[2,128,256]{2,1,0:T(8,128)(2,1)S(1)}, u32[]{:S(2)}, u32[]{:S(2)}) collective-permute-start(bf16[2,128,256]{2,1,0:T(8,128)(2,1)S(1)} %get-tuple-element.32), channel_id=1, source_target_pairs={{0,4},{2,6},{4,0},{6,2},{8,12},{10,14},{12,8},{14,10},{1,5},{3,7},... | collective-permute-start | bytes 393224 | tf_op jit(solution)/shard_map/ppermute | solution.py:199
  32.7 8.9 %collective-permute-start.8 = (bf16[2,128,256]{2,1,0:T(8,128)(2,1)S(1)}, bf16[2,128,256]{2,1,0:T(8,128)(2,1)S(1)}, u32[]{:S(2)}, u32[]{:S(2)}) collective-permute-start(bf16[2,128,256]{2,1,0:T(8,128)(2,1)S(1)} %get-tuple-element.33), channel_id=1, source_target_pairs={{0,6},{2,4},{4,2},{6,0},{8,14},{10,12},{12,10},{14,8},{1,7},{3,5},... | collective-permute-start | bytes 393224 | tf_op jit(solution)/shard_map/ppermute | solution.py:199
  36.9 6.4 %collective-permute-start.9 = (bf16[8,128,128]{2,1,0:T(8,128)(2,1)S(1)}, bf16[8,128,128]{2,1,0:T(8,128)(2,1)S(1)}, u32[]{:S(2)}, u32[]{:S(2)}) collective-permute-start(bf16[8,128,128]{2,1,0:T(8,128)(2,1)S(1)} %get-tuple-element.35), channel_id=1, source_target_pairs={{0,1},{1,0},{2,3},{3,2},{4,5},{5,4},{6,7},{7,6},{8,9},{9,8},{10,11... | collective-permute-start | bytes 786440 | tf_op jit(solution)/shard_map/ppermute | solution.py:235
  42.4 1.6 %collective-permute-start.10 = (bf16[8,128,128]{2,1,0:T(8,128)(2,1)S(1)}, bf16[8,128,128]{2,1,0:T(8,128)(2,1)S(1)}, u32[]{:S(2)}, u32[]{:S(2)}) collective-permute-start(bf16[8,128,128]{2,1,0:T(8,128)(2,1)S(1)} %get-tuple-element.37), channel_id=1, source_target_pairs={{0,1},{1,0},{2,3},{3,2},{4,5},{5,4},{6,7},{7,6},{8,9},{9,8},{10,11... | collective-permute-start | bytes 786440 | tf_op jit(solution)/shard_map/ppermute | solution.py:239

commit v5 on v4

v5 whole, which is shorter than its diff:
```python
import functools
import math

import jax
import jax.numpy as jnp
from jax import lax
from jax.experimental import pallas as pl
from jax.experimental.pallas import tpu as pltpu
from jax.sharding import PartitionSpec as P

NOCC = 1024
BLK = 128
NBLK = 4
NB = 512
GROUP = 16
MIB = 1024 * 1024
SMEM = pl.BlockSpec(memory_space=pltpu.SMEM)
VMEM = pl.BlockSpec(memory_space=pltpu.VMEM)


def first_kernel(place, pattern, blocks, occupied, ligand, masked, panel, first, second, orbitals, held, opened, sems):
    aux_rows, _, nu_width = blocks.shape
    get = [(blocks, held), (pattern, opened), (occupied, panel), (ligand, orbitals)]
    get = [pltpu.make_async_copy(source, target, sems.at[k]) for k, (source, target) in enumerate(get)]
    for copy in get:
        copy.start()

    def fill(panel_slot, blocks_slot):
        again = pltpu.make_async_copy(occupied, panel_slot, sems.at[len(get)])
        again.start()
        get[0].wait()
        get[1].wait()
        for q in range(aux_rows):
            for m in range(NBLK):
                for n in range(nu_width // BLK):
                    rows, columns = pl.ds(m * BLK, BLK), pl.ds(n * BLK, BLK)
                    wide = pl.ds(q * nu_width + n * BLK, BLK)
                    tile = held[q, rows, columns]
                    tile = jnp.where(opened[0, n, m] != 0, tile, jnp.zeros_like(tile))
                    masked[rows, wide] = tile
                    blocks_slot[rows, wide] = tile
        again.wait()

    pl.when(place[2] == 0)(functools.partial(fill, first, second))
    pl.when(place[2] != 0)(functools.partial(fill, second, first))
    for copy in get[2:]:
        copy.wait()


def slot_of(place, d):
    return (2 * (place[0] & 1) + place[1]) ^ d


def rows_kernel(place, masked, panel, got_first, got_second, turned, *outs):
    ni = turned.shape[1]
    _, _, nu_width = outs[0].shape
    aux_rows = outs[0].shape[0] // 2
    near = place[1] == place[0] // 2
    first_core = place[2] == 0

    def turn(source):
        for s in range(turned.shape[0]):
            turned[s] = source[:, s * ni : (s + 1) * ni].T

    pl.when(near)(functools.partial(turn, panel))
    pl.when(jnp.logical_and(jnp.logical_not(near), first_core))(functools.partial(turn, got_first))
    pl.when(jnp.logical_not(jnp.logical_or(near, first_core)))(functools.partial(turn, got_second))

    def half(source, first):
        for k, out in enumerate(outs):
            d = k ^ (3 * place[2]) if k in (1, 2) else k
            result = jnp.dot(turned[slot_of(place, d)], source[...], preferred_element_type=jnp.float32)
            result = result.astype(jnp.bfloat16)
            for q in range(aux_rows):
                out[first + q] = result[:, q * nu_width : (q + 1) * nu_width]

    half(masked, 0)
    pl.when(first_core)(functools.partial(half, got_second, aux_rows))
    pl.when(jnp.logical_not(first_core))(functools.partial(half, got_first, aux_rows))


def density_kernel(place, panel, got_first, got_second, masked, turned, *refs):
    messages, out = refs[:-1], refs[-1]
    _, ni, nu_width = messages[0].shape
    aux_rows = messages[0].shape[0] // 2
    own = pl.ds(pl.multiple_of(place[2] * nu_width, nu_width), nu_width)
    near = place[1] == place[0] // 2
    first_core = place[2] == 0

    def terms(panel):
        totals = [0.0] * aux_rows
        for k, message in enumerate(messages):
            d = k ^ (3 * place[2]) if k in (1, 2) else k
            rows = turned[slot_of(place, d), :, own].astype(jnp.float32)
            for q in range(aux_rows):
                totals[q] += jnp.sum(rows * message[q].astype(jnp.float32))
        for s in range(4):
            rows = panel[:, s * ni : (s + 1) * ni].T
            weights = panel[own, s * ni : (s + 1) * ni].T.astype(jnp.float32)
            result = jnp.dot(rows, masked[...], preferred_element_type=jnp.float32).astype(jnp.bfloat16)
            for q in range(aux_rows):
                totals[q] += jnp.sum(weights * result[:, q * nu_width : (q + 1) * nu_width].astype(jnp.float32))
        for q in range(aux_rows):
            out[q : q + 1, :] = jnp.full((1, out.shape[1]), totals[q], jnp.float32)

    pl.when(jnp.logical_not(near))(functools.partial(terms, panel))
    pl.when(jnp.logical_and(near, first_core))(functools.partial(terms, got_first))
    pl.when(jnp.logical_and(near, jnp.logical_not(first_core)))(functools.partial(terms, got_second))


def pair_kernel(place, after, ligand, *refs):
    arrived, own, sent = refs[:-2], refs[-2], refs[-1]
    aux_rows, ni, nu_width = arrived[0].shape
    width = ligand.shape[1]
    rows = ligand[pl.ds(pl.multiple_of(place[2] * nu_width, nu_width), nu_width), :]
    for k, message in enumerate(arrived):
        part = jnp.dot(
            message[...].reshape(aux_rows * ni, nu_width), rows, preferred_element_type=jnp.float32
        ).reshape(aux_rows, ni, width)
        there = k ^ 3 if k in (1, 2) else k
        own[k * aux_rows : (k + 1) * aux_rows] = part
        sent[there * aux_rows : (there + 1) * aux_rows] = part.astype(jnp.bfloat16)


def turn_kernel(*refs):
    messages, out = refs[:-1], refs[-1]
    nu_width = messages[0].shape[2]
    for g in range(out.shape[0]):
        here = pl.ds(g * GROUP, GROUP)
        out[g] = jnp.concatenate([x[:, here, :].reshape(-1, nu_width) for x in messages], axis=0).T


def cross_kernel(scale, turned, own, other, out, held, sem):
    ni, _, width = out.shape

    def step(g, carry):
        here = pl.ds(pl.multiple_of(g * GROUP, GROUP), GROUP)
        summed = ((own[:, here, :] + other[:, here, :].astype(jnp.float32)) * scale).astype(jnp.bfloat16)
        row = lax.broadcasted_iota(jnp.int32, (1, GROUP, width), 1)
        zero = jnp.zeros_like(summed)
        for i in range(0, GROUP, 2):
            both = [jnp.where(row == i + e, summed, zero).reshape(-1, width) for e in (0, 1)]
            result = jnp.dot(turned[g], jnp.concatenate(both, axis=1), preferred_element_type=jnp.float32)
            held[g * GROUP + i] = result[:, :width]
            held[g * GROUP + i + 1] = result[:, width:]
            if i % 4 == 2:
                done = pl.ds(g * GROUP + i - 2, 4)
                pltpu.make_async_copy(held.at[done], out.at[done], sem).start()
        return carry

    lax.fori_loop(0, ni // GROUP, step, 0)
    pltpu.make_async_copy(held, out, sem).wait()


def call(kernel, name, inputs, outputs, scratch=(), limit=16, scalars=1, flops=0, moved=1 << 20, in_spec=VMEM, out_spec=VMEM):
    inputs = list(inputs)
    results = pl.pallas_call(
        kernel,
        in_specs=[SMEM] * scalars + [in_spec] * (len(inputs) - scalars),
        out_specs=[out_spec] * len(outputs),
        out_shape=outputs,
        scratch_shapes=list(scratch),
        compiler_params=pltpu.CompilerParams(vmem_limit_bytes=limit * MIB),
        cost_estimate=pl.CostEstimate(flops=flops, bytes_accessed=moved, transcendentals=0),
        name=name,
    )(*inputs)
    return list(results)


def body(sizes, blocks, pattern, occupied, ligand):
    n_aux, n_orb, n_ao = sizes
    aux_rows, _, nu_width = blocks.shape
    owners = n_aux * n_orb
    ni = NOCC // owners
    q_total = aux_rows * owners
    panel_width = occupied.shape[1]
    width = ligand.shape[1]
    place = jnp.stack([lax.axis_index(name) for name in ("aux", "orb", "ao")]).astype(jnp.int32)
    bf16 = functools.partial(jax.ShapeDtypeStruct, dtype=jnp.bfloat16)
    f32 = functools.partial(jax.ShapeDtypeStruct, dtype=jnp.float32)

    swap = [(c, 1 - c) for c in range(n_ao)]
    axes = ("aux", "orb", "ao")
    everyone = [(a, o, c) for a in range(n_aux) for o in range(n_orb) for c in range(n_ao)]

    def send(x, target):
        number = lambda a, o, c: (a * n_orb + o) * n_ao + c
        return lax.ppermute(x, axes, [(number(*here), number(*target(*here))) for here in everyone])

    pattern = jnp.swapaxes(pattern, 1, 2)
    square = bf16((NB, panel_width))
    hbm = pl.BlockSpec(memory_space=pltpu.HBM)
    masked, panel, first, second, orbitals = call(
        first_kernel,
        "masked_blocks",
        (place, *(pltpu.with_memory_space_constraint(x, pltpu.HBM) for x in (pattern, blocks, occupied, ligand))),
        [square] * 4 + [bf16(ligand.shape)],
        [
            pltpu.VMEM(blocks.shape, jnp.bfloat16),
            pltpu.SMEM(pattern.shape, pattern.dtype),
            pltpu.SemaphoreType.DMA((5,)),
        ],
        in_spec=hbm,
    )
    got_first = send(first, lambda a, o, c: (a ^ 2, o, c) if c else (a, 1 - o, c))
    got_second = send(second, lambda a, o, c: (a, 1 - o, c) if c else (a ^ 2, o, c))

    work = 2 * NB * panel_width * nu_width * aux_rows
    turned, *rows = call(
        rows_kernel,
        "half_rows",
        (place, masked, panel, got_first, got_second),
        [bf16((4, ni, NB))] + [bf16((2 * aux_rows, ni, nu_width))] * 4,
        flops=2 * work,
    )
    arrived = [rows[0]]
    arrived.append(send(rows[1], lambda a, o, c: (a ^ 1, o, c) if c else (a, 1 - o, c)))
    arrived.append(send(rows[2], lambda a, o, c: (a, 1 - o, c) if c else (a ^ 1, o, c)))
    arrived.append(send(rows[3], lambda a, o, c: (a ^ 1, 1 - o, c)))

    value = call(
        density_kernel,
        "density_terms",
        (place, panel, got_first, got_second, masked, turned, *rows),
        [f32((aux_rows, 128))],
        flops=work,
    )[0]
    density = (value[:, 0] + lax.ppermute(value, "ao", swap)[:, 0]) / math.sqrt(NOCC)

    shape = (q_total, ni, width)
    own, given = call(
        pair_kernel,
        "pair_terms",
        (place, value, orbitals, *arrived),
        [f32(shape), bf16(shape)],
        flops=2 * q_total * ni * nu_width * width,
    )
    other = lax.ppermute(given, "ao", swap)
    columns = call(turn_kernel, "turned", arrived, [bf16((ni // GROUP, nu_width, q_total * GROUP))], scalars=0)[0]

    result = (ni, nu_width, width)
    cross_terms = call(
        functools.partial(cross_kernel, 1.0 / math.sqrt(q_total)),
        "cross_terms",
        (columns, own, other),
        [f32(result)],
        [pltpu.VMEM(result, jnp.float32), pltpu.SemaphoreType.DMA],
        limit=32,
        scalars=0,
        flops=32 * q_total * ni * nu_width * width,
        moved=18 * MIB,
        out_spec=hbm,
    )[0]
    return (density, cross_terms)


def plain_body(blocks, pattern, occupied, ligand):
    panels = lax.all_gather(occupied, "orb", axis=1, tiled=True)
    aux_rows = blocks.shape[0]
    nu_width = blocks.shape[2]
    nu_blocks = pattern.shape[2]
    opened = pattern[0].astype(jnp.bfloat16)
    masked = blocks.reshape(aux_rows, NBLK, BLK, nu_blocks, BLK) * opened[None, :, None, :, None]
    masked = masked.reshape(aux_rows, NB, nu_width)
    transformed = jnp.einsum(
        "qmn,mi->qin", masked, panels, preferred_element_type=jnp.float32
    ).astype(jnp.bfloat16)
    nu_start = lax.axis_index("ao") * nu_width
    own_rows = lax.dynamic_slice_in_dim(panels, nu_start, nu_width, 0)
    partial_value = jnp.einsum(
        "qin,ni->q", transformed, own_rows, preferred_element_type=jnp.float32
    )
    density = lax.psum(partial_value, "ao") / math.sqrt(NOCC)
    arrived = lax.all_to_all(transformed, ("aux", "orb"), split_axis=1, concat_axis=0, tiled=True)
    own_ligand = lax.dynamic_slice_in_dim(ligand, nu_start, nu_width, 0)
    pair_part = jnp.einsum("qin,nj->qij", arrived, own_ligand, preferred_element_type=jnp.float32)
    mixed_pairs = lax.psum(pair_part, "ao").astype(jnp.bfloat16)
    crossed = jnp.einsum("qin,qij->inj", arrived, mixed_pairs, preferred_element_type=jnp.float32)
    cross_terms = crossed / math.sqrt(arrived.shape[0])
    return (density, cross_terms)


def solution(mesh):
    sizes = (mesh.shape["aux"], mesh.shape["orb"], mesh.shape["ao"])
    kernels = sizes == (4, 2, 2)
    return jax.shard_map(
        functools.partial(body, sizes) if kernels else plain_body,
        mesh=mesh,
        in_specs=(
            P(("pose", "aux", "orb"), None, "ao"),
            P(("pose", "aux", "orb"), None, "ao"),
            P(None, "orb"),
            P(None, "pose"),
        ),
        out_specs=(P(("pose", "aux", "orb")), P(("pose", "aux", "orb"), "ao", None)),
        check_vma=False,
    )
```

time: 50.2 us -> 56.2 us (1.12)
  waiting for transfers between devices: 23.1 us -> 32.6 us
  starting transfers between devices: 13 us -> 9.71 us
  local copies, waits for them, and re-layouts: 0.63 us -> 0 us
  other arithmetic: 0.08 us -> 0.7 us
    ppermute x11 -> x7, waiting for transfers between devices: 23.1 us -> 32.6 us  [the longest x5 31.2 us: send(): lax.ppermute(x, axes, [(number(*here), number(*target(*here))) for here i...]
    ppermute x11 -> x7, starting transfers between devices: 13 us -> 9.71 us  [the longest x5 9.15 us: send(): lax.ppermute(x, axes, [(number(*here), number(*target(*here))) for here i...]
    div x0 -> x1, other arithmetic: none -> 0.63 us  [body(): (value[:, 0] + lax.ppermute(value, 'ao', swap)[:, 0]) / math.sqrt(NOCC)]
    slice x1 -> x0, local copies, waits for them, and re-layouts: 0.63 us -> none  [body(): return (density[:, 0], cross_terms)]
    pallas_call x8 -> x6, Pallas kernels: 12.6 us -> 12.3 us  [call(): pl.pallas_call(kernel, in_specs=[SMEM] * scalars + [in_spec] * (len(input...]
  transfers between devices with their start and end apart: 11 -> 7, of which waited for: 6 -> 4; matrix products, arithmetic and copies ran while one was open for 1% -> 1% of each run, Pallas kernels for 11% -> 3%
where the time goes in v5:
time: 56.2 us; the launch traced here: 56 us
  waiting for transfers between devices  32.6 us (58%)
  Pallas kernels  12.3 us (22%)
  starting transfers between devices  9.71 us (17%)
  other arithmetic  0.7 us (1%)
  between operations  0.69 us (1%)
    ppermute x5, waiting for transfers between devices, send(): lax.ppermute(x, axes, [(number(*here), number(*target(*here))) for here i...  31.2 us
    pallas_call x6, Pallas kernels, call(): pl.pallas_call(kernel, in_specs=[SMEM] * scalars + [in_spec] * (len(input...  12.3 us
    ppermute x5, starting transfers between devices, send(): lax.ppermute(x, axes, [(number(*here), number(*target(*here))) for here i...  9.15 us
    ppermute x1, waiting for transfers between devices, body(): lax.ppermute(value, 'ao', swap)[:, 0]  1.4 us
  transfers between devices with their start and end apart: 7, of which 4 were waited for; matrix products, arithmetic and copies ran while one was open for 1% of the time, Pallas kernels for 3%

profile of v5, /device:TPU:0, one launch (start us, length us, event | category | flops | bytes accessed | tf_op | source)
XLA Modules:
  0.0 56.0 jit_solution(11952718508173334657)
XLA Ops:
  0.6 0.1 pad_add_fusion.place
  0.7 2.1 %masked_blocks.1 = (bf16[512,512]{1,0:T(8,128)(2,1)S(1)}, bf16[512,512]{1,0:T(8,128)(2,1)S(1)}, bf16[512,512]{1,0:T(8,128)(2,1)S(1)}, bf16[512,512]{1,0:T(8,128)(2,1)S(1)}, bf16[512,128]{1,0:T(8,128)(2,1)S(1)}) custom-call(s32[3]{0:T(128)S(1)} %pad_add_fusion.place, s32[1,2,4]{2,1,0:T(2,128)} %bitcast.4, bf16[2,512,256]{2,1,0:T(8,128)(2,1)} %blocks.1, ...), custom_call_target="tpu_custom_call" | custom-call | bytes 1048576 | tf_op jit(solution)/shard_map/masked_blocks/pallas_call | solution.py:157
  2.8 3.0 %collective-permute-start = (bf16[512,512]{1,0:T(8,128)(2,1)S(1)}, bf16[512,512]{1,0:T(8,128)(2,1)S(1)}, u32[]{:S(2)}, u32[]{:S(2)}) collective-permute-start(bf16[512,512]{1,0:T(8,128)(2,1)S(1)} %get-tuple-element.15), channel_id=1, source_target_pairs={{0,2},{1,9},{2,0},{3,11},{4,6},{5,13},{6,4},{7,15},{8,10},{9,1},{1... | collective-permute-start | bytes 1572872 | tf_op jit(solution)/shard_map/ppermute | solution.py:188
  5.8 2.6 %collective-permute-start.1 = (bf16[512,512]{1,0:T(8,128)(2,1)S(1)}, bf16[512,512]{1,0:T(8,128)(2,1)S(1)}, u32[]{:S(2)}, u32[]{:S(2)}) collective-permute-start(bf16[512,512]{1,0:T(8,128)(2,1)S(1)} %get-tuple-element.16), channel_id=1, source_target_pairs={{0,8},{1,3},{2,10},{3,1},{4,12},{5,7},{6,14},{7,5},{8,0},{9,11},{1... | collective-permute-start | bytes 1572872 | tf_op jit(solution)/shard_map/ppermute | solution.py:188
  8.4 8.5 %collective-permute-done.got_first = bf16[512,512]{1,0:T(8,128)(2,1)S(1)} collective-permute-done((bf16[512,512]{1,0:T(8,128)(2,1)S(1)}, bf16[512,512]{1,0:T(8,128)(2,1)S(1)}, u32[]{:S(2)}, u32[]{:S(2)}) %collective-permute-start) | collective-permute-done | bytes 524320 | tf_op jit(solution)/shard_map/ppermute | solution.py:188
  16.9 13.1 %collective-permute-done.1.got_second = bf16[512,512]{1,0:T(8,128)(2,1)S(1)} collective-permute-done((bf16[512,512]{1,0:T(8,128)(2,1)S(1)}, bf16[512,512]{1,0:T(8,128)(2,1)S(1)}, u32[]{:S(2)}, u32[]{:S(2)}) %collective-permute-start.1) | collective-permute-done | bytes 524320 | tf_op jit(solution)/shard_map/ppermute | solution.py:188
  30.1 1.6 %half_rows.1 = (bf16[4,128,512]{2,1,0:T(8,128)(2,1)S(1)}, bf16[4,128,256]{2,1,0:T(8,128)(2,1)S(1)}, bf16[4,128,256]{2,1,0:T(8,128)(2,1)S(1)}, bf16[4,128,256]{2,1,0:T(8,128)(2,1)S(1)}, bf16[4,128,256]{2,1,0:T(8,128)(2,1)S(1)}) custom-call(s32[3]{0:T(128)S(1)} %pad_add_fusion.place, bf16[512,512]{1,0:T(8,128)(2,1)S(1)} %get-tuple-element.17.masked, ...), custom_call_target="tpu_custom_call" | custom-call | flops 536870912 | bytes 1048576 | tf_op jit(solution)/shard_map/half_rows/pallas_call | solution.py:157
  31.7 1.6 %collective-permute-start.3 = (bf16[4,128,256]{2,1,0:T(8,128)(2,1)S(1)}, bf16[4,128,256]{2,1,0:T(8,128)(2,1)S(1)}, u32[]{:S(2)}, u32[]{:S(2)}) collective-permute-start(bf16[4,128,256]{2,1,0:T(8,128)(2,1)S(1)} %get-tuple-element.20.refs_1_), channel_id=1, source_target_pairs={{0,2},{1,5},{2,0},{3,7},{4,6},{5,1},{6,4},{7,3},{8,10},{9,13},{10,... | collective-permute-start | bytes 786440 | tf_op jit(solution)/shard_map/ppermute | solution.py:188
  33.3 0.7 %collective-permute-start.4 = (bf16[4,128,256]{2,1,0:T(8,128)(2,1)S(1)}, bf16[4,128,256]{2,1,0:T(8,128)(2,1)S(1)}, u32[]{:S(2)}, u32[]{:S(2)}) collective-permute-start(bf16[4,128,256]{2,1,0:T(8,128)(2,1)S(1)} %get-tuple-element.21.refs_2_), channel_id=1, source_target_pairs={{0,4},{1,3},{2,6},{3,1},{4,0},{5,7},{6,2},{7,5},{8,12},{9,11},{10,... | collective-permute-start | bytes 786440 | tf_op jit(solution)/shard_map/ppermute | solution.py:188
  34.0 1.3 %collective-permute-start.5 = (bf16[4,128,256]{2,1,0:T(8,128)(2,1)S(1)}, bf16[4,128,256]{2,1,0:T(8,128)(2,1)S(1)}, u32[]{:S(2)}, u32[]{:S(2)}) collective-permute-start(bf16[4,128,256]{2,1,0:T(8,128)(2,1)S(1)} %get-tuple-element.22.refs_3_), channel_id=1, source_target_pairs={{0,6},{1,7},{2,4},{3,5},{4,2},{5,3},{6,0},{7,1},{8,14},{9,15},{10,... | collective-permute-start | bytes 786440 | tf_op jit(solution)/shard_map/ppermute | solution.py:188
  35.2 1.3 %density_terms.1.after = f32[2,128]{1,0:T(2,128)S(1)} custom-call(s32[3]{0:T(128)S(1)} %pad_add_fusion.place, bf16[512,512]{1,0:T(8,128)(2,1)S(1)} %get-tuple-element.14.panel, bf16[512,512]{1,0:T(8,128)(2,1)S(1)} %collective-permute-done.got_first, bf16[512,512]{1,0:T(8,128)(2,1)S(1)} %collective-permute-done.1.got_second, ...), custom_call_target="tpu_custom_call" | custom-call | flops 268435456 | bytes 1048576 | tf_op jit(solution)/shard_map/density_terms/pallas_call | solution.py:157
  36.6 9.5 %collective-permute-done.3.refs_1_ = bf16[4,128,256]{2,1,0:T(8,128)(2,1)S(1)} collective-permute-done((bf16[4,128,256]{2,1,0:T(8,128)(2,1)S(1)}, bf16[4,128,256]{2,1,0:T(8,128)(2,1)S(1)}, u32[]{:S(2)}, u32[]{:S(2)}) %collective-permute-start.3) | collective-permute-done | bytes 262176 | tf_op jit(solution)/shard_map/ppermute | solution.py:188
  46.1 0.0 collective-permute-done.4.refs_2_
  46.1 0.0 collective-permute-done.5.refs_3_
  46.1 1.0 %pair_terms.1 = (f32[16,128,128]{2,1,0:T(8,128)S(1)}, bf16[16,128,128]{2,1,0:T(8,128)(2,1)S(1)}) custom-call(s32[3]{0:T(128)S(1)} %pad_add_fusion.place, f32[2,128]{1,0:T(2,128)S(1)} %density_terms.1.after, bf16[512,128]{1,0:T(8,128)(2,1)S(1)} %get-tuple-element.23.ligand, bf16[4,128,256]{2,1,0:T(8,128)(2,1)S(1)} %get-tuple-element.19.refs_0_, ...), custom_call_target="tpu_custom_call" | custom-call | flops 134217728 | bytes 1048576 | tf_op jit(solution)/shard_map/pair_terms/pallas_call | solution.py:157
  47.1 0.1 collective-permute-start.6
  47.1 0.5 collective-permute-start.2
  47.6 1.4 %collective-permute-done.2 = f32[2,128]{1,0:T(2,128)S(1)} collective-permute-done((f32[2,128]{1,0:T(2,128)S(1)}, f32[2,128]{1,0:T(2,128)S(1)}, u32[]{:S(2)}, u32[]{:S(2)}) %collective-permute-start.2) | collective-permute-done | bytes 1056 | tf_op jit(solution)/shard_map/ppermute | solution.py:228
  49.0 0.6 %multiply_reduce_fusion = f32[2]{0:T(128)} fusion(f32[2,128]{1,0:T(2,128)S(1)} %collective-permute-done.2, f32[2,128]{1,0:T(2,128)S(1)} %density_terms.1.after), kind=kLoop, calls=%fused_computation | loop fusion | flops 4 | bytes 24 | tf_op jit(solution)/shard_map/div | solution.py:228
  49.7 0.3 turned.1
  50.0 0.0 collective-permute-done.6.other
  50.0 6.0 %cross_terms.1 = f32[128,256,128]{2,1,0:T(8,128)} custom-call(bf16[8,256,256]{2,1,0:T(8,128)(2,1)S(1)} %turned.1, f32[16,128,128]{2,1,0:T(8,128)S(1)} %get-tuple-element.24.own, bf16[16,128,128]{2,1,0:T(8,128)(2,1)S(1)} %collective-permute-done.6.other), custom_call_target="tpu_custom_call" | custom-call | flops 2147483648 | bytes 18874368 | tf_op jit(solution)/shard_map/cross_terms/pallas_call | solution.py:157
Async XLA Ops:
  2.8 14.1 %collective-permute-start = (bf16[512,512]{1,0:T(8,128)(2,1)S(1)}, bf16[512,512]{1,0:T(8,128)(2,1)S(1)}, u32[]{:S(2)}, u32[]{:S(2)}) collective-permute-start(bf16[512,512]{1,0:T(8,128)(2,1)S(1)} %get-tuple-element.15), channel_id=1, source_target_pairs={{0,2},{1,9},{2,0},{3,11},{4,6},{5,13},{6,4},{7,15},{8,10},{9,1},{1... | collective-permute-start | bytes 1572872 | tf_op jit(solution)/shard_map/ppermute | solution.py:188
  5.8 24.3 %collective-permute-start.1 = (bf16[512,512]{1,0:T(8,128)(2,1)S(1)}, bf16[512,512]{1,0:T(8,128)(2,1)S(1)}, u32[]{:S(2)}, u32[]{:S(2)}) collective-permute-start(bf16[512,512]{1,0:T(8,128)(2,1)S(1)} %get-tuple-element.16), channel_id=1, source_target_pairs={{0,8},{1,3},{2,10},{3,1},{4,12},{5,7},{6,14},{7,5},{8,0},{9,11},{1... | collective-permute-start | bytes 1572872 | tf_op jit(solution)/shard_map/ppermute | solution.py:188
  31.7 14.4 %collective-permute-start.3 = (bf16[4,128,256]{2,1,0:T(8,128)(2,1)S(1)}, bf16[4,128,256]{2,1,0:T(8,128)(2,1)S(1)}, u32[]{:S(2)}, u32[]{:S(2)}) collective-permute-start(bf16[4,128,256]{2,1,0:T(8,128)(2,1)S(1)} %get-tuple-element.20.refs_1_), channel_id=1, source_target_pairs={{0,2},{1,5},{2,0},{3,7},{4,6},{5,1},{6,4},{7,3},{8,10},{9,13},{10,... | collective-permute-start | bytes 786440 | tf_op jit(solution)/shard_map/ppermute | solution.py:188
  33.3 12.8 %collective-permute-start.4 = (bf16[4,128,256]{2,1,0:T(8,128)(2,1)S(1)}, bf16[4,128,256]{2,1,0:T(8,128)(2,1)S(1)}, u32[]{:S(2)}, u32[]{:S(2)}) collective-permute-start(bf16[4,128,256]{2,1,0:T(8,128)(2,1)S(1)} %get-tuple-element.21.refs_2_), channel_id=1, source_target_pairs={{0,4},{1,3},{2,6},{3,1},{4,0},{5,7},{6,2},{7,5},{8,12},{9,11},{10,... | collective-permute-start | bytes 786440 | tf_op jit(solution)/shard_map/ppermute | solution.py:188
  34.0 12.1 %collective-permute-start.5 = (bf16[4,128,256]{2,1,0:T(8,128)(2,1)S(1)}, bf16[4,128,256]{2,1,0:T(8,128)(2,1)S(1)}, u32[]{:S(2)}, u32[]{:S(2)}) collective-permute-start(bf16[4,128,256]{2,1,0:T(8,128)(2,1)S(1)} %get-tuple-element.22.refs_3_), channel_id=1, source_target_pairs={{0,6},{1,7},{2,4},{3,5},{4,2},{5,3},{6,0},{7,1},{8,14},{9,15},{10,... | collective-permute-start | bytes 786440 | tf_op jit(solution)/shard_map/ppermute | solution.py:188
  47.1 2.9 %collective-permute-start.6 = (bf16[16,128,128]{2,1,0:T(8,128)(2,1)S(1)}, bf16[16,128,128]{2,1,0:T(8,128)(2,1)S(1)}, u32[]{:S(2)}, u32[]{:S(2)}) collective-permute-start(bf16[16,128,128]{2,1,0:T(8,128)(2,1)S(1)} %get-tuple-element.25), channel_id=1, source_target_pairs={{0,1},{1,0},{2,3},{3,2},{4,5},{5,4},{6,7},{7,6},{8,9},{9,8},{10,11... | collective-permute-start | bytes 1572872 | tf_op jit(solution)/shard_map/ppermute | solution.py:238
  47.1 1.9 %collective-permute-start.2 = (f32[2,128]{1,0:T(2,128)S(1)}, f32[2,128]{1,0:T(2,128)S(1)}, u32[]{:S(2)}, u32[]{:S(2)}) collective-permute-start(f32[2,128]{1,0:T(2,128)S(1)} %density_terms.1.after), channel_id=1, source_target_pairs={{0,1},{1,0},{2,3},{3,2},{4,5},{5,4},{6,7},{7,6},{8,9},{9,8},{10,11... | collective-permute-start | bytes 3080 | tf_op jit(solution)/shard_map/ppermute | solution.py:228

commit v6 on v4

--- a/solution.py
+++ b/solution.py
@@ -18,9 +18,10 @@
 VMEM = pl.BlockSpec(memory_space=pltpu.VMEM)
 
 
-def masked_kernel(pattern, blocks, occupied, ligand, masked, panel, orbitals, held, opened, sems):
+def masked_kernel(place, pattern, blocks, occupied, ligand, masked, panel, part, orbitals, held, opened, sems):
     aux_rows, _, nu_width = blocks.shape
-    moves = ((blocks, held), (pattern, opened), (occupied, panel), (ligand, orbitals))
+    own = occupied.at[pl.ds(pl.multiple_of(place[2] * part.shape[0], part.shape[0]), part.shape[0])]
+    moves = ((blocks, held), (pattern, opened), (own, part), (occupied, panel), (ligand, orbitals))
     copies = [pltpu.make_async_copy(source, target, sems.at[k]) for k, (source, target) in enumerate(moves)]
     for copy in copies:
         copy.start()
@@ -47,53 +48,62 @@
             out[q] = jnp.dot(rows, masked[q], preferred_element_type=jnp.float32).astype(jnp.bfloat16)
 
 
-def own_kernel(place, occupied, other, masked, turned, *outs):
+def own_kernel(place, occupied, mine, theirs, masked, turned, *outs):
     ni = turned.shape[1]
     near = place[1] == place[0] // 2
 
-    def turn(panel):
+    @pl.when(near)
+    def _():
         for s in range(turned.shape[0]):
-            turned[s] = panel[:, s * ni : (s + 1) * ni].T
-
-    pl.when(near)(functools.partial(turn, occupied))
-    pl.when(jnp.logical_not(near))(functools.partial(turn, other))
+            turned[s] = occupied[:, s * ni : (s + 1) * ni].T
+
+    @pl.when(jnp.logical_not(near))
+    def _():
+        depth = mine.shape[0]
+        for e, rows in enumerate((mine, theirs)):
+            first = pl.multiple_of((place[2] ^ e) * depth, depth)
+            for s in range(turned.shape[0]):
+                turned[s, :, pl.ds(first, depth)] = rows[:, s * ni : (s + 1) * ni].T
+
     half_into(outs, place, turned, masked)
 
 
-def density_kernel(place, occupied, other, masked, turned, *refs):
-    messages, out = refs[:-1], refs[-1]
+def density_kernel(place, occupied, mine, theirs, masked, turned, *refs):
+    messages, out, panel = refs[:-2], refs[-2], refs[-1]
     aux_rows, ni, nu_width = messages[0].shape
+    depth = mine.shape[0]
     own = pl.ds(pl.multiple_of(place[2] * nu_width, nu_width), nu_width)
     near = place[1] == place[0] // 2
 
-    def near_terms(q):
-        total = 0.0
-        for d in range(4):
-            rows = turned[slot_of(place, d), :, own].astype(jnp.float32)
-            total += jnp.sum(rows * messages[d][q].astype(jnp.float32))
-        return total
-
-    def far_terms(panel):
-        totals = [near_terms(q) for q in range(aux_rows)]
-        for s in range(4):
-            rows = panel[:, s * ni : (s + 1) * ni].T
-            weights = panel[own, s * ni : (s + 1) * ni].T.astype(jnp.float32)
-            for q in range(aux_rows):
-                result = jnp.dot(rows, masked[q], preferred_element_type=jnp.float32).astype(jnp.bfloat16)
-                totals[q] += jnp.sum(weights * result.astype(jnp.float32))
+    @pl.when(near)
+    def _():
+        for e, rows in enumerate((mine, theirs)):
+            panel[pl.ds(pl.multiple_of((place[2] ^ e) * depth, depth), depth), :] = rows[...]
+
+    @pl.when(jnp.logical_not(near))
+    def _():
+        panel[...] = occupied[...]
+
+    totals = [0.0] * aux_rows
+    for d, message in enumerate(messages):
+        rows = turned[slot_of(place, d), :, own].astype(jnp.float32)
         for q in range(aux_rows):
-            out[q : q + 1, :] = jnp.full((1, out.shape[1]), totals[q], jnp.float32)
-
-    pl.when(near)(functools.partial(far_terms, other))
-    pl.when(jnp.logical_not(near))(functools.partial(far_terms, occupied))
-
-
-def far_kernel(place, value, value_there, masked, turned, density, *outs):
-    density[...] = (value[...] + value_there[...]) / math.sqrt(NOCC)
+            totals[q] += jnp.sum(rows * message[q].astype(jnp.float32))
+    for s in range(4):
+        rows = panel[:, s * ni : (s + 1) * ni].T
+        weights = panel[own, s * ni : (s + 1) * ni].T.astype(jnp.float32)
+        for q in range(aux_rows):
+            result = jnp.dot(rows, masked[q], preferred_element_type=jnp.float32).astype(jnp.bfloat16)
+            totals[q] += jnp.sum(weights * result.astype(jnp.float32))
+    for q in range(aux_rows):
+        out[q : q + 1, :] = jnp.full((1, out.shape[1]), totals[q], jnp.float32)
+
+
+def far_kernel(place, masked, turned, *outs):
     half_into(outs, place, turned, masked)
 
 
-def pair_kernel(place, after, ligand, *refs):
+def pair_kernel(place, before, earlier, ligand, *refs):
     arrived, own, sent = refs[:-2], refs[-2], refs[-1]
     aux_rows, ni, nu_width = arrived[0].shape
     width = ligand.shape[1]
@@ -114,8 +124,8 @@
         out[g] = jnp.concatenate([x[:, here, :].reshape(-1, nu_width) for x in messages], axis=0).T
 
 
-def pair_and_turn_kernel(place, after, ligand, *refs):
-    pair_kernel(place, after, ligand, *refs[:-1])
+def pair_and_turn_kernel(place, before, earlier, ligand, *refs):
+    pair_kernel(place, before, earlier, ligand, *refs[:-1])
     turn_kernel(*refs[:-3], refs[-1])
 
 
@@ -174,21 +184,21 @@
     across = [(a, a ^ 2) for a in range(n_aux)]
     swap = [(c, 1 - c) for c in range(n_ao)]
     pattern = jnp.swapaxes(pattern, 1, 2)
-    masked, panel, orbitals = call(
+    masked, panel, part, orbitals = call(
         masked_kernel,
         "masked_blocks",
-        (pltpu.with_memory_space_constraint(x, pltpu.HBM) for x in (pattern, blocks, occupied, ligand)),
-        [bf16(blocks.shape), bf16(occupied.shape), bf16(ligand.shape)],
+        (place, *(pltpu.with_memory_space_constraint(x, pltpu.HBM) for x in (pattern, blocks, occupied, ligand))),
+        [bf16(blocks.shape), bf16(occupied.shape), bf16((NB // n_ao, panel_width)), bf16(ligand.shape)],
         [
             pltpu.VMEM(blocks.shape, jnp.bfloat16),
             pltpu.SMEM(pattern.shape, pattern.dtype),
-            pltpu.SemaphoreType.DMA((4,)),
+            pltpu.SemaphoreType.DMA((5,)),
         ],
-        scalars=0,
         in_spec=pl.BlockSpec(memory_space=pltpu.HBM),
     )
     far_masked = lax.ppermute(masked, "aux", across)
-    other = lax.ppermute(panel, "orb", swap)
+    mine = lax.ppermute(part, "orb", swap)
+    theirs = lax.ppermute(mine, "ao", swap)
 
     def square(messages):
         arrived = [messages[0]] + [None] * 3
@@ -202,23 +212,20 @@
     work = 2 * NB * panel_width * nu_width * aux_rows
     messages = [bf16((aux_rows, ni, nu_width))] * 4
     turned, *own = call(
-        own_kernel, "own_half", (place, panel, other, masked), [bf16((4, ni, NB))] + messages, flops=work
+        own_kernel, "own_half", (place, panel, mine, theirs, masked), [bf16((4, ni, NB))] + messages, flops=work
     )
     own_here = square(own)
     value = call(
         density_kernel,
         "density_terms",
-        (place, panel, other, masked, turned, *own),
+        (place, panel, mine, theirs, masked, turned, *own),
         [f32((aux_rows, 128))],
+        [pltpu.VMEM(occupied.shape, jnp.bfloat16)],
         flops=work,
     )[0]
-    density, *far = call(
-        far_kernel,
-        "far_half",
-        (place, value, lax.ppermute(value, "ao", swap), far_masked, turned),
-        [f32((aux_rows, 128))] + messages,
-        flops=work,
-    )
+    value_there = lax.ppermute(value, "ao", swap)
+    density = (value[:, 0] + value_there[:, 0]) / math.sqrt(NOCC)
+    far = call(far_kernel, "far_half", (place, far_masked, turned), messages, flops=work)
     far_here = square(far)
 
     shape = (4 * aux_rows, ni, width)
@@ -228,13 +235,13 @@
     own_kept, own_given, own_rows = call(
         pair_and_turn_kernel,
         "own_pairs",
-        (place, density, orbitals, *own_here),
+        (place, value, far[0], orbitals, *own_here),
         kept_and_given + side,
         flops=pair_work,
     )
     own_pairs = (own_kept, lax.ppermute(own_given, "ao", swap))
     far_kept, far_given = call(
-        pair_kernel, "far_pairs", (place, density, orbitals, *far_here), kept_and_given, flops=pair_work
+        pair_kernel, "far_pairs", (place, value_there, own_pairs[1], orbitals, *far_here), kept_and_given, flops=pair_work
     )
     far_pairs = (far_kept, lax.ppermute(far_given, "ao", swap))
     far_rows = call(turn_kernel, "far_turned", far_here, side, scalars=0)[0]
@@ -252,7 +259,7 @@
         moved=18 * MIB,
         out_spec=pl.BlockSpec(memory_space=pltpu.HBM),
     )[0]
-    return (density[:, 0], cross_terms)
+    return (density, cross_terms)
 
 
 def plain_body(blocks, pattern, occupied, ligand):

time: 50.2 us -> 53.9 us (1.074)
  waiting for transfers between devices: 23.1 us -> 26.1 us
  Pallas kernels: 12.6 us -> 13.3 us
  local copies, waits for them, and re-layouts: 0.63 us -> 0 us
  other arithmetic: 0.08 us -> 0.7 us
    ppermute x1, waiting for transfers between devices: 7.53 us -> 11.7 us  [body(): far_masked = lax.ppermute(masked, 'aux', across)]
    ppermute x2 -> x3, waiting for transfers between devices: 9.26 us -> 6.32 us  [the longest x1 3.65 us: body(): mine = lax.ppermute(part, 'orb', swap)]
    ppermute x6, waiting for transfers between devices: 5.61 us -> 7.37 us  [square(): arrived[d] = lax.ppermute(messages[d], ('aux', 'orb'), moves)]
    pallas_call x8, Pallas kernels: 12.6 us -> 13.3 us  [call(): pl.pallas_call(kernel, in_specs=[SMEM] * scalars + [in_spec] * (len(input...]
    div x0 -> x1, other arithmetic: none -> 0.63 us  [body(): density = (value[:, 0] + value_there[:, 0]) / math.sqrt(NOCC)]
    slice x1 -> x0, local copies, waits for them, and re-layouts: 0.63 us -> none  [body(): return (density[:, 0], cross_terms)]
    ppermute x2 -> x3, starting transfers between devices: 3.07 us -> 3.01 us  [the longest x1 3 us: body(): mine = lax.ppermute(part, 'orb', swap)]
  transfers between devices with their start and end apart: 11 -> 12, of which waited for: 6 -> 10; matrix products, arithmetic and copies ran while one was open for 1% -> 1% of each run, Pallas kernels for 11% -> 7%
where the time goes in v6:
time: 53.9 us; the launch traced here: 53.7 us
  waiting for transfers between devices  26.1 us (48%)
  Pallas kernels  13.3 us (25%)
  starting transfers between devices  12.8 us (24%)
  between operations  0.72 us (1%)
  other arithmetic  0.7 us (1%)
    pallas_call x8, Pallas kernels, call(): pl.pallas_call(kernel, in_specs=[SMEM] * scalars + [in_spec] * (len(input...  13.3 us
    ppermute x1, waiting for transfers between devices, body(): far_masked = lax.ppermute(masked, 'aux', across)  11.7 us
    ppermute x6, waiting for transfers between devices, square(): arrived[d] = lax.ppermute(messages[d], ('aux', 'orb'), moves)  7.37 us
    ppermute x6, starting transfers between devices, square(): arrived[d] = lax.ppermute(messages[d], ('aux', 'orb'), moves)  7.11 us
    ppermute x1, waiting for transfers between devices, body(): mine = lax.ppermute(part, 'orb', swap)  3.65 us
    ppermute x1, starting transfers between devices, body(): mine = lax.ppermute(part, 'orb', swap)  3 us
    ppermute x1, starting transfers between devices, body(): far_masked = lax.ppermute(masked, 'aux', across)  2.59 us
    ppermute x1, waiting for transfers between devices, body(): theirs = lax.ppermute(mine, 'ao', swap)  1.53 us
  transfers between devices with their start and end apart: 12, of which 10 were waited for; matrix products, arithmetic and copies ran while one was open for 1% of the time, Pallas kernels for 7%

profile of v6, /device:TPU:0, one launch (start us, length us, event | category | flops | bytes accessed | tf_op | source)
XLA Modules:
  0.0 53.7 jit_solution(12764181577961538062)
XLA Ops:
  0.6 0.1 pad_add_fusion.place
  0.7 2.0 %masked_blocks.1 = (bf16[2,512,256]{2,1,0:T(8,128)(2,1)S(1)}, bf16[512,512]{1,0:T(8,128)(2,1)S(1)}, bf16[256,512]{1,0:T(8,128)(2,1)S(1)}, bf16[512,128]{1,0:T(8,128)(2,1)S(1)}) custom-call(s32[3]{0:T(128)S(1)} %pad_add_fusion.place, s32[1,2,4]{2,1,0:T(2,128)} %bitcast.4, bf16[2,512,256]{2,1,0:T(8,128)(2,1)} %blocks.1, bf16[512,512]{1,0:T(8,128)(2,1)} %occupied.1, ...), custom_call_target="tpu_custom_call" | custom-call | bytes 1048576 | tf_op jit(solution)/shard_map/masked_blocks/pallas_call | solution.py:159
  2.7 3.0 %collective-permute-start = (bf16[256,512]{1,0:T(8,128)(2,1)S(1)}, bf16[256,512]{1,0:T(8,128)(2,1)S(1)}, u32[]{:S(2)}, u32[]{:S(2)}) collective-permute-start(bf16[256,512]{1,0:T(8,128)(2,1)S(1)} %get-tuple-element.21), channel_id=1, source_target_pairs={{0,2},{2,0},{1,3},{3,1},{4,6},{6,4},{5,7},{7,5},{8,10},{10,8},{9,1... | collective-permute-start | bytes 786440 | tf_op jit(solution)/shard_map/ppermute | solution.py:200
  5.7 2.6 %collective-permute-start.3 = (bf16[2,512,256]{2,1,0:T(8,128)(2,1)S(1)}, bf16[2,512,256]{2,1,0:T(8,128)(2,1)S(1)}, u32[]{:S(2)}, u32[]{:S(2)}) collective-permute-start(bf16[2,512,256]{2,1,0:T(8,128)(2,1)S(1)} %get-tuple-element.22.masked), channel_id=1, source_target_pairs={{0,8},{4,12},{8,0},{12,4},{1,9},{5,13},{9,1},{13,5},{2,10},{6,14},... | collective-permute-start | bytes 1572872 | tf_op jit(solution)/shard_map/ppermute | solution.py:199
  8.3 3.6 %collective-permute-done.mine = bf16[256,512]{1,0:T(8,128)(2,1)S(1)} collective-permute-done((bf16[256,512]{1,0:T(8,128)(2,1)S(1)}, bf16[256,512]{1,0:T(8,128)(2,1)S(1)}, u32[]{:S(2)}, u32[]{:S(2)}) %collective-permute-start) | collective-permute-done | bytes 262176 | tf_op jit(solution)/shard_map/ppermute | solution.py:200
  11.9 0.0 collective-permute-start.1
  11.9 1.5 %collective-permute-done.1.theirs = bf16[256,512]{1,0:T(8,128)(2,1)S(1)} collective-permute-done((bf16[256,512]{1,0:T(8,128)(2,1)S(1)}, bf16[256,512]{1,0:T(8,128)(2,1)S(1)}, u32[]{:S(2)}, u32[]{:S(2)}) %collective-permute-start.1) | collective-permute-done | bytes 262176 | tf_op jit(solution)/shard_map/ppermute | solution.py:201
  13.5 1.2 %own_half.1 = (bf16[4,128,512]{2,1,0:T(8,128)(2,1)S(1)}, bf16[2,128,256]{2,1,0:T(8,128)(2,1)S(1)}, bf16[2,128,256]{2,1,0:T(8,128)(2,1)S(1)}, bf16[2,128,256]{2,1,0:T(8,128)(2,1)S(1)}, bf16[2,128,256]{2,1,0:T(8,128)(2,1)S(1)}) custom-call(s32[3]{0:T(128)S(1)} %pad_add_fusion.place, bf16[512,512]{1,0:T(8,128)(2,1)S(1)} %get-tuple-element.20.occupied, ...), custom_call_target="tpu_custom_call" | custom-call | flops 268435456 | bytes 1048576 | tf_op jit(solution)/shard_map/own_half/pallas_call | solution.py:159
  14.6 1.8 %collective-permute-start.4 = (bf16[2,128,256]{2,1,0:T(8,128)(2,1)S(1)}, bf16[2,128,256]{2,1,0:T(8,128)(2,1)S(1)}, u32[]{:S(2)}, u32[]{:S(2)}) collective-permute-start(bf16[2,128,256]{2,1,0:T(8,128)(2,1)S(1)} %get-tuple-element.25.refs_1_), channel_id=1, source_target_pairs={{0,2},{2,0},{4,6},{6,4},{8,10},{10,8},{12,14},{14,12},{1,3},{3,1},... | collective-permute-start | bytes 393224 | tf_op jit(solution)/shard_map/ppermute | solution.py:209
  16.5 1.6 %collective-permute-start.5 = (bf16[2,128,256]{2,1,0:T(8,128)(2,1)S(1)}, bf16[2,128,256]{2,1,0:T(8,128)(2,1)S(1)}, u32[]{:S(2)}, u32[]{:S(2)}) collective-permute-start(bf16[2,128,256]{2,1,0:T(8,128)(2,1)S(1)} %get-tuple-element.26.refs_2_), channel_id=1, source_target_pairs={{0,4},{2,6},{4,0},{6,2},{8,12},{10,14},{12,8},{14,10},{1,5},{3,7},... | collective-permute-start | bytes 393224 | tf_op jit(solution)/shard_map/ppermute | solution.py:209
  18.0 0.2 collective-permute-start.6
  18.2 1.3 %density_terms.1.before = f32[2,128]{1,0:T(2,128)S(1)} custom-call(s32[3]{0:T(128)S(1)} %pad_add_fusion.place, bf16[512,512]{1,0:T(8,128)(2,1)S(1)} %get-tuple-element.20.occupied, bf16[256,512]{1,0:T(8,128)(2,1)S(1)} %collective-permute-done.mine, bf16[256,512]{1,0:T(8,128)(2,1)S(1)} %collective-permute-done.1.theirs, ...), custom_call_target="tpu_custom_call" | custom-call | flops 268435456 | bytes 1048576 | tf_op jit(solution)/shard_map/density_terms/pallas_call | solution.py:159
  19.5 11.7 %collective-permute-done.3.masked = bf16[2,512,256]{2,1,0:T(8,128)(2,1)S(1)} collective-permute-done((bf16[2,512,256]{2,1,0:T(8,128)(2,1)S(1)}, bf16[2,512,256]{2,1,0:T(8,128)(2,1)S(1)}, u32[]{:S(2)}, u32[]{:S(2)}) %collective-permute-start.3) | collective-permute-done | bytes 524320 | tf_op jit(solution)/shard_map/ppermute | solution.py:199
  31.2 1.0 %far_half.1 = (bf16[2,128,256]{2,1,0:T(8,128)(2,1)S(1)}, bf16[2,128,256]{2,1,0:T(8,128)(2,1)S(1)}, bf16[2,128,256]{2,1,0:T(8,128)(2,1)S(1)}, bf16[2,128,256]{2,1,0:T(8,128)(2,1)S(1)}) custom-call(s32[3]{0:T(128)S(1)} %pad_add_fusion.place, bf16[2,512,256]{2,1,0:T(8,128)(2,1)S(1)} %collective-permute-done.3.masked, ...), custom_call_target="tpu_custom_call" | custom-call | flops 268435456 | bytes 1048576 | tf_op jit(solution)/shard_map/far_half/pallas_call | solution.py:159
  32.2 0.0 collective-permute-done.4.refs_1_
  32.2 0.7 %collective-permute-done.5.refs_2_ = bf16[2,128,256]{2,1,0:T(8,128)(2,1)S(1)} collective-permute-done((bf16[2,128,256]{2,1,0:T(8,128)(2,1)S(1)}, bf16[2,128,256]{2,1,0:T(8,128)(2,1)S(1)}, u32[]{:S(2)}, u32[]{:S(2)}) %collective-permute-start.5) | collective-permute-done | bytes 131104 | tf_op jit(solution)/shard_map/ppermute | solution.py:209
  33.0 1.4 %collective-permute-done.6.refs_3_ = bf16[2,128,256]{2,1,0:T(8,128)(2,1)S(1)} collective-permute-done((bf16[2,128,256]{2,1,0:T(8,128)(2,1)S(1)}, bf16[2,128,256]{2,1,0:T(8,128)(2,1)S(1)}, u32[]{:S(2)}, u32[]{:S(2)}) %collective-permute-start.6) | collective-permute-done | bytes 131104 | tf_op jit(solution)/shard_map/ppermute | solution.py:209
  34.4 0.8 %own_pairs.1 = (f32[8,128,128]{2,1,0:T(8,128)S(1)}, bf16[8,128,128]{2,1,0:T(8,128)(2,1)S(1)}, bf16[8,256,128]{2,1,0:T(8,128)(2,1)S(1)}) custom-call(s32[3]{0:T(128)S(1)} %pad_add_fusion.place, f32[2,128]{1,0:T(2,128)S(1)} %density_terms.1.before, bf16[2,128,256]{2,1,0:T(8,128)(2,1)S(1)} %get-tuple-element.28.earlier.refs_0_, ...), custom_call_target="tpu_custom_call" | custom-call | flops 67108864 | bytes 1048576 | tf_op jit(solution)/shard_map/own_pairs/pallas_call | solution.py:159
  35.2 0.1 collective-permute-start.10
  35.3 1.8 %collective-permute-start.7 = (bf16[2,128,256]{2,1,0:T(8,128)(2,1)S(1)}, bf16[2,128,256]{2,1,0:T(8,128)(2,1)S(1)}, u32[]{:S(2)}, u32[]{:S(2)}) collective-permute-start(bf16[2,128,256]{2,1,0:T(8,128)(2,1)S(1)} %get-tuple-element.31), channel_id=1, source_target_pairs={{0,2},{2,0},{4,6},{6,4},{8,10},{10,8},{12,14},{14,12},{1,3},{3,1},... | collective-permute-start | bytes 393224 | tf_op jit(solution)/shard_map/ppermute | solution.py:209
  37.1 0.0 collective-permute-start.8
  37.1 1.8 %collective-permute-start.9 = (bf16[2,128,256]{2,1,0:T(8,128)(2,1)S(1)}, bf16[2,128,256]{2,1,0:T(8,128)(2,1)S(1)}, u32[]{:S(2)}, u32[]{:S(2)}) collective-permute-start(bf16[2,128,256]{2,1,0:T(8,128)(2,1)S(1)} %get-tuple-element.33), channel_id=1, source_target_pairs={{0,6},{2,4},{4,2},{6,0},{8,14},{10,12},{12,10},{14,8},{1,7},{3,5},... | collective-permute-start | bytes 393224 | tf_op jit(solution)/shard_map/ppermute | solution.py:209
  38.9 0.0 collective-permute-start.2
  38.9 1.1 %collective-permute-done.2.before = f32[2,128]{1,0:T(2,128)S(1)} collective-permute-done((f32[2,128]{1,0:T(2,128)S(1)}, f32[2,128]{1,0:T(2,128)S(1)}, u32[]{:S(2)}, u32[]{:S(2)}) %collective-permute-start.2) | collective-permute-done | bytes 1056 | tf_op jit(solution)/shard_map/ppermute | solution.py:226
  40.0 1.2 %collective-permute-done.7.refs_1_ = bf16[2,128,256]{2,1,0:T(8,128)(2,1)S(1)} collective-permute-done((bf16[2,128,256]{2,1,0:T(8,128)(2,1)S(1)}, bf16[2,128,256]{2,1,0:T(8,128)(2,1)S(1)}, u32[]{:S(2)}, u32[]{:S(2)}) %collective-permute-start.7) | collective-permute-done | bytes 131104 | tf_op jit(solution)/shard_map/ppermute | solution.py:209
  41.2 2.2 %collective-permute-done.8.refs_2_ = bf16[2,128,256]{2,1,0:T(8,128)(2,1)S(1)} collective-permute-done((bf16[2,128,256]{2,1,0:T(8,128)(2,1)S(1)}, bf16[2,128,256]{2,1,0:T(8,128)(2,1)S(1)}, u32[]{:S(2)}, u32[]{:S(2)}) %collective-permute-start.8) | collective-permute-done | bytes 131104 | tf_op jit(solution)/shard_map/ppermute | solution.py:209
  43.4 1.8 %collective-permute-done.9.refs_3_ = bf16[2,128,256]{2,1,0:T(8,128)(2,1)S(1)} collective-permute-done((bf16[2,128,256]{2,1,0:T(8,128)(2,1)S(1)}, bf16[2,128,256]{2,1,0:T(8,128)(2,1)S(1)}, u32[]{:S(2)}, u32[]{:S(2)}) %collective-permute-start.9) | collective-permute-done | bytes 131104 | tf_op jit(solution)/shard_map/ppermute | solution.py:209
  45.2 0.0 collective-permute-done.10.earlier.refs_1_
  45.2 0.8 %far_pairs.1 = (f32[8,128,128]{2,1,0:T(8,128)S(1)}, bf16[8,128,128]{2,1,0:T(8,128)(2,1)S(1)}) custom-call(s32[3]{0:T(128)S(1)} %pad_add_fusion.place, f32[2,128]{1,0:T(2,128)S(1)} %collective-permute-done.2.before, bf16[8,128,128]{2,1,0:T(8,128)(2,1)S(1)} %collective-permute-done.10.earlier.refs_1_, bf16[512,128]{1,0:T(8,128)(2,1)S(1)} %get-tuple-element.29.ligand, ...), custom_call_target="tpu_custom_call" | custom-call | flops 67108864 | bytes 1048576 | tf_op jit(solution)/shard_map/far_pairs/pallas_call | solution.py:159
  46.1 0.1 collective-permute-start.11
  46.1 0.6 %multiply_reduce_fusion = f32[2]{0:T(128)} fusion(f32[2,128]{1,0:T(2,128)S(1)} %collective-permute-done.2.before, f32[2,128]{1,0:T(2,128)S(1)} %density_terms.1.before), kind=kLoop, calls=%fused_computation | loop fusion | flops 4 | bytes 24 | tf_op jit(solution)/shard_map/div | solution.py:227
  46.8 0.2 far_turned.1.far
  47.0 0.7 %collective-permute-done.11.refs_3_ = bf16[8,128,128]{2,1,0:T(8,128)(2,1)S(1)} collective-permute-done((bf16[8,128,128]{2,1,0:T(8,128)(2,1)S(1)}, bf16[8,128,128]{2,1,0:T(8,128)(2,1)S(1)}, u32[]{:S(2)}, u32[]{:S(2)}) %collective-permute-start.11) | collective-permute-done | bytes 262176 | tf_op jit(solution)/shard_map/ppermute | solution.py:246
  47.7 6.0 %cross_terms.1 = f32[128,256,128]{2,1,0:T(8,128)} custom-call(bf16[8,256,128]{2,1,0:T(8,128)(2,1)S(1)} %get-tuple-element.30.near, bf16[8,256,128]{2,1,0:T(8,128)(2,1)S(1)} %far_turned.1.far, f32[8,128,128]{2,1,0:T(8,128)S(1)} %get-tuple-element.34.refs_0_, bf16[8,128,128]{2,1,0:T(8,128)(2,1)S(1)} %collective-permute-done.10.earlier.refs_1_, ...), custom_call_target="tpu_custom_call" | custom-call | flops 2147483648 | bytes 18874368 | tf_op jit(solution)/shard_map/cross_terms/pallas_call | solution.py:159
Async XLA Ops:
  2.7 9.2 %collective-permute-start = (bf16[256,512]{1,0:T(8,128)(2,1)S(1)}, bf16[256,512]{1,0:T(8,128)(2,1)S(1)}, u32[]{:S(2)}, u32[]{:S(2)}) collective-permute-start(bf16[256,512]{1,0:T(8,128)(2,1)S(1)} %get-tuple-element.21), channel_id=1, source_target_pairs={{0,2},{2,0},{1,3},{3,1},{4,6},{6,4},{5,7},{7,5},{8,10},{10,8},{9,1... | collective-permute-start | bytes 786440 | tf_op jit(solution)/shard_map/ppermute | solution.py:200
  5.7 25.5 %collective-permute-start.3 = (bf16[2,512,256]{2,1,0:T(8,128)(2,1)S(1)}, bf16[2,512,256]{2,1,0:T(8,128)(2,1)S(1)}, u32[]{:S(2)}, u32[]{:S(2)}) collective-permute-start(bf16[2,512,256]{2,1,0:T(8,128)(2,1)S(1)} %get-tuple-element.22.masked), channel_id=1, source_target_pairs={{0,8},{4,12},{8,0},{12,4},{1,9},{5,13},{9,1},{13,5},{2,10},{6,14},... | collective-permute-start | bytes 1572872 | tf_op jit(solution)/shard_map/ppermute | solution.py:199
  11.9 1.5 %collective-permute-start.1 = (bf16[256,512]{1,0:T(8,128)(2,1)S(1)}, bf16[256,512]{1,0:T(8,128)(2,1)S(1)}, u32[]{:S(2)}, u32[]{:S(2)}) collective-permute-start(bf16[256,512]{1,0:T(8,128)(2,1)S(1)} %collective-permute-done.mine), channel_id=1, source_target_pairs={{0,1},{1,0},{2,3},{3,2},{4,5},{5,4},{6,7},{7,6},{8,9},{9,8},{10,11... | collective-permute-start | bytes 786440 | tf_op jit(solution)/shard_map/ppermute | solution.py:201
  14.6 17.6 %collective-permute-start.4 = (bf16[2,128,256]{2,1,0:T(8,128)(2,1)S(1)}, bf16[2,128,256]{2,1,0:T(8,128)(2,1)S(1)}, u32[]{:S(2)}, u32[]{:S(2)}) collective-permute-start(bf16[2,128,256]{2,1,0:T(8,128)(2,1)S(1)} %get-tuple-element.25.refs_1_), channel_id=1, source_target_pairs={{0,2},{2,0},{4,6},{6,4},{8,10},{10,8},{12,14},{14,12},{1,3},{3,1},... | collective-permute-start | bytes 393224 | tf_op jit(solution)/shard_map/ppermute | solution.py:209
  16.5 16.5 %collective-permute-start.5 = (bf16[2,128,256]{2,1,0:T(8,128)(2,1)S(1)}, bf16[2,128,256]{2,1,0:T(8,128)(2,1)S(1)}, u32[]{:S(2)}, u32[]{:S(2)}) collective-permute-start(bf16[2,128,256]{2,1,0:T(8,128)(2,1)S(1)} %get-tuple-element.26.refs_2_), channel_id=1, source_target_pairs={{0,4},{2,6},{4,0},{6,2},{8,12},{10,14},{12,8},{14,10},{1,5},{3,7},... | collective-permute-start | bytes 393224 | tf_op jit(solution)/shard_map/ppermute | solution.py:209
  18.0 16.4 %collective-permute-start.6 = (bf16[2,128,256]{2,1,0:T(8,128)(2,1)S(1)}, bf16[2,128,256]{2,1,0:T(8,128)(2,1)S(1)}, u32[]{:S(2)}, u32[]{:S(2)}) collective-permute-start(bf16[2,128,256]{2,1,0:T(8,128)(2,1)S(1)} %get-tuple-element.27.refs_3_), channel_id=1, source_target_pairs={{0,6},{2,4},{4,2},{6,0},{8,14},{10,12},{12,10},{14,8},{1,7},{3,5},... | collective-permute-start | bytes 393224 | tf_op jit(solution)/shard_map/ppermute | solution.py:209
  35.2 10.0 %collective-permute-start.10 = (bf16[8,128,128]{2,1,0:T(8,128)(2,1)S(1)}, bf16[8,128,128]{2,1,0:T(8,128)(2,1)S(1)}, u32[]{:S(2)}, u32[]{:S(2)}) collective-permute-start(bf16[8,128,128]{2,1,0:T(8,128)(2,1)S(1)} %get-tuple-element.35), channel_id=1, source_target_pairs={{0,1},{1,0},{2,3},{3,2},{4,5},{5,4},{6,7},{7,6},{8,9},{9,8},{10,11... | collective-permute-start | bytes 786440 | tf_op jit(solution)/shard_map/ppermute | solution.py:242
  35.3 5.9 %collective-permute-start.7 = (bf16[2,128,256]{2,1,0:T(8,128)(2,1)S(1)}, bf16[2,128,256]{2,1,0:T(8,128)(2,1)S(1)}, u32[]{:S(2)}, u32[]{:S(2)}) collective-permute-start(bf16[2,128,256]{2,1,0:T(8,128)(2,1)S(1)} %get-tuple-element.31), channel_id=1, source_target_pairs={{0,2},{2,0},{4,6},{6,4},{8,10},{10,8},{12,14},{14,12},{1,3},{3,1},... | collective-permute-start | bytes 393224 | tf_op jit(solution)/shard_map/ppermute | solution.py:209
  37.1 6.3 %collective-permute-start.8 = (bf16[2,128,256]{2,1,0:T(8,128)(2,1)S(1)}, bf16[2,128,256]{2,1,0:T(8,128)(2,1)S(1)}, u32[]{:S(2)}, u32[]{:S(2)}) collective-permute-start(bf16[2,128,256]{2,1,0:T(8,128)(2,1)S(1)} %get-tuple-element.32), channel_id=1, source_target_pairs={{0,4},{2,6},{4,0},{6,2},{8,12},{10,14},{12,8},{14,10},{1,5},{3,7},... | collective-permute-start | bytes 393224 | tf_op jit(solution)/shard_map/ppermute | solution.py:209
  37.1 8.1 %collective-permute-start.9 = (bf16[2,128,256]{2,1,0:T(8,128)(2,1)S(1)}, bf16[2,128,256]{2,1,0:T(8,128)(2,1)S(1)}, u32[]{:S(2)}, u32[]{:S(2)}) collective-permute-start(bf16[2,128,256]{2,1,0:T(8,128)(2,1)S(1)} %get-tuple-element.33), channel_id=1, source_target_pairs={{0,6},{2,4},{4,2},{6,0},{8,14},{10,12},{12,10},{14,8},{1,7},{3,5},... | collective-permute-start | bytes 393224 | tf_op jit(solution)/shard_map/ppermute | solution.py:209
  38.9 1.1 %collective-permute-start.2 = (f32[2,128]{1,0:T(2,128)S(1)}, f32[2,128]{1,0:T(2,128)S(1)}, u32[]{:S(2)}, u32[]{:S(2)}) collective-permute-start(f32[2,128]{1,0:T(2,128)S(1)} %density_terms.1.before), channel_id=1, source_target_pairs={{0,1},{1,0},{2,3},{3,2},{4,5},{5,4},{6,7},{7,6},{8,9},{9,8},{10,11... | collective-permute-start | bytes 3080 | tf_op jit(solution)/shard_map/ppermute | solution.py:226
  46.1 1.6 %collective-permute-start.11 = (bf16[8,128,128]{2,1,0:T(8,128)(2,1)S(1)}, bf16[8,128,128]{2,1,0:T(8,128)(2,1)S(1)}, u32[]{:S(2)}, u32[]{:S(2)}) collective-permute-start(bf16[8,128,128]{2,1,0:T(8,128)(2,1)S(1)} %get-tuple-element.37), channel_id=1, source_target_pairs={{0,1},{1,0},{2,3},{3,2},{4,5},{5,4},{6,7},{7,6},{8,9},{9,8},{10,11... | collective-permute-start | bytes 786440 | tf_op jit(solution)/shard_map/ppermute | solution.py:246

commit v7 on v6

--- a/solution.py
+++ b/solution.py
@@ -99,7 +99,7 @@
         out[q : q + 1, :] = jnp.full((1, out.shape[1]), totals[q], jnp.float32)
 
 
-def far_kernel(place, masked, turned, *outs):
+def far_kernel(place, before, masked, turned, *outs):
     half_into(outs, place, turned, masked)
 
 
@@ -225,7 +225,7 @@
     )[0]
     value_there = lax.ppermute(value, "ao", swap)
     density = (value[:, 0] + value_there[:, 0]) / math.sqrt(NOCC)
-    far = call(far_kernel, "far_half", (place, far_masked, turned), messages, flops=work)
+    far = call(far_kernel, "far_half", (place, value, far_masked, turned), messages, flops=work)
     far_here = square(far)
 
     shape = (4 * aux_rows, ni, width)
@@ -235,13 +235,13 @@
     own_kept, own_given, own_rows = call(
         pair_and_turn_kernel,
         "own_pairs",
-        (place, value, far[0], orbitals, *own_here),
+        (place, value_there, far[0], orbitals, *own_here),
         kept_and_given + side,
         flops=pair_work,
     )
     own_pairs = (own_kept, lax.ppermute(own_given, "ao", swap))
     far_kept, far_given = call(
-        pair_kernel, "far_pairs", (place, value_there, own_pairs[1], orbitals, *far_here), kept_and_given, flops=pair_work
+        pair_kernel, "far_pairs", (place, value_there, own_rows, orbitals, *far_here), kept_and_given, flops=pair_work
     )
     far_pairs = (far_kept, lax.ppermute(far_given, "ao", swap))
     far_rows = call(turn_kernel, "far_turned", far_here, side, scalars=0)[0]

time: 53.9 us -> 49.6 us (0.920)
  waiting for transfers between devices: 26.1 us -> 21.4 us
    ppermute x6, waiting for transfers between devices: 7.37 us -> 3.97 us  [square(): arrived[d] = lax.ppermute(messages[d], ('aux', 'orb'), moves)]
    ppermute x1, waiting for transfers between devices: 1.14 us -> 0.01 us  [body(): value_there = lax.ppermute(value, 'ao', swap)]
  transfers between devices with their start and end apart: 12 -> 12, of which waited for: 10 -> 8; matrix products, arithmetic and copies ran while one was open for 1% -> 1% of each run, Pallas kernels for 7% -> 9%
where the time goes in v7:
time: 49.6 us; the launch traced here: 49.5 us
  waiting for transfers between devices  21.4 us (43%)
  Pallas kernels  13.3 us (27%)
  starting transfers between devices  13.3 us (27%)
  between operations  0.71 us (1%)
  other arithmetic  0.7 us (1%)
    pallas_call x8, Pallas kernels, call(): pl.pallas_call(kernel, in_specs=[SMEM] * scalars + [in_spec] * (len(input...  13.3 us
    ppermute x1, waiting for transfers between devices, body(): far_masked = lax.ppermute(masked, 'aux', across)  11.6 us
    ppermute x6, starting transfers between devices, square(): arrived[d] = lax.ppermute(messages[d], ('aux', 'orb'), moves)  7.11 us
    ppermute x6, waiting for transfers between devices, square(): arrived[d] = lax.ppermute(messages[d], ('aux', 'orb'), moves)  3.97 us
    ppermute x1, waiting for transfers between devices, body(): mine = lax.ppermute(part, 'orb', swap)  3.65 us
    ppermute x1, starting transfers between devices, body(): mine = lax.ppermute(part, 'orb', swap)  3 us
    ppermute x1, starting transfers between devices, body(): far_masked = lax.ppermute(masked, 'aux', across)  2.59 us
    ppermute x1, waiting for transfers between devices, body(): theirs = lax.ppermute(mine, 'ao', swap)  1.53 us
  transfers between devices with their start and end apart: 12, of which 8 were waited for; matrix products, arithmetic and copies ran while one was open for 1% of the time, Pallas kernels for 9%

profile of v7, /device:TPU:0, one launch (start us, length us, event | category | flops | bytes accessed | tf_op | source)
XLA Modules:
  0.0 49.5 jit_solution(2353082273859496929)
XLA Ops:
  0.6 0.1 pad_add_fusion.place
  0.7 2.0 %masked_blocks.1 = (bf16[2,512,256]{2,1,0:T(8,128)(2,1)S(1)}, bf16[512,512]{1,0:T(8,128)(2,1)S(1)}, bf16[256,512]{1,0:T(8,128)(2,1)S(1)}, bf16[512,128]{1,0:T(8,128)(2,1)S(1)}) custom-call(s32[3]{0:T(128)S(1)} %pad_add_fusion.place, s32[1,2,4]{2,1,0:T(2,128)} %bitcast.4, bf16[2,512,256]{2,1,0:T(8,128)(2,1)} %blocks.1, bf16[512,512]{1,0:T(8,128)(2,1)} %occupied.1, ...), custom_call_target="tpu_custom_call" | custom-call | bytes 1048576 | tf_op jit(solution)/shard_map/masked_blocks/pallas_call | solution.py:159
  2.7 3.0 %collective-permute-start = (bf16[256,512]{1,0:T(8,128)(2,1)S(1)}, bf16[256,512]{1,0:T(8,128)(2,1)S(1)}, u32[]{:S(2)}, u32[]{:S(2)}) collective-permute-start(bf16[256,512]{1,0:T(8,128)(2,1)S(1)} %get-tuple-element.21), channel_id=1, source_target_pairs={{0,2},{2,0},{1,3},{3,1},{4,6},{6,4},{5,7},{7,5},{8,10},{10,8},{9,1... | collective-permute-start | bytes 786440 | tf_op jit(solution)/shard_map/ppermute | solution.py:200
  5.7 2.6 %collective-permute-start.3 = (bf16[2,512,256]{2,1,0:T(8,128)(2,1)S(1)}, bf16[2,512,256]{2,1,0:T(8,128)(2,1)S(1)}, u32[]{:S(2)}, u32[]{:S(2)}) collective-permute-start(bf16[2,512,256]{2,1,0:T(8,128)(2,1)S(1)} %get-tuple-element.22.masked), channel_id=1, source_target_pairs={{0,8},{4,12},{8,0},{12,4},{1,9},{5,13},{9,1},{13,5},{2,10},{6,14},... | collective-permute-start | bytes 1572872 | tf_op jit(solution)/shard_map/ppermute | solution.py:199
  8.3 3.6 %collective-permute-done.mine = bf16[256,512]{1,0:T(8,128)(2,1)S(1)} collective-permute-done((bf16[256,512]{1,0:T(8,128)(2,1)S(1)}, bf16[256,512]{1,0:T(8,128)(2,1)S(1)}, u32[]{:S(2)}, u32[]{:S(2)}) %collective-permute-start) | collective-permute-done | bytes 262176 | tf_op jit(solution)/shard_map/ppermute | solution.py:200
  11.9 0.0 collective-permute-start.1
  11.9 1.5 %collective-permute-done.1.theirs = bf16[256,512]{1,0:T(8,128)(2,1)S(1)} collective-permute-done((bf16[256,512]{1,0:T(8,128)(2,1)S(1)}, bf16[256,512]{1,0:T(8,128)(2,1)S(1)}, u32[]{:S(2)}, u32[]{:S(2)}) %collective-permute-start.1) | collective-permute-done | bytes 262176 | tf_op jit(solution)/shard_map/ppermute | solution.py:201
  13.5 1.2 %own_half.1 = (bf16[4,128,512]{2,1,0:T(8,128)(2,1)S(1)}, bf16[2,128,256]{2,1,0:T(8,128)(2,1)S(1)}, bf16[2,128,256]{2,1,0:T(8,128)(2,1)S(1)}, bf16[2,128,256]{2,1,0:T(8,128)(2,1)S(1)}, bf16[2,128,256]{2,1,0:T(8,128)(2,1)S(1)}) custom-call(s32[3]{0:T(128)S(1)} %pad_add_fusion.place, bf16[512,512]{1,0:T(8,128)(2,1)S(1)} %get-tuple-element.20.occupied, ...), custom_call_target="tpu_custom_call" | custom-call | flops 268435456 | bytes 1048576 | tf_op jit(solution)/shard_map/own_half/pallas_call | solution.py:159
  14.6 1.8 %collective-permute-start.4 = (bf16[2,128,256]{2,1,0:T(8,128)(2,1)S(1)}, bf16[2,128,256]{2,1,0:T(8,128)(2,1)S(1)}, u32[]{:S(2)}, u32[]{:S(2)}) collective-permute-start(bf16[2,128,256]{2,1,0:T(8,128)(2,1)S(1)} %get-tuple-element.25.refs_1_), channel_id=1, source_target_pairs={{0,2},{2,0},{4,6},{6,4},{8,10},{10,8},{12,14},{14,12},{1,3},{3,1},... | collective-permute-start | bytes 393224 | tf_op jit(solution)/shard_map/ppermute | solution.py:209
  16.5 1.6 %collective-permute-start.5 = (bf16[2,128,256]{2,1,0:T(8,128)(2,1)S(1)}, bf16[2,128,256]{2,1,0:T(8,128)(2,1)S(1)}, u32[]{:S(2)}, u32[]{:S(2)}) collective-permute-start(bf16[2,128,256]{2,1,0:T(8,128)(2,1)S(1)} %get-tuple-element.26.refs_2_), channel_id=1, source_target_pairs={{0,4},{2,6},{4,0},{6,2},{8,12},{10,14},{12,8},{14,10},{1,5},{3,7},... | collective-permute-start | bytes 393224 | tf_op jit(solution)/shard_map/ppermute | solution.py:209
  18.0 0.2 collective-permute-start.6
  18.2 1.3 %density_terms.1.before = f32[2,128]{1,0:T(2,128)S(1)} custom-call(s32[3]{0:T(128)S(1)} %pad_add_fusion.place, bf16[512,512]{1,0:T(8,128)(2,1)S(1)} %get-tuple-element.20.occupied, bf16[256,512]{1,0:T(8,128)(2,1)S(1)} %collective-permute-done.mine, bf16[256,512]{1,0:T(8,128)(2,1)S(1)} %collective-permute-done.1.theirs, ...), custom_call_target="tpu_custom_call" | custom-call | flops 268435456 | bytes 1048576 | tf_op jit(solution)/shard_map/density_terms/pallas_call | solution.py:159
  19.5 0.1 collective-permute-start.2
  19.6 11.6 %collective-permute-done.3.masked = bf16[2,512,256]{2,1,0:T(8,128)(2,1)S(1)} collective-permute-done((bf16[2,512,256]{2,1,0:T(8,128)(2,1)S(1)}, bf16[2,512,256]{2,1,0:T(8,128)(2,1)S(1)}, u32[]{:S(2)}, u32[]{:S(2)}) %collective-permute-start.3) | collective-permute-done | bytes 524320 | tf_op jit(solution)/shard_map/ppermute | solution.py:199
  31.2 1.0 %far_half.1 = (bf16[2,128,256]{2,1,0:T(8,128)(2,1)S(1)}, bf16[2,128,256]{2,1,0:T(8,128)(2,1)S(1)}, bf16[2,128,256]{2,1,0:T(8,128)(2,1)S(1)}, bf16[2,128,256]{2,1,0:T(8,128)(2,1)S(1)}) custom-call(s32[3]{0:T(128)S(1)} %pad_add_fusion.place, f32[2,128]{1,0:T(2,128)S(1)} %density_terms.1.before, bf16[2,512,256]{2,1,0:T(8,128)(2,1)S(1)} %collective-permute-done.3.masked, ...), custom_call_target="tpu_custom_call" | custom-call | flops 268435456 | bytes 1048576 | tf_op jit(solution)/shard_map/far_half/pallas_call | solution.py:159
  32.2 0.5 %collective-permute-start.7 = (bf16[2,128,256]{2,1,0:T(8,128)(2,1)S(1)}, bf16[2,128,256]{2,1,0:T(8,128)(2,1)S(1)}, u32[]{:S(2)}, u32[]{:S(2)}) collective-permute-start(bf16[2,128,256]{2,1,0:T(8,128)(2,1)S(1)} %get-tuple-element.31), channel_id=1, source_target_pairs={{0,2},{2,0},{4,6},{6,4},{8,10},{10,8},{12,14},{14,12},{1,3},{3,1},... | collective-permute-start | bytes 393224 | tf_op jit(solution)/shard_map/ppermute | solution.py:209
  32.8 0.0 collective-permute-done.2.before
  32.8 0.7 %collective-permute-start.8 = (bf16[2,128,256]{2,1,0:T(8,128)(2,1)S(1)}, bf16[2,128,256]{2,1,0:T(8,128)(2,1)S(1)}, u32[]{:S(2)}, u32[]{:S(2)}) collective-permute-start(bf16[2,128,256]{2,1,0:T(8,128)(2,1)S(1)} %get-tuple-element.32), channel_id=1, source_target_pairs={{0,4},{2,6},{4,0},{6,2},{8,12},{10,14},{12,8},{14,10},{1,5},{3,7},... | collective-permute-start | bytes 393224 | tf_op jit(solution)/shard_map/ppermute | solution.py:209
  33.4 0.0 collective-permute-done.4.refs_1_
  33.4 2.3 %collective-permute-start.9 = (bf16[2,128,256]{2,1,0:T(8,128)(2,1)S(1)}, bf16[2,128,256]{2,1,0:T(8,128)(2,1)S(1)}, u32[]{:S(2)}, u32[]{:S(2)}) collective-permute-start(bf16[2,128,256]{2,1,0:T(8,128)(2,1)S(1)} %get-tuple-element.33), channel_id=1, source_target_pairs={{0,6},{2,4},{4,2},{6,0},{8,14},{10,12},{12,10},{14,8},{1,7},{3,5},... | collective-permute-start | bytes 393224 | tf_op jit(solution)/shard_map/ppermute | solution.py:209
  35.8 0.0 collective-permute-done.5.refs_2_
  35.8 0.0 collective-permute-done.6.refs_3_
  35.8 0.8 %own_pairs.1 = (f32[8,128,128]{2,1,0:T(8,128)S(1)}, bf16[8,128,128]{2,1,0:T(8,128)(2,1)S(1)}, bf16[8,256,128]{2,1,0:T(8,128)(2,1)S(1)}) custom-call(s32[3]{0:T(128)S(1)} %pad_add_fusion.place, f32[2,128]{1,0:T(2,128)S(1)} %collective-permute-done.2.before, bf16[2,128,256]{2,1,0:T(8,128)(2,1)S(1)} %get-tuple-element.28.earlier.refs_0_, ...), custom_call_target="tpu_custom_call" | custom-call | flops 67108864 | bytes 1048576 | tf_op jit(solution)/shard_map/own_pairs/pallas_call | solution.py:159
  36.6 2.0 %collective-permute-done.7.refs_1_ = bf16[2,128,256]{2,1,0:T(8,128)(2,1)S(1)} collective-permute-done((bf16[2,128,256]{2,1,0:T(8,128)(2,1)S(1)}, bf16[2,128,256]{2,1,0:T(8,128)(2,1)S(1)}, u32[]{:S(2)}, u32[]{:S(2)}) %collective-permute-start.7) | collective-permute-done | bytes 131104 | tf_op jit(solution)/shard_map/ppermute | solution.py:209
  38.7 0.4 collective-permute-done.8.refs_2_
  39.1 1.5 %collective-permute-done.9.refs_3_ = bf16[2,128,256]{2,1,0:T(8,128)(2,1)S(1)} collective-permute-done((bf16[2,128,256]{2,1,0:T(8,128)(2,1)S(1)}, bf16[2,128,256]{2,1,0:T(8,128)(2,1)S(1)}, u32[]{:S(2)}, u32[]{:S(2)}) %collective-permute-start.9) | collective-permute-done | bytes 131104 | tf_op jit(solution)/shard_map/ppermute | solution.py:209
  40.6 0.8 %far_pairs.1 = (f32[8,128,128]{2,1,0:T(8,128)S(1)}, bf16[8,128,128]{2,1,0:T(8,128)(2,1)S(1)}) custom-call(s32[3]{0:T(128)S(1)} %pad_add_fusion.place, f32[2,128]{1,0:T(2,128)S(1)} %collective-permute-done.2.before, bf16[8,256,128]{2,1,0:T(8,128)(2,1)S(1)} %get-tuple-element.30.earlier.near, bf16[512,128]{1,0:T(8,128)(2,1)S(1)} %get-tuple-element.29.ligand, ...), custom_call_target="tpu_custom_call" | custom-call | flops 67108864 | bytes 1048576 | tf_op jit(solution)/shard_map/far_pairs/pallas_call | solution.py:159
  41.4 0.1 collective-permute-start.11
  41.5 0.5 %collective-permute-start.10 = (bf16[8,128,128]{2,1,0:T(8,128)(2,1)S(1)}, bf16[8,128,128]{2,1,0:T(8,128)(2,1)S(1)}, u32[]{:S(2)}, u32[]{:S(2)}) collective-permute-start(bf16[8,128,128]{2,1,0:T(8,128)(2,1)S(1)} %get-tuple-element.35), channel_id=1, source_target_pairs={{0,1},{1,0},{2,3},{3,2},{4,5},{5,4},{6,7},{7,6},{8,9},{9,8},{10,11... | collective-permute-start | bytes 786440 | tf_op jit(solution)/shard_map/ppermute | solution.py:242
  42.0 0.6 %multiply_reduce_fusion = f32[2]{0:T(128)} fusion(f32[2,128]{1,0:T(2,128)S(1)} %collective-permute-done.2.before, f32[2,128]{1,0:T(2,128)S(1)} %density_terms.1.before), kind=kLoop, calls=%fused_computation | loop fusion | flops 4 | bytes 24 | tf_op jit(solution)/shard_map/div | solution.py:227
  42.6 0.2 far_turned.1.far
  42.8 0.2 collective-permute-done.11.refs_3_
  43.0 0.4 collective-permute-done.10.refs_1_
  43.4 6.0 %cross_terms.1 = f32[128,256,128]{2,1,0:T(8,128)} custom-call(bf16[8,256,128]{2,1,0:T(8,128)(2,1)S(1)} %get-tuple-element.30.earlier.near, bf16[8,256,128]{2,1,0:T(8,128)(2,1)S(1)} %far_turned.1.far, f32[8,128,128]{2,1,0:T(8,128)S(1)} %get-tuple-element.34.refs_0_, bf16[8,128,128]{2,1,0:T(8,128)(2,1)S(1)} %collective-permute-done.10.refs_1_, ...), custom_call_target="tpu_custom_call" | custom-call | flops 2147483648 | bytes 18874368 | tf_op jit(solution)/shard_map/cross_terms/pallas_call | solution.py:159
Async XLA Ops:
  2.7 9.2 %collective-permute-start = (bf16[256,512]{1,0:T(8,128)(2,1)S(1)}, bf16[256,512]{1,0:T(8,128)(2,1)S(1)}, u32[]{:S(2)}, u32[]{:S(2)}) collective-permute-start(bf16[256,512]{1,0:T(8,128)(2,1)S(1)} %get-tuple-element.21), channel_id=1, source_target_pairs={{0,2},{2,0},{1,3},{3,1},{4,6},{6,4},{5,7},{7,5},{8,10},{10,8},{9,1... | collective-permute-start | bytes 786440 | tf_op jit(solution)/shard_map/ppermute | solution.py:200
  5.7 25.6 %collective-permute-start.3 = (bf16[2,512,256]{2,1,0:T(8,128)(2,1)S(1)}, bf16[2,512,256]{2,1,0:T(8,128)(2,1)S(1)}, u32[]{:S(2)}, u32[]{:S(2)}) collective-permute-start(bf16[2,512,256]{2,1,0:T(8,128)(2,1)S(1)} %get-tuple-element.22.masked), channel_id=1, source_target_pairs={{0,8},{4,12},{8,0},{12,4},{1,9},{5,13},{9,1},{13,5},{2,10},{6,14},... | collective-permute-start | bytes 1572872 | tf_op jit(solution)/shard_map/ppermute | solution.py:199
  11.9 1.5 %collective-permute-start.1 = (bf16[256,512]{1,0:T(8,128)(2,1)S(1)}, bf16[256,512]{1,0:T(8,128)(2,1)S(1)}, u32[]{:S(2)}, u32[]{:S(2)}) collective-permute-start(bf16[256,512]{1,0:T(8,128)(2,1)S(1)} %collective-permute-done.mine), channel_id=1, source_target_pairs={{0,1},{1,0},{2,3},{3,2},{4,5},{5,4},{6,7},{7,6},{8,9},{9,8},{10,11... | collective-permute-start | bytes 786440 | tf_op jit(solution)/shard_map/ppermute | solution.py:201
  14.6 18.8 %collective-permute-start.4 = (bf16[2,128,256]{2,1,0:T(8,128)(2,1)S(1)}, bf16[2,128,256]{2,1,0:T(8,128)(2,1)S(1)}, u32[]{:S(2)}, u32[]{:S(2)}) collective-permute-start(bf16[2,128,256]{2,1,0:T(8,128)(2,1)S(1)} %get-tuple-element.25.refs_1_), channel_id=1, source_target_pairs={{0,2},{2,0},{4,6},{6,4},{8,10},{10,8},{12,14},{14,12},{1,3},{3,1},... | collective-permute-start | bytes 393224 | tf_op jit(solution)/shard_map/ppermute | solution.py:209
  16.5 19.3 %collective-permute-start.5 = (bf16[2,128,256]{2,1,0:T(8,128)(2,1)S(1)}, bf16[2,128,256]{2,1,0:T(8,128)(2,1)S(1)}, u32[]{:S(2)}, u32[]{:S(2)}) collective-permute-start(bf16[2,128,256]{2,1,0:T(8,128)(2,1)S(1)} %get-tuple-element.26.refs_2_), channel_id=1, source_target_pairs={{0,4},{2,6},{4,0},{6,2},{8,12},{10,14},{12,8},{14,10},{1,5},{3,7},... | collective-permute-start | bytes 393224 | tf_op jit(solution)/shard_map/ppermute | solution.py:209
  18.0 17.8 %collective-permute-start.6 = (bf16[2,128,256]{2,1,0:T(8,128)(2,1)S(1)}, bf16[2,128,256]{2,1,0:T(8,128)(2,1)S(1)}, u32[]{:S(2)}, u32[]{:S(2)}) collective-permute-start(bf16[2,128,256]{2,1,0:T(8,128)(2,1)S(1)} %get-tuple-element.27.refs_3_), channel_id=1, source_target_pairs={{0,6},{2,4},{4,2},{6,0},{8,14},{10,12},{12,10},{14,8},{1,7},{3,5},... | collective-permute-start | bytes 393224 | tf_op jit(solution)/shard_map/ppermute | solution.py:209
  19.5 13.2 %collective-permute-start.2 = (f32[2,128]{1,0:T(2,128)S(1)}, f32[2,128]{1,0:T(2,128)S(1)}, u32[]{:S(2)}, u32[]{:S(2)}) collective-permute-start(f32[2,128]{1,0:T(2,128)S(1)} %density_terms.1.before), channel_id=1, source_target_pairs={{0,1},{1,0},{2,3},{3,2},{4,5},{5,4},{6,7},{7,6},{8,9},{9,8},{10,11... | collective-permute-start | bytes 3080 | tf_op jit(solution)/shard_map/ppermute | solution.py:226
  32.2 6.4 %collective-permute-start.7 = (bf16[2,128,256]{2,1,0:T(8,128)(2,1)S(1)}, bf16[2,128,256]{2,1,0:T(8,128)(2,1)S(1)}, u32[]{:S(2)}, u32[]{:S(2)}) collective-permute-start(bf16[2,128,256]{2,1,0:T(8,128)(2,1)S(1)} %get-tuple-element.31), channel_id=1, source_target_pairs={{0,2},{2,0},{4,6},{6,4},{8,10},{10,8},{12,14},{14,12},{1,3},{3,1},... | collective-permute-start | bytes 393224 | tf_op jit(solution)/shard_map/ppermute | solution.py:209
  32.8 6.3 %collective-permute-start.8 = (bf16[2,128,256]{2,1,0:T(8,128)(2,1)S(1)}, bf16[2,128,256]{2,1,0:T(8,128)(2,1)S(1)}, u32[]{:S(2)}, u32[]{:S(2)}) collective-permute-start(bf16[2,128,256]{2,1,0:T(8,128)(2,1)S(1)} %get-tuple-element.32), channel_id=1, source_target_pairs={{0,4},{2,6},{4,0},{6,2},{8,12},{10,14},{12,8},{14,10},{1,5},{3,7},... | collective-permute-start | bytes 393224 | tf_op jit(solution)/shard_map/ppermute | solution.py:209
  33.4 7.2 %collective-permute-start.9 = (bf16[2,128,256]{2,1,0:T(8,128)(2,1)S(1)}, bf16[2,128,256]{2,1,0:T(8,128)(2,1)S(1)}, u32[]{:S(2)}, u32[]{:S(2)}) collective-permute-start(bf16[2,128,256]{2,1,0:T(8,128)(2,1)S(1)} %get-tuple-element.33), channel_id=1, source_target_pairs={{0,6},{2,4},{4,2},{6,0},{8,14},{10,12},{12,10},{14,8},{1,7},{3,5},... | collective-permute-start | bytes 393224 | tf_op jit(solution)/shard_map/ppermute | solution.py:209
  41.4 1.6 %collective-permute-start.11 = (bf16[8,128,128]{2,1,0:T(8,128)(2,1)S(1)}, bf16[8,128,128]{2,1,0:T(8,128)(2,1)S(1)}, u32[]{:S(2)}, u32[]{:S(2)}) collective-permute-start(bf16[8,128,128]{2,1,0:T(8,128)(2,1)S(1)} %get-tuple-element.37), channel_id=1, source_target_pairs={{0,1},{1,0},{2,3},{3,2},{4,5},{5,4},{6,7},{7,6},{8,9},{9,8},{10,11... | collective-permute-start | bytes 786440 | tf_op jit(solution)/shard_map/ppermute | solution.py:246
  41.5 1.9 %collective-permute-start.10 = (bf16[8,128,128]{2,1,0:T(8,128)(2,1)S(1)}, bf16[8,128,128]{2,1,0:T(8,128)(2,1)S(1)}, u32[]{:S(2)}, u32[]{:S(2)}) collective-permute-start(bf16[8,128,128]{2,1,0:T(8,128)(2,1)S(1)} %get-tuple-element.35), channel_id=1, source_target_pairs={{0,1},{1,0},{2,3},{3,2},{4,5},{5,4},{6,7},{7,6},{8,9},{9,8},{10,11... | collective-permute-start | bytes 786440 | tf_op jit(solution)/shard_map/ppermute | solution.py:242

commit v8 on v4

--- a/solution.py
+++ b/solution.py
@@ -18,7 +18,8 @@
 VMEM = pl.BlockSpec(memory_space=pltpu.VMEM)
 
 
-def masked_kernel(pattern, blocks, occupied, ligand, masked, panel, orbitals, held, opened, sems):
+def masked_kernel(pattern, blocks, occupied, ligand, masked, panel, orbitals, *refs):
+    copies_out, (held, opened, sems) = refs[:-3], refs[-3:]
     aux_rows, _, nu_width = blocks.shape
     moves = ((blocks, held), (pattern, opened), (occupied, panel), (ligand, orbitals))
     copies = [pltpu.make_async_copy(source, target, sems.at[k]) for k, (source, target) in enumerate(moves)]
@@ -31,23 +32,29 @@
             for n in range(nu_width // BLK):
                 rows, columns = pl.ds(m * BLK, BLK), pl.ds(n * BLK, BLK)
                 tile = held[q, rows, columns]
-                masked[q, rows, columns] = jnp.where(opened[0, n, m] != 0, tile, jnp.zeros_like(tile))
+                tile = jnp.where(opened[0, n, m] != 0, tile, jnp.zeros_like(tile))
+                masked[q, rows, columns] = tile
+                copies_out[q][0, rows, columns] = tile
     for copy in copies[2:]:
         copy.wait()
 
 
+def after_kernel(block, before, out):
+    pass
+
+
 def slot_of(place, d):
     return (2 * (place[0] & 1) + place[1]) ^ d
 
 
-def half_into(outs, place, turned, masked):
+def half_into(outs, place, turned, parts):
     for d, out in enumerate(outs):
         rows = turned[slot_of(place, d)]
-        for q in range(out.shape[0]):
-            out[q] = jnp.dot(rows, masked[q], preferred_element_type=jnp.float32).astype(jnp.bfloat16)
-
-
-def own_kernel(place, occupied, other, masked, turned, *outs):
+        for q, (source, index) in enumerate(parts):
+            out[q] = jnp.dot(rows, source[index], preferred_element_type=jnp.float32).astype(jnp.bfloat16)
+
+
+def near_kernel(place, occupied, other, masked, far, turned, *outs):
     ni = turned.shape[1]
     near = place[1] == place[0] // 2
 
@@ -57,12 +64,13 @@
 
     pl.when(near)(functools.partial(turn, occupied))
     pl.when(jnp.logical_not(near))(functools.partial(turn, other))
-    half_into(outs, place, turned, masked)
+    half_into(outs, place, turned, [(masked, q) for q in range(masked.shape[0])] + [(far, 0)])
 
 
 def density_kernel(place, occupied, other, masked, turned, *refs):
     messages, out = refs[:-1], refs[-1]
-    aux_rows, ni, nu_width = messages[0].shape
+    aux_rows = masked.shape[0]
+    _, ni, nu_width = messages[0].shape
     own = pl.ds(pl.multiple_of(place[2] * nu_width, nu_width), nu_width)
     near = place[1] == place[0] // 2
 
@@ -88,12 +96,11 @@
     pl.when(jnp.logical_not(near))(functools.partial(far_terms, occupied))
 
 
-def far_kernel(place, value, value_there, masked, turned, density, *outs):
-    density[...] = (value[...] + value_there[...]) / math.sqrt(NOCC)
-    half_into(outs, place, turned, masked)
-
-
-def pair_kernel(place, after, ligand, *refs):
+def last_kernel(place, before, far, turned, *outs):
+    half_into(outs, place, turned, [(far, 0)])
+
+
+def pair_kernel(place, before, ligand, *refs):
     arrived, own, sent = refs[:-2], refs[-2], refs[-1]
     aux_rows, ni, nu_width = arrived[0].shape
     width = ligand.shape[1]
@@ -106,6 +113,13 @@
         sent[k * aux_rows : (k + 1) * aux_rows] = part.astype(jnp.bfloat16)
 
 
+def last_pair_kernel(place, before, near_sent, ligand, *refs):
+    sent = refs[-1]
+    near = near_sent.shape[0]
+    sent[:near] = near_sent[...]
+    pair_kernel(place, before, ligand, *refs[:-1], sent.at[near:])
+
+
 def turn_kernel(*refs):
     messages, out = refs[:-1], refs[-1]
     nu_width = messages[0].shape[2]
@@ -114,25 +128,19 @@
         out[g] = jnp.concatenate([x[:, here, :].reshape(-1, nu_width) for x in messages], axis=0).T
 
 
-def pair_and_turn_kernel(place, after, ligand, *refs):
-    pair_kernel(place, after, ligand, *refs[:-1])
-    turn_kernel(*refs[:-3], refs[-1])
-
-
-def cross_kernel(scale, near, far, *refs):
-    pairs, (out, held, sem) = refs[:4], refs[4:]
+def cross_kernel(scale, turned, *refs):
+    own, other, (out, held, sem) = refs[:-4], refs[-4], refs[-3:]
     ni, _, width = out.shape
 
     def step(g, carry):
         here = pl.ds(pl.multiple_of(g * GROUP, GROUP), GROUP)
-        turned = jnp.concatenate([near[g], far[g]], axis=1)
-        summed = [pairs[j][:, here, :] + pairs[j + 1][:, here, :].astype(jnp.float32) for j in (0, 2)]
-        summed = jnp.concatenate([(x * scale).astype(jnp.bfloat16) for x in summed], axis=0)
+        summed = jnp.concatenate([x[:, here, :] for x in own], axis=0) + other[:, here, :].astype(jnp.float32)
+        summed = (summed * scale).astype(jnp.bfloat16)
         row = lax.broadcasted_iota(jnp.int32, (1, GROUP, width), 1)
         zero = jnp.zeros_like(summed)
         for i in range(0, GROUP, 2):
             both = [jnp.where(row == i + e, summed, zero).reshape(-1, width) for e in (0, 1)]
-            result = jnp.dot(turned, jnp.concatenate(both, axis=1), preferred_element_type=jnp.float32)
+            result = jnp.dot(turned[g], jnp.concatenate(both, axis=1), preferred_element_type=jnp.float32)
             held[g * GROUP + i] = result[:, :width]
             held[g * GROUP + i + 1] = result[:, width:]
             if i % 4 == 2:
@@ -144,7 +152,7 @@
     pltpu.make_async_copy(held, out, sem).wait()
 
 
-def call(kernel, name, inputs, outputs, scratch=(), limit=16, scalars=1, flops=0, moved=1 << 20, in_spec=VMEM, out_spec=VMEM):
+def call(kernel, name, inputs, outputs, scratch=(), limit=16, scalars=1, flops=0, moved=1 << 20, in_spec=VMEM, out_spec=VMEM, aliases=None):
     inputs = list(inputs)
     results = pl.pallas_call(
         kernel,
@@ -154,6 +162,7 @@
         scratch_shapes=list(scratch),
         compiler_params=pltpu.CompilerParams(vmem_limit_bytes=limit * MIB),
         cost_estimate=pl.CostEstimate(flops=flops, bytes_accessed=moved, transcendentals=0),
+        input_output_aliases=aliases or {},
         name=name,
     )(*inputs)
     return list(results)
@@ -174,11 +183,12 @@
     across = [(a, a ^ 2) for a in range(n_aux)]
     swap = [(c, 1 - c) for c in range(n_ao)]
     pattern = jnp.swapaxes(pattern, 1, 2)
-    masked, panel, orbitals = call(
+    block = bf16((1, NB, nu_width))
+    masked, panel, orbitals, *parts = call(
         masked_kernel,
         "masked_blocks",
         (pltpu.with_memory_space_constraint(x, pltpu.HBM) for x in (pattern, blocks, occupied, ligand)),
-        [bf16(blocks.shape), bf16(occupied.shape), bf16(ligand.shape)],
+        [bf16(blocks.shape), bf16(occupied.shape), bf16(ligand.shape)] + [block] * aux_rows,
         [
             pltpu.VMEM(blocks.shape, jnp.bfloat16),
             pltpu.SMEM(pattern.shape, pattern.dtype),
@@ -187,8 +197,20 @@
         scalars=0,
         in_spec=pl.BlockSpec(memory_space=pltpu.HBM),
     )
-    far_masked = lax.ppermute(masked, "aux", across)
     other = lax.ppermute(panel, "orb", swap)
+    far = [lax.ppermute(parts[0], "aux", across)]
+    anywhere = pl.BlockSpec(memory_space=pl.ANY)
+    follower = call(
+        after_kernel,
+        "second_block",
+        (parts[1], far[0]),
+        [block],
+        scalars=0,
+        in_spec=anywhere,
+        out_spec=anywhere,
+        aliases={0: 0},
+    )[0]
+    far.append(lax.ppermute(follower, "aux", across))
 
     def square(messages):
         arrived = [messages[0]] + [None] * 3
@@ -199,51 +221,52 @@
             arrived[d] = lax.ppermute(messages[d], ("aux", "orb"), moves)
         return arrived
 
-    work = 2 * NB * panel_width * nu_width * aux_rows
-    messages = [bf16((aux_rows, ni, nu_width))] * 4
-    turned, *own = call(
-        own_kernel, "own_half", (place, panel, other, masked), [bf16((4, ni, NB))] + messages, flops=work
-    )
-    own_here = square(own)
+    work = 2 * NB * panel_width * nu_width
+    turned, *near = call(
+        near_kernel,
+        "near_rows",
+        (place, panel, other, masked, far[0]),
+        [bf16((4, ni, NB))] + [bf16((aux_rows + 1, ni, nu_width))] * 4,
+        flops=work * (aux_rows + 1),
+    )
+    near_here = square(near)
     value = call(
         density_kernel,
         "density_terms",
-        (place, panel, other, masked, turned, *own),
+        (place, panel, other, masked, turned, *near),
         [f32((aux_rows, 128))],
         flops=work,
     )[0]
-    density, *far = call(
-        far_kernel,
-        "far_half",
-        (place, value, lax.ppermute(value, "ao", swap), far_masked, turned),
-        [f32((aux_rows, 128))] + messages,
-        flops=work,
-    )
-    far_here = square(far)
-
-    shape = (4 * aux_rows, ni, width)
-    kept_and_given = [f32(shape), bf16(shape)]
-    side = [bf16((ni // GROUP, nu_width, 4 * aux_rows * GROUP))]
-    pair_work = 2 * shape[0] * ni * nu_width * width
-    own_kept, own_given, own_rows = call(
-        pair_and_turn_kernel,
-        "own_pairs",
-        (place, density, orbitals, *own_here),
-        kept_and_given + side,
-        flops=pair_work,
-    )
-    own_pairs = (own_kept, lax.ppermute(own_given, "ao", swap))
-    far_kept, far_given = call(
-        pair_kernel, "far_pairs", (place, density, orbitals, *far_here), kept_and_given, flops=pair_work
-    )
-    far_pairs = (far_kept, lax.ppermute(far_given, "ao", swap))
-    far_rows = call(turn_kernel, "far_turned", far_here, side, scalars=0)[0]
+    value_there = lax.ppermute(value, "ao", swap)
+    density = (value[:, 0] + value_there[:, 0]) / math.sqrt(NOCC)
+    last = call(last_kernel, "last_rows", (place, value, far[1], turned), [bf16((1, ni, nu_width))] * 4, flops=work)
+    last_here = square(last)
+
+    n_near, n_last = (4 * group[0].shape[0] for group in (near_here, last_here))
+    near_own, near_given = call(
+        pair_kernel,
+        "near_pairs",
+        (place, last[0], orbitals, *near_here),
+        [f32((n_near, ni, width)), bf16((n_near, ni, width))],
+        flops=2 * n_near * ni * nu_width * width,
+    )
+    last_own, given = call(
+        last_pair_kernel,
+        "last_pairs",
+        (place, value_there, near_given, orbitals, *last_here),
+        [f32((n_last, ni, width)), bf16((q_total, ni, width))],
+        flops=2 * n_last * ni * nu_width * width,
+    )
+    pairs = (near_own, last_own, lax.ppermute(given, "ao", swap))
+    columns = call(
+        turn_kernel, "turned", near_here + last_here, [bf16((ni // GROUP, nu_width, q_total * GROUP))], scalars=0
+    )[0]
 
     result = (ni, nu_width, width)
     cross_terms = call(
         functools.partial(cross_kernel, 1.0 / math.sqrt(q_total)),
         "cross_terms",
-        (own_rows, far_rows, *own_pairs, *far_pairs),
+        (columns, *pairs),
         [f32(result)],
         [pltpu.VMEM(result, jnp.float32), pltpu.SemaphoreType.DMA],
         limit=32,
@@ -252,7 +275,7 @@
         moved=18 * MIB,
         out_spec=pl.BlockSpec(memory_space=pltpu.HBM),
     )[0]
-    return (density[:, 0], cross_terms)
+    return (density, cross_terms)
 
 
 def plain_body(blocks, pattern, occupied, ligand):

time: 50.2 us -> 50.3 us (level)
  waiting for transfers between devices: 23.1 us -> 21.2 us
  starting transfers between devices: 13 us -> 14.8 us
  local copies, waits for them, and re-layouts: 0.63 us -> 0 us
  other arithmetic: 0.08 us -> 0.7 us
    ppermute x4, waiting for transfers between devices: 8.23 us -> 18.1 us  [the longest x1 11.7 us: body(): far = [lax.ppermute(parts[0], 'aux', across)]]
    ppermute x1, waiting for transfers between devices: 9.26 us -> 0.01 us  [body(): other = lax.ppermute(panel, 'orb', swap)]
    ppermute x6, waiting for transfers between devices: 5.61 us -> 3.02 us  [square(): arrived[d] = lax.ppermute(messages[d], ('aux', 'orb'), moves)]
    ppermute x6, starting transfers between devices: 7.17 us -> 9.13 us  [square(): arrived[d] = lax.ppermute(messages[d], ('aux', 'orb'), moves)]
    div x0 -> x1, other arithmetic: none -> 0.63 us  [body(): density = (value[:, 0] + value_there[:, 0]) / math.sqrt(NOCC)]
    slice x1 -> x0, local copies, waits for them, and re-layouts: 0.63 us -> none  [body(): return (density[:, 0], cross_terms)]
    pallas_call x8 -> x9, Pallas kernels: 12.6 us -> 12.7 us  [call(): pl.pallas_call(kernel, in_specs=[SMEM] * scalars + [in_spec] * (len(input...]
  transfers between devices with their start and end apart: 11 -> 11, of which waited for: 6 -> 5; matrix products, arithmetic and copies ran while one was open for 1% -> 1% of each run, Pallas kernels for 11% -> 9%
where the time goes in v8:
time: 50.3 us; the launch traced here: 50.1 us
  waiting for transfers between devices  21.2 us (42%)
  starting transfers between devices  14.8 us (29%)
  Pallas kernels  12.7 us (25%)
  between operations  0.72 us (1%)
  other arithmetic  0.7 us (1%)
    pallas_call x9, Pallas kernels, call(): pl.pallas_call(kernel, in_specs=[SMEM] * scalars + [in_spec] * (len(input...  12.7 us
    ppermute x1, waiting for transfers between devices, body(): far = [lax.ppermute(parts[0], 'aux', across)]  11.7 us
    ppermute x6, starting transfers between devices, square(): arrived[d] = lax.ppermute(messages[d], ('aux', 'orb'), moves)  9.13 us
    ppermute x1, waiting for transfers between devices, body(): far.append(lax.ppermute(follower, 'aux', across))  5.51 us
    ppermute x6, waiting for transfers between devices, square(): arrived[d] = lax.ppermute(messages[d], ('aux', 'orb'), moves)  3.02 us
    ppermute x1, starting transfers between devices, body(): other = lax.ppermute(panel, 'orb', swap)  3 us
    ppermute x1, starting transfers between devices, body(): far = [lax.ppermute(parts[0], 'aux', across)]  2.59 us
  transfers between devices with their start and end apart: 11, of which 5 were waited for; matrix products, arithmetic and copies ran while one was open for 1% of the time, Pallas kernels for 9%

profile of v8, /device:TPU:0, one launch (start us, length us, event | category | flops | bytes accessed | tf_op | source)
XLA Modules:
  0.0 50.1 jit_solution(10700183271587373867)
XLA Ops:
  0.6 1.3 %masked_blocks.1 = (bf16[2,512,256]{2,1,0:T(8,128)(2,1)S(1)}, bf16[512,512]{1,0:T(8,128)(2,1)S(1)}, bf16[512,128]{1,0:T(8,128)(2,1)S(1)}, bf16[1,512,256]{2,1,0:T(8,128)(2,1)S(1)}, bf16[1,512,256]{2,1,0:T(8,128)(2,1)S(1)}) custom-call(s32[1,2,4]{2,1,0:T(2,128)} %bitcast.4, bf16[2,512,256]{2,1,0:T(8,128)(2,1)} %blocks.1, bf16[512,512]{1,0:T(8,128)(2,1)} %occupied.1, ...), custom_call_target="tpu_custom_call" | custom-call | bytes 1048576 | tf_op jit(solution)/shard_map/masked_blocks/pallas_call | solution.py:157
  1.9 3.0 %collective-permute-start = (bf16[512,512]{1,0:T(8,128)(2,1)S(1)}, bf16[512,512]{1,0:T(8,128)(2,1)S(1)}, u32[]{:S(2)}, u32[]{:S(2)}) collective-permute-start(bf16[512,512]{1,0:T(8,128)(2,1)S(1)} %get-tuple-element.20.occupied), channel_id=1, source_target_pairs={{0,2},{2,0},{1,3},{3,1},{4,6},{6,4},{5,7},{7,5},{8,10},{10,8},{9,1... | collective-permute-start | bytes 1572872 | tf_op jit(solution)/shard_map/ppermute | solution.py:200
  4.9 2.6 %collective-permute-start.1 = (bf16[1,512,256]{2,1,0:T(8,128)(2,1)S(1)}, bf16[1,512,256]{2,1,0:T(8,128)(2,1)S(1)}, u32[]{:S(2)}, u32[]{:S(2)}) collective-permute-start(bf16[1,512,256]{2,1,0:T(8,128)(2,1)S(1)} %get-tuple-element.22), channel_id=1, source_target_pairs={{0,8},{4,12},{8,0},{12,4},{1,9},{5,13},{9,1},{13,5},{2,10},{6,14},... | collective-permute-start | bytes 786440 | tf_op jit(solution)/shard_map/ppermute | solution.py:201
  7.5 11.7 %collective-permute-done.1.far.before = bf16[1,512,256]{2,1,0:T(8,128)(2,1)S(1)} collective-permute-done((bf16[1,512,256]{2,1,0:T(8,128)(2,1)S(1)}, bf16[1,512,256]{2,1,0:T(8,128)(2,1)S(1)}, u32[]{:S(2)}, u32[]{:S(2)}) %collective-permute-start.1) | collective-permute-done | bytes 262176 | tf_op jit(solution)/shard_map/ppermute | solution.py:201
  19.2 0.0 collective-permute-start.6
  19.2 0.1 pad_add_fusion.place
  19.3 0.0 collective-permute-done.other
  19.3 1.3 %near_rows.1 = (bf16[4,128,512]{2,1,0:T(8,128)(2,1)S(1)}, bf16[3,128,256]{2,1,0:T(8,128)(2,1)S(1)}, bf16[3,128,256]{2,1,0:T(8,128)(2,1)S(1)}, bf16[3,128,256]{2,1,0:T(8,128)(2,1)S(1)}, bf16[3,128,256]{2,1,0:T(8,128)(2,1)S(1)}) custom-call(s32[3]{0:T(128)S(1)} %pad_add_fusion.place, bf16[512,512]{1,0:T(8,128)(2,1)S(1)} %get-tuple-element.20.occupied, ...), custom_call_target="tpu_custom_call" | custom-call | flops 402653184 | bytes 1048576 | tf_op jit(solution)/shard_map/near_rows/pallas_call | solution.py:157
  20.6 0.6 %collective-permute-start.3 = (bf16[3,128,256]{2,1,0:T(8,128)(2,1)S(1)}, bf16[3,128,256]{2,1,0:T(8,128)(2,1)S(1)}, u32[]{:S(2)}, u32[]{:S(2)}) collective-permute-start(bf16[3,128,256]{2,1,0:T(8,128)(2,1)S(1)} %get-tuple-element.25.refs_1_), channel_id=1, source_target_pairs={{0,2},{2,0},{4,6},{6,4},{8,10},{10,8},{12,14},{14,12},{1,3},{3,1},... | collective-permute-start | bytes 589832 | tf_op jit(solution)/shard_map/ppermute | solution.py:221
  21.1 4.1 %collective-permute-start.4 = (bf16[3,128,256]{2,1,0:T(8,128)(2,1)S(1)}, bf16[3,128,256]{2,1,0:T(8,128)(2,1)S(1)}, u32[]{:S(2)}, u32[]{:S(2)}) collective-permute-start(bf16[3,128,256]{2,1,0:T(8,128)(2,1)S(1)} %get-tuple-element.26.refs_2_), channel_id=1, source_target_pairs={{0,4},{2,6},{4,0},{6,2},{8,12},{10,14},{12,8},{14,10},{1,5},{3,7},... | collective-permute-start | bytes 589832 | tf_op jit(solution)/shard_map/ppermute | solution.py:221
  25.2 0.9 %collective-permute-start.5 = (bf16[3,128,256]{2,1,0:T(8,128)(2,1)S(1)}, bf16[3,128,256]{2,1,0:T(8,128)(2,1)S(1)}, u32[]{:S(2)}, u32[]{:S(2)}) collective-permute-start(bf16[3,128,256]{2,1,0:T(8,128)(2,1)S(1)} %get-tuple-element.27.refs_3_), channel_id=1, source_target_pairs={{0,6},{2,4},{4,2},{6,0},{8,14},{10,12},{12,10},{14,8},{1,7},{3,5},... | collective-permute-start | bytes 589832 | tf_op jit(solution)/shard_map/ppermute | solution.py:221
  26.2 1.3 %density_terms.1.before = f32[2,128]{1,0:T(2,128)S(1)} custom-call(s32[3]{0:T(128)S(1)} %pad_add_fusion.place, bf16[512,512]{1,0:T(8,128)(2,1)S(1)} %get-tuple-element.20.occupied, bf16[512,512]{1,0:T(8,128)(2,1)S(1)} %collective-permute-done.other, bf16[2,512,256]{2,1,0:T(8,128)(2,1)S(1)} %get-tuple-element.21.masked, ...), custom_call_target="tpu_custom_call" | custom-call | flops 134217728 | bytes 1048576 | tf_op jit(solution)/shard_map/density_terms/pallas_call | solution.py:157
  27.5 5.5 %collective-permute-done.6.far = bf16[1,512,256]{2,1,0:T(8,128)(2,1)S(1)} collective-permute-done((bf16[1,512,256]{2,1,0:T(8,128)(2,1)S(1)}, bf16[1,512,256]{2,1,0:T(8,128)(2,1)S(1)}, u32[]{:S(2)}, u32[]{:S(2)}) %collective-permute-start.6) | collective-permute-done | bytes 262176 | tf_op jit(solution)/shard_map/ppermute | solution.py:213
  33.0 0.8 %last_rows.1 = (bf16[1,128,256]{2,1,0:T(8,128)(2,1)S(1)}, bf16[1,128,256]{2,1,0:T(8,128)(2,1)S(1)}, bf16[1,128,256]{2,1,0:T(8,128)(2,1)S(1)}, bf16[1,128,256]{2,1,0:T(8,128)(2,1)S(1)}) custom-call(s32[3]{0:T(128)S(1)} %pad_add_fusion.place, f32[2,128]{1,0:T(2,128)S(1)} %density_terms.1.before, bf16[1,512,256]{2,1,0:T(8,128)(2,1)S(1)} %collective-permute-done.6.far, ...), custom_call_target="tpu_custom_call" | custom-call | flops 134217728 | bytes 1048576 | tf_op jit(solution)/shard_map/last_rows/pallas_call | solution.py:157
  33.8 0.6 %collective-permute-start.7 = (bf16[1,128,256]{2,1,0:T(8,128)(2,1)S(1)}, bf16[1,128,256]{2,1,0:T(8,128)(2,1)S(1)}, u32[]{:S(2)}, u32[]{:S(2)}) collective-permute-start(bf16[1,128,256]{2,1,0:T(8,128)(2,1)S(1)} %get-tuple-element.30), channel_id=1, source_target_pairs={{0,2},{2,0},{4,6},{6,4},{8,10},{10,8},{12,14},{14,12},{1,3},{3,1},... | collective-permute-start | bytes 196616 | tf_op jit(solution)/shard_map/ppermute | solution.py:221
  34.4 0.0 collective-permute-start.8
  34.4 0.0 collective-permute-done.3.refs_1_
  34.4 3.0 %collective-permute-start.9 = (bf16[1,128,256]{2,1,0:T(8,128)(2,1)S(1)}, bf16[1,128,256]{2,1,0:T(8,128)(2,1)S(1)}, u32[]{:S(2)}, u32[]{:S(2)}) collective-permute-start(bf16[1,128,256]{2,1,0:T(8,128)(2,1)S(1)} %get-tuple-element.32), channel_id=1, source_target_pairs={{0,6},{2,4},{4,2},{6,0},{8,14},{10,12},{12,10},{14,8},{1,7},{3,5},... | collective-permute-start | bytes 196616 | tf_op jit(solution)/shard_map/ppermute | solution.py:221
  37.4 0.0 collective-permute-done.4.refs_2_
  37.4 0.0 collective-permute-start.2
  37.4 2.5 %collective-permute-done.5.refs_3_ = bf16[3,128,256]{2,1,0:T(8,128)(2,1)S(1)} collective-permute-done((bf16[3,128,256]{2,1,0:T(8,128)(2,1)S(1)}, bf16[3,128,256]{2,1,0:T(8,128)(2,1)S(1)}, u32[]{:S(2)}, u32[]{:S(2)}) %collective-permute-start.5) | collective-permute-done | bytes 196640 | tf_op jit(solution)/shard_map/ppermute | solution.py:221
  39.8 0.9 %near_pairs.1 = (f32[12,128,128]{2,1,0:T(8,128)S(1)}, bf16[12,128,128]{2,1,0:T(8,128)(2,1)S(1)}) custom-call(s32[3]{0:T(128)S(1)} %pad_add_fusion.place, bf16[1,128,256]{2,1,0:T(8,128)(2,1)S(1)} %get-tuple-element.29.refs_4_.before.refs_0_, bf16[512,128]{1,0:T(8,128)(2,1)S(1)} %get-tuple-element.33.ligand, ...), custom_call_target="tpu_custom_call" | custom-call | flops 100663296 | bytes 1048576 | tf_op jit(solution)/shard_map/near_pairs/pallas_call | solution.py:157
  40.8 0.0 collective-permute-done.2.before
  40.8 0.0 collective-permute-done.7.refs_5_.refs_1_
  40.8 0.0 collective-permute-done.8.refs_6_.refs_2_
  40.8 0.5 %collective-permute-done.9.refs_7_.refs_3_ = bf16[1,128,256]{2,1,0:T(8,128)(2,1)S(1)} collective-permute-done((bf16[1,128,256]{2,1,0:T(8,128)(2,1)S(1)}, bf16[1,128,256]{2,1,0:T(8,128)(2,1)S(1)}, u32[]{:S(2)}, u32[]{:S(2)}) %collective-permute-start.9) | collective-permute-done | bytes 65568 | tf_op jit(solution)/shard_map/ppermute | solution.py:221
  41.3 0.8 %last_pairs.1 = (f32[4,128,128]{2,1,0:T(8,128)S(1)}, bf16[16,128,128]{2,1,0:T(8,128)(2,1)S(1)}) custom-call(s32[3]{0:T(128)S(1)} %pad_add_fusion.place, f32[2,128]{1,0:T(2,128)S(1)} %collective-permute-done.2.before, bf16[12,128,128]{2,1,0:T(8,128)(2,1)S(1)} %get-tuple-element.35.near_sent, bf16[512,128]{1,0:T(8,128)(2,1)S(1)} %get-tuple-element.33.ligand, ...), custom_call_target="tpu_custom_call" | custom-call | flops 33554432 | bytes 1048576 | tf_op jit(solution)/shard_map/last_pairs/pallas_call | solution.py:157
  42.1 0.1 collective-permute-start.10
  42.2 0.6 %multiply_reduce_fusion = f32[2]{0:T(128)} fusion(f32[2,128]{1,0:T(2,128)S(1)} %collective-permute-done.2.before, f32[2,128]{1,0:T(2,128)S(1)} %density_terms.1.before), kind=kLoop, calls=%fused_computation | loop fusion | flops 4 | bytes 24 | tf_op jit(solution)/shard_map/div | solution.py:241
  42.8 0.3 turned.1
  43.2 0.9 %collective-permute-done.10.refs_2_ = bf16[16,128,128]{2,1,0:T(8,128)(2,1)S(1)} collective-permute-done((bf16[16,128,128]{2,1,0:T(8,128)(2,1)S(1)}, bf16[16,128,128]{2,1,0:T(8,128)(2,1)S(1)}, u32[]{:S(2)}, u32[]{:S(2)}) %collective-permute-start.10) | collective-permute-done | bytes 524320 | tf_op jit(solution)/shard_map/ppermute | solution.py:260
  44.1 6.0 %cross_terms.1 = f32[128,256,128]{2,1,0:T(8,128)} custom-call(bf16[8,256,256]{2,1,0:T(8,128)(2,1)S(1)} %turned.1, f32[12,128,128]{2,1,0:T(8,128)S(1)} %get-tuple-element.34.refs_0_, f32[4,128,128]{2,1,0:T(8,128)S(1)} %get-tuple-element.36.refs_1_, bf16[16,128,128]{2,1,0:T(8,128)(2,1)S(1)} %collective-permute-done.10.refs_2_), custom_call_target="tpu_custom_call" | custom-call | flops 2147483648 | bytes 18874368 | tf_op jit(solution)/shard_map/cross_terms/pallas_call | solution.py:157
  (1 shorter events, 0.0 us)
Async XLA Ops:
  1.9 17.4 %collective-permute-start = (bf16[512,512]{1,0:T(8,128)(2,1)S(1)}, bf16[512,512]{1,0:T(8,128)(2,1)S(1)}, u32[]{:S(2)}, u32[]{:S(2)}) collective-permute-start(bf16[512,512]{1,0:T(8,128)(2,1)S(1)} %get-tuple-element.20.occupied), channel_id=1, source_target_pairs={{0,2},{2,0},{1,3},{3,1},{4,6},{6,4},{5,7},{7,5},{8,10},{10,8},{9,1... | collective-permute-start | bytes 1572872 | tf_op jit(solution)/shard_map/ppermute | solution.py:200
  4.9 14.3 %collective-permute-start.1 = (bf16[1,512,256]{2,1,0:T(8,128)(2,1)S(1)}, bf16[1,512,256]{2,1,0:T(8,128)(2,1)S(1)}, u32[]{:S(2)}, u32[]{:S(2)}) collective-permute-start(bf16[1,512,256]{2,1,0:T(8,128)(2,1)S(1)} %get-tuple-element.22), channel_id=1, source_target_pairs={{0,8},{4,12},{8,0},{12,4},{1,9},{5,13},{9,1},{13,5},{2,10},{6,14},... | collective-permute-start | bytes 786440 | tf_op jit(solution)/shard_map/ppermute | solution.py:201
  19.2 13.8 %collective-permute-start.6 = (bf16[1,512,256]{2,1,0:T(8,128)(2,1)S(1)}, bf16[1,512,256]{2,1,0:T(8,128)(2,1)S(1)}, u32[]{:S(2)}, u32[]{:S(2)}) collective-permute-start(bf16[1,512,256]{2,1,0:T(8,128)(2,1)S(1)} %second_block.1), channel_id=1, source_target_pairs={{0,8},{4,12},{8,0},{12,4},{1,9},{5,13},{9,1},{13,5},{2,10},{6,14},... | collective-permute-start | bytes 786440 | tf_op jit(solution)/shard_map/ppermute | solution.py:213
  20.6 13.8 %collective-permute-start.3 = (bf16[3,128,256]{2,1,0:T(8,128)(2,1)S(1)}, bf16[3,128,256]{2,1,0:T(8,128)(2,1)S(1)}, u32[]{:S(2)}, u32[]{:S(2)}) collective-permute-start(bf16[3,128,256]{2,1,0:T(8,128)(2,1)S(1)} %get-tuple-element.25.refs_1_), channel_id=1, source_target_pairs={{0,2},{2,0},{4,6},{6,4},{8,10},{10,8},{12,14},{14,12},{1,3},{3,1},... | collective-permute-start | bytes 589832 | tf_op jit(solution)/shard_map/ppermute | solution.py:221
  21.1 16.2 %collective-permute-start.4 = (bf16[3,128,256]{2,1,0:T(8,128)(2,1)S(1)}, bf16[3,128,256]{2,1,0:T(8,128)(2,1)S(1)}, u32[]{:S(2)}, u32[]{:S(2)}) collective-permute-start(bf16[3,128,256]{2,1,0:T(8,128)(2,1)S(1)} %get-tuple-element.26.refs_2_), channel_id=1, source_target_pairs={{0,4},{2,6},{4,0},{6,2},{8,12},{10,14},{12,8},{14,10},{1,5},{3,7},... | collective-permute-start | bytes 589832 | tf_op jit(solution)/shard_map/ppermute | solution.py:221
  25.2 14.6 %collective-permute-start.5 = (bf16[3,128,256]{2,1,0:T(8,128)(2,1)S(1)}, bf16[3,128,256]{2,1,0:T(8,128)(2,1)S(1)}, u32[]{:S(2)}, u32[]{:S(2)}) collective-permute-start(bf16[3,128,256]{2,1,0:T(8,128)(2,1)S(1)} %get-tuple-element.27.refs_3_), channel_id=1, source_target_pairs={{0,6},{2,4},{4,2},{6,0},{8,14},{10,12},{12,10},{14,8},{1,7},{3,5},... | collective-permute-start | bytes 589832 | tf_op jit(solution)/shard_map/ppermute | solution.py:221
  33.8 7.0 %collective-permute-start.7 = (bf16[1,128,256]{2,1,0:T(8,128)(2,1)S(1)}, bf16[1,128,256]{2,1,0:T(8,128)(2,1)S(1)}, u32[]{:S(2)}, u32[]{:S(2)}) collective-permute-start(bf16[1,128,256]{2,1,0:T(8,128)(2,1)S(1)} %get-tuple-element.30), channel_id=1, source_target_pairs={{0,2},{2,0},{4,6},{6,4},{8,10},{10,8},{12,14},{14,12},{1,3},{3,1},... | collective-permute-start | bytes 196616 | tf_op jit(solution)/shard_map/ppermute | solution.py:221
  34.4 6.4 %collective-permute-start.8 = (bf16[1,128,256]{2,1,0:T(8,128)(2,1)S(1)}, bf16[1,128,256]{2,1,0:T(8,128)(2,1)S(1)}, u32[]{:S(2)}, u32[]{:S(2)}) collective-permute-start(bf16[1,128,256]{2,1,0:T(8,128)(2,1)S(1)} %get-tuple-element.31), channel_id=1, source_target_pairs={{0,4},{2,6},{4,0},{6,2},{8,12},{10,14},{12,8},{14,10},{1,5},{3,7},... | collective-permute-start | bytes 196616 | tf_op jit(solution)/shard_map/ppermute | solution.py:221
  34.4 6.9 %collective-permute-start.9 = (bf16[1,128,256]{2,1,0:T(8,128)(2,1)S(1)}, bf16[1,128,256]{2,1,0:T(8,128)(2,1)S(1)}, u32[]{:S(2)}, u32[]{:S(2)}) collective-permute-start(bf16[1,128,256]{2,1,0:T(8,128)(2,1)S(1)} %get-tuple-element.32), channel_id=1, source_target_pairs={{0,6},{2,4},{4,2},{6,0},{8,14},{10,12},{12,10},{14,8},{1,7},{3,5},... | collective-permute-start | bytes 196616 | tf_op jit(solution)/shard_map/ppermute | solution.py:221
  37.4 3.4 %collective-permute-start.2 = (f32[2,128]{1,0:T(2,128)S(1)}, f32[2,128]{1,0:T(2,128)S(1)}, u32[]{:S(2)}, u32[]{:S(2)}) collective-permute-start(f32[2,128]{1,0:T(2,128)S(1)} %density_terms.1.before), channel_id=1, source_target_pairs={{0,1},{1,0},{2,3},{3,2},{4,5},{5,4},{6,7},{7,6},{8,9},{9,8},{10,11... | collective-permute-start | bytes 3080 | tf_op jit(solution)/shard_map/ppermute | solution.py:240
  42.1 2.0 %collective-permute-start.10 = (bf16[16,128,128]{2,1,0:T(8,128)(2,1)S(1)}, bf16[16,128,128]{2,1,0:T(8,128)(2,1)S(1)}, u32[]{:S(2)}, u32[]{:S(2)}) collective-permute-start(bf16[16,128,128]{2,1,0:T(8,128)(2,1)S(1)} %get-tuple-element.37), channel_id=1, source_target_pairs={{0,1},{1,0},{2,3},{3,2},{4,5},{5,4},{6,7},{7,6},{8,9},{9,8},{10,11... | collective-permute-start | bytes 1572872 | tf_op jit(solution)/shard_map/ppermute | solution.py:260

commit v9 on v7

--- a/solution.py
+++ b/solution.py
@@ -14,14 +14,13 @@
 NB = 512
 GROUP = 16
 MIB = 1024 * 1024
-SMEM = pl.BlockSpec(memory_space=pltpu.SMEM)
 VMEM = pl.BlockSpec(memory_space=pltpu.VMEM)
 
 
-def masked_kernel(place, pattern, blocks, occupied, ligand, masked, panel, part, orbitals, held, opened, sems):
+def masked_kernel(pattern, blocks, occupied, ligand, masked, panel, part, orbitals, held, opened, sems):
     aux_rows, _, nu_width = blocks.shape
-    own = occupied.at[pl.ds(pl.multiple_of(place[2] * part.shape[0], part.shape[0]), part.shape[0])]
-    moves = ((blocks, held), (pattern, opened), (own, part), (occupied, panel), (ligand, orbitals))
+    own = own_half_of(part.shape[0])
+    moves = ((blocks, held), (pattern, opened), (occupied.at[own], part), (occupied, panel), (ligand.at[own], orbitals))
     copies = [pltpu.make_async_copy(source, target, sems.at[k]) for k, (source, target) in enumerate(moves)]
     for copy in copies:
         copy.start()
@@ -37,48 +36,49 @@
         copy.wait()
 
 
-def slot_of(place, d):
-    return (2 * (place[0] & 1) + place[1]) ^ d
-
-
-def half_into(outs, place, turned, masked):
+def own_half_of(length):
+    return pl.ds(pl.multiple_of(lax.axis_index("ao") * length, length), length)
+
+
+def half_into(outs, turned, masked):
     for d, out in enumerate(outs):
-        rows = turned[slot_of(place, d)]
         for q in range(out.shape[0]):
-            out[q] = jnp.dot(rows, masked[q], preferred_element_type=jnp.float32).astype(jnp.bfloat16)
-
-
-def own_kernel(place, occupied, mine, theirs, masked, turned, *outs):
+            out[q] = jnp.dot(turned[d], masked[q], preferred_element_type=jnp.float32).astype(jnp.bfloat16)
+
+
+def own_kernel(occupied, mine, theirs, masked, turned, *outs):
+    aux, orb, ao = (lax.axis_index(name) for name in ("aux", "orb", "ao"))
     ni = turned.shape[1]
-    near = place[1] == place[0] // 2
+    here = 2 * (aux & 1) + orb
+    near = orb == aux // 2
 
     @pl.when(near)
     def _():
         for s in range(turned.shape[0]):
-            turned[s] = occupied[:, s * ni : (s + 1) * ni].T
+            turned[here ^ s] = occupied[:, s * ni : (s + 1) * ni].T
 
     @pl.when(jnp.logical_not(near))
     def _():
         depth = mine.shape[0]
         for e, rows in enumerate((mine, theirs)):
-            first = pl.multiple_of((place[2] ^ e) * depth, depth)
+            first = pl.multiple_of((ao ^ e) * depth, depth)
             for s in range(turned.shape[0]):
-                turned[s, :, pl.ds(first, depth)] = rows[:, s * ni : (s + 1) * ni].T
-
-    half_into(outs, place, turned, masked)
-
-
-def density_kernel(place, occupied, mine, theirs, masked, turned, *refs):
+                turned[here ^ s, :, pl.ds(first, depth)] = rows[:, s * ni : (s + 1) * ni].T
+
+    half_into(outs, turned, masked)
+
+
+def density_kernel(occupied, mine, theirs, masked, turned, *refs):
     messages, out, panel = refs[:-2], refs[-2], refs[-1]
     aux_rows, ni, nu_width = messages[0].shape
     depth = mine.shape[0]
-    own = pl.ds(pl.multiple_of(place[2] * nu_width, nu_width), nu_width)
-    near = place[1] == place[0] // 2
+    own = own_half_of(nu_width)
+    near = lax.axis_index("orb") == lax.axis_index("aux") // 2
 
     @pl.when(near)
     def _():
         for e, rows in enumerate((mine, theirs)):
-            panel[pl.ds(pl.multiple_of((place[2] ^ e) * depth, depth), depth), :] = rows[...]
+            panel[pl.ds(pl.multiple_of((lax.axis_index("ao") ^ e) * depth, depth), depth), :] = rows[...]
 
     @pl.when(jnp.logical_not(near))
     def _():
@@ -86,7 +86,7 @@
 
     totals = [0.0] * aux_rows
     for d, message in enumerate(messages):
-        rows = turned[slot_of(place, d), :, own].astype(jnp.float32)
+        rows = turned[d, :, own].astype(jnp.float32)
         for q in range(aux_rows):
             totals[q] += jnp.sum(rows * message[q].astype(jnp.float32))
     for s in range(4):
@@ -99,18 +99,17 @@
         out[q : q + 1, :] = jnp.full((1, out.shape[1]), totals[q], jnp.float32)
 
 
-def far_kernel(place, before, masked, turned, *outs):
-    half_into(outs, place, turned, masked)
-
-
-def pair_kernel(place, before, earlier, ligand, *refs):
+def far_kernel(before, masked, turned, *outs):
+    half_into(outs, turned, masked)
+
+
+def pair_kernel(before, earlier, ligand, *refs):
     arrived, own, sent = refs[:-2], refs[-2], refs[-1]
     aux_rows, ni, nu_width = arrived[0].shape
     width = ligand.shape[1]
-    rows = ligand[pl.ds(pl.multiple_of(place[2] * nu_width, nu_width), nu_width), :]
     for k, message in enumerate(arrived):
         part = jnp.dot(
-            message[...].reshape(aux_rows * ni, nu_width), rows, preferred_element_type=jnp.float32
+            message[...].reshape(aux_rows * ni, nu_width), ligand[...], preferred_element_type=jnp.float32
         ).reshape(aux_rows, ni, width)
         own[k * aux_rows : (k + 1) * aux_rows] = part
         sent[k * aux_rows : (k + 1) * aux_rows] = part.astype(jnp.bfloat16)
@@ -124,8 +123,8 @@
         out[g] = jnp.concatenate([x[:, here, :].reshape(-1, nu_width) for x in messages], axis=0).T
 
 
-def pair_and_turn_kernel(place, before, earlier, ligand, *refs):
-    pair_kernel(place, before, earlier, ligand, *refs[:-1])
+def pair_and_turn_kernel(before, earlier, ligand, *refs):
+    pair_kernel(before, earlier, ligand, *refs[:-1])
     turn_kernel(*refs[:-3], refs[-1])
 
 
@@ -154,11 +153,11 @@
     pltpu.make_async_copy(held, out, sem).wait()
 
 
-def call(kernel, name, inputs, outputs, scratch=(), limit=16, scalars=1, flops=0, moved=1 << 20, in_spec=VMEM, out_spec=VMEM):
+def call(kernel, name, inputs, outputs, scratch=(), limit=16, flops=0, moved=1 << 20, in_spec=VMEM, out_spec=VMEM):
     inputs = list(inputs)
     results = pl.pallas_call(
         kernel,
-        in_specs=[SMEM] * scalars + [in_spec] * (len(inputs) - scalars),
+        in_specs=[in_spec] * len(inputs),
         out_specs=[out_spec] * len(outputs),
         out_shape=outputs,
         scratch_shapes=list(scratch),
@@ -177,7 +176,6 @@
     q_total = aux_rows * owners
     panel_width = occupied.shape[1]
     width = ligand.shape[1]
-    place = jnp.stack([lax.axis_index(name) for name in ("aux", "orb", "ao")]).astype(jnp.int32)
     bf16 = functools.partial(jax.ShapeDtypeStruct, dtype=jnp.bfloat16)
     f32 = functools.partial(jax.ShapeDtypeStruct, dtype=jnp.float32)
 
@@ -187,8 +185,8 @@
     masked, panel, part, orbitals = call(
         masked_kernel,
         "masked_blocks",
-        (place, *(pltpu.with_memory_space_constraint(x, pltpu.HBM) for x in (pattern, blocks, occupied, ligand))),
-        [bf16(blocks.shape), bf16(occupied.shape), bf16((NB // n_ao, panel_width)), bf16(ligand.shape)],
+        (pltpu.with_memory_space_constraint(x, pltpu.HBM) for x in (pattern, blocks, occupied, ligand)),
+        [bf16(blocks.shape), bf16(occupied.shape), bf16((NB // n_ao, panel_width)), bf16((NB // n_ao, width))],
         [
             pltpu.VMEM(blocks.shape, jnp.bfloat16),
             pltpu.SMEM(pattern.shape, pattern.dtype),
@@ -212,20 +210,20 @@
     work = 2 * NB * panel_width * nu_width * aux_rows
     messages = [bf16((aux_rows, ni, nu_width))] * 4
     turned, *own = call(
-        own_kernel, "own_half", (place, panel, mine, theirs, masked), [bf16((4, ni, NB))] + messages, flops=work
+        own_kernel, "own_half", (panel, mine, theirs, masked), [bf16((4, ni, NB))] + messages, flops=work
     )
     own_here = square(own)
     value = call(
         density_kernel,
         "density_terms",
-        (place, panel, mine, theirs, masked, turned, *own),
+        (panel, mine, theirs, masked, turned, *own),
         [f32((aux_rows, 128))],
         [pltpu.VMEM(occupied.shape, jnp.bfloat16)],
         flops=work,
     )[0]
     value_there = lax.ppermute(value, "ao", swap)
     density = (value[:, 0] + value_there[:, 0]) / math.sqrt(NOCC)
-    far = call(far_kernel, "far_half", (place, value, far_masked, turned), messages, flops=work)
+    far = call(far_kernel, "far_half", (value, far_masked, turned), messages, flops=work)
     far_here = square(far)
 
     shape = (4 * aux_rows, ni, width)
@@ -235,16 +233,16 @@
     own_kept, own_given, own_rows = call(
         pair_and_turn_kernel,
         "own_pairs",
-        (place, value_there, far[0], orbitals, *own_here),
+        (value_there, far[0], orbitals, *own_here),
         kept_and_given + side,
         flops=pair_work,
     )
     own_pairs = (own_kept, lax.ppermute(own_given, "ao", swap))
     far_kept, far_given = call(
-        pair_kernel, "far_pairs", (place, value_there, own_rows, orbitals, *far_here), kept_and_given, flops=pair_work
+        pair_kernel, "far_pairs", (value_there, own_rows, orbitals, *far_here), kept_and_given, flops=pair_work
     )
     far_pairs = (far_kept, lax.ppermute(far_given, "ao", swap))
-    far_rows = call(turn_kernel, "far_turned", far_here, side, scalars=0)[0]
+    far_rows = call(turn_kernel, "far_turned", far_here, side)[0]
 
     result = (ni, nu_width, width)
     cross_terms = call(
@@ -254,7 +252,6 @@
         [f32(result)],
         [pltpu.VMEM(result, jnp.float32), pltpu.SemaphoreType.DMA],
         limit=32,
-        scalars=0,
         flops=32 * q_total * ni * nu_width * width,
         moved=18 * MIB,
         out_spec=pl.BlockSpec(memory_space=pltpu.HBM),

time: 49.6 us -> 47.9 us (0.966)
  Pallas kernels: 13.3 us -> 10 us
  waiting for transfers between devices: 21.4 us -> 23.1 us
    pallas_call x8, Pallas kernels: 13.3 us -> 10 us  [call(): pl.pallas_call(kernel, in_specs=[in_spec] * len(inputs), out_specs=[out_s...]
    ppermute x1, waiting for transfers between devices: 11.6 us -> 12.8 us  [body(): far_masked = lax.ppermute(masked, 'aux', across)]
    ppermute x6, waiting for transfers between devices: 3.97 us -> 4.52 us  [square(): arrived[d] = lax.ppermute(messages[d], ('aux', 'orb'), moves)]
  transfers between devices with their start and end apart: 12 -> 12, of which waited for: 8 -> 8; matrix products, arithmetic and copies ran while one was open for 1% -> 1% of each run, Pallas kernels for 9% -> 5%
where the time goes in v9:
time: 47.9 us; the launch traced here: 47.8 us
  waiting for transfers between devices  23.1 us (48%)
  starting transfers between devices  13.3 us (28%)
  Pallas kernels  10 us (21%)
  between operations  0.71 us (1%)
  other arithmetic  0.63 us (1%)
    ppermute x1, waiting for transfers between devices, body(): far_masked = lax.ppermute(masked, 'aux', across)  12.8 us
    pallas_call x8, Pallas kernels, call(): pl.pallas_call(kernel, in_specs=[in_spec] * len(inputs), out_specs=[out_s...  10 us
    ppermute x6, starting transfers between devices, square(): arrived[d] = lax.ppermute(messages[d], ('aux', 'orb'), moves)  7.11 us
    ppermute x6, waiting for transfers between devices, square(): arrived[d] = lax.ppermute(messages[d], ('aux', 'orb'), moves)  4.52 us
    ppermute x1, waiting for transfers between devices, body(): mine = lax.ppermute(part, 'orb', swap)  3.66 us
    ppermute x1, starting transfers between devices, body(): mine = lax.ppermute(part, 'orb', swap)  3 us
    ppermute x1, starting transfers between devices, body(): far_masked = lax.ppermute(masked, 'aux', across)  2.59 us
    ppermute x1, waiting for transfers between devices, body(): theirs = lax.ppermute(mine, 'ao', swap)  1.53 us
  transfers between devices with their start and end apart: 12, of which 8 were waited for; matrix products, arithmetic and copies ran while one was open for 1% of the time, Pallas kernels for 5%

profile of v9, /device:TPU:0, one launch (start us, length us, event | category | flops | bytes accessed | tf_op | source)
XLA Modules:
  0.0 47.8 jit_solution(16655516001508274601)
XLA Ops:
  0.6 1.4 %masked_blocks.1 = (bf16[2,512,256]{2,1,0:T(8,128)(2,1)S(1)}, bf16[512,512]{1,0:T(8,128)(2,1)S(1)}, bf16[256,512]{1,0:T(8,128)(2,1)S(1)}, bf16[256,128]{1,0:T(8,128)(2,1)S(1)}) custom-call(s32[1,2,4]{2,1,0:T(2,128)} %bitcast.1, bf16[2,512,256]{2,1,0:T(8,128)(2,1)} %blocks.1, bf16[512,512]{1,0:T(8,128)(2,1)} %occupied.1, bf16[512,128]{1,0:T(8,128)(2,1)} %ligand.1), custom_call_target="tpu_custom_call" | custom-call | bytes 1048576 | tf_op jit(solution)/shard_map/masked_blocks/pallas_call | solution.py:158
  2.0 3.0 %collective-permute-start = (bf16[256,512]{1,0:T(8,128)(2,1)S(1)}, bf16[256,512]{1,0:T(8,128)(2,1)S(1)}, u32[]{:S(2)}, u32[]{:S(2)}) collective-permute-start(bf16[256,512]{1,0:T(8,128)(2,1)S(1)} %get-tuple-element.21), channel_id=1, source_target_pairs={{0,2},{2,0},{1,3},{3,1},{4,6},{6,4},{5,7},{7,5},{8,10},{10,8},{9,1... | collective-permute-start | bytes 786440 | tf_op jit(solution)/shard_map/ppermute | solution.py:198
  5.0 2.6 %collective-permute-start.3 = (bf16[2,512,256]{2,1,0:T(8,128)(2,1)S(1)}, bf16[2,512,256]{2,1,0:T(8,128)(2,1)S(1)}, u32[]{:S(2)}, u32[]{:S(2)}) collective-permute-start(bf16[2,512,256]{2,1,0:T(8,128)(2,1)S(1)} %get-tuple-element.22.masked), channel_id=1, source_target_pairs={{0,8},{4,12},{8,0},{12,4},{1,9},{5,13},{9,1},{13,5},{2,10},{6,14},... | collective-permute-start | bytes 1572872 | tf_op jit(solution)/shard_map/ppermute | solution.py:197
  7.6 3.7 %collective-permute-done.mine = bf16[256,512]{1,0:T(8,128)(2,1)S(1)} collective-permute-done((bf16[256,512]{1,0:T(8,128)(2,1)S(1)}, bf16[256,512]{1,0:T(8,128)(2,1)S(1)}, u32[]{:S(2)}, u32[]{:S(2)}) %collective-permute-start) | collective-permute-done | bytes 262176 | tf_op jit(solution)/shard_map/ppermute | solution.py:198
  11.3 0.0 collective-permute-start.1
  11.3 1.5 %collective-permute-done.1.theirs = bf16[256,512]{1,0:T(8,128)(2,1)S(1)} collective-permute-done((bf16[256,512]{1,0:T(8,128)(2,1)S(1)}, bf16[256,512]{1,0:T(8,128)(2,1)S(1)}, u32[]{:S(2)}, u32[]{:S(2)}) %collective-permute-start.1) | collective-permute-done | bytes 262176 | tf_op jit(solution)/shard_map/ppermute | solution.py:199
  12.8 0.6 %own_half.1 = (bf16[4,128,512]{2,1,0:T(8,128)(2,1)S(1)}, bf16[2,128,256]{2,1,0:T(8,128)(2,1)S(1)}, bf16[2,128,256]{2,1,0:T(8,128)(2,1)S(1)}, bf16[2,128,256]{2,1,0:T(8,128)(2,1)S(1)}, bf16[2,128,256]{2,1,0:T(8,128)(2,1)S(1)}) custom-call(bf16[512,512]{1,0:T(8,128)(2,1)S(1)} %get-tuple-element.20.occupied, bf16[256,512]{1,0:T(8,128)(2,1)S(1)} %collective-permute-done.mine, ...), custom_call_target="tpu_custom_call" | custom-call | flops 268435456 | bytes 1048576 | tf_op jit(solution)/shard_map/own_half/pallas_call | solution.py:158
  13.5 1.8 %collective-permute-start.4 = (bf16[2,128,256]{2,1,0:T(8,128)(2,1)S(1)}, bf16[2,128,256]{2,1,0:T(8,128)(2,1)S(1)}, u32[]{:S(2)}, u32[]{:S(2)}) collective-permute-start(bf16[2,128,256]{2,1,0:T(8,128)(2,1)S(1)} %get-tuple-element.25.refs_1_), channel_id=1, source_target_pairs={{0,2},{2,0},{4,6},{6,4},{8,10},{10,8},{12,14},{14,12},{1,3},{3,1},... | collective-permute-start | bytes 393224 | tf_op jit(solution)/shard_map/ppermute | solution.py:207
  15.3 1.6 %collective-permute-start.5 = (bf16[2,128,256]{2,1,0:T(8,128)(2,1)S(1)}, bf16[2,128,256]{2,1,0:T(8,128)(2,1)S(1)}, u32[]{:S(2)}, u32[]{:S(2)}) collective-permute-start(bf16[2,128,256]{2,1,0:T(8,128)(2,1)S(1)} %get-tuple-element.26.refs_2_), channel_id=1, source_target_pairs={{0,4},{2,6},{4,0},{6,2},{8,12},{10,14},{12,8},{14,10},{1,5},{3,7},... | collective-permute-start | bytes 393224 | tf_op jit(solution)/shard_map/ppermute | solution.py:207
  16.9 0.2 collective-permute-start.6
  17.0 0.7 %density_terms.1.before = f32[2,128]{1,0:T(2,128)S(1)} custom-call(bf16[512,512]{1,0:T(8,128)(2,1)S(1)} %get-tuple-element.20.occupied, bf16[256,512]{1,0:T(8,128)(2,1)S(1)} %collective-permute-done.mine, bf16[256,512]{1,0:T(8,128)(2,1)S(1)} %collective-permute-done.1.theirs, bf16[2,512,256]{2,1,0:T(8,128)(2,1)S(1)} %get-tuple-element.22.masked, ...), custom_call_target="tpu_custom_call" | custom-call | flops 268435456 | bytes 1048576 | tf_op jit(solution)/shard_map/density_terms/pallas_call | solution.py:158
  17.8 0.1 collective-permute-start.2
  17.9 12.8 %collective-permute-done.3.masked = bf16[2,512,256]{2,1,0:T(8,128)(2,1)S(1)} collective-permute-done((bf16[2,512,256]{2,1,0:T(8,128)(2,1)S(1)}, bf16[2,512,256]{2,1,0:T(8,128)(2,1)S(1)}, u32[]{:S(2)}, u32[]{:S(2)}) %collective-permute-start.3) | collective-permute-done | bytes 524320 | tf_op jit(solution)/shard_map/ppermute | solution.py:197
  30.6 0.4 far_half.1
  31.1 0.5 %collective-permute-start.7 = (bf16[2,128,256]{2,1,0:T(8,128)(2,1)S(1)}, bf16[2,128,256]{2,1,0:T(8,128)(2,1)S(1)}, u32[]{:S(2)}, u32[]{:S(2)}) collective-permute-start(bf16[2,128,256]{2,1,0:T(8,128)(2,1)S(1)} %get-tuple-element.31), channel_id=1, source_target_pairs={{0,2},{2,0},{4,6},{6,4},{8,10},{10,8},{12,14},{14,12},{1,3},{3,1},... | collective-permute-start | bytes 393224 | tf_op jit(solution)/shard_map/ppermute | solution.py:207
  31.6 0.0 collective-permute-done.2.before
  31.6 0.7 %collective-permute-start.8 = (bf16[2,128,256]{2,1,0:T(8,128)(2,1)S(1)}, bf16[2,128,256]{2,1,0:T(8,128)(2,1)S(1)}, u32[]{:S(2)}, u32[]{:S(2)}) collective-permute-start(bf16[2,128,256]{2,1,0:T(8,128)(2,1)S(1)} %get-tuple-element.32), channel_id=1, source_target_pairs={{0,4},{2,6},{4,0},{6,2},{8,12},{10,14},{12,8},{14,10},{1,5},{3,7},... | collective-permute-start | bytes 393224 | tf_op jit(solution)/shard_map/ppermute | solution.py:207
  32.3 0.0 collective-permute-done.4.refs_1_
  32.3 2.3 %collective-permute-start.9 = (bf16[2,128,256]{2,1,0:T(8,128)(2,1)S(1)}, bf16[2,128,256]{2,1,0:T(8,128)(2,1)S(1)}, u32[]{:S(2)}, u32[]{:S(2)}) collective-permute-start(bf16[2,128,256]{2,1,0:T(8,128)(2,1)S(1)} %get-tuple-element.33), channel_id=1, source_target_pairs={{0,6},{2,4},{4,2},{6,0},{8,14},{10,12},{12,10},{14,8},{1,7},{3,5},... | collective-permute-start | bytes 393224 | tf_op jit(solution)/shard_map/ppermute | solution.py:207
  34.6 0.0 collective-permute-done.5.refs_2_
  34.6 0.0 collective-permute-done.6.refs_3_
  34.6 0.3 own_pairs.1
  34.9 2.6 %collective-permute-done.7.refs_1_ = bf16[2,128,256]{2,1,0:T(8,128)(2,1)S(1)} collective-permute-done((bf16[2,128,256]{2,1,0:T(8,128)(2,1)S(1)}, bf16[2,128,256]{2,1,0:T(8,128)(2,1)S(1)}, u32[]{:S(2)}, u32[]{:S(2)}) %collective-permute-start.7) | collective-permute-done | bytes 131104 | tf_op jit(solution)/shard_map/ppermute | solution.py:207
  37.5 0.4 collective-permute-done.8.refs_2_
  37.9 1.6 %collective-permute-done.9.refs_3_ = bf16[2,128,256]{2,1,0:T(8,128)(2,1)S(1)} collective-permute-done((bf16[2,128,256]{2,1,0:T(8,128)(2,1)S(1)}, bf16[2,128,256]{2,1,0:T(8,128)(2,1)S(1)}, u32[]{:S(2)}, u32[]{:S(2)}) %collective-permute-start.9) | collective-permute-done | bytes 131104 | tf_op jit(solution)/shard_map/ppermute | solution.py:207
  39.5 0.3 far_pairs.1
  39.7 0.1 collective-permute-start.11
  39.8 0.5 %collective-permute-start.10 = (bf16[8,128,128]{2,1,0:T(8,128)(2,1)S(1)}, bf16[8,128,128]{2,1,0:T(8,128)(2,1)S(1)}, u32[]{:S(2)}, u32[]{:S(2)}) collective-permute-start(bf16[8,128,128]{2,1,0:T(8,128)(2,1)S(1)} %get-tuple-element.35), channel_id=1, source_target_pairs={{0,1},{1,0},{2,3},{3,2},{4,5},{5,4},{6,7},{7,6},{8,9},{9,8},{10,11... | collective-permute-start | bytes 786440 | tf_op jit(solution)/shard_map/ppermute | solution.py:240
  40.3 0.6 %multiply_reduce_fusion = f32[2]{0:T(128)} fusion(f32[2,128]{1,0:T(2,128)S(1)} %collective-permute-done.2.before, f32[2,128]{1,0:T(2,128)S(1)} %density_terms.1.before), kind=kLoop, calls=%fused_computation | loop fusion | flops 4 | bytes 24 | tf_op jit(solution)/shard_map/div | solution.py:225
  40.9 0.2 far_turned.1.far
  41.1 0.2 collective-permute-done.11.refs_3_
  41.3 0.4 collective-permute-done.10.refs_1_
  41.7 6.0 %cross_terms.1 = f32[128,256,128]{2,1,0:T(8,128)} custom-call(bf16[8,256,128]{2,1,0:T(8,128)(2,1)S(1)} %get-tuple-element.30.earlier.near, bf16[8,256,128]{2,1,0:T(8,128)(2,1)S(1)} %far_turned.1.far, f32[8,128,128]{2,1,0:T(8,128)S(1)} %get-tuple-element.34.refs_0_, bf16[8,128,128]{2,1,0:T(8,128)(2,1)S(1)} %collective-permute-done.10.refs_1_, ...), custom_call_target="tpu_custom_call" | custom-call | flops 2147483648 | bytes 18874368 | tf_op jit(solution)/shard_map/cross_terms/pallas_call | solution.py:158
Async XLA Ops:
  2.0 9.3 %collective-permute-start = (bf16[256,512]{1,0:T(8,128)(2,1)S(1)}, bf16[256,512]{1,0:T(8,128)(2,1)S(1)}, u32[]{:S(2)}, u32[]{:S(2)}) collective-permute-start(bf16[256,512]{1,0:T(8,128)(2,1)S(1)} %get-tuple-element.21), channel_id=1, source_target_pairs={{0,2},{2,0},{1,3},{3,1},{4,6},{6,4},{5,7},{7,5},{8,10},{10,8},{9,1... | collective-permute-start | bytes 786440 | tf_op jit(solution)/shard_map/ppermute | solution.py:198
  5.0 25.6 %collective-permute-start.3 = (bf16[2,512,256]{2,1,0:T(8,128)(2,1)S(1)}, bf16[2,512,256]{2,1,0:T(8,128)(2,1)S(1)}, u32[]{:S(2)}, u32[]{:S(2)}) collective-permute-start(bf16[2,512,256]{2,1,0:T(8,128)(2,1)S(1)} %get-tuple-element.22.masked), channel_id=1, source_target_pairs={{0,8},{4,12},{8,0},{12,4},{1,9},{5,13},{9,1},{13,5},{2,10},{6,14},... | collective-permute-start | bytes 1572872 | tf_op jit(solution)/shard_map/ppermute | solution.py:197
  11.3 1.5 %collective-permute-start.1 = (bf16[256,512]{1,0:T(8,128)(2,1)S(1)}, bf16[256,512]{1,0:T(8,128)(2,1)S(1)}, u32[]{:S(2)}, u32[]{:S(2)}) collective-permute-start(bf16[256,512]{1,0:T(8,128)(2,1)S(1)} %collective-permute-done.mine), channel_id=1, source_target_pairs={{0,1},{1,0},{2,3},{3,2},{4,5},{5,4},{6,7},{7,6},{8,9},{9,8},{10,11... | collective-permute-start | bytes 786440 | tf_op jit(solution)/shard_map/ppermute | solution.py:199
  13.5 18.8 %collective-permute-start.4 = (bf16[2,128,256]{2,1,0:T(8,128)(2,1)S(1)}, bf16[2,128,256]{2,1,0:T(8,128)(2,1)S(1)}, u32[]{:S(2)}, u32[]{:S(2)}) collective-permute-start(bf16[2,128,256]{2,1,0:T(8,128)(2,1)S(1)} %get-tuple-element.25.refs_1_), channel_id=1, source_target_pairs={{0,2},{2,0},{4,6},{6,4},{8,10},{10,8},{12,14},{14,12},{1,3},{3,1},... | collective-permute-start | bytes 393224 | tf_op jit(solution)/shard_map/ppermute | solution.py:207
  15.3 19.3 %collective-permute-start.5 = (bf16[2,128,256]{2,1,0:T(8,128)(2,1)S(1)}, bf16[2,128,256]{2,1,0:T(8,128)(2,1)S(1)}, u32[]{:S(2)}, u32[]{:S(2)}) collective-permute-start(bf16[2,128,256]{2,1,0:T(8,128)(2,1)S(1)} %get-tuple-element.26.refs_2_), channel_id=1, source_target_pairs={{0,4},{2,6},{4,0},{6,2},{8,12},{10,14},{12,8},{14,10},{1,5},{3,7},... | collective-permute-start | bytes 393224 | tf_op jit(solution)/shard_map/ppermute | solution.py:207
  16.9 17.8 %collective-permute-start.6 = (bf16[2,128,256]{2,1,0:T(8,128)(2,1)S(1)}, bf16[2,128,256]{2,1,0:T(8,128)(2,1)S(1)}, u32[]{:S(2)}, u32[]{:S(2)}) collective-permute-start(bf16[2,128,256]{2,1,0:T(8,128)(2,1)S(1)} %get-tuple-element.27.refs_3_), channel_id=1, source_target_pairs={{0,6},{2,4},{4,2},{6,0},{8,14},{10,12},{12,10},{14,8},{1,7},{3,5},... | collective-permute-start | bytes 393224 | tf_op jit(solution)/shard_map/ppermute | solution.py:207
  17.8 13.8 %collective-permute-start.2 = (f32[2,128]{1,0:T(2,128)S(1)}, f32[2,128]{1,0:T(2,128)S(1)}, u32[]{:S(2)}, u32[]{:S(2)}) collective-permute-start(f32[2,128]{1,0:T(2,128)S(1)} %density_terms.1.before), channel_id=1, source_target_pairs={{0,1},{1,0},{2,3},{3,2},{4,5},{5,4},{6,7},{7,6},{8,9},{9,8},{10,11... | collective-permute-start | bytes 3080 | tf_op jit(solution)/shard_map/ppermute | solution.py:224
  31.1 6.4 %collective-permute-start.7 = (bf16[2,128,256]{2,1,0:T(8,128)(2,1)S(1)}, bf16[2,128,256]{2,1,0:T(8,128)(2,1)S(1)}, u32[]{:S(2)}, u32[]{:S(2)}) collective-permute-start(bf16[2,128,256]{2,1,0:T(8,128)(2,1)S(1)} %get-tuple-element.31), channel_id=1, source_target_pairs={{0,2},{2,0},{4,6},{6,4},{8,10},{10,8},{12,14},{14,12},{1,3},{3,1},... | collective-permute-start | bytes 393224 | tf_op jit(solution)/shard_map/ppermute | solution.py:207
  31.6 6.3 %collective-permute-start.8 = (bf16[2,128,256]{2,1,0:T(8,128)(2,1)S(1)}, bf16[2,128,256]{2,1,0:T(8,128)(2,1)S(1)}, u32[]{:S(2)}, u32[]{:S(2)}) collective-permute-start(bf16[2,128,256]{2,1,0:T(8,128)(2,1)S(1)} %get-tuple-element.32), channel_id=1, source_target_pairs={{0,4},{2,6},{4,0},{6,2},{8,12},{10,14},{12,8},{14,10},{1,5},{3,7},... | collective-permute-start | bytes 393224 | tf_op jit(solution)/shard_map/ppermute | solution.py:207
  32.3 7.2 %collective-permute-start.9 = (bf16[2,128,256]{2,1,0:T(8,128)(2,1)S(1)}, bf16[2,128,256]{2,1,0:T(8,128)(2,1)S(1)}, u32[]{:S(2)}, u32[]{:S(2)}) collective-permute-start(bf16[2,128,256]{2,1,0:T(8,128)(2,1)S(1)} %get-tuple-element.33), channel_id=1, source_target_pairs={{0,6},{2,4},{4,2},{6,0},{8,14},{10,12},{12,10},{14,8},{1,7},{3,5},... | collective-permute-start | bytes 393224 | tf_op jit(solution)/shard_map/ppermute | solution.py:207
  39.7 1.6 %collective-permute-start.11 = (bf16[8,128,128]{2,1,0:T(8,128)(2,1)S(1)}, bf16[8,128,128]{2,1,0:T(8,128)(2,1)S(1)}, u32[]{:S(2)}, u32[]{:S(2)}) collective-permute-start(bf16[8,128,128]{2,1,0:T(8,128)(2,1)S(1)} %get-tuple-element.37), channel_id=1, source_target_pairs={{0,1},{1,0},{2,3},{3,2},{4,5},{5,4},{6,7},{7,6},{8,9},{9,8},{10,11... | collective-permute-start | bytes 786440 | tf_op jit(solution)/shard_map/ppermute | solution.py:244
  39.8 1.9 %collective-permute-start.10 = (bf16[8,128,128]{2,1,0:T(8,128)(2,1)S(1)}, bf16[8,128,128]{2,1,0:T(8,128)(2,1)S(1)}, u32[]{:S(2)}, u32[]{:S(2)}) collective-permute-start(bf16[8,128,128]{2,1,0:T(8,128)(2,1)S(1)} %get-tuple-element.35), channel_id=1, source_target_pairs={{0,1},{1,0},{2,3},{3,2},{4,5},{5,4},{6,7},{7,6},{8,9},{9,8},{10,11... | collective-permute-start | bytes 786440 | tf_op jit(solution)/shard_map/ppermute | solution.py:240

commit v10 on v9

--- a/solution.py
+++ b/solution.py
@@ -50,12 +50,13 @@
     aux, orb, ao = (lax.axis_index(name) for name in ("aux", "orb", "ao"))
     ni = turned.shape[1]
     here = 2 * (aux & 1) + orb
+    place = lambda s: (4 - (here ^ s)) & 3
     near = orb == aux // 2
 
     @pl.when(near)
     def _():
         for s in range(turned.shape[0]):
-            turned[here ^ s] = occupied[:, s * ni : (s + 1) * ni].T
+            turned[place(s)] = occupied[:, s * ni : (s + 1) * ni].T
 
     @pl.when(jnp.logical_not(near))
     def _():
@@ -63,7 +64,7 @@
         for e, rows in enumerate((mine, theirs)):
             first = pl.multiple_of((ao ^ e) * depth, depth)
             for s in range(turned.shape[0]):
-                turned[here ^ s, :, pl.ds(first, depth)] = rows[:, s * ni : (s + 1) * ni].T
+                turned[place(s), :, pl.ds(first, depth)] = rows[:, s * ni : (s + 1) * ni].T
 
     half_into(outs, turned, masked)
 
@@ -199,12 +200,12 @@
     theirs = lax.ppermute(mine, "ao", swap)
 
     def square(messages):
-        arrived = [messages[0]] + [None] * 3
-        for d in (3, 2, 1):
+        arrived = [messages[0]]
+        for message, d in zip(messages[1:], (3, 2, 1)):
             moves = [
                 (a * n_orb + o, (a ^ (d >> 1)) * n_orb + (o ^ (d & 1))) for a in range(n_aux) for o in range(n_orb)
             ]
-            arrived[d] = lax.ppermute(messages[d], ("aux", "orb"), moves)
+            arrived.append(lax.ppermute(message, ("aux", "orb"), moves))
         return arrived
 
     work = 2 * NB * panel_width * nu_width * aux_rows

time: 47.9 us -> 47.6 us (level)
  no operation moved by 1% of the time
where the time goes in v10:
time: 47.6 us; the launch traced here: 47.4 us
  waiting for transfers between devices  22.7 us (48%)
  starting transfers between devices  13.3 us (28%)
  Pallas kernels  10 us (21%)
  between operations  0.71 us (1%)
  other arithmetic  0.63 us (1%)
    ppermute x1, waiting for transfers between devices, body(): far_masked = lax.ppermute(masked, 'aux', across)  12.8 us
    pallas_call x8, Pallas kernels, call(): pl.pallas_call(kernel, in_specs=[in_spec] * len(inputs), out_specs=[out_s...  10 us
    ppermute x6, starting transfers between devices, square(): arrived.append(lax.ppermute(message, ('aux', 'orb'), moves))  7.11 us
    ppermute x6, waiting for transfers between devices, square(): arrived.append(lax.ppermute(message, ('aux', 'orb'), moves))  4.2 us
    ppermute x1, waiting for transfers between devices, body(): mine = lax.ppermute(part, 'orb', swap)  3.66 us
    ppermute x1, starting transfers between devices, body(): mine = lax.ppermute(part, 'orb', swap)  3 us
    ppermute x1, starting transfers between devices, body(): far_masked = lax.ppermute(masked, 'aux', across)  2.59 us
    ppermute x1, waiting for transfers between devices, body(): theirs = lax.ppermute(mine, 'ao', swap)  1.53 us
  transfers between devices with their start and end apart: 12, of which 8 were waited for; matrix products, arithmetic and copies ran while one was open for 1% of the time, Pallas kernels for 5%

profile of v10, /device:TPU:0, one launch (start us, length us, event | category | flops | bytes accessed | tf_op | source)
XLA Modules:
  0.0 47.4 jit_solution(4591809128965116208)
XLA Ops:
  0.6 1.4 %masked_blocks.1 = (bf16[2,512,256]{2,1,0:T(8,128)(2,1)S(1)}, bf16[512,512]{1,0:T(8,128)(2,1)S(1)}, bf16[256,512]{1,0:T(8,128)(2,1)S(1)}, bf16[256,128]{1,0:T(8,128)(2,1)S(1)}) custom-call(s32[1,2,4]{2,1,0:T(2,128)} %bitcast.1, bf16[2,512,256]{2,1,0:T(8,128)(2,1)} %blocks.1, bf16[512,512]{1,0:T(8,128)(2,1)} %occupied.1, bf16[512,128]{1,0:T(8,128)(2,1)} %ligand.1), custom_call_target="tpu_custom_call" | custom-call | bytes 1048576 | tf_op jit(solution)/shard_map/masked_blocks/pallas_call | solution.py:159
  2.0 3.0 %collective-permute-start = (bf16[256,512]{1,0:T(8,128)(2,1)S(1)}, bf16[256,512]{1,0:T(8,128)(2,1)S(1)}, u32[]{:S(2)}, u32[]{:S(2)}) collective-permute-start(bf16[256,512]{1,0:T(8,128)(2,1)S(1)} %get-tuple-element.21), channel_id=1, source_target_pairs={{0,2},{2,0},{1,3},{3,1},{4,6},{6,4},{5,7},{7,5},{8,10},{10,8},{9,1... | collective-permute-start | bytes 786440 | tf_op jit(solution)/shard_map/ppermute | solution.py:199
  5.0 2.6 %collective-permute-start.3 = (bf16[2,512,256]{2,1,0:T(8,128)(2,1)S(1)}, bf16[2,512,256]{2,1,0:T(8,128)(2,1)S(1)}, u32[]{:S(2)}, u32[]{:S(2)}) collective-permute-start(bf16[2,512,256]{2,1,0:T(8,128)(2,1)S(1)} %get-tuple-element.22.masked), channel_id=1, source_target_pairs={{0,8},{4,12},{8,0},{12,4},{1,9},{5,13},{9,1},{13,5},{2,10},{6,14},... | collective-permute-start | bytes 1572872 | tf_op jit(solution)/shard_map/ppermute | solution.py:198
  7.6 3.7 %collective-permute-done.mine = bf16[256,512]{1,0:T(8,128)(2,1)S(1)} collective-permute-done((bf16[256,512]{1,0:T(8,128)(2,1)S(1)}, bf16[256,512]{1,0:T(8,128)(2,1)S(1)}, u32[]{:S(2)}, u32[]{:S(2)}) %collective-permute-start) | collective-permute-done | bytes 262176 | tf_op jit(solution)/shard_map/ppermute | solution.py:199
  11.3 0.0 collective-permute-start.1
  11.3 1.5 %collective-permute-done.1.theirs = bf16[256,512]{1,0:T(8,128)(2,1)S(1)} collective-permute-done((bf16[256,512]{1,0:T(8,128)(2,1)S(1)}, bf16[256,512]{1,0:T(8,128)(2,1)S(1)}, u32[]{:S(2)}, u32[]{:S(2)}) %collective-permute-start.1) | collective-permute-done | bytes 262176 | tf_op jit(solution)/shard_map/ppermute | solution.py:200
  12.8 0.6 %own_half.1 = (bf16[4,128,512]{2,1,0:T(8,128)(2,1)S(1)}, bf16[2,128,256]{2,1,0:T(8,128)(2,1)S(1)}, bf16[2,128,256]{2,1,0:T(8,128)(2,1)S(1)}, bf16[2,128,256]{2,1,0:T(8,128)(2,1)S(1)}, bf16[2,128,256]{2,1,0:T(8,128)(2,1)S(1)}) custom-call(bf16[512,512]{1,0:T(8,128)(2,1)S(1)} %get-tuple-element.20.occupied, bf16[256,512]{1,0:T(8,128)(2,1)S(1)} %collective-permute-done.mine, ...), custom_call_target="tpu_custom_call" | custom-call | flops 268435456 | bytes 1048576 | tf_op jit(solution)/shard_map/own_half/pallas_call | solution.py:159
  13.5 2.8 %collective-permute-start.4 = (bf16[2,128,256]{2,1,0:T(8,128)(2,1)S(1)}, bf16[2,128,256]{2,1,0:T(8,128)(2,1)S(1)}, u32[]{:S(2)}, u32[]{:S(2)}) collective-permute-start(bf16[2,128,256]{2,1,0:T(8,128)(2,1)S(1)} %get-tuple-element.25.refs_1_), channel_id=1, source_target_pairs={{0,6},{2,4},{4,2},{6,0},{8,14},{10,12},{12,10},{14,8},{1,7},{3,5},... | collective-permute-start | bytes 393224 | tf_op jit(solution)/shard_map/ppermute | solution.py:208
  16.3 0.4 collective-permute-start.5
  16.7 0.3 collective-permute-start.6
  17.0 0.7 %density_terms.1.before = f32[2,128]{1,0:T(2,128)S(1)} custom-call(bf16[512,512]{1,0:T(8,128)(2,1)S(1)} %get-tuple-element.20.occupied, bf16[256,512]{1,0:T(8,128)(2,1)S(1)} %collective-permute-done.mine, bf16[256,512]{1,0:T(8,128)(2,1)S(1)} %collective-permute-done.1.theirs, bf16[2,512,256]{2,1,0:T(8,128)(2,1)S(1)} %get-tuple-element.22.masked, ...), custom_call_target="tpu_custom_call" | custom-call | flops 268435456 | bytes 1048576 | tf_op jit(solution)/shard_map/density_terms/pallas_call | solution.py:159
  17.8 0.1 collective-permute-start.2
  17.9 12.8 %collective-permute-done.3.masked = bf16[2,512,256]{2,1,0:T(8,128)(2,1)S(1)} collective-permute-done((bf16[2,512,256]{2,1,0:T(8,128)(2,1)S(1)}, bf16[2,512,256]{2,1,0:T(8,128)(2,1)S(1)}, u32[]{:S(2)}, u32[]{:S(2)}) %collective-permute-start.3) | collective-permute-done | bytes 524320 | tf_op jit(solution)/shard_map/ppermute | solution.py:198
  30.6 0.4 far_half.1
  31.1 0.6 %collective-permute-start.7 = (bf16[2,128,256]{2,1,0:T(8,128)(2,1)S(1)}, bf16[2,128,256]{2,1,0:T(8,128)(2,1)S(1)}, u32[]{:S(2)}, u32[]{:S(2)}) collective-permute-start(bf16[2,128,256]{2,1,0:T(8,128)(2,1)S(1)} %get-tuple-element.31), channel_id=1, source_target_pairs={{0,6},{2,4},{4,2},{6,0},{8,14},{10,12},{12,10},{14,8},{1,7},{3,5},... | collective-permute-start | bytes 393224 | tf_op jit(solution)/shard_map/ppermute | solution.py:208
  31.7 0.0 collective-permute-done.2.before
  31.7 1.4 %collective-permute-start.8 = (bf16[2,128,256]{2,1,0:T(8,128)(2,1)S(1)}, bf16[2,128,256]{2,1,0:T(8,128)(2,1)S(1)}, u32[]{:S(2)}, u32[]{:S(2)}) collective-permute-start(bf16[2,128,256]{2,1,0:T(8,128)(2,1)S(1)} %get-tuple-element.32), channel_id=1, source_target_pairs={{0,4},{2,6},{4,0},{6,2},{8,12},{10,14},{12,8},{14,10},{1,5},{3,7},... | collective-permute-start | bytes 393224 | tf_op jit(solution)/shard_map/ppermute | solution.py:208
  33.1 0.0 collective-permute-done.4.refs_1_
  33.1 1.5 %collective-permute-start.9 = (bf16[2,128,256]{2,1,0:T(8,128)(2,1)S(1)}, bf16[2,128,256]{2,1,0:T(8,128)(2,1)S(1)}, u32[]{:S(2)}, u32[]{:S(2)}) collective-permute-start(bf16[2,128,256]{2,1,0:T(8,128)(2,1)S(1)} %get-tuple-element.33), channel_id=1, source_target_pairs={{0,2},{2,0},{4,6},{6,4},{8,10},{10,8},{12,14},{14,12},{1,3},{3,1},... | collective-permute-start | bytes 393224 | tf_op jit(solution)/shard_map/ppermute | solution.py:208
  34.6 0.0 collective-permute-done.5.refs_2_
  34.6 0.0 collective-permute-done.6.refs_3_
  34.6 0.3 own_pairs.1
  34.9 2.9 %collective-permute-done.7.refs_1_ = bf16[2,128,256]{2,1,0:T(8,128)(2,1)S(1)} collective-permute-done((bf16[2,128,256]{2,1,0:T(8,128)(2,1)S(1)}, bf16[2,128,256]{2,1,0:T(8,128)(2,1)S(1)}, u32[]{:S(2)}, u32[]{:S(2)}) %collective-permute-start.7) | collective-permute-done | bytes 131104 | tf_op jit(solution)/shard_map/ppermute | solution.py:208
  37.8 1.0 %collective-permute-done.8.refs_2_ = bf16[2,128,256]{2,1,0:T(8,128)(2,1)S(1)} collective-permute-done((bf16[2,128,256]{2,1,0:T(8,128)(2,1)S(1)}, bf16[2,128,256]{2,1,0:T(8,128)(2,1)S(1)}, u32[]{:S(2)}, u32[]{:S(2)}) %collective-permute-start.8) | collective-permute-done | bytes 131104 | tf_op jit(solution)/shard_map/ppermute | solution.py:208
  38.8 0.3 collective-permute-done.9.refs_3_
  39.1 0.3 far_pairs.1
  39.4 0.1 collective-permute-start.11
  39.5 0.5 %collective-permute-start.10 = (bf16[8,128,128]{2,1,0:T(8,128)(2,1)S(1)}, bf16[8,128,128]{2,1,0:T(8,128)(2,1)S(1)}, u32[]{:S(2)}, u32[]{:S(2)}) collective-permute-start(bf16[8,128,128]{2,1,0:T(8,128)(2,1)S(1)} %get-tuple-element.35), channel_id=1, source_target_pairs={{0,1},{1,0},{2,3},{3,2},{4,5},{5,4},{6,7},{7,6},{8,9},{9,8},{10,11... | collective-permute-start | bytes 786440 | tf_op jit(solution)/shard_map/ppermute | solution.py:241
  40.0 0.6 %multiply_reduce_fusion = f32[2]{0:T(128)} fusion(f32[2,128]{1,0:T(2,128)S(1)} %collective-permute-done.2.before, f32[2,128]{1,0:T(2,128)S(1)} %density_terms.1.before), kind=kLoop, calls=%fused_computation | loop fusion | flops 4 | bytes 24 | tf_op jit(solution)/shard_map/div | solution.py:226
  40.6 0.2 far_turned.1.far
  40.8 0.2 collective-permute-done.11.refs_3_
  41.0 0.4 collective-permute-done.10.refs_1_
  41.4 6.0 %cross_terms.1 = f32[128,256,128]{2,1,0:T(8,128)} custom-call(bf16[8,256,128]{2,1,0:T(8,128)(2,1)S(1)} %get-tuple-element.30.earlier.near, bf16[8,256,128]{2,1,0:T(8,128)(2,1)S(1)} %far_turned.1.far, f32[8,128,128]{2,1,0:T(8,128)S(1)} %get-tuple-element.34.refs_0_, bf16[8,128,128]{2,1,0:T(8,128)(2,1)S(1)} %collective-permute-done.10.refs_1_, ...), custom_call_target="tpu_custom_call" | custom-call | flops 2147483648 | bytes 18874368 | tf_op jit(solution)/shard_map/cross_terms/pallas_call | solution.py:159
Async XLA Ops:
  2.0 9.3 %collective-permute-start = (bf16[256,512]{1,0:T(8,128)(2,1)S(1)}, bf16[256,512]{1,0:T(8,128)(2,1)S(1)}, u32[]{:S(2)}, u32[]{:S(2)}) collective-permute-start(bf16[256,512]{1,0:T(8,128)(2,1)S(1)} %get-tuple-element.21), channel_id=1, source_target_pairs={{0,2},{2,0},{1,3},{3,1},{4,6},{6,4},{5,7},{7,5},{8,10},{10,8},{9,1... | collective-permute-start | bytes 786440 | tf_op jit(solution)/shard_map/ppermute | solution.py:199
  5.0 25.6 %collective-permute-start.3 = (bf16[2,512,256]{2,1,0:T(8,128)(2,1)S(1)}, bf16[2,512,256]{2,1,0:T(8,128)(2,1)S(1)}, u32[]{:S(2)}, u32[]{:S(2)}) collective-permute-start(bf16[2,512,256]{2,1,0:T(8,128)(2,1)S(1)} %get-tuple-element.22.masked), channel_id=1, source_target_pairs={{0,8},{4,12},{8,0},{12,4},{1,9},{5,13},{9,1},{13,5},{2,10},{6,14},... | collective-permute-start | bytes 1572872 | tf_op jit(solution)/shard_map/ppermute | solution.py:198
  11.3 1.5 %collective-permute-start.1 = (bf16[256,512]{1,0:T(8,128)(2,1)S(1)}, bf16[256,512]{1,0:T(8,128)(2,1)S(1)}, u32[]{:S(2)}, u32[]{:S(2)}) collective-permute-start(bf16[256,512]{1,0:T(8,128)(2,1)S(1)} %collective-permute-done.mine), channel_id=1, source_target_pairs={{0,1},{1,0},{2,3},{3,2},{4,5},{5,4},{6,7},{7,6},{8,9},{9,8},{10,11... | collective-permute-start | bytes 786440 | tf_op jit(solution)/shard_map/ppermute | solution.py:200
  13.5 19.6 %collective-permute-start.4 = (bf16[2,128,256]{2,1,0:T(8,128)(2,1)S(1)}, bf16[2,128,256]{2,1,0:T(8,128)(2,1)S(1)}, u32[]{:S(2)}, u32[]{:S(2)}) collective-permute-start(bf16[2,128,256]{2,1,0:T(8,128)(2,1)S(1)} %get-tuple-element.25.refs_1_), channel_id=1, source_target_pairs={{0,6},{2,4},{4,2},{6,0},{8,14},{10,12},{12,10},{14,8},{1,7},{3,5},... | collective-permute-start | bytes 393224 | tf_op jit(solution)/shard_map/ppermute | solution.py:208
  16.3 18.3 %collective-permute-start.5 = (bf16[2,128,256]{2,1,0:T(8,128)(2,1)S(1)}, bf16[2,128,256]{2,1,0:T(8,128)(2,1)S(1)}, u32[]{:S(2)}, u32[]{:S(2)}) collective-permute-start(bf16[2,128,256]{2,1,0:T(8,128)(2,1)S(1)} %get-tuple-element.26.refs_2_), channel_id=1, source_target_pairs={{0,4},{2,6},{4,0},{6,2},{8,12},{10,14},{12,8},{14,10},{1,5},{3,7},... | collective-permute-start | bytes 393224 | tf_op jit(solution)/shard_map/ppermute | solution.py:208
  16.7 17.9 %collective-permute-start.6 = (bf16[2,128,256]{2,1,0:T(8,128)(2,1)S(1)}, bf16[2,128,256]{2,1,0:T(8,128)(2,1)S(1)}, u32[]{:S(2)}, u32[]{:S(2)}) collective-permute-start(bf16[2,128,256]{2,1,0:T(8,128)(2,1)S(1)} %get-tuple-element.27.refs_3_), channel_id=1, source_target_pairs={{0,2},{2,0},{4,6},{6,4},{8,10},{10,8},{12,14},{14,12},{1,3},{3,1},... | collective-permute-start | bytes 393224 | tf_op jit(solution)/shard_map/ppermute | solution.py:208
  17.8 13.9 %collective-permute-start.2 = (f32[2,128]{1,0:T(2,128)S(1)}, f32[2,128]{1,0:T(2,128)S(1)}, u32[]{:S(2)}, u32[]{:S(2)}) collective-permute-start(f32[2,128]{1,0:T(2,128)S(1)} %density_terms.1.before), channel_id=1, source_target_pairs={{0,1},{1,0},{2,3},{3,2},{4,5},{5,4},{6,7},{7,6},{8,9},{9,8},{10,11... | collective-permute-start | bytes 3080 | tf_op jit(solution)/shard_map/ppermute | solution.py:225
  31.1 6.8 %collective-permute-start.7 = (bf16[2,128,256]{2,1,0:T(8,128)(2,1)S(1)}, bf16[2,128,256]{2,1,0:T(8,128)(2,1)S(1)}, u32[]{:S(2)}, u32[]{:S(2)}) collective-permute-start(bf16[2,128,256]{2,1,0:T(8,128)(2,1)S(1)} %get-tuple-element.31), channel_id=1, source_target_pairs={{0,6},{2,4},{4,2},{6,0},{8,14},{10,12},{12,10},{14,8},{1,7},{3,5},... | collective-permute-start | bytes 393224 | tf_op jit(solution)/shard_map/ppermute | solution.py:208
  31.7 7.1 %collective-permute-start.8 = (bf16[2,128,256]{2,1,0:T(8,128)(2,1)S(1)}, bf16[2,128,256]{2,1,0:T(8,128)(2,1)S(1)}, u32[]{:S(2)}, u32[]{:S(2)}) collective-permute-start(bf16[2,128,256]{2,1,0:T(8,128)(2,1)S(1)} %get-tuple-element.32), channel_id=1, source_target_pairs={{0,4},{2,6},{4,0},{6,2},{8,12},{10,14},{12,8},{14,10},{1,5},{3,7},... | collective-permute-start | bytes 393224 | tf_op jit(solution)/shard_map/ppermute | solution.py:208
  33.1 6.0 %collective-permute-start.9 = (bf16[2,128,256]{2,1,0:T(8,128)(2,1)S(1)}, bf16[2,128,256]{2,1,0:T(8,128)(2,1)S(1)}, u32[]{:S(2)}, u32[]{:S(2)}) collective-permute-start(bf16[2,128,256]{2,1,0:T(8,128)(2,1)S(1)} %get-tuple-element.33), channel_id=1, source_target_pairs={{0,2},{2,0},{4,6},{6,4},{8,10},{10,8},{12,14},{14,12},{1,3},{3,1},... | collective-permute-start | bytes 393224 | tf_op jit(solution)/shard_map/ppermute | solution.py:208
  39.4 1.6 %collective-permute-start.11 = (bf16[8,128,128]{2,1,0:T(8,128)(2,1)S(1)}, bf16[8,128,128]{2,1,0:T(8,128)(2,1)S(1)}, u32[]{:S(2)}, u32[]{:S(2)}) collective-permute-start(bf16[8,128,128]{2,1,0:T(8,128)(2,1)S(1)} %get-tuple-element.37), channel_id=1, source_target_pairs={{0,1},{1,0},{2,3},{3,2},{4,5},{5,4},{6,7},{7,6},{8,9},{9,8},{10,11... | collective-permute-start | bytes 786440 | tf_op jit(solution)/shard_map/ppermute | solution.py:245
  39.5 1.9 %collective-permute-start.10 = (bf16[8,128,128]{2,1,0:T(8,128)(2,1)S(1)}, bf16[8,128,128]{2,1,0:T(8,128)(2,1)S(1)}, u32[]{:S(2)}, u32[]{:S(2)}) collective-permute-start(bf16[8,128,128]{2,1,0:T(8,128)(2,1)S(1)} %get-tuple-element.35), channel_id=1, source_target_pairs={{0,1},{1,0},{2,3},{3,2},{4,5},{5,4},{6,7},{7,6},{8,9},{9,8},{10,11... | collective-permute-start | bytes 786440 | tf_op jit(solution)/shard_map/ppermute | solution.py:241

commit v11 on v10

--- a/solution.py
+++ b/solution.py
@@ -17,10 +17,10 @@
 VMEM = pl.BlockSpec(memory_space=pltpu.VMEM)
 
 
-def masked_kernel(pattern, blocks, occupied, ligand, masked, panel, part, orbitals, held, opened, sems):
+def masked_kernel(pattern, blocks, occupied, ligand, masked, panel, orbitals, held, opened, sems):
     aux_rows, _, nu_width = blocks.shape
-    own = own_half_of(part.shape[0])
-    moves = ((blocks, held), (pattern, opened), (occupied.at[own], part), (occupied, panel), (ligand.at[own], orbitals))
+    own = own_half_of(orbitals.shape[0])
+    moves = ((blocks, held), (pattern, opened), (occupied, panel), (ligand.at[own], orbitals))
     copies = [pltpu.make_async_copy(source, target, sems.at[k]) for k, (source, target) in enumerate(moves)]
     for copy in copies:
         copy.start()
@@ -46,8 +46,8 @@
             out[q] = jnp.dot(turned[d], masked[q], preferred_element_type=jnp.float32).astype(jnp.bfloat16)
 
 
-def own_kernel(occupied, mine, theirs, masked, turned, *outs):
-    aux, orb, ao = (lax.axis_index(name) for name in ("aux", "orb", "ao"))
+def own_kernel(occupied, other, masked, turned, *outs):
+    aux, orb = lax.axis_index("aux"), lax.axis_index("orb")
     ni = turned.shape[1]
     here = 2 * (aux & 1) + orb
     place = lambda s: (4 - (here ^ s)) & 3
@@ -60,26 +60,21 @@
 
     @pl.when(jnp.logical_not(near))
     def _():
-        depth = mine.shape[0]
-        for e, rows in enumerate((mine, theirs)):
-            first = pl.multiple_of((ao ^ e) * depth, depth)
-            for s in range(turned.shape[0]):
-                turned[place(s), :, pl.ds(first, depth)] = rows[:, s * ni : (s + 1) * ni].T
+        for s in range(turned.shape[0]):
+            turned[place(s)] = other[:, s * ni : (s + 1) * ni].T
 
     half_into(outs, turned, masked)
 
 
-def density_kernel(occupied, mine, theirs, masked, turned, *refs):
+def density_kernel(occupied, other, masked, turned, *refs):
     messages, out, panel = refs[:-2], refs[-2], refs[-1]
     aux_rows, ni, nu_width = messages[0].shape
-    depth = mine.shape[0]
     own = own_half_of(nu_width)
     near = lax.axis_index("orb") == lax.axis_index("aux") // 2
 
     @pl.when(near)
     def _():
-        for e, rows in enumerate((mine, theirs)):
-            panel[pl.ds(pl.multiple_of((lax.axis_index("ao") ^ e) * depth, depth), depth), :] = rows[...]
+        panel[...] = other[...]
 
     @pl.when(jnp.logical_not(near))
     def _():
@@ -100,7 +95,19 @@
         out[q : q + 1, :] = jnp.full((1, out.shape[1]), totals[q], jnp.float32)
 
 
-def far_kernel(before, masked, turned, *outs):
+def open_kernel(pattern, opened):
+    for m in range(NBLK):
+        for n in range(opened.shape[1] // BLK):
+            value = jnp.where(pattern[0, n, m] != 0, 1.0, 0.0)
+            opened[pl.ds(m * BLK, BLK), pl.ds(n * BLK, BLK)] = jnp.full((BLK, BLK), value, jnp.float32)
+
+
+def far_kernel(before, opened, blocks, turned, *refs):
+    outs, masked = refs[:-1], refs[-1]
+    keep = opened[...] != 0
+    for q in range(blocks.shape[0]):
+        tile = blocks[q]
+        masked[q] = jnp.where(keep, tile, jnp.zeros_like(tile))
     half_into(outs, turned, masked)
 
 
@@ -183,21 +190,27 @@
     across = [(a, a ^ 2) for a in range(n_aux)]
     swap = [(c, 1 - c) for c in range(n_ao)]
     pattern = jnp.swapaxes(pattern, 1, 2)
-    masked, panel, part, orbitals = call(
+    masked, panel, orbitals = call(
         masked_kernel,
         "masked_blocks",
         (pltpu.with_memory_space_constraint(x, pltpu.HBM) for x in (pattern, blocks, occupied, ligand)),
-        [bf16(blocks.shape), bf16(occupied.shape), bf16((NB // n_ao, panel_width)), bf16((NB // n_ao, width))],
+        [bf16(blocks.shape), bf16(occupied.shape), bf16((NB // n_ao, width))],
         [
             pltpu.VMEM(blocks.shape, jnp.bfloat16),
             pltpu.SMEM(pattern.shape, pattern.dtype),
-            pltpu.SemaphoreType.DMA((5,)),
+            pltpu.SemaphoreType.DMA((4,)),
         ],
         in_spec=pl.BlockSpec(memory_space=pltpu.HBM),
     )
-    far_masked = lax.ppermute(masked, "aux", across)
-    mine = lax.ppermute(part, "orb", swap)
-    theirs = lax.ppermute(mine, "ao", swap)
+    far_blocks = lax.ppermute(blocks, "aux", across)
+    opened = call(
+        open_kernel,
+        "open_blocks",
+        (lax.ppermute(pattern, "aux", across),),
+        [f32((NB, nu_width))],
+        in_spec=pl.BlockSpec(memory_space=pltpu.SMEM),
+    )[0]
+    other = lax.ppermute(occupied, "orb", swap)
 
     def square(messages):
         arrived = [messages[0]]
@@ -211,20 +224,27 @@
     work = 2 * NB * panel_width * nu_width * aux_rows
     messages = [bf16((aux_rows, ni, nu_width))] * 4
     turned, *own = call(
-        own_kernel, "own_half", (panel, mine, theirs, masked), [bf16((4, ni, NB))] + messages, flops=work
+        own_kernel, "own_half", (panel, other, masked), [bf16((4, ni, NB))] + messages, flops=work
     )
     own_here = square(own)
     value = call(
         density_kernel,
         "density_terms",
-        (panel, mine, theirs, masked, turned, *own),
+        (panel, other, masked, turned, *own),
         [f32((aux_rows, 128))],
         [pltpu.VMEM(occupied.shape, jnp.bfloat16)],
         flops=work,
     )[0]
     value_there = lax.ppermute(value, "ao", swap)
     density = (value[:, 0] + value_there[:, 0]) / math.sqrt(NOCC)
-    far = call(far_kernel, "far_half", (value, far_masked, turned), messages, flops=work)
+    far = call(
+        far_kernel,
+        "far_half",
+        (value, opened, far_blocks, turned),
+        messages,
+        [pltpu.VMEM(blocks.shape, jnp.bfloat16)],
+        flops=work,
+    )
     far_here = square(far)
 
     shape = (4 * aux_rows, ni, width)

time: 47.6 us -> 50.9 us (1.069)
  starting transfers between devices: 13.3 us -> 16.5 us
    ppermute x3, starting transfers between devices: 5.6 us -> 8.18 us  [the longest x1 3 us: body(): other = lax.ppermute(occupied, 'orb', swap)]
    ppermute x3, waiting for transfers between devices: 18 us -> 16 us  [the longest x1 8.3 us: body(): other = lax.ppermute(occupied, 'orb', swap)]
    ppermute x6, waiting for transfers between devices: 4.2 us -> 5.86 us  [square(): arrived.append(lax.ppermute(message, ('aux', 'orb'), moves))]
    ppermute x6, starting transfers between devices: 7.11 us -> 7.66 us  [square(): arrived.append(lax.ppermute(message, ('aux', 'orb'), moves))]
    pallas_call x8 -> x9, Pallas kernels: 10 us -> 10.5 us  [call(): pl.pallas_call(kernel, in_specs=[in_spec] * len(inputs), out_specs=[out_s...]
  transfers between devices with their start and end apart: 12 -> 12, of which waited for: 8 -> 6; matrix products, arithmetic and copies ran while one was open for 1% -> 1% of each run, Pallas kernels for 5% -> 8%
where the time goes in v11:
time: 50.9 us; the launch traced here: 50.7 us
  waiting for transfers between devices  22.4 us (44%)
  starting transfers between devices  16.5 us (32%)
  Pallas kernels  10.5 us (21%)
  between operations  0.72 us (1%)
  other arithmetic  0.63 us (1%)
    pallas_call x9, Pallas kernels, call(): pl.pallas_call(kernel, in_specs=[in_spec] * len(inputs), out_specs=[out_s...  10.5 us
    ppermute x1, waiting for transfers between devices, body(): other = lax.ppermute(occupied, 'orb', swap)  8.3 us
    ppermute x1, waiting for transfers between devices, body(): lax.ppermute(pattern, 'aux', across)  7.71 us
    ppermute x6, starting transfers between devices, square(): arrived.append(lax.ppermute(message, ('aux', 'orb'), moves))  7.66 us
    ppermute x6, waiting for transfers between devices, square(): arrived.append(lax.ppermute(message, ('aux', 'orb'), moves))  5.86 us
    ppermute x1, starting transfers between devices, body(): other = lax.ppermute(occupied, 'orb', swap)  3 us
    ppermute x1, starting transfers between devices, body(): lax.ppermute(pattern, 'aux', across)  2.59 us
    ppermute x1, starting transfers between devices, body(): far_blocks = lax.ppermute(blocks, 'aux', across)  2.59 us
  transfers between devices with their start and end apart: 12, of which 6 were waited for; matrix products, arithmetic and copies ran while one was open for 1% of the time, Pallas kernels for 8%

profile of v11, /device:TPU:0, one launch (start us, length us, event | category | flops | bytes accessed | tf_op | source)
XLA Modules:
  0.0 50.7 jit_solution(16168668947184860164)
XLA Ops:
  0.6 3.0 %collective-permute-start = (bf16[512,512]{1,0:T(8,128)(2,1)}, bf16[512,512]{1,0:T(8,128)(2,1)S(1)}, u32[]{:S(2)}, u32[]{:S(2)}) collective-permute-start(bf16[512,512]{1,0:T(8,128)(2,1)} %occupied.1), channel_id=1, source_target_pairs={{0,2},{2,0},{1,3},{3,1},{4,6},{6,4},{5,7},{7,5},{8,10},{10,8},{9,1... | collective-permute-start | bytes 1572872 | tf_op jit(solution)/shard_map/ppermute | solution.py:213
  3.6 2.6 %collective-permute-start.3 = (bf16[2,512,256]{2,1,0:T(8,128)(2,1)}, bf16[2,512,256]{2,1,0:T(8,128)(2,1)S(1)}, u32[]{:S(2)}, u32[]{:S(2)}) collective-permute-start(bf16[2,512,256]{2,1,0:T(8,128)(2,1)} %blocks.1), channel_id=1, source_target_pairs={{0,8},{4,12},{8,0},{12,4},{1,9},{5,13},{9,1},{13,5},{2,10},{6,14},... | collective-permute-start | bytes 1572872 | tf_op jit(solution)/shard_map/ppermute | solution.py:205
  6.2 1.2 %masked_blocks.1 = (bf16[2,512,256]{2,1,0:T(8,128)(2,1)S(1)}, bf16[512,512]{1,0:T(8,128)(2,1)S(1)}, bf16[256,128]{1,0:T(8,128)(2,1)S(1)}) custom-call(s32[1,2,4]{2,1,0:T(2,128)} %bitcast.1, bf16[2,512,256]{2,1,0:T(8,128)(2,1)} %blocks.1, bf16[512,512]{1,0:T(8,128)(2,1)} %occupied.1, bf16[512,128]{1,0:T(8,128)(2,1)} %ligand.1), custom_call_target="tpu_custom_call" | custom-call | bytes 1048576 | tf_op jit(solution)/shard_map/masked_blocks/pallas_call | solution.py:166
  7.5 8.3 %collective-permute-done.other = bf16[512,512]{1,0:T(8,128)(2,1)S(1)} collective-permute-done((bf16[512,512]{1,0:T(8,128)(2,1)}, bf16[512,512]{1,0:T(8,128)(2,1)S(1)}, u32[]{:S(2)}, u32[]{:S(2)}) %collective-permute-start) | collective-permute-done | bytes 524320 | tf_op jit(solution)/shard_map/ppermute | solution.py:213
  15.8 0.6 %own_half.1 = (bf16[4,128,512]{2,1,0:T(8,128)(2,1)S(1)}, bf16[2,128,256]{2,1,0:T(8,128)(2,1)S(1)}, bf16[2,128,256]{2,1,0:T(8,128)(2,1)S(1)}, bf16[2,128,256]{2,1,0:T(8,128)(2,1)S(1)}, bf16[2,128,256]{2,1,0:T(8,128)(2,1)S(1)}) custom-call(bf16[512,512]{1,0:T(8,128)(2,1)S(1)} %get-tuple-element.19.occupied, bf16[512,512]{1,0:T(8,128)(2,1)S(1)} %collective-permute-done.other, ...), custom_call_target="tpu_custom_call" | custom-call | flops 268435456 | bytes 1048576 | tf_op jit(solution)/shard_map/own_half/pallas_call | solution.py:166
  16.4 2.8 %collective-permute-start.4 = (bf16[2,128,256]{2,1,0:T(8,128)(2,1)S(1)}, bf16[2,128,256]{2,1,0:T(8,128)(2,1)S(1)}, u32[]{:S(2)}, u32[]{:S(2)}) collective-permute-start(bf16[2,128,256]{2,1,0:T(8,128)(2,1)S(1)} %get-tuple-element.23.refs_1_), channel_id=1, source_target_pairs={{0,6},{2,4},{4,2},{6,0},{8,14},{10,12},{12,10},{14,8},{1,7},{3,5},... | collective-permute-start | bytes 393224 | tf_op jit(solution)/shard_map/ppermute | solution.py:221
  19.2 2.6 %collective-permute-start.2 = (s32[1,2,4]{2,1,0:T(2,128)}, s32[1,2,4]{2,1,0:T(2,128)S(1)}, u32[]{:S(2)}, u32[]{:S(2)}) collective-permute-start(s32[1,2,4]{2,1,0:T(2,128)} %bitcast.2), channel_id=1, source_target_pairs={{0,8},{4,12},{8,0},{12,4},{1,9},{5,13},{9,1},{13,5},{2,10},{6,14},... | collective-permute-start | bytes 104 | tf_op jit(solution)/shard_map/ppermute | solution.py:209
  21.8 7.7 %collective-permute-done.2.pattern = s32[1,2,4]{2,1,0:T(2,128)S(1)} collective-permute-done((s32[1,2,4]{2,1,0:T(2,128)}, s32[1,2,4]{2,1,0:T(2,128)S(1)}, u32[]{:S(2)}, u32[]{:S(2)}) %collective-permute-start.2) | collective-permute-done | bytes 64 | tf_op jit(solution)/shard_map/ppermute | solution.py:209
  29.5 0.6 %open_blocks.1.opened = f32[512,256]{1,0:T(8,128)S(1)} custom-call(s32[1,2,4]{2,1,0:T(2,128)S(1)} %collective-permute-done.2.pattern), custom_call_target="tpu_custom_call" | custom-call | bytes 1048576 | tf_op jit(solution)/shard_map/open_blocks/pallas_call | solution.py:166
  30.1 0.8 %collective-permute-start.5 = (bf16[2,128,256]{2,1,0:T(8,128)(2,1)S(1)}, bf16[2,128,256]{2,1,0:T(8,128)(2,1)S(1)}, u32[]{:S(2)}, u32[]{:S(2)}) collective-permute-start(bf16[2,128,256]{2,1,0:T(8,128)(2,1)S(1)} %get-tuple-element.24.refs_2_), channel_id=1, source_target_pairs={{0,4},{2,6},{4,0},{6,2},{8,12},{10,14},{12,8},{14,10},{1,5},{3,7},... | collective-permute-start | bytes 393224 | tf_op jit(solution)/shard_map/ppermute | solution.py:221
  30.9 0.5 %collective-permute-start.6 = (bf16[2,128,256]{2,1,0:T(8,128)(2,1)S(1)}, bf16[2,128,256]{2,1,0:T(8,128)(2,1)S(1)}, u32[]{:S(2)}, u32[]{:S(2)}) collective-permute-start(bf16[2,128,256]{2,1,0:T(8,128)(2,1)S(1)} %get-tuple-element.25.refs_3_), channel_id=1, source_target_pairs={{0,2},{2,0},{4,6},{6,4},{8,10},{10,8},{12,14},{14,12},{1,3},{3,1},... | collective-permute-start | bytes 393224 | tf_op jit(solution)/shard_map/ppermute | solution.py:221
  31.4 0.7 %density_terms.1.before = f32[2,128]{1,0:T(2,128)S(1)} custom-call(bf16[512,512]{1,0:T(8,128)(2,1)S(1)} %get-tuple-element.19.occupied, bf16[512,512]{1,0:T(8,128)(2,1)S(1)} %collective-permute-done.other, bf16[2,512,256]{2,1,0:T(8,128)(2,1)S(1)} %get-tuple-element.20.masked, bf16[4,128,512]{2,1,0:T(8,128)(2,1)S(1)} %get-tuple-element.21.turned, ...), custom_call_target="tpu_custom_call" | custom-call | flops 268435456 | bytes 1048576 | tf_op jit(solution)/shard_map/density_terms/pallas_call | solution.py:166
  32.2 0.1 collective-permute-start.1
  32.2 0.0 collective-permute-done.3.blocks
  32.2 0.5 far_half.1
  32.7 2.3 %collective-permute-start.7 = (bf16[2,128,256]{2,1,0:T(8,128)(2,1)S(1)}, bf16[2,128,256]{2,1,0:T(8,128)(2,1)S(1)}, u32[]{:S(2)}, u32[]{:S(2)}) collective-permute-start(bf16[2,128,256]{2,1,0:T(8,128)(2,1)S(1)} %get-tuple-element.29), channel_id=1, source_target_pairs={{0,6},{2,4},{4,2},{6,0},{8,14},{10,12},{12,10},{14,8},{1,7},{3,5},... | collective-permute-start | bytes 393224 | tf_op jit(solution)/shard_map/ppermute | solution.py:221
  35.0 0.0 collective-permute-done.1.before
  35.0 0.7 %collective-permute-start.8 = (bf16[2,128,256]{2,1,0:T(8,128)(2,1)S(1)}, bf16[2,128,256]{2,1,0:T(8,128)(2,1)S(1)}, u32[]{:S(2)}, u32[]{:S(2)}) collective-permute-start(bf16[2,128,256]{2,1,0:T(8,128)(2,1)S(1)} %get-tuple-element.30), channel_id=1, source_target_pairs={{0,4},{2,6},{4,0},{6,2},{8,12},{10,14},{12,8},{14,10},{1,5},{3,7},... | collective-permute-start | bytes 393224 | tf_op jit(solution)/shard_map/ppermute | solution.py:221
  35.7 0.0 collective-permute-done.4.refs_1_
  35.7 0.5 %collective-permute-start.9 = (bf16[2,128,256]{2,1,0:T(8,128)(2,1)S(1)}, bf16[2,128,256]{2,1,0:T(8,128)(2,1)S(1)}, u32[]{:S(2)}, u32[]{:S(2)}) collective-permute-start(bf16[2,128,256]{2,1,0:T(8,128)(2,1)S(1)} %get-tuple-element.31), channel_id=1, source_target_pairs={{0,2},{2,0},{4,6},{6,4},{8,10},{10,8},{12,14},{14,12},{1,3},{3,1},... | collective-permute-start | bytes 393224 | tf_op jit(solution)/shard_map/ppermute | solution.py:221
  36.3 0.0 collective-permute-done.5.refs_2_
  36.3 0.0 collective-permute-done.6.refs_3_
  36.3 0.3 own_pairs.1
  36.6 3.4 %collective-permute-done.7.refs_1_ = bf16[2,128,256]{2,1,0:T(8,128)(2,1)S(1)} collective-permute-done((bf16[2,128,256]{2,1,0:T(8,128)(2,1)S(1)}, bf16[2,128,256]{2,1,0:T(8,128)(2,1)S(1)}, u32[]{:S(2)}, u32[]{:S(2)}) %collective-permute-start.7) | collective-permute-done | bytes 131104 | tf_op jit(solution)/shard_map/ppermute | solution.py:221
  40.0 2.5 %collective-permute-done.8.refs_2_ = bf16[2,128,256]{2,1,0:T(8,128)(2,1)S(1)} collective-permute-done((bf16[2,128,256]{2,1,0:T(8,128)(2,1)S(1)}, bf16[2,128,256]{2,1,0:T(8,128)(2,1)S(1)}, u32[]{:S(2)}, u32[]{:S(2)}) %collective-permute-start.8) | collective-permute-done | bytes 131104 | tf_op jit(solution)/shard_map/ppermute | solution.py:221
  42.4 0.0 collective-permute-done.9.refs_3_
  42.4 0.3 far_pairs.1
  42.7 0.1 collective-permute-start.11
  42.8 0.5 collective-permute-start.10
  43.3 0.6 %multiply_reduce_fusion = f32[2]{0:T(128)} fusion(f32[2,128]{1,0:T(2,128)S(1)} %collective-permute-done.1.before, f32[2,128]{1,0:T(2,128)S(1)} %density_terms.1.before), kind=kLoop, calls=%fused_computation | loop fusion | flops 4 | bytes 24 | tf_op jit(solution)/shard_map/div | solution.py:239
  43.9 0.2 far_turned.1.far
  44.1 0.2 collective-permute-done.11.refs_3_
  44.3 0.4 collective-permute-done.10.refs_1_
  44.7 6.0 %cross_terms.1 = f32[128,256,128]{2,1,0:T(8,128)} custom-call(bf16[8,256,128]{2,1,0:T(8,128)(2,1)S(1)} %get-tuple-element.28.earlier.near, bf16[8,256,128]{2,1,0:T(8,128)(2,1)S(1)} %far_turned.1.far, f32[8,128,128]{2,1,0:T(8,128)S(1)} %get-tuple-element.32.refs_0_, bf16[8,128,128]{2,1,0:T(8,128)(2,1)S(1)} %collective-permute-done.10.refs_1_, ...), custom_call_target="tpu_custom_call" | custom-call | flops 2147483648 | bytes 18874368 | tf_op jit(solution)/shard_map/cross_terms/pallas_call | solution.py:166
Async XLA Ops:
  0.6 15.1 %collective-permute-start = (bf16[512,512]{1,0:T(8,128)(2,1)}, bf16[512,512]{1,0:T(8,128)(2,1)S(1)}, u32[]{:S(2)}, u32[]{:S(2)}) collective-permute-start(bf16[512,512]{1,0:T(8,128)(2,1)} %occupied.1), channel_id=1, source_target_pairs={{0,2},{2,0},{1,3},{3,1},{4,6},{6,4},{5,7},{7,5},{8,10},{10,8},{9,1... | collective-permute-start | bytes 1572872 | tf_op jit(solution)/shard_map/ppermute | solution.py:213
  3.6 28.6 %collective-permute-start.3 = (bf16[2,512,256]{2,1,0:T(8,128)(2,1)}, bf16[2,512,256]{2,1,0:T(8,128)(2,1)S(1)}, u32[]{:S(2)}, u32[]{:S(2)}) collective-permute-start(bf16[2,512,256]{2,1,0:T(8,128)(2,1)} %blocks.1), channel_id=1, source_target_pairs={{0,8},{4,12},{8,0},{12,4},{1,9},{5,13},{9,1},{13,5},{2,10},{6,14},... | collective-permute-start | bytes 1572872 | tf_op jit(solution)/shard_map/ppermute | solution.py:205
  16.4 19.3 %collective-permute-start.4 = (bf16[2,128,256]{2,1,0:T(8,128)(2,1)S(1)}, bf16[2,128,256]{2,1,0:T(8,128)(2,1)S(1)}, u32[]{:S(2)}, u32[]{:S(2)}) collective-permute-start(bf16[2,128,256]{2,1,0:T(8,128)(2,1)S(1)} %get-tuple-element.23.refs_1_), channel_id=1, source_target_pairs={{0,6},{2,4},{4,2},{6,0},{8,14},{10,12},{12,10},{14,8},{1,7},{3,5},... | collective-permute-start | bytes 393224 | tf_op jit(solution)/shard_map/ppermute | solution.py:221
  19.2 10.3 %collective-permute-start.2 = (s32[1,2,4]{2,1,0:T(2,128)}, s32[1,2,4]{2,1,0:T(2,128)S(1)}, u32[]{:S(2)}, u32[]{:S(2)}) collective-permute-start(s32[1,2,4]{2,1,0:T(2,128)} %bitcast.2), channel_id=1, source_target_pairs={{0,8},{4,12},{8,0},{12,4},{1,9},{5,13},{9,1},{13,5},{2,10},{6,14},... | collective-permute-start | bytes 104 | tf_op jit(solution)/shard_map/ppermute | solution.py:209
  30.1 6.2 %collective-permute-start.5 = (bf16[2,128,256]{2,1,0:T(8,128)(2,1)S(1)}, bf16[2,128,256]{2,1,0:T(8,128)(2,1)S(1)}, u32[]{:S(2)}, u32[]{:S(2)}) collective-permute-start(bf16[2,128,256]{2,1,0:T(8,128)(2,1)S(1)} %get-tuple-element.24.refs_2_), channel_id=1, source_target_pairs={{0,4},{2,6},{4,0},{6,2},{8,12},{10,14},{12,8},{14,10},{1,5},{3,7},... | collective-permute-start | bytes 393224 | tf_op jit(solution)/shard_map/ppermute | solution.py:221
  30.9 5.4 %collective-permute-start.6 = (bf16[2,128,256]{2,1,0:T(8,128)(2,1)S(1)}, bf16[2,128,256]{2,1,0:T(8,128)(2,1)S(1)}, u32[]{:S(2)}, u32[]{:S(2)}) collective-permute-start(bf16[2,128,256]{2,1,0:T(8,128)(2,1)S(1)} %get-tuple-element.25.refs_3_), channel_id=1, source_target_pairs={{0,2},{2,0},{4,6},{6,4},{8,10},{10,8},{12,14},{14,12},{1,3},{3,1},... | collective-permute-start | bytes 393224 | tf_op jit(solution)/shard_map/ppermute | solution.py:221
  32.2 2.9 %collective-permute-start.1 = (f32[2,128]{1,0:T(2,128)S(1)}, f32[2,128]{1,0:T(2,128)S(1)}, u32[]{:S(2)}, u32[]{:S(2)}) collective-permute-start(f32[2,128]{1,0:T(2,128)S(1)} %density_terms.1.before), channel_id=1, source_target_pairs={{0,1},{1,0},{2,3},{3,2},{4,5},{5,4},{6,7},{7,6},{8,9},{9,8},{10,11... | collective-permute-start | bytes 3080 | tf_op jit(solution)/shard_map/ppermute | solution.py:238
  32.7 7.3 %collective-permute-start.7 = (bf16[2,128,256]{2,1,0:T(8,128)(2,1)S(1)}, bf16[2,128,256]{2,1,0:T(8,128)(2,1)S(1)}, u32[]{:S(2)}, u32[]{:S(2)}) collective-permute-start(bf16[2,128,256]{2,1,0:T(8,128)(2,1)S(1)} %get-tuple-element.29), channel_id=1, source_target_pairs={{0,6},{2,4},{4,2},{6,0},{8,14},{10,12},{12,10},{14,8},{1,7},{3,5},... | collective-permute-start | bytes 393224 | tf_op jit(solution)/shard_map/ppermute | solution.py:221
  35.0 7.4 %collective-permute-start.8 = (bf16[2,128,256]{2,1,0:T(8,128)(2,1)S(1)}, bf16[2,128,256]{2,1,0:T(8,128)(2,1)S(1)}, u32[]{:S(2)}, u32[]{:S(2)}) collective-permute-start(bf16[2,128,256]{2,1,0:T(8,128)(2,1)S(1)} %get-tuple-element.30), channel_id=1, source_target_pairs={{0,4},{2,6},{4,0},{6,2},{8,12},{10,14},{12,8},{14,10},{1,5},{3,7},... | collective-permute-start | bytes 393224 | tf_op jit(solution)/shard_map/ppermute | solution.py:221
  35.7 6.7 %collective-permute-start.9 = (bf16[2,128,256]{2,1,0:T(8,128)(2,1)S(1)}, bf16[2,128,256]{2,1,0:T(8,128)(2,1)S(1)}, u32[]{:S(2)}, u32[]{:S(2)}) collective-permute-start(bf16[2,128,256]{2,1,0:T(8,128)(2,1)S(1)} %get-tuple-element.31), channel_id=1, source_target_pairs={{0,2},{2,0},{4,6},{6,4},{8,10},{10,8},{12,14},{14,12},{1,3},{3,1},... | collective-permute-start | bytes 393224 | tf_op jit(solution)/shard_map/ppermute | solution.py:221
  42.7 1.6 %collective-permute-start.11 = (bf16[8,128,128]{2,1,0:T(8,128)(2,1)S(1)}, bf16[8,128,128]{2,1,0:T(8,128)(2,1)S(1)}, u32[]{:S(2)}, u32[]{:S(2)}) collective-permute-start(bf16[8,128,128]{2,1,0:T(8,128)(2,1)S(1)} %get-tuple-element.35), channel_id=1, source_target_pairs={{0,1},{1,0},{2,3},{3,2},{4,5},{5,4},{6,7},{7,6},{8,9},{9,8},{10,11... | collective-permute-start | bytes 786440 | tf_op jit(solution)/shard_map/ppermute | solution.py:265
  42.8 1.9 %collective-permute-start.10 = (bf16[8,128,128]{2,1,0:T(8,128)(2,1)S(1)}, bf16[8,128,128]{2,1,0:T(8,128)(2,1)S(1)}, u32[]{:S(2)}, u32[]{:S(2)}) collective-permute-start(bf16[8,128,128]{2,1,0:T(8,128)(2,1)S(1)} %get-tuple-element.33), channel_id=1, source_target_pairs={{0,1},{1,0},{2,3},{3,2},{4,5},{5,4},{6,7},{7,6},{8,9},{9,8},{10,11... | collective-permute-start | bytes 786440 | tf_op jit(solution)/shard_map/ppermute | solution.py:261

commit v12 on v10

--- a/solution.py
+++ b/solution.py
@@ -17,7 +17,7 @@
 VMEM = pl.BlockSpec(memory_space=pltpu.VMEM)
 
 
-def masked_kernel(pattern, blocks, occupied, ligand, masked, panel, part, orbitals, held, opened, sems):
+def masked_kernel(pattern, blocks, occupied, ligand, masked, again, panel, part, orbitals, held, opened, sems):
     aux_rows, _, nu_width = blocks.shape
     own = own_half_of(part.shape[0])
     moves = ((blocks, held), (pattern, opened), (occupied.at[own], part), (occupied, panel), (ligand.at[own], orbitals))
@@ -31,13 +31,19 @@
             for n in range(nu_width // BLK):
                 rows, columns = pl.ds(m * BLK, BLK), pl.ds(n * BLK, BLK)
                 tile = held[q, rows, columns]
-                masked[q, rows, columns] = jnp.where(opened[0, n, m] != 0, tile, jnp.zeros_like(tile))
+                tile = jnp.where(opened[0, n, m] != 0, tile, jnp.zeros_like(tile))
+                masked[q, rows, columns] = tile
+                again[q, rows, columns] = tile
     for copy in copies[2:]:
         copy.wait()
 
 
 def own_half_of(length):
     return pl.ds(pl.multiple_of(lax.axis_index("ao") * length, length), length)
+
+
+def after_kernel(block, before, out):
+    pass
 
 
 def half_into(outs, turned, masked):
@@ -100,8 +106,11 @@
         out[q : q + 1, :] = jnp.full((1, out.shape[1]), totals[q], jnp.float32)
 
 
-def far_kernel(before, masked, turned, *outs):
-    half_into(outs, turned, masked)
+def far_kernel(before, inward, outward, turned, *outs):
+    aux = lax.axis_index("aux")
+    inner = jnp.logical_or(aux == 1, aux == 2)
+    pl.when(inner)(functools.partial(half_into, outs, turned, inward))
+    pl.when(jnp.logical_not(inner))(functools.partial(half_into, outs, turned, outward))
 
 
 def pair_kernel(before, earlier, ligand, *refs):
@@ -154,7 +163,7 @@
     pltpu.make_async_copy(held, out, sem).wait()
 
 
-def call(kernel, name, inputs, outputs, scratch=(), limit=16, flops=0, moved=1 << 20, in_spec=VMEM, out_spec=VMEM):
+def call(kernel, name, inputs, outputs, scratch=(), limit=16, flops=0, moved=1 << 20, in_spec=VMEM, out_spec=VMEM, aliases=None):
     inputs = list(inputs)
     results = pl.pallas_call(
         kernel,
@@ -164,6 +173,7 @@
         scratch_shapes=list(scratch),
         compiler_params=pltpu.CompilerParams(vmem_limit_bytes=limit * MIB),
         cost_estimate=pl.CostEstimate(flops=flops, bytes_accessed=moved, transcendentals=0),
+        input_output_aliases=aliases or {},
         name=name,
     )(*inputs)
     return list(results)
@@ -180,14 +190,14 @@
     bf16 = functools.partial(jax.ShapeDtypeStruct, dtype=jnp.bfloat16)
     f32 = functools.partial(jax.ShapeDtypeStruct, dtype=jnp.float32)
 
-    across = [(a, a ^ 2) for a in range(n_aux)]
     swap = [(c, 1 - c) for c in range(n_ao)]
     pattern = jnp.swapaxes(pattern, 1, 2)
-    masked, panel, part, orbitals = call(
+    masked, again, panel, part, orbitals = call(
         masked_kernel,
         "masked_blocks",
         (pltpu.with_memory_space_constraint(x, pltpu.HBM) for x in (pattern, blocks, occupied, ligand)),
-        [bf16(blocks.shape), bf16(occupied.shape), bf16((NB // n_ao, panel_width)), bf16((NB // n_ao, width))],
+        [bf16(blocks.shape)] * 2
+        + [bf16(occupied.shape), bf16((NB // n_ao, panel_width)), bf16((NB // n_ao, width))],
         [
             pltpu.VMEM(blocks.shape, jnp.bfloat16),
             pltpu.SMEM(pattern.shape, pattern.dtype),
@@ -195,7 +205,18 @@
         ],
         in_spec=pl.BlockSpec(memory_space=pltpu.HBM),
     )
-    far_masked = lax.ppermute(masked, "aux", across)
+    inward = lax.ppermute(masked, "aux", [(0, 2), (3, 1)])
+    anywhere = pl.BlockSpec(memory_space=pl.ANY)
+    follower = call(
+        after_kernel,
+        "inner_blocks",
+        (again, inward),
+        [bf16(blocks.shape)],
+        in_spec=anywhere,
+        out_spec=anywhere,
+        aliases={0: 0},
+    )[0]
+    outward = lax.ppermute(follower, "aux", [(1, 3), (2, 0)])
     mine = lax.ppermute(part, "orb", swap)
     theirs = lax.ppermute(mine, "ao", swap)
 
@@ -224,7 +245,7 @@
     )[0]
     value_there = lax.ppermute(value, "ao", swap)
     density = (value[:, 0] + value_there[:, 0]) / math.sqrt(NOCC)
-    far = call(far_kernel, "far_half", (value, far_masked, turned), messages, flops=work)
+    far = call(far_kernel, "far_half", (value, inward, outward, turned), messages, flops=work)
     far_here = square(far)
 
     shape = (4 * aux_rows, ni, width)

time: 47.6 us -> 54.9 us (1.15)
  waiting for transfers between devices: 22.7 us -> 26.4 us
  starting transfers between devices: 13.3 us -> 16.9 us
    ppermute x1 -> x2, starting transfers between devices: 2.59 us -> 7.25 us  [the longest x1 5.97 us: body(): inward = lax.ppermute(masked, 'aux', [(0, 2), (3, 1)])]
    ppermute x1 -> x2, waiting for transfers between devices: 12.8 us -> 16.7 us  [the longest x1 9.52 us: body(): inward = lax.ppermute(masked, 'aux', [(0, 2), (3, 1)])]
    ppermute x1, waiting for transfers between devices: 3.66 us -> 0.01 us  [body(): mine = lax.ppermute(part, 'orb', swap)]
    ppermute x6, waiting for transfers between devices: 4.2 us -> 7.49 us  [square(): arrived.append(lax.ppermute(message, ('aux', 'orb'), moves))]
    ppermute x1, starting transfers between devices: 3 us -> 1.56 us  [body(): mine = lax.ppermute(part, 'orb', swap)]
    ppermute x6, starting transfers between devices: 7.11 us -> 7.76 us  [square(): arrived.append(lax.ppermute(message, ('aux', 'orb'), moves))]
    pallas_call x8 -> x9, Pallas kernels: 10 us -> 10 us  [call(): pl.pallas_call(kernel, in_specs=[in_spec] * len(inputs), out_specs=[out_s...]
  transfers between devices with their start and end apart: 12 -> 13, of which waited for: 8 -> 9; matrix products, arithmetic and copies ran while one was open for 1% -> 1% of each run, Pallas kernels for 5% -> 5%
where the time goes in v12:
time: 54.9 us; the launch traced here: 54.7 us
  waiting for transfers between devices  26.4 us (48%)
  starting transfers between devices  16.9 us (31%)
  Pallas kernels  10 us (18%)
  between operations  0.77 us (1%)
  other arithmetic  0.63 us (1%)
    pallas_call x9, Pallas kernels, call(): pl.pallas_call(kernel, in_specs=[in_spec] * len(inputs), out_specs=[out_s...  10 us
    ppermute x1, waiting for transfers between devices, body(): inward = lax.ppermute(masked, 'aux', [(0, 2), (3, 1)])  9.52 us
    ppermute x6, starting transfers between devices, square(): arrived.append(lax.ppermute(message, ('aux', 'orb'), moves))  7.76 us
    ppermute x6, waiting for transfers between devices, square(): arrived.append(lax.ppermute(message, ('aux', 'orb'), moves))  7.49 us
    ppermute x1, waiting for transfers between devices, body(): outward = lax.ppermute(follower, 'aux', [(1, 3), (2, 0)])  7.18 us
    ppermute x1, starting transfers between devices, body(): inward = lax.ppermute(masked, 'aux', [(0, 2), (3, 1)])  5.97 us
    ppermute x1, starting transfers between devices, body(): mine = lax.ppermute(part, 'orb', swap)  1.56 us
    ppermute x1, waiting for transfers between devices, body(): theirs = lax.ppermute(mine, 'ao', swap)  1.52 us
  transfers between devices with their start and end apart: 13, of which 9 were waited for; matrix products, arithmetic and copies ran while one was open for 1% of the time, Pallas kernels for 5%

profile of v12, /device:TPU:0, one launch (start us, length us, event | category | flops | bytes accessed | tf_op | source)
XLA Modules:
  0.0 54.7 jit_solution(3689593268507271442)
XLA Ops:
  0.6 1.4 %masked_blocks.1 = (bf16[2,512,256]{2,1,0:T(8,128)(2,1)S(1)}, bf16[2,512,256]{2,1,0:T(8,128)(2,1)S(1)}, bf16[512,512]{1,0:T(8,128)(2,1)S(1)}, bf16[256,512]{1,0:T(8,128)(2,1)S(1)}, bf16[256,128]{1,0:T(8,128)(2,1)S(1)}) custom-call(s32[1,2,4]{2,1,0:T(2,128)} %bitcast.1, bf16[2,512,256]{2,1,0:T(8,128)(2,1)} %blocks.1, bf16[512,512]{1,0:T(8,128)(2,1)} %occupied.1, ...), custom_call_target="tpu_custom_call" | custom-call | bytes 1048576 | tf_op jit(solution)/shard_map/masked_blocks/pallas_call | solution.py:168
  2.0 6.0 %collective-permute-start.3 = (bf16[2,512,256]{2,1,0:T(8,128)(2,1)S(1)}, bf16[2,512,256]{2,1,0:T(8,128)(2,1)S(1)}, u32[]{:S(2)}, u32[]{:S(2)}) collective-permute-start(bf16[2,512,256]{2,1,0:T(8,128)(2,1)S(1)} %get-tuple-element.23.masked), channel_id=1, source_target_pairs={{0,8},{12,4},{1,9},{13,5},{2,10},{14,6},{3,11},{15,7},{16,24},{28,... | collective-permute-start | bytes 1572872 | tf_op jit(solution)/shard_map/ppermute | solution.py:208
  8.0 1.6 %collective-permute-start = (bf16[256,512]{1,0:T(8,128)(2,1)S(1)}, bf16[256,512]{1,0:T(8,128)(2,1)S(1)}, u32[]{:S(2)}, u32[]{:S(2)}) collective-permute-start(bf16[256,512]{1,0:T(8,128)(2,1)S(1)} %get-tuple-element.22), channel_id=1, source_target_pairs={{0,2},{2,0},{1,3},{3,1},{4,6},{6,4},{5,7},{7,5},{8,10},{10,8},{9,1... | collective-permute-start | bytes 786440 | tf_op jit(solution)/shard_map/ppermute | solution.py:220
  9.6 9.5 %collective-permute-done.3.before.inward = bf16[2,512,256]{2,1,0:T(8,128)(2,1)S(1)} collective-permute-done((bf16[2,512,256]{2,1,0:T(8,128)(2,1)S(1)}, bf16[2,512,256]{2,1,0:T(8,128)(2,1)S(1)}, u32[]{:S(2)}, u32[]{:S(2)}) %collective-permute-start.3) | collective-permute-done | bytes 524320 | tf_op jit(solution)/shard_map/ppermute | solution.py:208
  19.1 1.3 %collective-permute-start.4 = (bf16[2,512,256]{2,1,0:T(8,128)(2,1)S(1)}, bf16[2,512,256]{2,1,0:T(8,128)(2,1)S(1)}, u32[]{:S(2)}, u32[]{:S(2)}) collective-permute-start(bf16[2,512,256]{2,1,0:T(8,128)(2,1)S(1)} %inner_blocks.1), channel_id=1, source_target_pairs={{4,12},{8,0},{5,13},{9,1},{6,14},{10,2},{7,15},{11,3},{20,28},{24,... | collective-permute-start | bytes 1572872 | tf_op jit(solution)/shard_map/ppermute | solution.py:219
  20.4 0.0 collective-permute-done.mine
  20.4 0.1 collective-permute-start.1
  20.5 1.5 %collective-permute-done.1.theirs = bf16[256,512]{1,0:T(8,128)(2,1)S(1)} collective-permute-done((bf16[256,512]{1,0:T(8,128)(2,1)S(1)}, bf16[256,512]{1,0:T(8,128)(2,1)S(1)}, u32[]{:S(2)}, u32[]{:S(2)}) %collective-permute-start.1) | collective-permute-done | bytes 262176 | tf_op jit(solution)/shard_map/ppermute | solution.py:221
  22.0 0.6 %own_half.1 = (bf16[4,128,512]{2,1,0:T(8,128)(2,1)S(1)}, bf16[2,128,256]{2,1,0:T(8,128)(2,1)S(1)}, bf16[2,128,256]{2,1,0:T(8,128)(2,1)S(1)}, bf16[2,128,256]{2,1,0:T(8,128)(2,1)S(1)}, bf16[2,128,256]{2,1,0:T(8,128)(2,1)S(1)}) custom-call(bf16[512,512]{1,0:T(8,128)(2,1)S(1)} %get-tuple-element.21.occupied, bf16[256,512]{1,0:T(8,128)(2,1)S(1)} %collective-permute-done.mine, ...), custom_call_target="tpu_custom_call" | custom-call | flops 268435456 | bytes 1048576 | tf_op jit(solution)/shard_map/own_half/pallas_call | solution.py:168
  22.6 3.5 %collective-permute-start.5 = (bf16[2,128,256]{2,1,0:T(8,128)(2,1)S(1)}, bf16[2,128,256]{2,1,0:T(8,128)(2,1)S(1)}, u32[]{:S(2)}, u32[]{:S(2)}) collective-permute-start(bf16[2,128,256]{2,1,0:T(8,128)(2,1)S(1)} %get-tuple-element.26.refs_1_), channel_id=1, source_target_pairs={{0,6},{2,4},{4,2},{6,0},{8,14},{10,12},{12,10},{14,8},{1,7},{3,5},... | collective-permute-start | bytes 393224 | tf_op jit(solution)/shard_map/ppermute | solution.py:229
  26.2 0.0 collective-permute-start.6
  26.2 0.6 %collective-permute-start.7 = (bf16[2,128,256]{2,1,0:T(8,128)(2,1)S(1)}, bf16[2,128,256]{2,1,0:T(8,128)(2,1)S(1)}, u32[]{:S(2)}, u32[]{:S(2)}) collective-permute-start(bf16[2,128,256]{2,1,0:T(8,128)(2,1)S(1)} %get-tuple-element.28.refs_3_), channel_id=1, source_target_pairs={{0,2},{2,0},{4,6},{6,4},{8,10},{10,8},{12,14},{14,12},{1,3},{3,1},... | collective-permute-start | bytes 393224 | tf_op jit(solution)/shard_map/ppermute | solution.py:229
  26.8 0.7 %density_terms.1.before = f32[2,128]{1,0:T(2,128)S(1)} custom-call(bf16[512,512]{1,0:T(8,128)(2,1)S(1)} %get-tuple-element.21.occupied, bf16[256,512]{1,0:T(8,128)(2,1)S(1)} %collective-permute-done.mine, bf16[256,512]{1,0:T(8,128)(2,1)S(1)} %collective-permute-done.1.theirs, bf16[2,512,256]{2,1,0:T(8,128)(2,1)S(1)} %get-tuple-element.23.masked, ...), custom_call_target="tpu_custom_call" | custom-call | flops 268435456 | bytes 1048576 | tf_op jit(solution)/shard_map/density_terms/pallas_call | solution.py:168
  27.6 0.1 collective-permute-start.2
  27.7 7.2 %collective-permute-done.4.outward = bf16[2,512,256]{2,1,0:T(8,128)(2,1)S(1)} collective-permute-done((bf16[2,512,256]{2,1,0:T(8,128)(2,1)S(1)}, bf16[2,512,256]{2,1,0:T(8,128)(2,1)S(1)}, u32[]{:S(2)}, u32[]{:S(2)}) %collective-permute-start.4) | collective-permute-done | bytes 524320 | tf_op jit(solution)/shard_map/ppermute | solution.py:219
  34.8 0.4 far_half.1
  35.3 0.1 collective-permute-start.8
  35.4 0.0 collective-permute-done.2.before
  35.4 2.9 %collective-permute-start.9 = (bf16[2,128,256]{2,1,0:T(8,128)(2,1)S(1)}, bf16[2,128,256]{2,1,0:T(8,128)(2,1)S(1)}, u32[]{:S(2)}, u32[]{:S(2)}) collective-permute-start(bf16[2,128,256]{2,1,0:T(8,128)(2,1)S(1)} %get-tuple-element.34), channel_id=1, source_target_pairs={{0,4},{2,6},{4,0},{6,2},{8,12},{10,14},{12,8},{14,10},{1,5},{3,7},... | collective-permute-start | bytes 393224 | tf_op jit(solution)/shard_map/ppermute | solution.py:229
  38.3 0.2 collective-permute-done.5.refs_1_
  38.5 0.6 %collective-permute-start.10 = (bf16[2,128,256]{2,1,0:T(8,128)(2,1)S(1)}, bf16[2,128,256]{2,1,0:T(8,128)(2,1)S(1)}, u32[]{:S(2)}, u32[]{:S(2)}) collective-permute-start(bf16[2,128,256]{2,1,0:T(8,128)(2,1)S(1)} %get-tuple-element.35), channel_id=1, source_target_pairs={{0,2},{2,0},{4,6},{6,4},{8,10},{10,8},{12,14},{14,12},{1,3},{3,1},... | collective-permute-start | bytes 393224 | tf_op jit(solution)/shard_map/ppermute | solution.py:229
  39.1 1.3 %collective-permute-done.6.refs_2_ = bf16[2,128,256]{2,1,0:T(8,128)(2,1)S(1)} collective-permute-done((bf16[2,128,256]{2,1,0:T(8,128)(2,1)S(1)}, bf16[2,128,256]{2,1,0:T(8,128)(2,1)S(1)}, u32[]{:S(2)}, u32[]{:S(2)}) %collective-permute-start.6) | collective-permute-done | bytes 131104 | tf_op jit(solution)/shard_map/ppermute | solution.py:229
  40.4 0.0 collective-permute-done.7.refs_3_
  40.4 0.3 own_pairs.1
  40.7 0.1 collective-permute-start.11
  40.8 3.4 %collective-permute-done.8.refs_1_ = bf16[2,128,256]{2,1,0:T(8,128)(2,1)S(1)} collective-permute-done((bf16[2,128,256]{2,1,0:T(8,128)(2,1)S(1)}, bf16[2,128,256]{2,1,0:T(8,128)(2,1)S(1)}, u32[]{:S(2)}, u32[]{:S(2)}) %collective-permute-start.8) | collective-permute-done | bytes 131104 | tf_op jit(solution)/shard_map/ppermute | solution.py:229
  44.2 1.8 %collective-permute-done.9.refs_2_ = bf16[2,128,256]{2,1,0:T(8,128)(2,1)S(1)} collective-permute-done((bf16[2,128,256]{2,1,0:T(8,128)(2,1)S(1)}, bf16[2,128,256]{2,1,0:T(8,128)(2,1)S(1)}, u32[]{:S(2)}, u32[]{:S(2)}) %collective-permute-start.9) | collective-permute-done | bytes 131104 | tf_op jit(solution)/shard_map/ppermute | solution.py:229
  46.0 0.7 %collective-permute-done.10.refs_3_ = bf16[2,128,256]{2,1,0:T(8,128)(2,1)S(1)} collective-permute-done((bf16[2,128,256]{2,1,0:T(8,128)(2,1)S(1)}, bf16[2,128,256]{2,1,0:T(8,128)(2,1)S(1)}, u32[]{:S(2)}, u32[]{:S(2)}) %collective-permute-start.10) | collective-permute-done | bytes 131104 | tf_op jit(solution)/shard_map/ppermute | solution.py:229
  46.7 0.3 far_pairs.1
  47.0 0.1 collective-permute-start.12
  47.1 0.6 %multiply_reduce_fusion = f32[2]{0:T(128)} fusion(f32[2,128]{1,0:T(2,128)S(1)} %collective-permute-done.2.before, f32[2,128]{1,0:T(2,128)S(1)} %density_terms.1.before), kind=kLoop, calls=%fused_computation | loop fusion | flops 4 | bytes 24 | tf_op jit(solution)/shard_map/div | solution.py:247
  47.7 0.2 far_turned.1.far
  47.9 0.0 collective-permute-done.11.refs_1_
  47.9 0.7 %collective-permute-done.12.refs_3_ = bf16[8,128,128]{2,1,0:T(8,128)(2,1)S(1)} collective-permute-done((bf16[8,128,128]{2,1,0:T(8,128)(2,1)S(1)}, bf16[8,128,128]{2,1,0:T(8,128)(2,1)S(1)}, u32[]{:S(2)}, u32[]{:S(2)}) %collective-permute-start.12) | collective-permute-done | bytes 262176 | tf_op jit(solution)/shard_map/ppermute | solution.py:266
  48.6 6.0 %cross_terms.1 = f32[128,256,128]{2,1,0:T(8,128)} custom-call(bf16[8,256,128]{2,1,0:T(8,128)(2,1)S(1)} %get-tuple-element.32.earlier.near, bf16[8,256,128]{2,1,0:T(8,128)(2,1)S(1)} %far_turned.1.far, f32[8,128,128]{2,1,0:T(8,128)S(1)} %get-tuple-element.36.refs_0_, bf16[8,128,128]{2,1,0:T(8,128)(2,1)S(1)} %collective-permute-done.11.refs_1_, ...), custom_call_target="tpu_custom_call" | custom-call | flops 2147483648 | bytes 18874368 | tf_op jit(solution)/shard_map/cross_terms/pallas_call | solution.py:168
  (1 shorter events, 0.0 us)
Async XLA Ops:
  2.0 17.1 %collective-permute-start.3 = (bf16[2,512,256]{2,1,0:T(8,128)(2,1)S(1)}, bf16[2,512,256]{2,1,0:T(8,128)(2,1)S(1)}, u32[]{:S(2)}, u32[]{:S(2)}) collective-permute-start(bf16[2,512,256]{2,1,0:T(8,128)(2,1)S(1)} %get-tuple-element.23.masked), channel_id=1, source_target_pairs={{0,8},{12,4},{1,9},{13,5},{2,10},{14,6},{3,11},{15,7},{16,24},{28,... | collective-permute-start | bytes 1572872 | tf_op jit(solution)/shard_map/ppermute | solution.py:208
  8.0 12.4 %collective-permute-start = (bf16[256,512]{1,0:T(8,128)(2,1)S(1)}, bf16[256,512]{1,0:T(8,128)(2,1)S(1)}, u32[]{:S(2)}, u32[]{:S(2)}) collective-permute-start(bf16[256,512]{1,0:T(8,128)(2,1)S(1)} %get-tuple-element.22), channel_id=1, source_target_pairs={{0,2},{2,0},{1,3},{3,1},{4,6},{6,4},{5,7},{7,5},{8,10},{10,8},{9,1... | collective-permute-start | bytes 786440 | tf_op jit(solution)/shard_map/ppermute | solution.py:220
  19.1 15.7 %collective-permute-start.4 = (bf16[2,512,256]{2,1,0:T(8,128)(2,1)S(1)}, bf16[2,512,256]{2,1,0:T(8,128)(2,1)S(1)}, u32[]{:S(2)}, u32[]{:S(2)}) collective-permute-start(bf16[2,512,256]{2,1,0:T(8,128)(2,1)S(1)} %inner_blocks.1), channel_id=1, source_target_pairs={{4,12},{8,0},{5,13},{9,1},{6,14},{10,2},{7,15},{11,3},{20,28},{24,... | collective-permute-start | bytes 1572872 | tf_op jit(solution)/shard_map/ppermute | solution.py:219
  20.4 1.6 %collective-permute-start.1 = (bf16[256,512]{1,0:T(8,128)(2,1)S(1)}, bf16[256,512]{1,0:T(8,128)(2,1)S(1)}, u32[]{:S(2)}, u32[]{:S(2)}) collective-permute-start(bf16[256,512]{1,0:T(8,128)(2,1)S(1)} %collective-permute-done.mine), channel_id=1, source_target_pairs={{0,1},{1,0},{2,3},{3,2},{4,5},{5,4},{6,7},{7,6},{8,9},{9,8},{10,11... | collective-permute-start | bytes 786440 | tf_op jit(solution)/shard_map/ppermute | solution.py:221
  22.6 15.9 %collective-permute-start.5 = (bf16[2,128,256]{2,1,0:T(8,128)(2,1)S(1)}, bf16[2,128,256]{2,1,0:T(8,128)(2,1)S(1)}, u32[]{:S(2)}, u32[]{:S(2)}) collective-permute-start(bf16[2,128,256]{2,1,0:T(8,128)(2,1)S(1)} %get-tuple-element.26.refs_1_), channel_id=1, source_target_pairs={{0,6},{2,4},{4,2},{6,0},{8,14},{10,12},{12,10},{14,8},{1,7},{3,5},... | collective-permute-start | bytes 393224 | tf_op jit(solution)/shard_map/ppermute | solution.py:229
  26.2 14.2 %collective-permute-start.6 = (bf16[2,128,256]{2,1,0:T(8,128)(2,1)S(1)}, bf16[2,128,256]{2,1,0:T(8,128)(2,1)S(1)}, u32[]{:S(2)}, u32[]{:S(2)}) collective-permute-start(bf16[2,128,256]{2,1,0:T(8,128)(2,1)S(1)} %get-tuple-element.27.refs_2_), channel_id=1, source_target_pairs={{0,4},{2,6},{4,0},{6,2},{8,12},{10,14},{12,8},{14,10},{1,5},{3,7},... | collective-permute-start | bytes 393224 | tf_op jit(solution)/shard_map/ppermute | solution.py:229
  26.2 14.2 %collective-permute-start.7 = (bf16[2,128,256]{2,1,0:T(8,128)(2,1)S(1)}, bf16[2,128,256]{2,1,0:T(8,128)(2,1)S(1)}, u32[]{:S(2)}, u32[]{:S(2)}) collective-permute-start(bf16[2,128,256]{2,1,0:T(8,128)(2,1)S(1)} %get-tuple-element.28.refs_3_), channel_id=1, source_target_pairs={{0,2},{2,0},{4,6},{6,4},{8,10},{10,8},{12,14},{14,12},{1,3},{3,1},... | collective-permute-start | bytes 393224 | tf_op jit(solution)/shard_map/ppermute | solution.py:229
  27.6 7.8 %collective-permute-start.2 = (f32[2,128]{1,0:T(2,128)S(1)}, f32[2,128]{1,0:T(2,128)S(1)}, u32[]{:S(2)}, u32[]{:S(2)}) collective-permute-start(f32[2,128]{1,0:T(2,128)S(1)} %density_terms.1.before), channel_id=1, source_target_pairs={{0,1},{1,0},{2,3},{3,2},{4,5},{5,4},{6,7},{7,6},{8,9},{9,8},{10,11... | collective-permute-start | bytes 3080 | tf_op jit(solution)/shard_map/ppermute | solution.py:246
  35.3 8.9 %collective-permute-start.8 = (bf16[2,128,256]{2,1,0:T(8,128)(2,1)S(1)}, bf16[2,128,256]{2,1,0:T(8,128)(2,1)S(1)}, u32[]{:S(2)}, u32[]{:S(2)}) collective-permute-start(bf16[2,128,256]{2,1,0:T(8,128)(2,1)S(1)} %get-tuple-element.33), channel_id=1, source_target_pairs={{0,6},{2,4},{4,2},{6,0},{8,14},{10,12},{12,10},{14,8},{1,7},{3,5},... | collective-permute-start | bytes 393224 | tf_op jit(solution)/shard_map/ppermute | solution.py:229
  35.4 10.6 %collective-permute-start.9 = (bf16[2,128,256]{2,1,0:T(8,128)(2,1)S(1)}, bf16[2,128,256]{2,1,0:T(8,128)(2,1)S(1)}, u32[]{:S(2)}, u32[]{:S(2)}) collective-permute-start(bf16[2,128,256]{2,1,0:T(8,128)(2,1)S(1)} %get-tuple-element.34), channel_id=1, source_target_pairs={{0,4},{2,6},{4,0},{6,2},{8,12},{10,14},{12,8},{14,10},{1,5},{3,7},... | collective-permute-start | bytes 393224 | tf_op jit(solution)/shard_map/ppermute | solution.py:229
  38.5 8.2 %collective-permute-start.10 = (bf16[2,128,256]{2,1,0:T(8,128)(2,1)S(1)}, bf16[2,128,256]{2,1,0:T(8,128)(2,1)S(1)}, u32[]{:S(2)}, u32[]{:S(2)}) collective-permute-start(bf16[2,128,256]{2,1,0:T(8,128)(2,1)S(1)} %get-tuple-element.35), channel_id=1, source_target_pairs={{0,2},{2,0},{4,6},{6,4},{8,10},{10,8},{12,14},{14,12},{1,3},{3,1},... | collective-permute-start | bytes 393224 | tf_op jit(solution)/shard_map/ppermute | solution.py:229
  40.7 7.2 %collective-permute-start.11 = (bf16[8,128,128]{2,1,0:T(8,128)(2,1)S(1)}, bf16[8,128,128]{2,1,0:T(8,128)(2,1)S(1)}, u32[]{:S(2)}, u32[]{:S(2)}) collective-permute-start(bf16[8,128,128]{2,1,0:T(8,128)(2,1)S(1)} %get-tuple-element.37), channel_id=1, source_target_pairs={{0,1},{1,0},{2,3},{3,2},{4,5},{5,4},{6,7},{7,6},{8,9},{9,8},{10,11... | collective-permute-start | bytes 786440 | tf_op jit(solution)/shard_map/ppermute | solution.py:262
  47.0 1.6 %collective-permute-start.12 = (bf16[8,128,128]{2,1,0:T(8,128)(2,1)S(1)}, bf16[8,128,128]{2,1,0:T(8,128)(2,1)S(1)}, u32[]{:S(2)}, u32[]{:S(2)}) collective-permute-start(bf16[8,128,128]{2,1,0:T(8,128)(2,1)S(1)} %get-tuple-element.39), channel_id=1, source_target_pairs={{0,1},{1,0},{2,3},{3,2},{4,5},{5,4},{6,7},{7,6},{8,9},{9,8},{10,11... | collective-permute-start | bytes 786440 | tf_op jit(solution)/shard_map/ppermute | solution.py:266

commit v13 on v10

--- a/solution.py
+++ b/solution.py
@@ -150,7 +150,7 @@
                 pltpu.make_async_copy(held.at[done], out.at[done], sem).start()
         return carry
 
-    lax.fori_loop(0, ni // GROUP, step, 0)
+    lax.fori_loop(0, ni // GROUP, step, 0, unroll=4)
     pltpu.make_async_copy(held, out, sem).wait()
 
 

time: 47.6 us -> 47.6 us (level)
  no operation moved by 1% of the time
where the time goes in v13:
time: 47.6 us; the launch traced here: 47.4 us
  waiting for transfers between devices  22.7 us (48%)
  starting transfers between devices  13.3 us (28%)
  Pallas kernels  10 us (21%)
  between operations  0.71 us (1%)
  other arithmetic  0.63 us (1%)
    ppermute x1, waiting for transfers between devices, body(): far_masked = lax.ppermute(masked, 'aux', across)  12.8 us
    pallas_call x8, Pallas kernels, call(): pl.pallas_call(kernel, in_specs=[in_spec] * len(inputs), out_specs=[out_s...  10 us
    ppermute x6, starting transfers between devices, square(): arrived.append(lax.ppermute(message, ('aux', 'orb'), moves))  7.11 us
    ppermute x6, waiting for transfers between devices, square(): arrived.append(lax.ppermute(message, ('aux', 'orb'), moves))  4.2 us
    ppermute x1, waiting for transfers between devices, body(): mine = lax.ppermute(part, 'orb', swap)  3.66 us
    ppermute x1, starting transfers between devices, body(): mine = lax.ppermute(part, 'orb', swap)  3 us
    ppermute x1, starting transfers between devices, body(): far_masked = lax.ppermute(masked, 'aux', across)  2.59 us
    ppermute x1, waiting for transfers between devices, body(): theirs = lax.ppermute(mine, 'ao', swap)  1.53 us
  transfers between devices with their start and end apart: 12, of which 8 were waited for; matrix products, arithmetic and copies ran while one was open for 1% of the time, Pallas kernels for 5%

profile of v13, /device:TPU:0, one launch (start us, length us, event | category | flops | bytes accessed | tf_op | source)
XLA Modules:
  0.0 47.4 jit_solution(6705563387939963880)
XLA Ops:
  0.6 1.4 %masked_blocks.1 = (bf16[2,512,256]{2,1,0:T(8,128)(2,1)S(1)}, bf16[512,512]{1,0:T(8,128)(2,1)S(1)}, bf16[256,512]{1,0:T(8,128)(2,1)S(1)}, bf16[256,128]{1,0:T(8,128)(2,1)S(1)}) custom-call(s32[1,2,4]{2,1,0:T(2,128)} %bitcast.1, bf16[2,512,256]{2,1,0:T(8,128)(2,1)} %blocks.1, bf16[512,512]{1,0:T(8,128)(2,1)} %occupied.1, bf16[512,128]{1,0:T(8,128)(2,1)} %ligand.1), custom_call_target="tpu_custom_call" | custom-call | bytes 1048576 | tf_op jit(solution)/shard_map/masked_blocks/pallas_call | solution.py:159
  2.0 3.0 %collective-permute-start = (bf16[256,512]{1,0:T(8,128)(2,1)S(1)}, bf16[256,512]{1,0:T(8,128)(2,1)S(1)}, u32[]{:S(2)}, u32[]{:S(2)}) collective-permute-start(bf16[256,512]{1,0:T(8,128)(2,1)S(1)} %get-tuple-element.21), channel_id=1, source_target_pairs={{0,2},{2,0},{1,3},{3,1},{4,6},{6,4},{5,7},{7,5},{8,10},{10,8},{9,1... | collective-permute-start | bytes 786440 | tf_op jit(solution)/shard_map/ppermute | solution.py:199
  5.0 2.6 %collective-permute-start.3 = (bf16[2,512,256]{2,1,0:T(8,128)(2,1)S(1)}, bf16[2,512,256]{2,1,0:T(8,128)(2,1)S(1)}, u32[]{:S(2)}, u32[]{:S(2)}) collective-permute-start(bf16[2,512,256]{2,1,0:T(8,128)(2,1)S(1)} %get-tuple-element.22.masked), channel_id=1, source_target_pairs={{0,8},{4,12},{8,0},{12,4},{1,9},{5,13},{9,1},{13,5},{2,10},{6,14},... | collective-permute-start | bytes 1572872 | tf_op jit(solution)/shard_map/ppermute | solution.py:198
  7.6 3.7 %collective-permute-done.mine = bf16[256,512]{1,0:T(8,128)(2,1)S(1)} collective-permute-done((bf16[256,512]{1,0:T(8,128)(2,1)S(1)}, bf16[256,512]{1,0:T(8,128)(2,1)S(1)}, u32[]{:S(2)}, u32[]{:S(2)}) %collective-permute-start) | collective-permute-done | bytes 262176 | tf_op jit(solution)/shard_map/ppermute | solution.py:199
  11.3 0.0 collective-permute-start.1
  11.3 1.5 %collective-permute-done.1.theirs = bf16[256,512]{1,0:T(8,128)(2,1)S(1)} collective-permute-done((bf16[256,512]{1,0:T(8,128)(2,1)S(1)}, bf16[256,512]{1,0:T(8,128)(2,1)S(1)}, u32[]{:S(2)}, u32[]{:S(2)}) %collective-permute-start.1) | collective-permute-done | bytes 262176 | tf_op jit(solution)/shard_map/ppermute | solution.py:200
  12.8 0.6 %own_half.1 = (bf16[4,128,512]{2,1,0:T(8,128)(2,1)S(1)}, bf16[2,128,256]{2,1,0:T(8,128)(2,1)S(1)}, bf16[2,128,256]{2,1,0:T(8,128)(2,1)S(1)}, bf16[2,128,256]{2,1,0:T(8,128)(2,1)S(1)}, bf16[2,128,256]{2,1,0:T(8,128)(2,1)S(1)}) custom-call(bf16[512,512]{1,0:T(8,128)(2,1)S(1)} %get-tuple-element.20.occupied, bf16[256,512]{1,0:T(8,128)(2,1)S(1)} %collective-permute-done.mine, ...), custom_call_target="tpu_custom_call" | custom-call | flops 268435456 | bytes 1048576 | tf_op jit(solution)/shard_map/own_half/pallas_call | solution.py:159
  13.5 2.8 %collective-permute-start.4 = (bf16[2,128,256]{2,1,0:T(8,128)(2,1)S(1)}, bf16[2,128,256]{2,1,0:T(8,128)(2,1)S(1)}, u32[]{:S(2)}, u32[]{:S(2)}) collective-permute-start(bf16[2,128,256]{2,1,0:T(8,128)(2,1)S(1)} %get-tuple-element.25.refs_1_), channel_id=1, source_target_pairs={{0,6},{2,4},{4,2},{6,0},{8,14},{10,12},{12,10},{14,8},{1,7},{3,5},... | collective-permute-start | bytes 393224 | tf_op jit(solution)/shard_map/ppermute | solution.py:208
  16.3 0.4 collective-permute-start.5
  16.7 0.3 collective-permute-start.6
  17.0 0.7 %density_terms.1.before = f32[2,128]{1,0:T(2,128)S(1)} custom-call(bf16[512,512]{1,0:T(8,128)(2,1)S(1)} %get-tuple-element.20.occupied, bf16[256,512]{1,0:T(8,128)(2,1)S(1)} %collective-permute-done.mine, bf16[256,512]{1,0:T(8,128)(2,1)S(1)} %collective-permute-done.1.theirs, bf16[2,512,256]{2,1,0:T(8,128)(2,1)S(1)} %get-tuple-element.22.masked, ...), custom_call_target="tpu_custom_call" | custom-call | flops 268435456 | bytes 1048576 | tf_op jit(solution)/shard_map/density_terms/pallas_call | solution.py:159
  17.8 0.1 collective-permute-start.2
  17.9 12.8 %collective-permute-done.3.masked = bf16[2,512,256]{2,1,0:T(8,128)(2,1)S(1)} collective-permute-done((bf16[2,512,256]{2,1,0:T(8,128)(2,1)S(1)}, bf16[2,512,256]{2,1,0:T(8,128)(2,1)S(1)}, u32[]{:S(2)}, u32[]{:S(2)}) %collective-permute-start.3) | collective-permute-done | bytes 524320 | tf_op jit(solution)/shard_map/ppermute | solution.py:198
  30.6 0.4 far_half.1
  31.1 0.6 %collective-permute-start.7 = (bf16[2,128,256]{2,1,0:T(8,128)(2,1)S(1)}, bf16[2,128,256]{2,1,0:T(8,128)(2,1)S(1)}, u32[]{:S(2)}, u32[]{:S(2)}) collective-permute-start(bf16[2,128,256]{2,1,0:T(8,128)(2,1)S(1)} %get-tuple-element.31), channel_id=1, source_target_pairs={{0,6},{2,4},{4,2},{6,0},{8,14},{10,12},{12,10},{14,8},{1,7},{3,5},... | collective-permute-start | bytes 393224 | tf_op jit(solution)/shard_map/ppermute | solution.py:208
  31.7 0.0 collective-permute-done.2.before
  31.7 1.4 %collective-permute-start.8 = (bf16[2,128,256]{2,1,0:T(8,128)(2,1)S(1)}, bf16[2,128,256]{2,1,0:T(8,128)(2,1)S(1)}, u32[]{:S(2)}, u32[]{:S(2)}) collective-permute-start(bf16[2,128,256]{2,1,0:T(8,128)(2,1)S(1)} %get-tuple-element.32), channel_id=1, source_target_pairs={{0,4},{2,6},{4,0},{6,2},{8,12},{10,14},{12,8},{14,10},{1,5},{3,7},... | collective-permute-start | bytes 393224 | tf_op jit(solution)/shard_map/ppermute | solution.py:208
  33.1 0.0 collective-permute-done.4.refs_1_
  33.1 1.5 %collective-permute-start.9 = (bf16[2,128,256]{2,1,0:T(8,128)(2,1)S(1)}, bf16[2,128,256]{2,1,0:T(8,128)(2,1)S(1)}, u32[]{:S(2)}, u32[]{:S(2)}) collective-permute-start(bf16[2,128,256]{2,1,0:T(8,128)(2,1)S(1)} %get-tuple-element.33), channel_id=1, source_target_pairs={{0,2},{2,0},{4,6},{6,4},{8,10},{10,8},{12,14},{14,12},{1,3},{3,1},... | collective-permute-start | bytes 393224 | tf_op jit(solution)/shard_map/ppermute | solution.py:208
  34.6 0.0 collective-permute-done.5.refs_2_
  34.6 0.0 collective-permute-done.6.refs_3_
  34.6 0.3 own_pairs.1
  34.9 2.9 %collective-permute-done.7.refs_1_ = bf16[2,128,256]{2,1,0:T(8,128)(2,1)S(1)} collective-permute-done((bf16[2,128,256]{2,1,0:T(8,128)(2,1)S(1)}, bf16[2,128,256]{2,1,0:T(8,128)(2,1)S(1)}, u32[]{:S(2)}, u32[]{:S(2)}) %collective-permute-start.7) | collective-permute-done | bytes 131104 | tf_op jit(solution)/shard_map/ppermute | solution.py:208
  37.8 1.0 %collective-permute-done.8.refs_2_ = bf16[2,128,256]{2,1,0:T(8,128)(2,1)S(1)} collective-permute-done((bf16[2,128,256]{2,1,0:T(8,128)(2,1)S(1)}, bf16[2,128,256]{2,1,0:T(8,128)(2,1)S(1)}, u32[]{:S(2)}, u32[]{:S(2)}) %collective-permute-start.8) | collective-permute-done | bytes 131104 | tf_op jit(solution)/shard_map/ppermute | solution.py:208
  38.8 0.3 collective-permute-done.9.refs_3_
  39.1 0.3 far_pairs.1
  39.4 0.1 collective-permute-start.11
  39.5 0.5 %collective-permute-start.10 = (bf16[8,128,128]{2,1,0:T(8,128)(2,1)S(1)}, bf16[8,128,128]{2,1,0:T(8,128)(2,1)S(1)}, u32[]{:S(2)}, u32[]{:S(2)}) collective-permute-start(bf16[8,128,128]{2,1,0:T(8,128)(2,1)S(1)} %get-tuple-element.35), channel_id=1, source_target_pairs={{0,1},{1,0},{2,3},{3,2},{4,5},{5,4},{6,7},{7,6},{8,9},{9,8},{10,11... | collective-permute-start | bytes 786440 | tf_op jit(solution)/shard_map/ppermute | solution.py:241
  40.0 0.6 %multiply_reduce_fusion = f32[2]{0:T(128)} fusion(f32[2,128]{1,0:T(2,128)S(1)} %collective-permute-done.2.before, f32[2,128]{1,0:T(2,128)S(1)} %density_terms.1.before), kind=kLoop, calls=%fused_computation | loop fusion | flops 4 | bytes 24 | tf_op jit(solution)/shard_map/div | solution.py:226
  40.6 0.2 far_turned.1.far
  40.8 0.2 collective-permute-done.11.refs_3_
  41.0 0.4 collective-permute-done.10.refs_1_
  41.4 6.0 %cross_terms.1 = f32[128,256,128]{2,1,0:T(8,128)} custom-call(bf16[8,256,128]{2,1,0:T(8,128)(2,1)S(1)} %get-tuple-element.30.earlier.near, bf16[8,256,128]{2,1,0:T(8,128)(2,1)S(1)} %far_turned.1.far, f32[8,128,128]{2,1,0:T(8,128)S(1)} %get-tuple-element.34.refs_0_, bf16[8,128,128]{2,1,0:T(8,128)(2,1)S(1)} %collective-permute-done.10.refs_1_, ...), custom_call_target="tpu_custom_call" | custom-call | flops 2147483648 | bytes 18874368 | tf_op jit(solution)/shard_map/cross_terms/pallas_call | solution.py:159
Async XLA Ops:
  2.0 9.3 %collective-permute-start = (bf16[256,512]{1,0:T(8,128)(2,1)S(1)}, bf16[256,512]{1,0:T(8,128)(2,1)S(1)}, u32[]{:S(2)}, u32[]{:S(2)}) collective-permute-start(bf16[256,512]{1,0:T(8,128)(2,1)S(1)} %get-tuple-element.21), channel_id=1, source_target_pairs={{0,2},{2,0},{1,3},{3,1},{4,6},{6,4},{5,7},{7,5},{8,10},{10,8},{9,1... | collective-permute-start | bytes 786440 | tf_op jit(solution)/shard_map/ppermute | solution.py:199
  5.0 25.6 %collective-permute-start.3 = (bf16[2,512,256]{2,1,0:T(8,128)(2,1)S(1)}, bf16[2,512,256]{2,1,0:T(8,128)(2,1)S(1)}, u32[]{:S(2)}, u32[]{:S(2)}) collective-permute-start(bf16[2,512,256]{2,1,0:T(8,128)(2,1)S(1)} %get-tuple-element.22.masked), channel_id=1, source_target_pairs={{0,8},{4,12},{8,0},{12,4},{1,9},{5,13},{9,1},{13,5},{2,10},{6,14},... | collective-permute-start | bytes 1572872 | tf_op jit(solution)/shard_map/ppermute | solution.py:198
  11.3 1.5 %collective-permute-start.1 = (bf16[256,512]{1,0:T(8,128)(2,1)S(1)}, bf16[256,512]{1,0:T(8,128)(2,1)S(1)}, u32[]{:S(2)}, u32[]{:S(2)}) collective-permute-start(bf16[256,512]{1,0:T(8,128)(2,1)S(1)} %collective-permute-done.mine), channel_id=1, source_target_pairs={{0,1},{1,0},{2,3},{3,2},{4,5},{5,4},{6,7},{7,6},{8,9},{9,8},{10,11... | collective-permute-start | bytes 786440 | tf_op jit(solution)/shard_map/ppermute | solution.py:200
  13.5 19.6 %collective-permute-start.4 = (bf16[2,128,256]{2,1,0:T(8,128)(2,1)S(1)}, bf16[2,128,256]{2,1,0:T(8,128)(2,1)S(1)}, u32[]{:S(2)}, u32[]{:S(2)}) collective-permute-start(bf16[2,128,256]{2,1,0:T(8,128)(2,1)S(1)} %get-tuple-element.25.refs_1_), channel_id=1, source_target_pairs={{0,6},{2,4},{4,2},{6,0},{8,14},{10,12},{12,10},{14,8},{1,7},{3,5},... | collective-permute-start | bytes 393224 | tf_op jit(solution)/shard_map/ppermute | solution.py:208
  16.3 18.3 %collective-permute-start.5 = (bf16[2,128,256]{2,1,0:T(8,128)(2,1)S(1)}, bf16[2,128,256]{2,1,0:T(8,128)(2,1)S(1)}, u32[]{:S(2)}, u32[]{:S(2)}) collective-permute-start(bf16[2,128,256]{2,1,0:T(8,128)(2,1)S(1)} %get-tuple-element.26.refs_2_), channel_id=1, source_target_pairs={{0,4},{2,6},{4,0},{6,2},{8,12},{10,14},{12,8},{14,10},{1,5},{3,7},... | collective-permute-start | bytes 393224 | tf_op jit(solution)/shard_map/ppermute | solution.py:208
  16.7 17.9 %collective-permute-start.6 = (bf16[2,128,256]{2,1,0:T(8,128)(2,1)S(1)}, bf16[2,128,256]{2,1,0:T(8,128)(2,1)S(1)}, u32[]{:S(2)}, u32[]{:S(2)}) collective-permute-start(bf16[2,128,256]{2,1,0:T(8,128)(2,1)S(1)} %get-tuple-element.27.refs_3_), channel_id=1, source_target_pairs={{0,2},{2,0},{4,6},{6,4},{8,10},{10,8},{12,14},{14,12},{1,3},{3,1},... | collective-permute-start | bytes 393224 | tf_op jit(solution)/shard_map/ppermute | solution.py:208
  17.8 13.9 %collective-permute-start.2 = (f32[2,128]{1,0:T(2,128)S(1)}, f32[2,128]{1,0:T(2,128)S(1)}, u32[]{:S(2)}, u32[]{:S(2)}) collective-permute-start(f32[2,128]{1,0:T(2,128)S(1)} %density_terms.1.before), channel_id=1, source_target_pairs={{0,1},{1,0},{2,3},{3,2},{4,5},{5,4},{6,7},{7,6},{8,9},{9,8},{10,11... | collective-permute-start | bytes 3080 | tf_op jit(solution)/shard_map/ppermute | solution.py:225
  31.1 6.8 %collective-permute-start.7 = (bf16[2,128,256]{2,1,0:T(8,128)(2,1)S(1)}, bf16[2,128,256]{2,1,0:T(8,128)(2,1)S(1)}, u32[]{:S(2)}, u32[]{:S(2)}) collective-permute-start(bf16[2,128,256]{2,1,0:T(8,128)(2,1)S(1)} %get-tuple-element.31), channel_id=1, source_target_pairs={{0,6},{2,4},{4,2},{6,0},{8,14},{10,12},{12,10},{14,8},{1,7},{3,5},... | collective-permute-start | bytes 393224 | tf_op jit(solution)/shard_map/ppermute | solution.py:208
  31.7 7.1 %collective-permute-start.8 = (bf16[2,128,256]{2,1,0:T(8,128)(2,1)S(1)}, bf16[2,128,256]{2,1,0:T(8,128)(2,1)S(1)}, u32[]{:S(2)}, u32[]{:S(2)}) collective-permute-start(bf16[2,128,256]{2,1,0:T(8,128)(2,1)S(1)} %get-tuple-element.32), channel_id=1, source_target_pairs={{0,4},{2,6},{4,0},{6,2},{8,12},{10,14},{12,8},{14,10},{1,5},{3,7},... | collective-permute-start | bytes 393224 | tf_op jit(solution)/shard_map/ppermute | solution.py:208
  33.1 6.0 %collective-permute-start.9 = (bf16[2,128,256]{2,1,0:T(8,128)(2,1)S(1)}, bf16[2,128,256]{2,1,0:T(8,128)(2,1)S(1)}, u32[]{:S(2)}, u32[]{:S(2)}) collective-permute-start(bf16[2,128,256]{2,1,0:T(8,128)(2,1)S(1)} %get-tuple-element.33), channel_id=1, source_target_pairs={{0,2},{2,0},{4,6},{6,4},{8,10},{10,8},{12,14},{14,12},{1,3},{3,1},... | collective-permute-start | bytes 393224 | tf_op jit(solution)/shard_map/ppermute | solution.py:208
  39.4 1.6 %collective-permute-start.11 = (bf16[8,128,128]{2,1,0:T(8,128)(2,1)S(1)}, bf16[8,128,128]{2,1,0:T(8,128)(2,1)S(1)}, u32[]{:S(2)}, u32[]{:S(2)}) collective-permute-start(bf16[8,128,128]{2,1,0:T(8,128)(2,1)S(1)} %get-tuple-element.37), channel_id=1, source_target_pairs={{0,1},{1,0},{2,3},{3,2},{4,5},{5,4},{6,7},{7,6},{8,9},{9,8},{10,11... | collective-permute-start | bytes 786440 | tf_op jit(solution)/shard_map/ppermute | solution.py:245
  39.5 1.9 %collective-permute-start.10 = (bf16[8,128,128]{2,1,0:T(8,128)(2,1)S(1)}, bf16[8,128,128]{2,1,0:T(8,128)(2,1)S(1)}, u32[]{:S(2)}, u32[]{:S(2)}) collective-permute-start(bf16[8,128,128]{2,1,0:T(8,128)(2,1)S(1)} %get-tuple-element.35), channel_id=1, source_target_pairs={{0,1},{1,0},{2,3},{3,2},{4,5},{5,4},{6,7},{7,6},{8,9},{9,8},{10,11... | collective-permute-start | bytes 786440 | tf_op jit(solution)/shard_map/ppermute | solution.py:241

commit v14 on v13

--- a/solution.py
+++ b/solution.py
@@ -116,6 +116,10 @@
         sent[k * aux_rows : (k + 1) * aux_rows] = part.astype(jnp.bfloat16)
 
 
+def mark_kernel(*refs):
+    refs[-1][...] = jnp.zeros_like(refs[-1])
+
+
 def turn_kernel(*refs):
     messages, out = refs[:-1], refs[-1]
     nu_width = messages[0].shape[2]
@@ -239,8 +243,11 @@
         flops=pair_work,
     )
     own_pairs = (own_kept, lax.ppermute(own_given, "ao", swap))
+    all_here = call(
+        mark_kernel, "far_rows_here", far_here, [f32((8, 128))], flops=1 << 34, in_spec=pl.BlockSpec(memory_space=pl.ANY)
+    )[0]
     far_kept, far_given = call(
-        pair_kernel, "far_pairs", (value_there, own_rows, orbitals, *far_here), kept_and_given, flops=pair_work
+        pair_kernel, "far_pairs", (all_here, own_pairs[1], orbitals, *far_here), kept_and_given, flops=pair_work
     )
     far_pairs = (far_kept, lax.ppermute(far_given, "ao", swap))
     far_rows = call(turn_kernel, "far_turned", far_here, side)[0]

time: 47.6 us -> 47.2 us (level)
    ppermute x1, waiting for transfers between devices: 0.2 us -> 0.7 us  [body(): far_pairs = (far_kept, lax.ppermute(far_given, 'ao', swap))]
    pallas_call x8 -> x9, Pallas kernels: 10 us -> 10 us  [call(): pl.pallas_call(kernel, in_specs=[in_spec] * len(inputs), out_specs=[out_s...]
  transfers between devices with their start and end apart: 12 -> 12, of which waited for: 8 -> 7; matrix products, arithmetic and copies ran while one was open for 1% -> 1% of each run, Pallas kernels for 5% -> 5%
where the time goes in v14:
time: 47.2 us; the launch traced here: 47.1 us
  waiting for transfers between devices  22.8 us (48%)
  starting transfers between devices  12.9 us (27%)
  Pallas kernels  10 us (21%)
  between operations  0.72 us (2%)
  other arithmetic  0.63 us (1%)
    ppermute x1, waiting for transfers between devices, body(): far_masked = lax.ppermute(masked, 'aux', across)  12.8 us
    pallas_call x9, Pallas kernels, call(): pl.pallas_call(kernel, in_specs=[in_spec] * len(inputs), out_specs=[out_s...  10 us
    ppermute x6, starting transfers between devices, square(): arrived.append(lax.ppermute(message, ('aux', 'orb'), moves))  7.11 us
    ppermute x6, waiting for transfers between devices, square(): arrived.append(lax.ppermute(message, ('aux', 'orb'), moves))  4.12 us
    ppermute x1, waiting for transfers between devices, body(): mine = lax.ppermute(part, 'orb', swap)  3.66 us
    ppermute x1, starting transfers between devices, body(): mine = lax.ppermute(part, 'orb', swap)  3 us
    ppermute x1, starting transfers between devices, body(): far_masked = lax.ppermute(masked, 'aux', across)  2.59 us
    ppermute x1, waiting for transfers between devices, body(): theirs = lax.ppermute(mine, 'ao', swap)  1.53 us
  transfers between devices with their start and end apart: 12, of which 7 were waited for; matrix products, arithmetic and copies ran while one was open for 1% of the time, Pallas kernels for 5%

profile of v14, /device:TPU:0, one launch (start us, length us, event | category | flops | bytes accessed | tf_op | source)
XLA Modules:
  0.0 47.1 jit_solution(12031570367710206219)
XLA Ops:
  0.6 1.4 %masked_blocks.1 = (bf16[2,512,256]{2,1,0:T(8,128)(2,1)S(1)}, bf16[512,512]{1,0:T(8,128)(2,1)S(1)}, bf16[256,512]{1,0:T(8,128)(2,1)S(1)}, bf16[256,128]{1,0:T(8,128)(2,1)S(1)}) custom-call(s32[1,2,4]{2,1,0:T(2,128)} %bitcast.1, bf16[2,512,256]{2,1,0:T(8,128)(2,1)} %blocks.1, bf16[512,512]{1,0:T(8,128)(2,1)} %occupied.1, bf16[512,128]{1,0:T(8,128)(2,1)} %ligand.1), custom_call_target="tpu_custom_call" | custom-call | bytes 1048576 | tf_op jit(solution)/shard_map/masked_blocks/pallas_call | solution.py:163
  2.0 3.0 %collective-permute-start = (bf16[256,512]{1,0:T(8,128)(2,1)S(1)}, bf16[256,512]{1,0:T(8,128)(2,1)S(1)}, u32[]{:S(2)}, u32[]{:S(2)}) collective-permute-start(bf16[256,512]{1,0:T(8,128)(2,1)S(1)} %get-tuple-element.21), channel_id=1, source_target_pairs={{0,2},{2,0},{1,3},{3,1},{4,6},{6,4},{5,7},{7,5},{8,10},{10,8},{9,1... | collective-permute-start | bytes 786440 | tf_op jit(solution)/shard_map/ppermute | solution.py:203
  5.0 2.6 %collective-permute-start.3 = (bf16[2,512,256]{2,1,0:T(8,128)(2,1)S(1)}, bf16[2,512,256]{2,1,0:T(8,128)(2,1)S(1)}, u32[]{:S(2)}, u32[]{:S(2)}) collective-permute-start(bf16[2,512,256]{2,1,0:T(8,128)(2,1)S(1)} %get-tuple-element.22.masked), channel_id=1, source_target_pairs={{0,8},{4,12},{8,0},{12,4},{1,9},{5,13},{9,1},{13,5},{2,10},{6,14},... | collective-permute-start | bytes 1572872 | tf_op jit(solution)/shard_map/ppermute | solution.py:202
  7.6 3.7 %collective-permute-done.mine = bf16[256,512]{1,0:T(8,128)(2,1)S(1)} collective-permute-done((bf16[256,512]{1,0:T(8,128)(2,1)S(1)}, bf16[256,512]{1,0:T(8,128)(2,1)S(1)}, u32[]{:S(2)}, u32[]{:S(2)}) %collective-permute-start) | collective-permute-done | bytes 262176 | tf_op jit(solution)/shard_map/ppermute | solution.py:203
  11.3 0.0 collective-permute-start.1
  11.3 1.5 %collective-permute-done.1.theirs = bf16[256,512]{1,0:T(8,128)(2,1)S(1)} collective-permute-done((bf16[256,512]{1,0:T(8,128)(2,1)S(1)}, bf16[256,512]{1,0:T(8,128)(2,1)S(1)}, u32[]{:S(2)}, u32[]{:S(2)}) %collective-permute-start.1) | collective-permute-done | bytes 262176 | tf_op jit(solution)/shard_map/ppermute | solution.py:204
  12.8 0.6 %own_half.1 = (bf16[4,128,512]{2,1,0:T(8,128)(2,1)S(1)}, bf16[2,128,256]{2,1,0:T(8,128)(2,1)S(1)}, bf16[2,128,256]{2,1,0:T(8,128)(2,1)S(1)}, bf16[2,128,256]{2,1,0:T(8,128)(2,1)S(1)}, bf16[2,128,256]{2,1,0:T(8,128)(2,1)S(1)}) custom-call(bf16[512,512]{1,0:T(8,128)(2,1)S(1)} %get-tuple-element.20.occupied, bf16[256,512]{1,0:T(8,128)(2,1)S(1)} %collective-permute-done.mine, ...), custom_call_target="tpu_custom_call" | custom-call | flops 268435456 | bytes 1048576 | tf_op jit(solution)/shard_map/own_half/pallas_call | solution.py:163
  13.5 2.8 %collective-permute-start.4 = (bf16[2,128,256]{2,1,0:T(8,128)(2,1)S(1)}, bf16[2,128,256]{2,1,0:T(8,128)(2,1)S(1)}, u32[]{:S(2)}, u32[]{:S(2)}) collective-permute-start(bf16[2,128,256]{2,1,0:T(8,128)(2,1)S(1)} %get-tuple-element.25.refs_1_), channel_id=1, source_target_pairs={{0,6},{2,4},{4,2},{6,0},{8,14},{10,12},{12,10},{14,8},{1,7},{3,5},... | collective-permute-start | bytes 393224 | tf_op jit(solution)/shard_map/ppermute | solution.py:212
  16.3 0.4 collective-permute-start.5
  16.7 0.3 collective-permute-start.6
  17.0 0.7 %density_terms.1.before = f32[2,128]{1,0:T(2,128)S(1)} custom-call(bf16[512,512]{1,0:T(8,128)(2,1)S(1)} %get-tuple-element.20.occupied, bf16[256,512]{1,0:T(8,128)(2,1)S(1)} %collective-permute-done.mine, bf16[256,512]{1,0:T(8,128)(2,1)S(1)} %collective-permute-done.1.theirs, bf16[2,512,256]{2,1,0:T(8,128)(2,1)S(1)} %get-tuple-element.22.masked, ...), custom_call_target="tpu_custom_call" | custom-call | flops 268435456 | bytes 1048576 | tf_op jit(solution)/shard_map/density_terms/pallas_call | solution.py:163
  17.8 0.1 collective-permute-start.2
  17.9 12.8 %collective-permute-done.3.masked = bf16[2,512,256]{2,1,0:T(8,128)(2,1)S(1)} collective-permute-done((bf16[2,512,256]{2,1,0:T(8,128)(2,1)S(1)}, bf16[2,512,256]{2,1,0:T(8,128)(2,1)S(1)}, u32[]{:S(2)}, u32[]{:S(2)}) %collective-permute-start.3) | collective-permute-done | bytes 524320 | tf_op jit(solution)/shard_map/ppermute | solution.py:202
  30.6 0.4 far_half.1
  31.1 0.6 %collective-permute-start.7 = (bf16[2,128,256]{2,1,0:T(8,128)(2,1)S(1)}, bf16[2,128,256]{2,1,0:T(8,128)(2,1)S(1)}, u32[]{:S(2)}, u32[]{:S(2)}) collective-permute-start(bf16[2,128,256]{2,1,0:T(8,128)(2,1)S(1)} %get-tuple-element.31), channel_id=1, source_target_pairs={{0,6},{2,4},{4,2},{6,0},{8,14},{10,12},{12,10},{14,8},{1,7},{3,5},... | collective-permute-start | bytes 393224 | tf_op jit(solution)/shard_map/ppermute | solution.py:212
  31.7 0.0 collective-permute-done.2.before
  31.7 1.4 %collective-permute-start.8 = (bf16[2,128,256]{2,1,0:T(8,128)(2,1)S(1)}, bf16[2,128,256]{2,1,0:T(8,128)(2,1)S(1)}, u32[]{:S(2)}, u32[]{:S(2)}) collective-permute-start(bf16[2,128,256]{2,1,0:T(8,128)(2,1)S(1)} %get-tuple-element.32), channel_id=1, source_target_pairs={{0,4},{2,6},{4,0},{6,2},{8,12},{10,14},{12,8},{14,10},{1,5},{3,7},... | collective-permute-start | bytes 393224 | tf_op jit(solution)/shard_map/ppermute | solution.py:212
  33.1 0.0 collective-permute-done.4.refs_1_
  33.1 1.5 %collective-permute-start.9 = (bf16[2,128,256]{2,1,0:T(8,128)(2,1)S(1)}, bf16[2,128,256]{2,1,0:T(8,128)(2,1)S(1)}, u32[]{:S(2)}, u32[]{:S(2)}) collective-permute-start(bf16[2,128,256]{2,1,0:T(8,128)(2,1)S(1)} %get-tuple-element.33), channel_id=1, source_target_pairs={{0,2},{2,0},{4,6},{6,4},{8,10},{10,8},{12,14},{14,12},{1,3},{3,1},... | collective-permute-start | bytes 393224 | tf_op jit(solution)/shard_map/ppermute | solution.py:212
  34.6 0.0 collective-permute-done.5.refs_2_
  34.6 0.0 collective-permute-done.6.refs_3_
  34.6 0.3 own_pairs.1
  34.9 0.1 collective-permute-start.10
  35.0 2.8 %collective-permute-done.7.refs_1_ = bf16[2,128,256]{2,1,0:T(8,128)(2,1)S(1)} collective-permute-done((bf16[2,128,256]{2,1,0:T(8,128)(2,1)S(1)}, bf16[2,128,256]{2,1,0:T(8,128)(2,1)S(1)}, u32[]{:S(2)}, u32[]{:S(2)}) %collective-permute-start.7) | collective-permute-done | bytes 131104 | tf_op jit(solution)/shard_map/ppermute | solution.py:212
  37.8 1.0 %collective-permute-done.8.refs_2_ = bf16[2,128,256]{2,1,0:T(8,128)(2,1)S(1)} collective-permute-done((bf16[2,128,256]{2,1,0:T(8,128)(2,1)S(1)}, bf16[2,128,256]{2,1,0:T(8,128)(2,1)S(1)}, u32[]{:S(2)}, u32[]{:S(2)}) %collective-permute-start.8) | collective-permute-done | bytes 131104 | tf_op jit(solution)/shard_map/ppermute | solution.py:212
  38.8 0.3 collective-permute-done.9.refs_3_
  39.1 0.0 collective-permute-done.10.earlier.refs_1_
  39.1 0.3 far_pairs.1
  39.4 0.1 collective-permute-start.11
  39.5 0.6 %multiply_reduce_fusion = f32[2]{0:T(128)} fusion(f32[2,128]{1,0:T(2,128)S(1)} %collective-permute-done.2.before, f32[2,128]{1,0:T(2,128)S(1)} %density_terms.1.before), kind=kLoop, calls=%fused_computation | loop fusion | flops 4 | bytes 24 | tf_op jit(solution)/shard_map/div | solution.py:230
  40.1 0.2 far_turned.1.far
  40.3 0.7 %collective-permute-done.11.refs_3_ = bf16[8,128,128]{2,1,0:T(8,128)(2,1)S(1)} collective-permute-done((bf16[8,128,128]{2,1,0:T(8,128)(2,1)S(1)}, bf16[8,128,128]{2,1,0:T(8,128)(2,1)S(1)}, u32[]{:S(2)}, u32[]{:S(2)}) %collective-permute-start.11) | collective-permute-done | bytes 262176 | tf_op jit(solution)/shard_map/ppermute | solution.py:252
  41.0 6.0 %cross_terms.1 = f32[128,256,128]{2,1,0:T(8,128)} custom-call(bf16[8,256,128]{2,1,0:T(8,128)(2,1)S(1)} %get-tuple-element.30.near, bf16[8,256,128]{2,1,0:T(8,128)(2,1)S(1)} %far_turned.1.far, f32[8,128,128]{2,1,0:T(8,128)S(1)} %get-tuple-element.34.refs_0_, bf16[8,128,128]{2,1,0:T(8,128)(2,1)S(1)} %collective-permute-done.10.earlier.refs_1_, ...), custom_call_target="tpu_custom_call" | custom-call | flops 2147483648 | bytes 18874368 | tf_op jit(solution)/shard_map/cross_terms/pallas_call | solution.py:163
  (1 shorter events, 0.0 us)
Async XLA Ops:
  2.0 9.3 %collective-permute-start = (bf16[256,512]{1,0:T(8,128)(2,1)S(1)}, bf16[256,512]{1,0:T(8,128)(2,1)S(1)}, u32[]{:S(2)}, u32[]{:S(2)}) collective-permute-start(bf16[256,512]{1,0:T(8,128)(2,1)S(1)} %get-tuple-element.21), channel_id=1, source_target_pairs={{0,2},{2,0},{1,3},{3,1},{4,6},{6,4},{5,7},{7,5},{8,10},{10,8},{9,1... | collective-permute-start | bytes 786440 | tf_op jit(solution)/shard_map/ppermute | solution.py:203
  5.0 25.6 %collective-permute-start.3 = (bf16[2,512,256]{2,1,0:T(8,128)(2,1)S(1)}, bf16[2,512,256]{2,1,0:T(8,128)(2,1)S(1)}, u32[]{:S(2)}, u32[]{:S(2)}) collective-permute-start(bf16[2,512,256]{2,1,0:T(8,128)(2,1)S(1)} %get-tuple-element.22.masked), channel_id=1, source_target_pairs={{0,8},{4,12},{8,0},{12,4},{1,9},{5,13},{9,1},{13,5},{2,10},{6,14},... | collective-permute-start | bytes 1572872 | tf_op jit(solution)/shard_map/ppermute | solution.py:202
  11.3 1.5 %collective-permute-start.1 = (bf16[256,512]{1,0:T(8,128)(2,1)S(1)}, bf16[256,512]{1,0:T(8,128)(2,1)S(1)}, u32[]{:S(2)}, u32[]{:S(2)}) collective-permute-start(bf16[256,512]{1,0:T(8,128)(2,1)S(1)} %collective-permute-done.mine), channel_id=1, source_target_pairs={{0,1},{1,0},{2,3},{3,2},{4,5},{5,4},{6,7},{7,6},{8,9},{9,8},{10,11... | collective-permute-start | bytes 786440 | tf_op jit(solution)/shard_map/ppermute | solution.py:204
  13.5 19.6 %collective-permute-start.4 = (bf16[2,128,256]{2,1,0:T(8,128)(2,1)S(1)}, bf16[2,128,256]{2,1,0:T(8,128)(2,1)S(1)}, u32[]{:S(2)}, u32[]{:S(2)}) collective-permute-start(bf16[2,128,256]{2,1,0:T(8,128)(2,1)S(1)} %get-tuple-element.25.refs_1_), channel_id=1, source_target_pairs={{0,6},{2,4},{4,2},{6,0},{8,14},{10,12},{12,10},{14,8},{1,7},{3,5},... | collective-permute-start | bytes 393224 | tf_op jit(solution)/shard_map/ppermute | solution.py:212
  16.3 18.3 %collective-permute-start.5 = (bf16[2,128,256]{2,1,0:T(8,128)(2,1)S(1)}, bf16[2,128,256]{2,1,0:T(8,128)(2,1)S(1)}, u32[]{:S(2)}, u32[]{:S(2)}) collective-permute-start(bf16[2,128,256]{2,1,0:T(8,128)(2,1)S(1)} %get-tuple-element.26.refs_2_), channel_id=1, source_target_pairs={{0,4},{2,6},{4,0},{6,2},{8,12},{10,14},{12,8},{14,10},{1,5},{3,7},... | collective-permute-start | bytes 393224 | tf_op jit(solution)/shard_map/ppermute | solution.py:212
  16.7 17.9 %collective-permute-start.6 = (bf16[2,128,256]{2,1,0:T(8,128)(2,1)S(1)}, bf16[2,128,256]{2,1,0:T(8,128)(2,1)S(1)}, u32[]{:S(2)}, u32[]{:S(2)}) collective-permute-start(bf16[2,128,256]{2,1,0:T(8,128)(2,1)S(1)} %get-tuple-element.27.refs_3_), channel_id=1, source_target_pairs={{0,2},{2,0},{4,6},{6,4},{8,10},{10,8},{12,14},{14,12},{1,3},{3,1},... | collective-permute-start | bytes 393224 | tf_op jit(solution)/shard_map/ppermute | solution.py:212
  17.8 13.9 %collective-permute-start.2 = (f32[2,128]{1,0:T(2,128)S(1)}, f32[2,128]{1,0:T(2,128)S(1)}, u32[]{:S(2)}, u32[]{:S(2)}) collective-permute-start(f32[2,128]{1,0:T(2,128)S(1)} %density_terms.1.before), channel_id=1, source_target_pairs={{0,1},{1,0},{2,3},{3,2},{4,5},{5,4},{6,7},{7,6},{8,9},{9,8},{10,11... | collective-permute-start | bytes 3080 | tf_op jit(solution)/shard_map/ppermute | solution.py:229
  31.1 6.8 %collective-permute-start.7 = (bf16[2,128,256]{2,1,0:T(8,128)(2,1)S(1)}, bf16[2,128,256]{2,1,0:T(8,128)(2,1)S(1)}, u32[]{:S(2)}, u32[]{:S(2)}) collective-permute-start(bf16[2,128,256]{2,1,0:T(8,128)(2,1)S(1)} %get-tuple-element.31), channel_id=1, source_target_pairs={{0,6},{2,4},{4,2},{6,0},{8,14},{10,12},{12,10},{14,8},{1,7},{3,5},... | collective-permute-start | bytes 393224 | tf_op jit(solution)/shard_map/ppermute | solution.py:212
  31.7 7.1 %collective-permute-start.8 = (bf16[2,128,256]{2,1,0:T(8,128)(2,1)S(1)}, bf16[2,128,256]{2,1,0:T(8,128)(2,1)S(1)}, u32[]{:S(2)}, u32[]{:S(2)}) collective-permute-start(bf16[2,128,256]{2,1,0:T(8,128)(2,1)S(1)} %get-tuple-element.32), channel_id=1, source_target_pairs={{0,4},{2,6},{4,0},{6,2},{8,12},{10,14},{12,8},{14,10},{1,5},{3,7},... | collective-permute-start | bytes 393224 | tf_op jit(solution)/shard_map/ppermute | solution.py:212
  33.1 6.0 %collective-permute-start.9 = (bf16[2,128,256]{2,1,0:T(8,128)(2,1)S(1)}, bf16[2,128,256]{2,1,0:T(8,128)(2,1)S(1)}, u32[]{:S(2)}, u32[]{:S(2)}) collective-permute-start(bf16[2,128,256]{2,1,0:T(8,128)(2,1)S(1)} %get-tuple-element.33), channel_id=1, source_target_pairs={{0,2},{2,0},{4,6},{6,4},{8,10},{10,8},{12,14},{14,12},{1,3},{3,1},... | collective-permute-start | bytes 393224 | tf_op jit(solution)/shard_map/ppermute | solution.py:212
  34.9 4.2 %collective-permute-start.10 = (bf16[8,128,128]{2,1,0:T(8,128)(2,1)S(1)}, bf16[8,128,128]{2,1,0:T(8,128)(2,1)S(1)}, u32[]{:S(2)}, u32[]{:S(2)}) collective-permute-start(bf16[8,128,128]{2,1,0:T(8,128)(2,1)S(1)} %get-tuple-element.35), channel_id=1, source_target_pairs={{0,1},{1,0},{2,3},{3,2},{4,5},{5,4},{6,7},{7,6},{8,9},{9,8},{10,11... | collective-permute-start | bytes 786440 | tf_op jit(solution)/shard_map/ppermute | solution.py:245
  39.4 1.6 %collective-permute-start.11 = (bf16[8,128,128]{2,1,0:T(8,128)(2,1)S(1)}, bf16[8,128,128]{2,1,0:T(8,128)(2,1)S(1)}, u32[]{:S(2)}, u32[]{:S(2)}) collective-permute-start(bf16[8,128,128]{2,1,0:T(8,128)(2,1)S(1)} %get-tuple-element.37), channel_id=1, source_target_pairs={{0,1},{1,0},{2,3},{3,2},{4,5},{5,4},{6,7},{7,6},{8,9},{9,8},{10,11... | collective-permute-start | bytes 786440 | tf_op jit(solution)/shard_map/ppermute | solution.py:252

commit v15 on v14

--- a/solution.py
+++ b/solution.py
@@ -17,10 +17,9 @@
 VMEM = pl.BlockSpec(memory_space=pltpu.VMEM)
 
 
-def masked_kernel(pattern, blocks, occupied, ligand, masked, panel, part, orbitals, held, opened, sems):
+def masked_kernel(pattern, blocks, occupied, masked, part, held, opened, sems):
     aux_rows, _, nu_width = blocks.shape
-    own = own_half_of(part.shape[0])
-    moves = ((blocks, held), (pattern, opened), (occupied.at[own], part), (occupied, panel), (ligand.at[own], orbitals))
+    moves = ((blocks, held), (pattern, opened), (occupied.at[own_half_of(part.shape[0])], part))
     copies = [pltpu.make_async_copy(source, target, sems.at[k]) for k, (source, target) in enumerate(moves)]
     for copy in copies:
         copy.start()
@@ -38,6 +37,15 @@
 
 def own_half_of(length):
     return pl.ds(pl.multiple_of(lax.axis_index("ao") * length, length), length)
+
+
+def panel_kernel(occupied, ligand, panel, orbitals, sems):
+    moves = ((occupied, panel), (ligand.at[own_half_of(orbitals.shape[0])], orbitals))
+    copies = [pltpu.make_async_copy(source, target, sems.at[k]) for k, (source, target) in enumerate(moves)]
+    for copy in copies:
+        copy.start()
+    for copy in copies:
+        copy.wait()
 
 
 def half_into(outs, turned, masked):
@@ -187,21 +195,31 @@
     across = [(a, a ^ 2) for a in range(n_aux)]
     swap = [(c, 1 - c) for c in range(n_ao)]
     pattern = jnp.swapaxes(pattern, 1, 2)
-    masked, panel, part, orbitals = call(
+    in_hbm = functools.partial(pltpu.with_memory_space_constraint, memory_space=pltpu.HBM)
+    hbm = pl.BlockSpec(memory_space=pltpu.HBM)
+    masked, part = call(
         masked_kernel,
         "masked_blocks",
-        (pltpu.with_memory_space_constraint(x, pltpu.HBM) for x in (pattern, blocks, occupied, ligand)),
-        [bf16(blocks.shape), bf16(occupied.shape), bf16((NB // n_ao, panel_width)), bf16((NB // n_ao, width))],
+        (in_hbm(pattern), in_hbm(blocks), in_hbm(occupied)),
+        [bf16(blocks.shape), bf16((NB // n_ao, panel_width))],
         [
             pltpu.VMEM(blocks.shape, jnp.bfloat16),
             pltpu.SMEM(pattern.shape, pattern.dtype),
-            pltpu.SemaphoreType.DMA((5,)),
+            pltpu.SemaphoreType.DMA((3,)),
         ],
-        in_spec=pl.BlockSpec(memory_space=pltpu.HBM),
+        in_spec=hbm,
     )
     far_masked = lax.ppermute(masked, "aux", across)
     mine = lax.ppermute(part, "orb", swap)
     theirs = lax.ppermute(mine, "ao", swap)
+    panel, orbitals = call(
+        panel_kernel,
+        "own_panel",
+        (in_hbm(occupied), in_hbm(ligand)),
+        [bf16(occupied.shape), bf16((NB // n_ao, width))],
+        [pltpu.SemaphoreType.DMA((2,))],
+        in_spec=hbm,
+    )
 
     def square(messages):
         arrived = [messages[0]]

time: 47.2 us -> 47.1 us (level)
  waiting for transfers between devices: 22.8 us -> 21.8 us
  Pallas kernels: 10 us -> 10.9 us
    ppermute x1, waiting for transfers between devices: 1.53 us -> 0.46 us  [body(): theirs = lax.ppermute(mine, 'ao', swap)]
    pallas_call x9 -> x10, Pallas kernels: 10 us -> 10.9 us  [call(): pl.pallas_call(kernel, in_specs=[in_spec] * len(inputs), out_specs=[out_s...]
  transfers between devices with their start and end apart: 12 -> 12, of which waited for: 7 -> 7; matrix products, arithmetic and copies ran while one was open for 1% -> 1% of each run, Pallas kernels for 5% -> 7%
where the time goes in v15:
time: 47.1 us; the launch traced here: 46.9 us
  waiting for transfers between devices  21.8 us (46%)
  starting transfers between devices  12.9 us (27%)
  Pallas kernels  10.9 us (23%)
  between operations  0.72 us (2%)
  other arithmetic  0.63 us (1%)
    ppermute x1, waiting for transfers between devices, body(): far_masked = lax.ppermute(masked, 'aux', across)  12.8 us
    pallas_call x10, Pallas kernels, call(): pl.pallas_call(kernel, in_specs=[in_spec] * len(inputs), out_specs=[out_s...  10.9 us
    ppermute x6, starting transfers between devices, square(): arrived.append(lax.ppermute(message, ('aux', 'orb'), moves))  7.11 us
    ppermute x6, waiting for transfers between devices, square(): arrived.append(lax.ppermute(message, ('aux', 'orb'), moves))  4.12 us
    ppermute x1, waiting for transfers between devices, body(): mine = lax.ppermute(part, 'orb', swap)  3.72 us
    ppermute x1, starting transfers between devices, body(): mine = lax.ppermute(part, 'orb', swap)  3 us
    ppermute x1, starting transfers between devices, body(): far_masked = lax.ppermute(masked, 'aux', across)  2.59 us
  transfers between devices with their start and end apart: 12, of which 7 were waited for; matrix products, arithmetic and copies ran while one was open for 1% of the time, Pallas kernels for 7%

profile of v15, /device:TPU:0, one launch (start us, length us, event | category | flops | bytes accessed | tf_op | source)
XLA Modules:
  0.0 46.9 jit_solution(7658270484065846921)
XLA Ops:
  0.6 1.2 %masked_blocks.1 = (bf16[2,512,256]{2,1,0:T(8,128)(2,1)S(1)}, bf16[256,512]{1,0:T(8,128)(2,1)S(1)}) custom-call(s32[1,2,4]{2,1,0:T(2,128)} %bitcast.1, bf16[2,512,256]{2,1,0:T(8,128)(2,1)} %blocks.1, bf16[512,512]{1,0:T(8,128)(2,1)} %occupied.3), custom_call_target="tpu_custom_call" | custom-call | bytes 1048576 | tf_op jit(solution)/shard_map/masked_blocks/pallas_call | solution.py:171
  1.8 3.0 %collective-permute-start = (bf16[256,512]{1,0:T(8,128)(2,1)S(1)}, bf16[256,512]{1,0:T(8,128)(2,1)S(1)}, u32[]{:S(2)}, u32[]{:S(2)}) collective-permute-start(bf16[256,512]{1,0:T(8,128)(2,1)S(1)} %get-tuple-element.21), channel_id=1, source_target_pairs={{0,2},{2,0},{1,3},{3,1},{4,6},{6,4},{5,7},{7,5},{8,10},{10,8},{9,1... | collective-permute-start | bytes 786440 | tf_op jit(solution)/shard_map/ppermute | solution.py:213
  4.8 2.6 %collective-permute-start.3 = (bf16[2,512,256]{2,1,0:T(8,128)(2,1)S(1)}, bf16[2,512,256]{2,1,0:T(8,128)(2,1)S(1)}, u32[]{:S(2)}, u32[]{:S(2)}) collective-permute-start(bf16[2,512,256]{2,1,0:T(8,128)(2,1)S(1)} %get-tuple-element.22.masked), channel_id=1, source_target_pairs={{0,8},{4,12},{8,0},{12,4},{1,9},{5,13},{9,1},{13,5},{2,10},{6,14},... | collective-permute-start | bytes 1572872 | tf_op jit(solution)/shard_map/ppermute | solution.py:212
  7.4 3.7 %collective-permute-done.mine = bf16[256,512]{1,0:T(8,128)(2,1)S(1)} collective-permute-done((bf16[256,512]{1,0:T(8,128)(2,1)S(1)}, bf16[256,512]{1,0:T(8,128)(2,1)S(1)}, u32[]{:S(2)}, u32[]{:S(2)}) %collective-permute-start) | collective-permute-done | bytes 262176 | tf_op jit(solution)/shard_map/ppermute | solution.py:213
  11.1 0.0 collective-permute-start.1
  11.1 1.1 %own_panel.1 = (bf16[512,512]{1,0:T(8,128)(2,1)S(1)}, bf16[256,128]{1,0:T(8,128)(2,1)S(1)}) custom-call(bf16[512,512]{1,0:T(8,128)(2,1)} %occupied.3, bf16[512,128]{1,0:T(8,128)(2,1)} %ligand.1), custom_call_target="tpu_custom_call" | custom-call | bytes 1048576 | tf_op jit(solution)/shard_map/own_panel/pallas_call | solution.py:171
  12.2 0.5 collective-permute-done.1.theirs
  12.7 0.6 %own_half.1 = (bf16[4,128,512]{2,1,0:T(8,128)(2,1)S(1)}, bf16[2,128,256]{2,1,0:T(8,128)(2,1)S(1)}, bf16[2,128,256]{2,1,0:T(8,128)(2,1)S(1)}, bf16[2,128,256]{2,1,0:T(8,128)(2,1)S(1)}, bf16[2,128,256]{2,1,0:T(8,128)(2,1)S(1)}) custom-call(bf16[512,512]{1,0:T(8,128)(2,1)S(1)} %get-tuple-element.20.occupied, bf16[256,512]{1,0:T(8,128)(2,1)S(1)} %collective-permute-done.mine, ...), custom_call_target="tpu_custom_call" | custom-call | flops 268435456 | bytes 1048576 | tf_op jit(solution)/shard_map/own_half/pallas_call | solution.py:171
  13.3 2.8 %collective-permute-start.4 = (bf16[2,128,256]{2,1,0:T(8,128)(2,1)S(1)}, bf16[2,128,256]{2,1,0:T(8,128)(2,1)S(1)}, u32[]{:S(2)}, u32[]{:S(2)}) collective-permute-start(bf16[2,128,256]{2,1,0:T(8,128)(2,1)S(1)} %get-tuple-element.25.refs_1_), channel_id=1, source_target_pairs={{0,6},{2,4},{4,2},{6,0},{8,14},{10,12},{12,10},{14,8},{1,7},{3,5},... | collective-permute-start | bytes 393224 | tf_op jit(solution)/shard_map/ppermute | solution.py:230
  16.1 0.5 collective-permute-start.5
  16.6 0.3 collective-permute-start.6
  16.9 0.7 %density_terms.1.before = f32[2,128]{1,0:T(2,128)S(1)} custom-call(bf16[512,512]{1,0:T(8,128)(2,1)S(1)} %get-tuple-element.20.occupied, bf16[256,512]{1,0:T(8,128)(2,1)S(1)} %collective-permute-done.mine, bf16[256,512]{1,0:T(8,128)(2,1)S(1)} %collective-permute-done.1.theirs, bf16[2,512,256]{2,1,0:T(8,128)(2,1)S(1)} %get-tuple-element.22.masked, ...), custom_call_target="tpu_custom_call" | custom-call | flops 268435456 | bytes 1048576 | tf_op jit(solution)/shard_map/density_terms/pallas_call | solution.py:171
  17.6 0.1 collective-permute-start.2
  17.7 12.8 %collective-permute-done.3.masked = bf16[2,512,256]{2,1,0:T(8,128)(2,1)S(1)} collective-permute-done((bf16[2,512,256]{2,1,0:T(8,128)(2,1)S(1)}, bf16[2,512,256]{2,1,0:T(8,128)(2,1)S(1)}, u32[]{:S(2)}, u32[]{:S(2)}) %collective-permute-start.3) | collective-permute-done | bytes 524320 | tf_op jit(solution)/shard_map/ppermute | solution.py:212
  30.5 0.4 far_half.1
  30.9 0.7 %collective-permute-start.7 = (bf16[2,128,256]{2,1,0:T(8,128)(2,1)S(1)}, bf16[2,128,256]{2,1,0:T(8,128)(2,1)S(1)}, u32[]{:S(2)}, u32[]{:S(2)}) collective-permute-start(bf16[2,128,256]{2,1,0:T(8,128)(2,1)S(1)} %get-tuple-element.31), channel_id=1, source_target_pairs={{0,6},{2,4},{4,2},{6,0},{8,14},{10,12},{12,10},{14,8},{1,7},{3,5},... | collective-permute-start | bytes 393224 | tf_op jit(solution)/shard_map/ppermute | solution.py:230
  31.6 0.0 collective-permute-done.2.before
  31.6 1.4 %collective-permute-start.8 = (bf16[2,128,256]{2,1,0:T(8,128)(2,1)S(1)}, bf16[2,128,256]{2,1,0:T(8,128)(2,1)S(1)}, u32[]{:S(2)}, u32[]{:S(2)}) collective-permute-start(bf16[2,128,256]{2,1,0:T(8,128)(2,1)S(1)} %get-tuple-element.32), channel_id=1, source_target_pairs={{0,4},{2,6},{4,0},{6,2},{8,12},{10,14},{12,8},{14,10},{1,5},{3,7},... | collective-permute-start | bytes 393224 | tf_op jit(solution)/shard_map/ppermute | solution.py:230
  32.9 0.0 collective-permute-done.4.refs_1_
  32.9 1.5 %collective-permute-start.9 = (bf16[2,128,256]{2,1,0:T(8,128)(2,1)S(1)}, bf16[2,128,256]{2,1,0:T(8,128)(2,1)S(1)}, u32[]{:S(2)}, u32[]{:S(2)}) collective-permute-start(bf16[2,128,256]{2,1,0:T(8,128)(2,1)S(1)} %get-tuple-element.33), channel_id=1, source_target_pairs={{0,2},{2,0},{4,6},{6,4},{8,10},{10,8},{12,14},{14,12},{1,3},{3,1},... | collective-permute-start | bytes 393224 | tf_op jit(solution)/shard_map/ppermute | solution.py:230
  34.5 0.0 collective-permute-done.5.refs_2_
  34.5 0.0 collective-permute-done.6.refs_3_
  34.5 0.3 own_pairs.1
  34.8 0.1 collective-permute-start.10
  34.9 2.8 %collective-permute-done.7.refs_1_ = bf16[2,128,256]{2,1,0:T(8,128)(2,1)S(1)} collective-permute-done((bf16[2,128,256]{2,1,0:T(8,128)(2,1)S(1)}, bf16[2,128,256]{2,1,0:T(8,128)(2,1)S(1)}, u32[]{:S(2)}, u32[]{:S(2)}) %collective-permute-start.7) | collective-permute-done | bytes 131104 | tf_op jit(solution)/shard_map/ppermute | solution.py:230
  37.7 1.0 %collective-permute-done.8.refs_2_ = bf16[2,128,256]{2,1,0:T(8,128)(2,1)S(1)} collective-permute-done((bf16[2,128,256]{2,1,0:T(8,128)(2,1)S(1)}, bf16[2,128,256]{2,1,0:T(8,128)(2,1)S(1)}, u32[]{:S(2)}, u32[]{:S(2)}) %collective-permute-start.8) | collective-permute-done | bytes 131104 | tf_op jit(solution)/shard_map/ppermute | solution.py:230
  38.7 0.3 collective-permute-done.9.refs_3_
  39.0 0.0 collective-permute-done.10.earlier.refs_1_
  39.0 0.3 far_pairs.1
  39.3 0.1 collective-permute-start.11
  39.3 0.6 %multiply_reduce_fusion = f32[2]{0:T(128)} fusion(f32[2,128]{1,0:T(2,128)S(1)} %collective-permute-done.2.before, f32[2,128]{1,0:T(2,128)S(1)} %density_terms.1.before), kind=kLoop, calls=%fused_computation | loop fusion | flops 4 | bytes 24 | tf_op jit(solution)/shard_map/div | solution.py:248
  40.0 0.2 far_turned.1.far
  40.2 0.7 %collective-permute-done.11.refs_3_ = bf16[8,128,128]{2,1,0:T(8,128)(2,1)S(1)} collective-permute-done((bf16[8,128,128]{2,1,0:T(8,128)(2,1)S(1)}, bf16[8,128,128]{2,1,0:T(8,128)(2,1)S(1)}, u32[]{:S(2)}, u32[]{:S(2)}) %collective-permute-start.11) | collective-permute-done | bytes 262176 | tf_op jit(solution)/shard_map/ppermute | solution.py:270
  40.9 6.0 %cross_terms.1 = f32[128,256,128]{2,1,0:T(8,128)} custom-call(bf16[8,256,128]{2,1,0:T(8,128)(2,1)S(1)} %get-tuple-element.30.near, bf16[8,256,128]{2,1,0:T(8,128)(2,1)S(1)} %far_turned.1.far, f32[8,128,128]{2,1,0:T(8,128)S(1)} %get-tuple-element.34.refs_0_, bf16[8,128,128]{2,1,0:T(8,128)(2,1)S(1)} %collective-permute-done.10.earlier.refs_1_, ...), custom_call_target="tpu_custom_call" | custom-call | flops 2147483648 | bytes 18874368 | tf_op jit(solution)/shard_map/cross_terms/pallas_call | solution.py:171
  (1 shorter events, 0.0 us)
Async XLA Ops:
  1.8 9.3 %collective-permute-start = (bf16[256,512]{1,0:T(8,128)(2,1)S(1)}, bf16[256,512]{1,0:T(8,128)(2,1)S(1)}, u32[]{:S(2)}, u32[]{:S(2)}) collective-permute-start(bf16[256,512]{1,0:T(8,128)(2,1)S(1)} %get-tuple-element.21), channel_id=1, source_target_pairs={{0,2},{2,0},{1,3},{3,1},{4,6},{6,4},{5,7},{7,5},{8,10},{10,8},{9,1... | collective-permute-start | bytes 786440 | tf_op jit(solution)/shard_map/ppermute | solution.py:213
  4.8 25.6 %collective-permute-start.3 = (bf16[2,512,256]{2,1,0:T(8,128)(2,1)S(1)}, bf16[2,512,256]{2,1,0:T(8,128)(2,1)S(1)}, u32[]{:S(2)}, u32[]{:S(2)}) collective-permute-start(bf16[2,512,256]{2,1,0:T(8,128)(2,1)S(1)} %get-tuple-element.22.masked), channel_id=1, source_target_pairs={{0,8},{4,12},{8,0},{12,4},{1,9},{5,13},{9,1},{13,5},{2,10},{6,14},... | collective-permute-start | bytes 1572872 | tf_op jit(solution)/shard_map/ppermute | solution.py:212
  11.1 1.5 %collective-permute-start.1 = (bf16[256,512]{1,0:T(8,128)(2,1)S(1)}, bf16[256,512]{1,0:T(8,128)(2,1)S(1)}, u32[]{:S(2)}, u32[]{:S(2)}) collective-permute-start(bf16[256,512]{1,0:T(8,128)(2,1)S(1)} %collective-permute-done.mine), channel_id=1, source_target_pairs={{0,1},{1,0},{2,3},{3,2},{4,5},{5,4},{6,7},{7,6},{8,9},{9,8},{10,11... | collective-permute-start | bytes 786440 | tf_op jit(solution)/shard_map/ppermute | solution.py:214
  13.3 19.6 %collective-permute-start.4 = (bf16[2,128,256]{2,1,0:T(8,128)(2,1)S(1)}, bf16[2,128,256]{2,1,0:T(8,128)(2,1)S(1)}, u32[]{:S(2)}, u32[]{:S(2)}) collective-permute-start(bf16[2,128,256]{2,1,0:T(8,128)(2,1)S(1)} %get-tuple-element.25.refs_1_), channel_id=1, source_target_pairs={{0,6},{2,4},{4,2},{6,0},{8,14},{10,12},{12,10},{14,8},{1,7},{3,5},... | collective-permute-start | bytes 393224 | tf_op jit(solution)/shard_map/ppermute | solution.py:230
  16.1 18.3 %collective-permute-start.5 = (bf16[2,128,256]{2,1,0:T(8,128)(2,1)S(1)}, bf16[2,128,256]{2,1,0:T(8,128)(2,1)S(1)}, u32[]{:S(2)}, u32[]{:S(2)}) collective-permute-start(bf16[2,128,256]{2,1,0:T(8,128)(2,1)S(1)} %get-tuple-element.26.refs_2_), channel_id=1, source_target_pairs={{0,4},{2,6},{4,0},{6,2},{8,12},{10,14},{12,8},{14,10},{1,5},{3,7},... | collective-permute-start | bytes 393224 | tf_op jit(solution)/shard_map/ppermute | solution.py:230
  16.6 17.9 %collective-permute-start.6 = (bf16[2,128,256]{2,1,0:T(8,128)(2,1)S(1)}, bf16[2,128,256]{2,1,0:T(8,128)(2,1)S(1)}, u32[]{:S(2)}, u32[]{:S(2)}) collective-permute-start(bf16[2,128,256]{2,1,0:T(8,128)(2,1)S(1)} %get-tuple-element.27.refs_3_), channel_id=1, source_target_pairs={{0,2},{2,0},{4,6},{6,4},{8,10},{10,8},{12,14},{14,12},{1,3},{3,1},... | collective-permute-start | bytes 393224 | tf_op jit(solution)/shard_map/ppermute | solution.py:230
  17.6 13.9 %collective-permute-start.2 = (f32[2,128]{1,0:T(2,128)S(1)}, f32[2,128]{1,0:T(2,128)S(1)}, u32[]{:S(2)}, u32[]{:S(2)}) collective-permute-start(f32[2,128]{1,0:T(2,128)S(1)} %density_terms.1.before), channel_id=1, source_target_pairs={{0,1},{1,0},{2,3},{3,2},{4,5},{5,4},{6,7},{7,6},{8,9},{9,8},{10,11... | collective-permute-start | bytes 3080 | tf_op jit(solution)/shard_map/ppermute | solution.py:247
  30.9 6.8 %collective-permute-start.7 = (bf16[2,128,256]{2,1,0:T(8,128)(2,1)S(1)}, bf16[2,128,256]{2,1,0:T(8,128)(2,1)S(1)}, u32[]{:S(2)}, u32[]{:S(2)}) collective-permute-start(bf16[2,128,256]{2,1,0:T(8,128)(2,1)S(1)} %get-tuple-element.31), channel_id=1, source_target_pairs={{0,6},{2,4},{4,2},{6,0},{8,14},{10,12},{12,10},{14,8},{1,7},{3,5},... | collective-permute-start | bytes 393224 | tf_op jit(solution)/shard_map/ppermute | solution.py:230
  31.6 7.1 %collective-permute-start.8 = (bf16[2,128,256]{2,1,0:T(8,128)(2,1)S(1)}, bf16[2,128,256]{2,1,0:T(8,128)(2,1)S(1)}, u32[]{:S(2)}, u32[]{:S(2)}) collective-permute-start(bf16[2,128,256]{2,1,0:T(8,128)(2,1)S(1)} %get-tuple-element.32), channel_id=1, source_target_pairs={{0,4},{2,6},{4,0},{6,2},{8,12},{10,14},{12,8},{14,10},{1,5},{3,7},... | collective-permute-start | bytes 393224 | tf_op jit(solution)/shard_map/ppermute | solution.py:230
  32.9 6.0 %collective-permute-start.9 = (bf16[2,128,256]{2,1,0:T(8,128)(2,1)S(1)}, bf16[2,128,256]{2,1,0:T(8,128)(2,1)S(1)}, u32[]{:S(2)}, u32[]{:S(2)}) collective-permute-start(bf16[2,128,256]{2,1,0:T(8,128)(2,1)S(1)} %get-tuple-element.33), channel_id=1, source_target_pairs={{0,2},{2,0},{4,6},{6,4},{8,10},{10,8},{12,14},{14,12},{1,3},{3,1},... | collective-permute-start | bytes 393224 | tf_op jit(solution)/shard_map/ppermute | solution.py:230
  34.8 4.2 %collective-permute-start.10 = (bf16[8,128,128]{2,1,0:T(8,128)(2,1)S(1)}, bf16[8,128,128]{2,1,0:T(8,128)(2,1)S(1)}, u32[]{:S(2)}, u32[]{:S(2)}) collective-permute-start(bf16[8,128,128]{2,1,0:T(8,128)(2,1)S(1)} %get-tuple-element.35), channel_id=1, source_target_pairs={{0,1},{1,0},{2,3},{3,2},{4,5},{5,4},{6,7},{7,6},{8,9},{9,8},{10,11... | collective-permute-start | bytes 786440 | tf_op jit(solution)/shard_map/ppermute | solution.py:263
  39.3 1.6 %collective-permute-start.11 = (bf16[8,128,128]{2,1,0:T(8,128)(2,1)S(1)}, bf16[8,128,128]{2,1,0:T(8,128)(2,1)S(1)}, u32[]{:S(2)}, u32[]{:S(2)}) collective-permute-start(bf16[8,128,128]{2,1,0:T(8,128)(2,1)S(1)} %get-tuple-element.37), channel_id=1, source_target_pairs={{0,1},{1,0},{2,3},{3,2},{4,5},{5,4},{6,7},{7,6},{8,9},{9,8},{10,11... | collective-permute-start | bytes 786440 | tf_op jit(solution)/shard_map/ppermute | solution.py:270

commit v16 on v15

--- a/solution.py
+++ b/solution.py
@@ -192,7 +192,7 @@
     bf16 = functools.partial(jax.ShapeDtypeStruct, dtype=jnp.bfloat16)
     f32 = functools.partial(jax.ShapeDtypeStruct, dtype=jnp.float32)
 
-    across = [(a, a ^ 2) for a in range(n_aux)]
+    across = [(a, n_aux - 1 - a) for a in range(n_aux)]
     swap = [(c, 1 - c) for c in range(n_ao)]
     pattern = jnp.swapaxes(pattern, 1, 2)
     in_hbm = functools.partial(pltpu.with_memory_space_constraint, memory_space=pltpu.HBM)

time: 47.1 us -> 45.4 us (0.964)
  waiting for transfers between devices: 21.8 us -> 10.9 us
  starting transfers between devices: 12.9 us -> 22.1 us
    ppermute x1, waiting for transfers between devices: 12.8 us -> 3.17 us  [body(): far_masked = lax.ppermute(masked, 'aux', across)]
    ppermute x6, starting transfers between devices: 7.11 us -> 15.3 us  [square(): arrived.append(lax.ppermute(message, ('aux', 'orb'), moves))]
    ppermute x1, starting transfers between devices: 2.59 us -> 3.6 us  [body(): far_masked = lax.ppermute(masked, 'aux', across)]
    ppermute x1, waiting for transfers between devices: 3.72 us -> 2.7 us  [body(): mine = lax.ppermute(part, 'orb', swap)]
where the time goes in v16:
time: 45.4 us; the launch traced here: 45.2 us
  starting transfers between devices  22.1 us (49%)
  Pallas kernels  10.9 us (24%)
  waiting for transfers between devices  10.9 us (24%)
  between operations  0.72 us (2%)
  other arithmetic  0.63 us (1%)
    ppermute x6, starting transfers between devices, square(): arrived.append(lax.ppermute(message, ('aux', 'orb'), moves))  15.3 us
    pallas_call x10, Pallas kernels, call(): pl.pallas_call(kernel, in_specs=[in_spec] * len(inputs), out_specs=[out_s...  10.9 us
    ppermute x6, waiting for transfers between devices, square(): arrived.append(lax.ppermute(message, ('aux', 'orb'), moves))  3.81 us
    ppermute x1, starting transfers between devices, body(): far_masked = lax.ppermute(masked, 'aux', across)  3.6 us
    ppermute x1, waiting for transfers between devices, body(): far_masked = lax.ppermute(masked, 'aux', across)  3.17 us
    ppermute x1, starting transfers between devices, body(): mine = lax.ppermute(part, 'orb', swap)  3 us
    ppermute x1, waiting for transfers between devices, body(): mine = lax.ppermute(part, 'orb', swap)  2.7 us
  transfers between devices with their start and end apart: 12, of which 7 were waited for; matrix products, arithmetic and copies ran while one was open for 1% of the time, Pallas kernels for 7%

profile of v16, /device:TPU:0, one launch (start us, length us, event | category | flops | bytes accessed | tf_op | source)
XLA Modules:
  0.0 45.2 jit_solution(14993894581341233835)
XLA Ops:
  0.6 1.2 %masked_blocks.1 = (bf16[2,512,256]{2,1,0:T(8,128)(2,1)S(1)}, bf16[256,512]{1,0:T(8,128)(2,1)S(1)}) custom-call(s32[1,2,4]{2,1,0:T(2,128)} %bitcast.1, bf16[2,512,256]{2,1,0:T(8,128)(2,1)} %blocks.1, bf16[512,512]{1,0:T(8,128)(2,1)} %occupied.3), custom_call_target="tpu_custom_call" | custom-call | bytes 1048576 | tf_op jit(solution)/shard_map/masked_blocks/pallas_call | solution.py:171
  1.8 3.0 %collective-permute-start = (bf16[256,512]{1,0:T(8,128)(2,1)S(1)}, bf16[256,512]{1,0:T(8,128)(2,1)S(1)}, u32[]{:S(2)}, u32[]{:S(2)}) collective-permute-start(bf16[256,512]{1,0:T(8,128)(2,1)S(1)} %get-tuple-element.21), channel_id=1, source_target_pairs={{0,2},{2,0},{1,3},{3,1},{4,6},{6,4},{5,7},{7,5},{8,10},{10,8},{9,1... | collective-permute-start | bytes 786440 | tf_op jit(solution)/shard_map/ppermute | solution.py:213
  4.8 3.6 %collective-permute-start.3 = (bf16[2,512,256]{2,1,0:T(8,128)(2,1)S(1)}, bf16[2,512,256]{2,1,0:T(8,128)(2,1)S(1)}, u32[]{:S(2)}, u32[]{:S(2)}) collective-permute-start(bf16[2,512,256]{2,1,0:T(8,128)(2,1)S(1)} %get-tuple-element.22.masked), channel_id=1, source_target_pairs={{0,12},{4,8},{8,4},{12,0},{1,13},{5,9},{9,5},{13,1},{2,14},{6,10},... | collective-permute-start | bytes 1572872 | tf_op jit(solution)/shard_map/ppermute | solution.py:212
  8.4 2.7 %collective-permute-done.mine = bf16[256,512]{1,0:T(8,128)(2,1)S(1)} collective-permute-done((bf16[256,512]{1,0:T(8,128)(2,1)S(1)}, bf16[256,512]{1,0:T(8,128)(2,1)S(1)}, u32[]{:S(2)}, u32[]{:S(2)}) %collective-permute-start) | collective-permute-done | bytes 262176 | tf_op jit(solution)/shard_map/ppermute | solution.py:213
  11.1 0.0 collective-permute-start.1
  11.1 1.1 %own_panel.1 = (bf16[512,512]{1,0:T(8,128)(2,1)S(1)}, bf16[256,128]{1,0:T(8,128)(2,1)S(1)}) custom-call(bf16[512,512]{1,0:T(8,128)(2,1)} %occupied.3, bf16[512,128]{1,0:T(8,128)(2,1)} %ligand.1), custom_call_target="tpu_custom_call" | custom-call | bytes 1048576 | tf_op jit(solution)/shard_map/own_panel/pallas_call | solution.py:171
  12.2 0.5 %collective-permute-done.1.theirs = bf16[256,512]{1,0:T(8,128)(2,1)S(1)} collective-permute-done((bf16[256,512]{1,0:T(8,128)(2,1)S(1)}, bf16[256,512]{1,0:T(8,128)(2,1)S(1)}, u32[]{:S(2)}, u32[]{:S(2)}) %collective-permute-start.1) | collective-permute-done | bytes 262176 | tf_op jit(solution)/shard_map/ppermute | solution.py:214
  12.7 0.6 %own_half.1 = (bf16[4,128,512]{2,1,0:T(8,128)(2,1)S(1)}, bf16[2,128,256]{2,1,0:T(8,128)(2,1)S(1)}, bf16[2,128,256]{2,1,0:T(8,128)(2,1)S(1)}, bf16[2,128,256]{2,1,0:T(8,128)(2,1)S(1)}, bf16[2,128,256]{2,1,0:T(8,128)(2,1)S(1)}) custom-call(bf16[512,512]{1,0:T(8,128)(2,1)S(1)} %get-tuple-element.20.occupied, bf16[256,512]{1,0:T(8,128)(2,1)S(1)} %collective-permute-done.mine, ...), custom_call_target="tpu_custom_call" | custom-call | flops 268435456 | bytes 1048576 | tf_op jit(solution)/shard_map/own_half/pallas_call | solution.py:171
  13.3 2.8 %collective-permute-start.4 = (bf16[2,128,256]{2,1,0:T(8,128)(2,1)S(1)}, bf16[2,128,256]{2,1,0:T(8,128)(2,1)S(1)}, u32[]{:S(2)}, u32[]{:S(2)}) collective-permute-start(bf16[2,128,256]{2,1,0:T(8,128)(2,1)S(1)} %get-tuple-element.25.refs_1_), channel_id=1, source_target_pairs={{0,6},{2,4},{4,2},{6,0},{8,14},{10,12},{12,10},{14,8},{1,7},{3,5},... | collective-permute-start | bytes 393224 | tf_op jit(solution)/shard_map/ppermute | solution.py:230
  16.1 0.5 collective-permute-start.5
  16.6 0.3 collective-permute-start.6
  16.9 0.7 %density_terms.1.before = f32[2,128]{1,0:T(2,128)S(1)} custom-call(bf16[512,512]{1,0:T(8,128)(2,1)S(1)} %get-tuple-element.20.occupied, bf16[256,512]{1,0:T(8,128)(2,1)S(1)} %collective-permute-done.mine, bf16[256,512]{1,0:T(8,128)(2,1)S(1)} %collective-permute-done.1.theirs, bf16[2,512,256]{2,1,0:T(8,128)(2,1)S(1)} %get-tuple-element.22.masked, ...), custom_call_target="tpu_custom_call" | custom-call | flops 268435456 | bytes 1048576 | tf_op jit(solution)/shard_map/density_terms/pallas_call | solution.py:171
  17.6 0.1 collective-permute-start.2
  17.7 3.2 %collective-permute-done.3.masked = bf16[2,512,256]{2,1,0:T(8,128)(2,1)S(1)} collective-permute-done((bf16[2,512,256]{2,1,0:T(8,128)(2,1)S(1)}, bf16[2,512,256]{2,1,0:T(8,128)(2,1)S(1)}, u32[]{:S(2)}, u32[]{:S(2)}) %collective-permute-start.3) | collective-permute-done | bytes 524320 | tf_op jit(solution)/shard_map/ppermute | solution.py:212
  20.9 0.4 far_half.1
  21.3 10.2 %collective-permute-start.7 = (bf16[2,128,256]{2,1,0:T(8,128)(2,1)S(1)}, bf16[2,128,256]{2,1,0:T(8,128)(2,1)S(1)}, u32[]{:S(2)}, u32[]{:S(2)}) collective-permute-start(bf16[2,128,256]{2,1,0:T(8,128)(2,1)S(1)} %get-tuple-element.31), channel_id=1, source_target_pairs={{0,6},{2,4},{4,2},{6,0},{8,14},{10,12},{12,10},{14,8},{1,7},{3,5},... | collective-permute-start | bytes 393224 | tf_op jit(solution)/shard_map/ppermute | solution.py:230
  31.5 0.0 collective-permute-done.2.before
  31.5 0.1 collective-permute-start.8
  31.6 0.0 collective-permute-done.4.refs_1_
  31.6 1.4 %collective-permute-start.9 = (bf16[2,128,256]{2,1,0:T(8,128)(2,1)S(1)}, bf16[2,128,256]{2,1,0:T(8,128)(2,1)S(1)}, u32[]{:S(2)}, u32[]{:S(2)}) collective-permute-start(bf16[2,128,256]{2,1,0:T(8,128)(2,1)S(1)} %get-tuple-element.33), channel_id=1, source_target_pairs={{0,2},{2,0},{4,6},{6,4},{8,10},{10,8},{12,14},{14,12},{1,3},{3,1},... | collective-permute-start | bytes 393224 | tf_op jit(solution)/shard_map/ppermute | solution.py:230
  33.1 0.0 collective-permute-done.5.refs_2_
  33.1 0.0 collective-permute-done.6.refs_3_
  33.1 0.3 own_pairs.1
  33.4 0.1 collective-permute-start.10
  33.5 1.6 %collective-permute-done.7.refs_1_ = bf16[2,128,256]{2,1,0:T(8,128)(2,1)S(1)} collective-permute-done((bf16[2,128,256]{2,1,0:T(8,128)(2,1)S(1)}, bf16[2,128,256]{2,1,0:T(8,128)(2,1)S(1)}, u32[]{:S(2)}, u32[]{:S(2)}) %collective-permute-start.7) | collective-permute-done | bytes 131104 | tf_op jit(solution)/shard_map/ppermute | solution.py:230
  35.1 2.1 %collective-permute-done.8.refs_2_ = bf16[2,128,256]{2,1,0:T(8,128)(2,1)S(1)} collective-permute-done((bf16[2,128,256]{2,1,0:T(8,128)(2,1)S(1)}, bf16[2,128,256]{2,1,0:T(8,128)(2,1)S(1)}, u32[]{:S(2)}, u32[]{:S(2)}) %collective-permute-start.8) | collective-permute-done | bytes 131104 | tf_op jit(solution)/shard_map/ppermute | solution.py:230
  37.2 0.1 collective-permute-done.9.refs_3_
  37.3 0.0 collective-permute-done.10.earlier.refs_1_
  37.3 0.3 far_pairs.1
  37.6 0.1 collective-permute-start.11
  37.6 0.6 %multiply_reduce_fusion = f32[2]{0:T(128)} fusion(f32[2,128]{1,0:T(2,128)S(1)} %collective-permute-done.2.before, f32[2,128]{1,0:T(2,128)S(1)} %density_terms.1.before), kind=kLoop, calls=%fused_computation | loop fusion | flops 4 | bytes 24 | tf_op jit(solution)/shard_map/div | solution.py:248
  38.3 0.2 far_turned.1.far
  38.5 0.7 %collective-permute-done.11.refs_3_ = bf16[8,128,128]{2,1,0:T(8,128)(2,1)S(1)} collective-permute-done((bf16[8,128,128]{2,1,0:T(8,128)(2,1)S(1)}, bf16[8,128,128]{2,1,0:T(8,128)(2,1)S(1)}, u32[]{:S(2)}, u32[]{:S(2)}) %collective-permute-start.11) | collective-permute-done | bytes 262176 | tf_op jit(solution)/shard_map/ppermute | solution.py:270
  39.2 6.0 %cross_terms.1 = f32[128,256,128]{2,1,0:T(8,128)} custom-call(bf16[8,256,128]{2,1,0:T(8,128)(2,1)S(1)} %get-tuple-element.30.near, bf16[8,256,128]{2,1,0:T(8,128)(2,1)S(1)} %far_turned.1.far, f32[8,128,128]{2,1,0:T(8,128)S(1)} %get-tuple-element.34.refs_0_, bf16[8,128,128]{2,1,0:T(8,128)(2,1)S(1)} %collective-permute-done.10.earlier.refs_1_, ...), custom_call_target="tpu_custom_call" | custom-call | flops 2147483648 | bytes 18874368 | tf_op jit(solution)/shard_map/cross_terms/pallas_call | solution.py:171
  (1 shorter events, 0.0 us)
Async XLA Ops:
  1.8 9.3 %collective-permute-start = (bf16[256,512]{1,0:T(8,128)(2,1)S(1)}, bf16[256,512]{1,0:T(8,128)(2,1)S(1)}, u32[]{:S(2)}, u32[]{:S(2)}) collective-permute-start(bf16[256,512]{1,0:T(8,128)(2,1)S(1)} %get-tuple-element.21), channel_id=1, source_target_pairs={{0,2},{2,0},{1,3},{3,1},{4,6},{6,4},{5,7},{7,5},{8,10},{10,8},{9,1... | collective-permute-start | bytes 786440 | tf_op jit(solution)/shard_map/ppermute | solution.py:213
  4.8 16.0 %collective-permute-start.3 = (bf16[2,512,256]{2,1,0:T(8,128)(2,1)S(1)}, bf16[2,512,256]{2,1,0:T(8,128)(2,1)S(1)}, u32[]{:S(2)}, u32[]{:S(2)}) collective-permute-start(bf16[2,512,256]{2,1,0:T(8,128)(2,1)S(1)} %get-tuple-element.22.masked), channel_id=1, source_target_pairs={{0,12},{4,8},{8,4},{12,0},{1,13},{5,9},{9,5},{13,1},{2,14},{6,10},... | collective-permute-start | bytes 1572872 | tf_op jit(solution)/shard_map/ppermute | solution.py:212
  11.1 1.5 %collective-permute-start.1 = (bf16[256,512]{1,0:T(8,128)(2,1)S(1)}, bf16[256,512]{1,0:T(8,128)(2,1)S(1)}, u32[]{:S(2)}, u32[]{:S(2)}) collective-permute-start(bf16[256,512]{1,0:T(8,128)(2,1)S(1)} %collective-permute-done.mine), channel_id=1, source_target_pairs={{0,1},{1,0},{2,3},{3,2},{4,5},{5,4},{6,7},{7,6},{8,9},{9,8},{10,11... | collective-permute-start | bytes 786440 | tf_op jit(solution)/shard_map/ppermute | solution.py:214
  13.3 18.3 %collective-permute-start.4 = (bf16[2,128,256]{2,1,0:T(8,128)(2,1)S(1)}, bf16[2,128,256]{2,1,0:T(8,128)(2,1)S(1)}, u32[]{:S(2)}, u32[]{:S(2)}) collective-permute-start(bf16[2,128,256]{2,1,0:T(8,128)(2,1)S(1)} %get-tuple-element.25.refs_1_), channel_id=1, source_target_pairs={{0,6},{2,4},{4,2},{6,0},{8,14},{10,12},{12,10},{14,8},{1,7},{3,5},... | collective-permute-start | bytes 393224 | tf_op jit(solution)/shard_map/ppermute | solution.py:230
  16.1 17.0 %collective-permute-start.5 = (bf16[2,128,256]{2,1,0:T(8,128)(2,1)S(1)}, bf16[2,128,256]{2,1,0:T(8,128)(2,1)S(1)}, u32[]{:S(2)}, u32[]{:S(2)}) collective-permute-start(bf16[2,128,256]{2,1,0:T(8,128)(2,1)S(1)} %get-tuple-element.26.refs_2_), channel_id=1, source_target_pairs={{0,4},{2,6},{4,0},{6,2},{8,12},{10,14},{12,8},{14,10},{1,5},{3,7},... | collective-permute-start | bytes 393224 | tf_op jit(solution)/shard_map/ppermute | solution.py:230
  16.6 16.5 %collective-permute-start.6 = (bf16[2,128,256]{2,1,0:T(8,128)(2,1)S(1)}, bf16[2,128,256]{2,1,0:T(8,128)(2,1)S(1)}, u32[]{:S(2)}, u32[]{:S(2)}) collective-permute-start(bf16[2,128,256]{2,1,0:T(8,128)(2,1)S(1)} %get-tuple-element.27.refs_3_), channel_id=1, source_target_pairs={{0,2},{2,0},{4,6},{6,4},{8,10},{10,8},{12,14},{14,12},{1,3},{3,1},... | collective-permute-start | bytes 393224 | tf_op jit(solution)/shard_map/ppermute | solution.py:230
  17.6 13.9 %collective-permute-start.2 = (f32[2,128]{1,0:T(2,128)S(1)}, f32[2,128]{1,0:T(2,128)S(1)}, u32[]{:S(2)}, u32[]{:S(2)}) collective-permute-start(f32[2,128]{1,0:T(2,128)S(1)} %density_terms.1.before), channel_id=1, source_target_pairs={{0,1},{1,0},{2,3},{3,2},{4,5},{5,4},{6,7},{7,6},{8,9},{9,8},{10,11... | collective-permute-start | bytes 3080 | tf_op jit(solution)/shard_map/ppermute | solution.py:247
  21.3 13.8 %collective-permute-start.7 = (bf16[2,128,256]{2,1,0:T(8,128)(2,1)S(1)}, bf16[2,128,256]{2,1,0:T(8,128)(2,1)S(1)}, u32[]{:S(2)}, u32[]{:S(2)}) collective-permute-start(bf16[2,128,256]{2,1,0:T(8,128)(2,1)S(1)} %get-tuple-element.31), channel_id=1, source_target_pairs={{0,6},{2,4},{4,2},{6,0},{8,14},{10,12},{12,10},{14,8},{1,7},{3,5},... | collective-permute-start | bytes 393224 | tf_op jit(solution)/shard_map/ppermute | solution.py:230
  31.5 5.6 %collective-permute-start.8 = (bf16[2,128,256]{2,1,0:T(8,128)(2,1)S(1)}, bf16[2,128,256]{2,1,0:T(8,128)(2,1)S(1)}, u32[]{:S(2)}, u32[]{:S(2)}) collective-permute-start(bf16[2,128,256]{2,1,0:T(8,128)(2,1)S(1)} %get-tuple-element.32), channel_id=1, source_target_pairs={{0,4},{2,6},{4,0},{6,2},{8,12},{10,14},{12,8},{14,10},{1,5},{3,7},... | collective-permute-start | bytes 393224 | tf_op jit(solution)/shard_map/ppermute | solution.py:230
  31.6 5.6 %collective-permute-start.9 = (bf16[2,128,256]{2,1,0:T(8,128)(2,1)S(1)}, bf16[2,128,256]{2,1,0:T(8,128)(2,1)S(1)}, u32[]{:S(2)}, u32[]{:S(2)}) collective-permute-start(bf16[2,128,256]{2,1,0:T(8,128)(2,1)S(1)} %get-tuple-element.33), channel_id=1, source_target_pairs={{0,2},{2,0},{4,6},{6,4},{8,10},{10,8},{12,14},{14,12},{1,3},{3,1},... | collective-permute-start | bytes 393224 | tf_op jit(solution)/shard_map/ppermute | solution.py:230
  33.4 3.9 %collective-permute-start.10 = (bf16[8,128,128]{2,1,0:T(8,128)(2,1)S(1)}, bf16[8,128,128]{2,1,0:T(8,128)(2,1)S(1)}, u32[]{:S(2)}, u32[]{:S(2)}) collective-permute-start(bf16[8,128,128]{2,1,0:T(8,128)(2,1)S(1)} %get-tuple-element.35), channel_id=1, source_target_pairs={{0,1},{1,0},{2,3},{3,2},{4,5},{5,4},{6,7},{7,6},{8,9},{9,8},{10,11... | collective-permute-start | bytes 786440 | tf_op jit(solution)/shard_map/ppermute | solution.py:263
  37.6 1.6 %collective-permute-start.11 = (bf16[8,128,128]{2,1,0:T(8,128)(2,1)S(1)}, bf16[8,128,128]{2,1,0:T(8,128)(2,1)S(1)}, u32[]{:S(2)}, u32[]{:S(2)}) collective-permute-start(bf16[8,128,128]{2,1,0:T(8,128)(2,1)S(1)} %get-tuple-element.37), channel_id=1, source_target_pairs={{0,1},{1,0},{2,3},{3,2},{4,5},{5,4},{6,7},{7,6},{8,9},{9,8},{10,11... | collective-permute-start | bytes 786440 | tf_op jit(solution)/shard_map/ppermute | solution.py:270

commit v17 on v16

--- a/solution.py
+++ b/solution.py
@@ -58,7 +58,7 @@
     aux, orb, ao = (lax.axis_index(name) for name in ("aux", "orb", "ao"))
     ni = turned.shape[1]
     here = 2 * (aux & 1) + orb
-    place = lambda s: (4 - (here ^ s)) & 3
+    place = lambda s: (here ^ s) ^ ((here ^ s) >> 1)
     near = orb == aux // 2
 
     @pl.when(near)
@@ -223,7 +223,7 @@
 
     def square(messages):
         arrived = [messages[0]]
-        for message, d in zip(messages[1:], (3, 2, 1)):
+        for message, d in zip(messages[1:], (1, 3, 2)):
             moves = [
                 (a * n_orb + o, (a ^ (d >> 1)) * n_orb + (o ^ (d & 1))) for a in range(n_aux) for o in range(n_orb)
             ]

time: 45.4 us -> 46.1 us (1.015)
  waiting for transfers between devices: 10.9 us -> 11.6 us
    ppermute x6, waiting for transfers between devices: 3.81 us -> 4.57 us  [square(): arrived.append(lax.ppermute(message, ('aux', 'orb'), moves))]
  transfers between devices with their start and end apart: 12 -> 12, of which waited for: 7 -> 6; matrix products, arithmetic and copies ran while one was open for 1% -> 1% of each run, Pallas kernels for 7% -> 7%
where the time goes in v17:
time: 46.1 us; the launch traced here: 45.9 us
  starting transfers between devices  22.1 us (48%)
  waiting for transfers between devices  11.6 us (25%)
  Pallas kernels  10.9 us (24%)
  between operations  0.74 us (2%)
  other arithmetic  0.63 us (1%)
    ppermute x6, starting transfers between devices, square(): arrived.append(lax.ppermute(message, ('aux', 'orb'), moves))  15.3 us
    pallas_call x10, Pallas kernels, call(): pl.pallas_call(kernel, in_specs=[in_spec] * len(inputs), out_specs=[out_s...  10.9 us
    ppermute x6, waiting for transfers between devices, square(): arrived.append(lax.ppermute(message, ('aux', 'orb'), moves))  4.57 us
    ppermute x1, starting transfers between devices, body(): far_masked = lax.ppermute(masked, 'aux', across)  3.6 us
    ppermute x1, waiting for transfers between devices, body(): far_masked = lax.ppermute(masked, 'aux', across)  3.11 us
    ppermute x1, starting transfers between devices, body(): mine = lax.ppermute(part, 'orb', swap)  3 us
    ppermute x1, waiting for transfers between devices, body(): mine = lax.ppermute(part, 'orb', swap)  2.7 us
  transfers between devices with their start and end apart: 12, of which 6 were waited for; matrix products, arithmetic and copies ran while one was open for 1% of the time, Pallas kernels for 7%

profile of v17, /device:TPU:0, one launch (start us, length us, event | category | flops | bytes accessed | tf_op | source)
XLA Modules:
  0.0 45.9 jit_solution(11410884259976250109)
XLA Ops:
  0.6 1.2 %masked_blocks.1 = (bf16[2,512,256]{2,1,0:T(8,128)(2,1)S(1)}, bf16[256,512]{1,0:T(8,128)(2,1)S(1)}) custom-call(s32[1,2,4]{2,1,0:T(2,128)} %bitcast.1, bf16[2,512,256]{2,1,0:T(8,128)(2,1)} %blocks.1, bf16[512,512]{1,0:T(8,128)(2,1)} %occupied.3), custom_call_target="tpu_custom_call" | custom-call | bytes 1048576 | tf_op jit(solution)/shard_map/masked_blocks/pallas_call | solution.py:171
  1.8 3.0 %collective-permute-start = (bf16[256,512]{1,0:T(8,128)(2,1)S(1)}, bf16[256,512]{1,0:T(8,128)(2,1)S(1)}, u32[]{:S(2)}, u32[]{:S(2)}) collective-permute-start(bf16[256,512]{1,0:T(8,128)(2,1)S(1)} %get-tuple-element.21), channel_id=1, source_target_pairs={{0,2},{2,0},{1,3},{3,1},{4,6},{6,4},{5,7},{7,5},{8,10},{10,8},{9,1... | collective-permute-start | bytes 786440 | tf_op jit(solution)/shard_map/ppermute | solution.py:213
  4.8 3.6 %collective-permute-start.3 = (bf16[2,512,256]{2,1,0:T(8,128)(2,1)S(1)}, bf16[2,512,256]{2,1,0:T(8,128)(2,1)S(1)}, u32[]{:S(2)}, u32[]{:S(2)}) collective-permute-start(bf16[2,512,256]{2,1,0:T(8,128)(2,1)S(1)} %get-tuple-element.22.masked), channel_id=1, source_target_pairs={{0,12},{4,8},{8,4},{12,0},{1,13},{5,9},{9,5},{13,1},{2,14},{6,10},... | collective-permute-start | bytes 1572872 | tf_op jit(solution)/shard_map/ppermute | solution.py:212
  8.4 2.7 %collective-permute-done.mine = bf16[256,512]{1,0:T(8,128)(2,1)S(1)} collective-permute-done((bf16[256,512]{1,0:T(8,128)(2,1)S(1)}, bf16[256,512]{1,0:T(8,128)(2,1)S(1)}, u32[]{:S(2)}, u32[]{:S(2)}) %collective-permute-start) | collective-permute-done | bytes 262176 | tf_op jit(solution)/shard_map/ppermute | solution.py:213
  11.1 0.0 collective-permute-start.1
  11.1 1.1 %own_panel.1 = (bf16[512,512]{1,0:T(8,128)(2,1)S(1)}, bf16[256,128]{1,0:T(8,128)(2,1)S(1)}) custom-call(bf16[512,512]{1,0:T(8,128)(2,1)} %occupied.3, bf16[512,128]{1,0:T(8,128)(2,1)} %ligand.1), custom_call_target="tpu_custom_call" | custom-call | bytes 1048576 | tf_op jit(solution)/shard_map/own_panel/pallas_call | solution.py:171
  12.2 0.5 %collective-permute-done.1.theirs = bf16[256,512]{1,0:T(8,128)(2,1)S(1)} collective-permute-done((bf16[256,512]{1,0:T(8,128)(2,1)S(1)}, bf16[256,512]{1,0:T(8,128)(2,1)S(1)}, u32[]{:S(2)}, u32[]{:S(2)}) %collective-permute-start.1) | collective-permute-done | bytes 262176 | tf_op jit(solution)/shard_map/ppermute | solution.py:214
  12.7 0.6 %own_half.1 = (bf16[4,128,512]{2,1,0:T(8,128)(2,1)S(1)}, bf16[2,128,256]{2,1,0:T(8,128)(2,1)S(1)}, bf16[2,128,256]{2,1,0:T(8,128)(2,1)S(1)}, bf16[2,128,256]{2,1,0:T(8,128)(2,1)S(1)}, bf16[2,128,256]{2,1,0:T(8,128)(2,1)S(1)}) custom-call(bf16[512,512]{1,0:T(8,128)(2,1)S(1)} %get-tuple-element.20.occupied, bf16[256,512]{1,0:T(8,128)(2,1)S(1)} %collective-permute-done.mine, ...), custom_call_target="tpu_custom_call" | custom-call | flops 268435456 | bytes 1048576 | tf_op jit(solution)/shard_map/own_half/pallas_call | solution.py:171
  13.3 1.8 %collective-permute-start.4 = (bf16[2,128,256]{2,1,0:T(8,128)(2,1)S(1)}, bf16[2,128,256]{2,1,0:T(8,128)(2,1)S(1)}, u32[]{:S(2)}, u32[]{:S(2)}) collective-permute-start(bf16[2,128,256]{2,1,0:T(8,128)(2,1)S(1)} %get-tuple-element.25.refs_1_), channel_id=1, source_target_pairs={{0,2},{2,0},{4,6},{6,4},{8,10},{10,8},{12,14},{14,12},{1,3},{3,1},... | collective-permute-start | bytes 393224 | tf_op jit(solution)/shard_map/ppermute | solution.py:230
  15.1 1.5 %collective-permute-start.5 = (bf16[2,128,256]{2,1,0:T(8,128)(2,1)S(1)}, bf16[2,128,256]{2,1,0:T(8,128)(2,1)S(1)}, u32[]{:S(2)}, u32[]{:S(2)}) collective-permute-start(bf16[2,128,256]{2,1,0:T(8,128)(2,1)S(1)} %get-tuple-element.26.refs_2_), channel_id=1, source_target_pairs={{0,6},{2,4},{4,2},{6,0},{8,14},{10,12},{12,10},{14,8},{1,7},{3,5},... | collective-permute-start | bytes 393224 | tf_op jit(solution)/shard_map/ppermute | solution.py:230
  16.7 0.2 collective-permute-start.6
  16.9 0.7 %density_terms.1.before = f32[2,128]{1,0:T(2,128)S(1)} custom-call(bf16[512,512]{1,0:T(8,128)(2,1)S(1)} %get-tuple-element.20.occupied, bf16[256,512]{1,0:T(8,128)(2,1)S(1)} %collective-permute-done.mine, bf16[256,512]{1,0:T(8,128)(2,1)S(1)} %collective-permute-done.1.theirs, bf16[2,512,256]{2,1,0:T(8,128)(2,1)S(1)} %get-tuple-element.22.masked, ...), custom_call_target="tpu_custom_call" | custom-call | flops 268435456 | bytes 1048576 | tf_op jit(solution)/shard_map/density_terms/pallas_call | solution.py:171
  17.6 0.1 collective-permute-start.2
  17.7 3.1 %collective-permute-done.3.masked = bf16[2,512,256]{2,1,0:T(8,128)(2,1)S(1)} collective-permute-done((bf16[2,512,256]{2,1,0:T(8,128)(2,1)S(1)}, bf16[2,512,256]{2,1,0:T(8,128)(2,1)S(1)}, u32[]{:S(2)}, u32[]{:S(2)}) %collective-permute-start.3) | collective-permute-done | bytes 524320 | tf_op jit(solution)/shard_map/ppermute | solution.py:212
  20.8 0.4 far_half.1
  21.3 0.6 %collective-permute-start.7 = (bf16[2,128,256]{2,1,0:T(8,128)(2,1)S(1)}, bf16[2,128,256]{2,1,0:T(8,128)(2,1)S(1)}, u32[]{:S(2)}, u32[]{:S(2)}) collective-permute-start(bf16[2,128,256]{2,1,0:T(8,128)(2,1)S(1)} %get-tuple-element.31), channel_id=1, source_target_pairs={{0,2},{2,0},{4,6},{6,4},{8,10},{10,8},{12,14},{14,12},{1,3},{3,1},... | collective-permute-start | bytes 393224 | tf_op jit(solution)/shard_map/ppermute | solution.py:230
  21.9 0.0 collective-permute-done.2.before
  21.9 11.2 %collective-permute-start.8 = (bf16[2,128,256]{2,1,0:T(8,128)(2,1)S(1)}, bf16[2,128,256]{2,1,0:T(8,128)(2,1)S(1)}, u32[]{:S(2)}, u32[]{:S(2)}) collective-permute-start(bf16[2,128,256]{2,1,0:T(8,128)(2,1)S(1)} %get-tuple-element.32), channel_id=1, source_target_pairs={{0,6},{2,4},{4,2},{6,0},{8,14},{10,12},{12,10},{14,8},{1,7},{3,5},... | collective-permute-start | bytes 393224 | tf_op jit(solution)/shard_map/ppermute | solution.py:230
  33.0 0.0 collective-permute-done.4.refs_1_
  33.0 0.0 collective-permute-start.9
  33.0 0.0 collective-permute-done.5.refs_2_
  33.0 0.0 collective-permute-done.6.refs_3_
  33.0 0.3 own_pairs.1
  33.3 0.1 collective-permute-start.10
  33.4 0.0 collective-permute-done.7.refs_1_
  33.4 3.5 %collective-permute-done.8.refs_2_ = bf16[2,128,256]{2,1,0:T(8,128)(2,1)S(1)} collective-permute-done((bf16[2,128,256]{2,1,0:T(8,128)(2,1)S(1)}, bf16[2,128,256]{2,1,0:T(8,128)(2,1)S(1)}, u32[]{:S(2)}, u32[]{:S(2)}) %collective-permute-start.8) | collective-permute-done | bytes 131104 | tf_op jit(solution)/shard_map/ppermute | solution.py:230
  36.9 1.0 %collective-permute-done.9.refs_3_ = bf16[2,128,256]{2,1,0:T(8,128)(2,1)S(1)} collective-permute-done((bf16[2,128,256]{2,1,0:T(8,128)(2,1)S(1)}, bf16[2,128,256]{2,1,0:T(8,128)(2,1)S(1)}, u32[]{:S(2)}, u32[]{:S(2)}) %collective-permute-start.9) | collective-permute-done | bytes 131104 | tf_op jit(solution)/shard_map/ppermute | solution.py:230
  38.0 0.0 collective-permute-done.10.earlier.refs_1_
  38.0 0.3 far_pairs.1
  38.3 0.1 collective-permute-start.11
  38.4 0.6 %multiply_reduce_fusion = f32[2]{0:T(128)} fusion(f32[2,128]{1,0:T(2,128)S(1)} %collective-permute-done.2.before, f32[2,128]{1,0:T(2,128)S(1)} %density_terms.1.before), kind=kLoop, calls=%fused_computation | loop fusion | flops 4 | bytes 24 | tf_op jit(solution)/shard_map/div | solution.py:248
  39.0 0.2 far_turned.1.far
  39.2 0.7 %collective-permute-done.11.refs_3_ = bf16[8,128,128]{2,1,0:T(8,128)(2,1)S(1)} collective-permute-done((bf16[8,128,128]{2,1,0:T(8,128)(2,1)S(1)}, bf16[8,128,128]{2,1,0:T(8,128)(2,1)S(1)}, u32[]{:S(2)}, u32[]{:S(2)}) %collective-permute-start.11) | collective-permute-done | bytes 262176 | tf_op jit(solution)/shard_map/ppermute | solution.py:270
  39.9 6.0 %cross_terms.1 = f32[128,256,128]{2,1,0:T(8,128)} custom-call(bf16[8,256,128]{2,1,0:T(8,128)(2,1)S(1)} %get-tuple-element.30.near, bf16[8,256,128]{2,1,0:T(8,128)(2,1)S(1)} %far_turned.1.far, f32[8,128,128]{2,1,0:T(8,128)S(1)} %get-tuple-element.34.refs_0_, bf16[8,128,128]{2,1,0:T(8,128)(2,1)S(1)} %collective-permute-done.10.earlier.refs_1_, ...), custom_call_target="tpu_custom_call" | custom-call | flops 2147483648 | bytes 18874368 | tf_op jit(solution)/shard_map/cross_terms/pallas_call | solution.py:171
  (1 shorter events, 0.0 us)
Async XLA Ops:
  1.8 9.3 %collective-permute-start = (bf16[256,512]{1,0:T(8,128)(2,1)S(1)}, bf16[256,512]{1,0:T(8,128)(2,1)S(1)}, u32[]{:S(2)}, u32[]{:S(2)}) collective-permute-start(bf16[256,512]{1,0:T(8,128)(2,1)S(1)} %get-tuple-element.21), channel_id=1, source_target_pairs={{0,2},{2,0},{1,3},{3,1},{4,6},{6,4},{5,7},{7,5},{8,10},{10,8},{9,1... | collective-permute-start | bytes 786440 | tf_op jit(solution)/shard_map/ppermute | solution.py:213
  4.8 16.0 %collective-permute-start.3 = (bf16[2,512,256]{2,1,0:T(8,128)(2,1)S(1)}, bf16[2,512,256]{2,1,0:T(8,128)(2,1)S(1)}, u32[]{:S(2)}, u32[]{:S(2)}) collective-permute-start(bf16[2,512,256]{2,1,0:T(8,128)(2,1)S(1)} %get-tuple-element.22.masked), channel_id=1, source_target_pairs={{0,12},{4,8},{8,4},{12,0},{1,13},{5,9},{9,5},{13,1},{2,14},{6,10},... | collective-permute-start | bytes 1572872 | tf_op jit(solution)/shard_map/ppermute | solution.py:212
  11.1 1.5 %collective-permute-start.1 = (bf16[256,512]{1,0:T(8,128)(2,1)S(1)}, bf16[256,512]{1,0:T(8,128)(2,1)S(1)}, u32[]{:S(2)}, u32[]{:S(2)}) collective-permute-start(bf16[256,512]{1,0:T(8,128)(2,1)S(1)} %collective-permute-done.mine), channel_id=1, source_target_pairs={{0,1},{1,0},{2,3},{3,2},{4,5},{5,4},{6,7},{7,6},{8,9},{9,8},{10,11... | collective-permute-start | bytes 786440 | tf_op jit(solution)/shard_map/ppermute | solution.py:214
  13.3 19.7 %collective-permute-start.4 = (bf16[2,128,256]{2,1,0:T(8,128)(2,1)S(1)}, bf16[2,128,256]{2,1,0:T(8,128)(2,1)S(1)}, u32[]{:S(2)}, u32[]{:S(2)}) collective-permute-start(bf16[2,128,256]{2,1,0:T(8,128)(2,1)S(1)} %get-tuple-element.25.refs_1_), channel_id=1, source_target_pairs={{0,2},{2,0},{4,6},{6,4},{8,10},{10,8},{12,14},{14,12},{1,3},{3,1},... | collective-permute-start | bytes 393224 | tf_op jit(solution)/shard_map/ppermute | solution.py:230
  15.1 17.9 %collective-permute-start.5 = (bf16[2,128,256]{2,1,0:T(8,128)(2,1)S(1)}, bf16[2,128,256]{2,1,0:T(8,128)(2,1)S(1)}, u32[]{:S(2)}, u32[]{:S(2)}) collective-permute-start(bf16[2,128,256]{2,1,0:T(8,128)(2,1)S(1)} %get-tuple-element.26.refs_2_), channel_id=1, source_target_pairs={{0,6},{2,4},{4,2},{6,0},{8,14},{10,12},{12,10},{14,8},{1,7},{3,5},... | collective-permute-start | bytes 393224 | tf_op jit(solution)/shard_map/ppermute | solution.py:230
  16.7 16.4 %collective-permute-start.6 = (bf16[2,128,256]{2,1,0:T(8,128)(2,1)S(1)}, bf16[2,128,256]{2,1,0:T(8,128)(2,1)S(1)}, u32[]{:S(2)}, u32[]{:S(2)}) collective-permute-start(bf16[2,128,256]{2,1,0:T(8,128)(2,1)S(1)} %get-tuple-element.27.refs_3_), channel_id=1, source_target_pairs={{0,4},{2,6},{4,0},{6,2},{8,12},{10,14},{12,8},{14,10},{1,5},{3,7},... | collective-permute-start | bytes 393224 | tf_op jit(solution)/shard_map/ppermute | solution.py:230
  17.6 4.2 %collective-permute-start.2 = (f32[2,128]{1,0:T(2,128)S(1)}, f32[2,128]{1,0:T(2,128)S(1)}, u32[]{:S(2)}, u32[]{:S(2)}) collective-permute-start(f32[2,128]{1,0:T(2,128)S(1)} %density_terms.1.before), channel_id=1, source_target_pairs={{0,1},{1,0},{2,3},{3,2},{4,5},{5,4},{6,7},{7,6},{8,9},{9,8},{10,11... | collective-permute-start | bytes 3080 | tf_op jit(solution)/shard_map/ppermute | solution.py:247
  21.3 12.2 %collective-permute-start.7 = (bf16[2,128,256]{2,1,0:T(8,128)(2,1)S(1)}, bf16[2,128,256]{2,1,0:T(8,128)(2,1)S(1)}, u32[]{:S(2)}, u32[]{:S(2)}) collective-permute-start(bf16[2,128,256]{2,1,0:T(8,128)(2,1)S(1)} %get-tuple-element.31), channel_id=1, source_target_pairs={{0,2},{2,0},{4,6},{6,4},{8,10},{10,8},{12,14},{14,12},{1,3},{3,1},... | collective-permute-start | bytes 393224 | tf_op jit(solution)/shard_map/ppermute | solution.py:230
  21.9 15.1 %collective-permute-start.8 = (bf16[2,128,256]{2,1,0:T(8,128)(2,1)S(1)}, bf16[2,128,256]{2,1,0:T(8,128)(2,1)S(1)}, u32[]{:S(2)}, u32[]{:S(2)}) collective-permute-start(bf16[2,128,256]{2,1,0:T(8,128)(2,1)S(1)} %get-tuple-element.32), channel_id=1, source_target_pairs={{0,6},{2,4},{4,2},{6,0},{8,14},{10,12},{12,10},{14,8},{1,7},{3,5},... | collective-permute-start | bytes 393224 | tf_op jit(solution)/shard_map/ppermute | solution.py:230
  33.0 5.0 %collective-permute-start.9 = (bf16[2,128,256]{2,1,0:T(8,128)(2,1)S(1)}, bf16[2,128,256]{2,1,0:T(8,128)(2,1)S(1)}, u32[]{:S(2)}, u32[]{:S(2)}) collective-permute-start(bf16[2,128,256]{2,1,0:T(8,128)(2,1)S(1)} %get-tuple-element.33), channel_id=1, source_target_pairs={{0,4},{2,6},{4,0},{6,2},{8,12},{10,14},{12,8},{14,10},{1,5},{3,7},... | collective-permute-start | bytes 393224 | tf_op jit(solution)/shard_map/ppermute | solution.py:230
  33.3 4.7 %collective-permute-start.10 = (bf16[8,128,128]{2,1,0:T(8,128)(2,1)S(1)}, bf16[8,128,128]{2,1,0:T(8,128)(2,1)S(1)}, u32[]{:S(2)}, u32[]{:S(2)}) collective-permute-start(bf16[8,128,128]{2,1,0:T(8,128)(2,1)S(1)} %get-tuple-element.35), channel_id=1, source_target_pairs={{0,1},{1,0},{2,3},{3,2},{4,5},{5,4},{6,7},{7,6},{8,9},{9,8},{10,11... | collective-permute-start | bytes 786440 | tf_op jit(solution)/shard_map/ppermute | solution.py:263
  38.3 1.6 %collective-permute-start.11 = (bf16[8,128,128]{2,1,0:T(8,128)(2,1)S(1)}, bf16[8,128,128]{2,1,0:T(8,128)(2,1)S(1)}, u32[]{:S(2)}, u32[]{:S(2)}) collective-permute-start(bf16[8,128,128]{2,1,0:T(8,128)(2,1)S(1)} %get-tuple-element.37), channel_id=1, source_target_pairs={{0,1},{1,0},{2,3},{3,2},{4,5},{5,4},{6,7},{7,6},{8,9},{9,8},{10,11... | collective-permute-start | bytes 786440 | tf_op jit(solution)/shard_map/ppermute | solution.py:270

commit v18 on v17

--- a/solution.py
+++ b/solution.py
@@ -58,7 +58,7 @@
     aux, orb, ao = (lax.axis_index(name) for name in ("aux", "orb", "ao"))
     ni = turned.shape[1]
     here = 2 * (aux & 1) + orb
-    place = lambda s: (here ^ s) ^ ((here ^ s) >> 1)
+    place = lambda s: jnp.where((here ^ s) == 0, 0, lax.rem((here ^ s) + 1, 3) + 1)
     near = orb == aux // 2
 
     @pl.when(near)
@@ -223,7 +223,7 @@
 
     def square(messages):
         arrived = [messages[0]]
-        for message, d in zip(messages[1:], (1, 3, 2)):
+        for message, d in zip(messages[1:], (2, 3, 1)):
             moves = [
                 (a * n_orb + o, (a ^ (d >> 1)) * n_orb + (o ^ (d & 1))) for a in range(n_aux) for o in range(n_orb)
             ]

time: 46.1 us -> 46.8 us (1.015)
  waiting for transfers between devices: 11.6 us -> 12.9 us
  starting transfers between devices: 22.1 us -> 21.5 us
    ppermute x1, waiting for transfers between devices: 3.11 us -> 3.81 us  [body(): far_masked = lax.ppermute(masked, 'aux', across)]
    ppermute x6, waiting for transfers between devices: 4.57 us -> 5.2 us  [square(): arrived.append(lax.ppermute(message, ('aux', 'orb'), moves))]
    ppermute x6, starting transfers between devices: 15.3 us -> 14.7 us  [square(): arrived.append(lax.ppermute(message, ('aux', 'orb'), moves))]
  transfers between devices with their start and end apart: 12 -> 12, of which waited for: 6 -> 7; matrix products, arithmetic and copies ran while one was open for 1% -> 1% of each run, Pallas kernels for 7% -> 7%
where the time goes in v18:
time: 46.8 us; the launch traced here: 46.6 us
  starting transfers between devices  21.5 us (46%)
  waiting for transfers between devices  12.9 us (28%)
  Pallas kernels  10.9 us (23%)
  between operations  0.72 us (2%)
  other arithmetic  0.63 us (1%)
    ppermute x6, starting transfers between devices, square(): arrived.append(lax.ppermute(message, ('aux', 'orb'), moves))  14.7 us
    pallas_call x10, Pallas kernels, call(): pl.pallas_call(kernel, in_specs=[in_spec] * len(inputs), out_specs=[out_s...  10.9 us
    ppermute x6, waiting for transfers between devices, square(): arrived.append(lax.ppermute(message, ('aux', 'orb'), moves))  5.2 us
    ppermute x1, waiting for transfers between devices, body(): far_masked = lax.ppermute(masked, 'aux', across)  3.81 us
    ppermute x1, starting transfers between devices, body(): far_masked = lax.ppermute(masked, 'aux', across)  3.6 us
    ppermute x1, starting transfers between devices, body(): mine = lax.ppermute(part, 'orb', swap)  3 us
    ppermute x1, waiting for transfers between devices, body(): mine = lax.ppermute(part, 'orb', swap)  2.7 us
  transfers between devices with their start and end apart: 12, of which 7 were waited for; matrix products, arithmetic and copies ran while one was open for 1% of the time, Pallas kernels for 7%

profile of v18, /device:TPU:0, one launch (start us, length us, event | category | flops | bytes accessed | tf_op | source)
XLA Modules:
  0.0 46.6 jit_solution(17827151482422588395)
XLA Ops:
  0.6 1.2 %masked_blocks.1 = (bf16[2,512,256]{2,1,0:T(8,128)(2,1)S(1)}, bf16[256,512]{1,0:T(8,128)(2,1)S(1)}) custom-call(s32[1,2,4]{2,1,0:T(2,128)} %bitcast.1, bf16[2,512,256]{2,1,0:T(8,128)(2,1)} %blocks.1, bf16[512,512]{1,0:T(8,128)(2,1)} %occupied.3), custom_call_target="tpu_custom_call" | custom-call | bytes 1048576 | tf_op jit(solution)/shard_map/masked_blocks/pallas_call | solution.py:171
  1.8 3.0 %collective-permute-start = (bf16[256,512]{1,0:T(8,128)(2,1)S(1)}, bf16[256,512]{1,0:T(8,128)(2,1)S(1)}, u32[]{:S(2)}, u32[]{:S(2)}) collective-permute-start(bf16[256,512]{1,0:T(8,128)(2,1)S(1)} %get-tuple-element.21), channel_id=1, source_target_pairs={{0,2},{2,0},{1,3},{3,1},{4,6},{6,4},{5,7},{7,5},{8,10},{10,8},{9,1... | collective-permute-start | bytes 786440 | tf_op jit(solution)/shard_map/ppermute | solution.py:213
  4.8 3.6 %collective-permute-start.3 = (bf16[2,512,256]{2,1,0:T(8,128)(2,1)S(1)}, bf16[2,512,256]{2,1,0:T(8,128)(2,1)S(1)}, u32[]{:S(2)}, u32[]{:S(2)}) collective-permute-start(bf16[2,512,256]{2,1,0:T(8,128)(2,1)S(1)} %get-tuple-element.22.masked), channel_id=1, source_target_pairs={{0,12},{4,8},{8,4},{12,0},{1,13},{5,9},{9,5},{13,1},{2,14},{6,10},... | collective-permute-start | bytes 1572872 | tf_op jit(solution)/shard_map/ppermute | solution.py:212
  8.4 2.7 %collective-permute-done.mine = bf16[256,512]{1,0:T(8,128)(2,1)S(1)} collective-permute-done((bf16[256,512]{1,0:T(8,128)(2,1)S(1)}, bf16[256,512]{1,0:T(8,128)(2,1)S(1)}, u32[]{:S(2)}, u32[]{:S(2)}) %collective-permute-start) | collective-permute-done | bytes 262176 | tf_op jit(solution)/shard_map/ppermute | solution.py:213
  11.1 0.0 collective-permute-start.1
  11.1 1.1 %own_panel.1 = (bf16[512,512]{1,0:T(8,128)(2,1)S(1)}, bf16[256,128]{1,0:T(8,128)(2,1)S(1)}) custom-call(bf16[512,512]{1,0:T(8,128)(2,1)} %occupied.3, bf16[512,128]{1,0:T(8,128)(2,1)} %ligand.1), custom_call_target="tpu_custom_call" | custom-call | bytes 1048576 | tf_op jit(solution)/shard_map/own_panel/pallas_call | solution.py:171
  12.2 0.5 collective-permute-done.1.theirs
  12.7 0.6 %own_half.1 = (bf16[4,128,512]{2,1,0:T(8,128)(2,1)S(1)}, bf16[2,128,256]{2,1,0:T(8,128)(2,1)S(1)}, bf16[2,128,256]{2,1,0:T(8,128)(2,1)S(1)}, bf16[2,128,256]{2,1,0:T(8,128)(2,1)S(1)}, bf16[2,128,256]{2,1,0:T(8,128)(2,1)S(1)}) custom-call(bf16[512,512]{1,0:T(8,128)(2,1)S(1)} %get-tuple-element.20.occupied, bf16[256,512]{1,0:T(8,128)(2,1)S(1)} %collective-permute-done.mine, ...), custom_call_target="tpu_custom_call" | custom-call | flops 268435456 | bytes 1048576 | tf_op jit(solution)/shard_map/own_half/pallas_call | solution.py:171
  13.3 1.9 %collective-permute-start.4 = (bf16[2,128,256]{2,1,0:T(8,128)(2,1)S(1)}, bf16[2,128,256]{2,1,0:T(8,128)(2,1)S(1)}, u32[]{:S(2)}, u32[]{:S(2)}) collective-permute-start(bf16[2,128,256]{2,1,0:T(8,128)(2,1)S(1)} %get-tuple-element.25.refs_1_), channel_id=1, source_target_pairs={{0,4},{2,6},{4,0},{6,2},{8,12},{10,14},{12,8},{14,10},{1,5},{3,7},... | collective-permute-start | bytes 393224 | tf_op jit(solution)/shard_map/ppermute | solution.py:230
  15.2 1.4 %collective-permute-start.5 = (bf16[2,128,256]{2,1,0:T(8,128)(2,1)S(1)}, bf16[2,128,256]{2,1,0:T(8,128)(2,1)S(1)}, u32[]{:S(2)}, u32[]{:S(2)}) collective-permute-start(bf16[2,128,256]{2,1,0:T(8,128)(2,1)S(1)} %get-tuple-element.26.refs_2_), channel_id=1, source_target_pairs={{0,6},{2,4},{4,2},{6,0},{8,14},{10,12},{12,10},{14,8},{1,7},{3,5},... | collective-permute-start | bytes 393224 | tf_op jit(solution)/shard_map/ppermute | solution.py:230
  16.6 0.3 collective-permute-start.6
  16.9 0.7 %density_terms.1.before = f32[2,128]{1,0:T(2,128)S(1)} custom-call(bf16[512,512]{1,0:T(8,128)(2,1)S(1)} %get-tuple-element.20.occupied, bf16[256,512]{1,0:T(8,128)(2,1)S(1)} %collective-permute-done.mine, bf16[256,512]{1,0:T(8,128)(2,1)S(1)} %collective-permute-done.1.theirs, bf16[2,512,256]{2,1,0:T(8,128)(2,1)S(1)} %get-tuple-element.22.masked, ...), custom_call_target="tpu_custom_call" | custom-call | flops 268435456 | bytes 1048576 | tf_op jit(solution)/shard_map/density_terms/pallas_call | solution.py:171
  17.6 0.1 collective-permute-start.2
  17.7 3.8 %collective-permute-done.3.masked = bf16[2,512,256]{2,1,0:T(8,128)(2,1)S(1)} collective-permute-done((bf16[2,512,256]{2,1,0:T(8,128)(2,1)S(1)}, bf16[2,512,256]{2,1,0:T(8,128)(2,1)S(1)}, u32[]{:S(2)}, u32[]{:S(2)}) %collective-permute-start.3) | collective-permute-done | bytes 524320 | tf_op jit(solution)/shard_map/ppermute | solution.py:212
  21.5 0.4 far_half.1
  22.0 9.6 %collective-permute-start.7 = (bf16[2,128,256]{2,1,0:T(8,128)(2,1)S(1)}, bf16[2,128,256]{2,1,0:T(8,128)(2,1)S(1)}, u32[]{:S(2)}, u32[]{:S(2)}) collective-permute-start(bf16[2,128,256]{2,1,0:T(8,128)(2,1)S(1)} %get-tuple-element.31), channel_id=1, source_target_pairs={{0,4},{2,6},{4,0},{6,2},{8,12},{10,14},{12,8},{14,10},{1,5},{3,7},... | collective-permute-start | bytes 393224 | tf_op jit(solution)/shard_map/ppermute | solution.py:230
  31.5 0.0 collective-permute-done.2.before
  31.6 0.1 collective-permute-start.8
  31.6 0.0 collective-permute-done.4.refs_1_
  31.6 1.5 %collective-permute-start.9 = (bf16[2,128,256]{2,1,0:T(8,128)(2,1)S(1)}, bf16[2,128,256]{2,1,0:T(8,128)(2,1)S(1)}, u32[]{:S(2)}, u32[]{:S(2)}) collective-permute-start(bf16[2,128,256]{2,1,0:T(8,128)(2,1)S(1)} %get-tuple-element.33), channel_id=1, source_target_pairs={{0,2},{2,0},{4,6},{6,4},{8,10},{10,8},{12,14},{14,12},{1,3},{3,1},... | collective-permute-start | bytes 393224 | tf_op jit(solution)/shard_map/ppermute | solution.py:230
  33.1 0.0 collective-permute-done.5.refs_2_
  33.1 0.0 collective-permute-done.6.refs_3_
  33.1 0.3 own_pairs.1
  33.4 0.1 collective-permute-start.10
  33.5 2.3 %collective-permute-done.7.refs_1_ = bf16[2,128,256]{2,1,0:T(8,128)(2,1)S(1)} collective-permute-done((bf16[2,128,256]{2,1,0:T(8,128)(2,1)S(1)}, bf16[2,128,256]{2,1,0:T(8,128)(2,1)S(1)}, u32[]{:S(2)}, u32[]{:S(2)}) %collective-permute-start.7) | collective-permute-done | bytes 131104 | tf_op jit(solution)/shard_map/ppermute | solution.py:230
  35.8 1.7 %collective-permute-done.8.refs_2_ = bf16[2,128,256]{2,1,0:T(8,128)(2,1)S(1)} collective-permute-done((bf16[2,128,256]{2,1,0:T(8,128)(2,1)S(1)}, bf16[2,128,256]{2,1,0:T(8,128)(2,1)S(1)}, u32[]{:S(2)}, u32[]{:S(2)}) %collective-permute-start.8) | collective-permute-done | bytes 131104 | tf_op jit(solution)/shard_map/ppermute | solution.py:230
  37.5 1.2 %collective-permute-done.9.refs_3_ = bf16[2,128,256]{2,1,0:T(8,128)(2,1)S(1)} collective-permute-done((bf16[2,128,256]{2,1,0:T(8,128)(2,1)S(1)}, bf16[2,128,256]{2,1,0:T(8,128)(2,1)S(1)}, u32[]{:S(2)}, u32[]{:S(2)}) %collective-permute-start.9) | collective-permute-done | bytes 131104 | tf_op jit(solution)/shard_map/ppermute | solution.py:230
  38.7 0.0 collective-permute-done.10.earlier.refs_1_
  38.7 0.3 far_pairs.1
  39.0 0.1 collective-permute-start.11
  39.0 0.6 %multiply_reduce_fusion = f32[2]{0:T(128)} fusion(f32[2,128]{1,0:T(2,128)S(1)} %collective-permute-done.2.before, f32[2,128]{1,0:T(2,128)S(1)} %density_terms.1.before), kind=kLoop, calls=%fused_computation | loop fusion | flops 4 | bytes 24 | tf_op jit(solution)/shard_map/div | solution.py:248
  39.7 0.2 far_turned.1.far
  39.9 0.7 %collective-permute-done.11.refs_3_ = bf16[8,128,128]{2,1,0:T(8,128)(2,1)S(1)} collective-permute-done((bf16[8,128,128]{2,1,0:T(8,128)(2,1)S(1)}, bf16[8,128,128]{2,1,0:T(8,128)(2,1)S(1)}, u32[]{:S(2)}, u32[]{:S(2)}) %collective-permute-start.11) | collective-permute-done | bytes 262176 | tf_op jit(solution)/shard_map/ppermute | solution.py:270
  40.6 6.0 %cross_terms.1 = f32[128,256,128]{2,1,0:T(8,128)} custom-call(bf16[8,256,128]{2,1,0:T(8,128)(2,1)S(1)} %get-tuple-element.30.near, bf16[8,256,128]{2,1,0:T(8,128)(2,1)S(1)} %far_turned.1.far, f32[8,128,128]{2,1,0:T(8,128)S(1)} %get-tuple-element.34.refs_0_, bf16[8,128,128]{2,1,0:T(8,128)(2,1)S(1)} %collective-permute-done.10.earlier.refs_1_, ...), custom_call_target="tpu_custom_call" | custom-call | flops 2147483648 | bytes 18874368 | tf_op jit(solution)/shard_map/cross_terms/pallas_call | solution.py:171
  (1 shorter events, 0.0 us)
Async XLA Ops:
  1.8 9.3 %collective-permute-start = (bf16[256,512]{1,0:T(8,128)(2,1)S(1)}, bf16[256,512]{1,0:T(8,128)(2,1)S(1)}, u32[]{:S(2)}, u32[]{:S(2)}) collective-permute-start(bf16[256,512]{1,0:T(8,128)(2,1)S(1)} %get-tuple-element.21), channel_id=1, source_target_pairs={{0,2},{2,0},{1,3},{3,1},{4,6},{6,4},{5,7},{7,5},{8,10},{10,8},{9,1... | collective-permute-start | bytes 786440 | tf_op jit(solution)/shard_map/ppermute | solution.py:213
  4.8 16.7 %collective-permute-start.3 = (bf16[2,512,256]{2,1,0:T(8,128)(2,1)S(1)}, bf16[2,512,256]{2,1,0:T(8,128)(2,1)S(1)}, u32[]{:S(2)}, u32[]{:S(2)}) collective-permute-start(bf16[2,512,256]{2,1,0:T(8,128)(2,1)S(1)} %get-tuple-element.22.masked), channel_id=1, source_target_pairs={{0,12},{4,8},{8,4},{12,0},{1,13},{5,9},{9,5},{13,1},{2,14},{6,10},... | collective-permute-start | bytes 1572872 | tf_op jit(solution)/shard_map/ppermute | solution.py:212
  11.1 1.5 %collective-permute-start.1 = (bf16[256,512]{1,0:T(8,128)(2,1)S(1)}, bf16[256,512]{1,0:T(8,128)(2,1)S(1)}, u32[]{:S(2)}, u32[]{:S(2)}) collective-permute-start(bf16[256,512]{1,0:T(8,128)(2,1)S(1)} %collective-permute-done.mine), channel_id=1, source_target_pairs={{0,1},{1,0},{2,3},{3,2},{4,5},{5,4},{6,7},{7,6},{8,9},{9,8},{10,11... | collective-permute-start | bytes 786440 | tf_op jit(solution)/shard_map/ppermute | solution.py:214
  13.3 18.3 %collective-permute-start.4 = (bf16[2,128,256]{2,1,0:T(8,128)(2,1)S(1)}, bf16[2,128,256]{2,1,0:T(8,128)(2,1)S(1)}, u32[]{:S(2)}, u32[]{:S(2)}) collective-permute-start(bf16[2,128,256]{2,1,0:T(8,128)(2,1)S(1)} %get-tuple-element.25.refs_1_), channel_id=1, source_target_pairs={{0,4},{2,6},{4,0},{6,2},{8,12},{10,14},{12,8},{14,10},{1,5},{3,7},... | collective-permute-start | bytes 393224 | tf_op jit(solution)/shard_map/ppermute | solution.py:230
  15.2 17.9 %collective-permute-start.5 = (bf16[2,128,256]{2,1,0:T(8,128)(2,1)S(1)}, bf16[2,128,256]{2,1,0:T(8,128)(2,1)S(1)}, u32[]{:S(2)}, u32[]{:S(2)}) collective-permute-start(bf16[2,128,256]{2,1,0:T(8,128)(2,1)S(1)} %get-tuple-element.26.refs_2_), channel_id=1, source_target_pairs={{0,6},{2,4},{4,2},{6,0},{8,14},{10,12},{12,10},{14,8},{1,7},{3,5},... | collective-permute-start | bytes 393224 | tf_op jit(solution)/shard_map/ppermute | solution.py:230
  16.6 16.5 %collective-permute-start.6 = (bf16[2,128,256]{2,1,0:T(8,128)(2,1)S(1)}, bf16[2,128,256]{2,1,0:T(8,128)(2,1)S(1)}, u32[]{:S(2)}, u32[]{:S(2)}) collective-permute-start(bf16[2,128,256]{2,1,0:T(8,128)(2,1)S(1)} %get-tuple-element.27.refs_3_), channel_id=1, source_target_pairs={{0,2},{2,0},{4,6},{6,4},{8,10},{10,8},{12,14},{14,12},{1,3},{3,1},... | collective-permute-start | bytes 393224 | tf_op jit(solution)/shard_map/ppermute | solution.py:230
  17.6 13.9 %collective-permute-start.2 = (f32[2,128]{1,0:T(2,128)S(1)}, f32[2,128]{1,0:T(2,128)S(1)}, u32[]{:S(2)}, u32[]{:S(2)}) collective-permute-start(f32[2,128]{1,0:T(2,128)S(1)} %density_terms.1.before), channel_id=1, source_target_pairs={{0,1},{1,0},{2,3},{3,2},{4,5},{5,4},{6,7},{7,6},{8,9},{9,8},{10,11... | collective-permute-start | bytes 3080 | tf_op jit(solution)/shard_map/ppermute | solution.py:247
  22.0 13.8 %collective-permute-start.7 = (bf16[2,128,256]{2,1,0:T(8,128)(2,1)S(1)}, bf16[2,128,256]{2,1,0:T(8,128)(2,1)S(1)}, u32[]{:S(2)}, u32[]{:S(2)}) collective-permute-start(bf16[2,128,256]{2,1,0:T(8,128)(2,1)S(1)} %get-tuple-element.31), channel_id=1, source_target_pairs={{0,4},{2,6},{4,0},{6,2},{8,12},{10,14},{12,8},{14,10},{1,5},{3,7},... | collective-permute-start | bytes 393224 | tf_op jit(solution)/shard_map/ppermute | solution.py:230
  31.6 5.9 %collective-permute-start.8 = (bf16[2,128,256]{2,1,0:T(8,128)(2,1)S(1)}, bf16[2,128,256]{2,1,0:T(8,128)(2,1)S(1)}, u32[]{:S(2)}, u32[]{:S(2)}) collective-permute-start(bf16[2,128,256]{2,1,0:T(8,128)(2,1)S(1)} %get-tuple-element.32), channel_id=1, source_target_pairs={{0,6},{2,4},{4,2},{6,0},{8,14},{10,12},{12,10},{14,8},{1,7},{3,5},... | collective-permute-start | bytes 393224 | tf_op jit(solution)/shard_map/ppermute | solution.py:230
  31.6 7.1 %collective-permute-start.9 = (bf16[2,128,256]{2,1,0:T(8,128)(2,1)S(1)}, bf16[2,128,256]{2,1,0:T(8,128)(2,1)S(1)}, u32[]{:S(2)}, u32[]{:S(2)}) collective-permute-start(bf16[2,128,256]{2,1,0:T(8,128)(2,1)S(1)} %get-tuple-element.33), channel_id=1, source_target_pairs={{0,2},{2,0},{4,6},{6,4},{8,10},{10,8},{12,14},{14,12},{1,3},{3,1},... | collective-permute-start | bytes 393224 | tf_op jit(solution)/shard_map/ppermute | solution.py:230
  33.4 5.3 %collective-permute-start.10 = (bf16[8,128,128]{2,1,0:T(8,128)(2,1)S(1)}, bf16[8,128,128]{2,1,0:T(8,128)(2,1)S(1)}, u32[]{:S(2)}, u32[]{:S(2)}) collective-permute-start(bf16[8,128,128]{2,1,0:T(8,128)(2,1)S(1)} %get-tuple-element.35), channel_id=1, source_target_pairs={{0,1},{1,0},{2,3},{3,2},{4,5},{5,4},{6,7},{7,6},{8,9},{9,8},{10,11... | collective-permute-start | bytes 786440 | tf_op jit(solution)/shard_map/ppermute | solution.py:263
  39.0 1.6 %collective-permute-start.11 = (bf16[8,128,128]{2,1,0:T(8,128)(2,1)S(1)}, bf16[8,128,128]{2,1,0:T(8,128)(2,1)S(1)}, u32[]{:S(2)}, u32[]{:S(2)}) collective-permute-start(bf16[8,128,128]{2,1,0:T(8,128)(2,1)S(1)} %get-tuple-element.37), channel_id=1, source_target_pairs={{0,1},{1,0},{2,3},{3,2},{4,5},{5,4},{6,7},{7,6},{8,9},{9,8},{10,11... | collective-permute-start | bytes 786440 | tf_op jit(solution)/shard_map/ppermute | solution.py:270

commit v19 on v16

--- a/solution.py
+++ b/solution.py
@@ -157,9 +157,8 @@
             result = jnp.dot(turned, jnp.concatenate(both, axis=1), preferred_element_type=jnp.float32)
             held[g * GROUP + i] = result[:, :width]
             held[g * GROUP + i + 1] = result[:, width:]
-            if i % 4 == 2:
-                done = pl.ds(g * GROUP + i - 2, 4)
-                pltpu.make_async_copy(held.at[done], out.at[done], sem).start()
+            done = pl.ds(g * GROUP + i, 2)
+            pltpu.make_async_copy(held.at[done], out.at[done], sem).start()
         return carry
 
     lax.fori_loop(0, ni // GROUP, step, 0, unroll=4)

time: 45.4 us -> 45.3 us (level)
  no operation moved by 1% of the time
where the time goes in v19:
time: 45.3 us; the launch traced here: 45.2 us
  starting transfers between devices  22.1 us (49%)
  waiting for transfers between devices  10.9 us (24%)
  Pallas kernels  10.8 us (24%)
  between operations  0.72 us (2%)
  other arithmetic  0.63 us (1%)
    ppermute x6, starting transfers between devices, square(): arrived.append(lax.ppermute(message, ('aux', 'orb'), moves))  15.3 us
    pallas_call x10, Pallas kernels, call(): pl.pallas_call(kernel, in_specs=[in_spec] * len(inputs), out_specs=[out_s...  10.8 us
    ppermute x6, waiting for transfers between devices, square(): arrived.append(lax.ppermute(message, ('aux', 'orb'), moves))  3.81 us
    ppermute x1, starting transfers between devices, body(): far_masked = lax.ppermute(masked, 'aux', across)  3.6 us
    ppermute x1, waiting for transfers between devices, body(): far_masked = lax.ppermute(masked, 'aux', across)  3.17 us
    ppermute x1, starting transfers between devices, body(): mine = lax.ppermute(part, 'orb', swap)  3 us
    ppermute x1, waiting for transfers between devices, body(): mine = lax.ppermute(part, 'orb', swap)  2.7 us
  transfers between devices with their start and end apart: 12, of which 7 were waited for; matrix products, arithmetic and copies ran while one was open for 1% of the time, Pallas kernels for 7%

profile of v19, /device:TPU:0, one launch (start us, length us, event | category | flops | bytes accessed | tf_op | source)
XLA Modules:
  0.0 45.2 jit_solution(12524084641928621362)
XLA Ops:
  0.6 1.2 %masked_blocks.1 = (bf16[2,512,256]{2,1,0:T(8,128)(2,1)S(1)}, bf16[256,512]{1,0:T(8,128)(2,1)S(1)}) custom-call(s32[1,2,4]{2,1,0:T(2,128)} %bitcast.1, bf16[2,512,256]{2,1,0:T(8,128)(2,1)} %blocks.1, bf16[512,512]{1,0:T(8,128)(2,1)} %occupied.3), custom_call_target="tpu_custom_call" | custom-call | bytes 1048576 | tf_op jit(solution)/shard_map/masked_blocks/pallas_call | solution.py:170
  1.8 3.0 %collective-permute-start = (bf16[256,512]{1,0:T(8,128)(2,1)S(1)}, bf16[256,512]{1,0:T(8,128)(2,1)S(1)}, u32[]{:S(2)}, u32[]{:S(2)}) collective-permute-start(bf16[256,512]{1,0:T(8,128)(2,1)S(1)} %get-tuple-element.21), channel_id=1, source_target_pairs={{0,2},{2,0},{1,3},{3,1},{4,6},{6,4},{5,7},{7,5},{8,10},{10,8},{9,1... | collective-permute-start | bytes 786440 | tf_op jit(solution)/shard_map/ppermute | solution.py:212
  4.8 3.6 %collective-permute-start.3 = (bf16[2,512,256]{2,1,0:T(8,128)(2,1)S(1)}, bf16[2,512,256]{2,1,0:T(8,128)(2,1)S(1)}, u32[]{:S(2)}, u32[]{:S(2)}) collective-permute-start(bf16[2,512,256]{2,1,0:T(8,128)(2,1)S(1)} %get-tuple-element.22.masked), channel_id=1, source_target_pairs={{0,12},{4,8},{8,4},{12,0},{1,13},{5,9},{9,5},{13,1},{2,14},{6,10},... | collective-permute-start | bytes 1572872 | tf_op jit(solution)/shard_map/ppermute | solution.py:211
  8.4 2.7 %collective-permute-done.mine = bf16[256,512]{1,0:T(8,128)(2,1)S(1)} collective-permute-done((bf16[256,512]{1,0:T(8,128)(2,1)S(1)}, bf16[256,512]{1,0:T(8,128)(2,1)S(1)}, u32[]{:S(2)}, u32[]{:S(2)}) %collective-permute-start) | collective-permute-done | bytes 262176 | tf_op jit(solution)/shard_map/ppermute | solution.py:212
  11.1 0.0 collective-permute-start.1
  11.1 1.1 %own_panel.1 = (bf16[512,512]{1,0:T(8,128)(2,1)S(1)}, bf16[256,128]{1,0:T(8,128)(2,1)S(1)}) custom-call(bf16[512,512]{1,0:T(8,128)(2,1)} %occupied.3, bf16[512,128]{1,0:T(8,128)(2,1)} %ligand.1), custom_call_target="tpu_custom_call" | custom-call | bytes 1048576 | tf_op jit(solution)/shard_map/own_panel/pallas_call | solution.py:170
  12.2 0.5 %collective-permute-done.1.theirs = bf16[256,512]{1,0:T(8,128)(2,1)S(1)} collective-permute-done((bf16[256,512]{1,0:T(8,128)(2,1)S(1)}, bf16[256,512]{1,0:T(8,128)(2,1)S(1)}, u32[]{:S(2)}, u32[]{:S(2)}) %collective-permute-start.1) | collective-permute-done | bytes 262176 | tf_op jit(solution)/shard_map/ppermute | solution.py:213
  12.7 0.6 %own_half.1 = (bf16[4,128,512]{2,1,0:T(8,128)(2,1)S(1)}, bf16[2,128,256]{2,1,0:T(8,128)(2,1)S(1)}, bf16[2,128,256]{2,1,0:T(8,128)(2,1)S(1)}, bf16[2,128,256]{2,1,0:T(8,128)(2,1)S(1)}, bf16[2,128,256]{2,1,0:T(8,128)(2,1)S(1)}) custom-call(bf16[512,512]{1,0:T(8,128)(2,1)S(1)} %get-tuple-element.20.occupied, bf16[256,512]{1,0:T(8,128)(2,1)S(1)} %collective-permute-done.mine, ...), custom_call_target="tpu_custom_call" | custom-call | flops 268435456 | bytes 1048576 | tf_op jit(solution)/shard_map/own_half/pallas_call | solution.py:170
  13.3 2.8 %collective-permute-start.4 = (bf16[2,128,256]{2,1,0:T(8,128)(2,1)S(1)}, bf16[2,128,256]{2,1,0:T(8,128)(2,1)S(1)}, u32[]{:S(2)}, u32[]{:S(2)}) collective-permute-start(bf16[2,128,256]{2,1,0:T(8,128)(2,1)S(1)} %get-tuple-element.25.refs_1_), channel_id=1, source_target_pairs={{0,6},{2,4},{4,2},{6,0},{8,14},{10,12},{12,10},{14,8},{1,7},{3,5},... | collective-permute-start | bytes 393224 | tf_op jit(solution)/shard_map/ppermute | solution.py:229
  16.1 0.5 collective-permute-start.5
  16.6 0.3 collective-permute-start.6
  16.9 0.7 %density_terms.1.before = f32[2,128]{1,0:T(2,128)S(1)} custom-call(bf16[512,512]{1,0:T(8,128)(2,1)S(1)} %get-tuple-element.20.occupied, bf16[256,512]{1,0:T(8,128)(2,1)S(1)} %collective-permute-done.mine, bf16[256,512]{1,0:T(8,128)(2,1)S(1)} %collective-permute-done.1.theirs, bf16[2,512,256]{2,1,0:T(8,128)(2,1)S(1)} %get-tuple-element.22.masked, ...), custom_call_target="tpu_custom_call" | custom-call | flops 268435456 | bytes 1048576 | tf_op jit(solution)/shard_map/density_terms/pallas_call | solution.py:170
  17.6 0.1 collective-permute-start.2
  17.7 3.2 %collective-permute-done.3.masked = bf16[2,512,256]{2,1,0:T(8,128)(2,1)S(1)} collective-permute-done((bf16[2,512,256]{2,1,0:T(8,128)(2,1)S(1)}, bf16[2,512,256]{2,1,0:T(8,128)(2,1)S(1)}, u32[]{:S(2)}, u32[]{:S(2)}) %collective-permute-start.3) | collective-permute-done | bytes 524320 | tf_op jit(solution)/shard_map/ppermute | solution.py:211
  20.9 0.4 far_half.1
  21.3 10.2 %collective-permute-start.7 = (bf16[2,128,256]{2,1,0:T(8,128)(2,1)S(1)}, bf16[2,128,256]{2,1,0:T(8,128)(2,1)S(1)}, u32[]{:S(2)}, u32[]{:S(2)}) collective-permute-start(bf16[2,128,256]{2,1,0:T(8,128)(2,1)S(1)} %get-tuple-element.31), channel_id=1, source_target_pairs={{0,6},{2,4},{4,2},{6,0},{8,14},{10,12},{12,10},{14,8},{1,7},{3,5},... | collective-permute-start | bytes 393224 | tf_op jit(solution)/shard_map/ppermute | solution.py:229
  31.5 0.0 collective-permute-done.2.before
  31.5 0.1 collective-permute-start.8
  31.6 0.0 collective-permute-done.4.refs_1_
  31.6 1.4 %collective-permute-start.9 = (bf16[2,128,256]{2,1,0:T(8,128)(2,1)S(1)}, bf16[2,128,256]{2,1,0:T(8,128)(2,1)S(1)}, u32[]{:S(2)}, u32[]{:S(2)}) collective-permute-start(bf16[2,128,256]{2,1,0:T(8,128)(2,1)S(1)} %get-tuple-element.33), channel_id=1, source_target_pairs={{0,2},{2,0},{4,6},{6,4},{8,10},{10,8},{12,14},{14,12},{1,3},{3,1},... | collective-permute-start | bytes 393224 | tf_op jit(solution)/shard_map/ppermute | solution.py:229
  33.1 0.0 collective-permute-done.5.refs_2_
  33.1 0.0 collective-permute-done.6.refs_3_
  33.1 0.3 own_pairs.1
  33.4 0.1 collective-permute-start.10
  33.5 1.6 %collective-permute-done.7.refs_1_ = bf16[2,128,256]{2,1,0:T(8,128)(2,1)S(1)} collective-permute-done((bf16[2,128,256]{2,1,0:T(8,128)(2,1)S(1)}, bf16[2,128,256]{2,1,0:T(8,128)(2,1)S(1)}, u32[]{:S(2)}, u32[]{:S(2)}) %collective-permute-start.7) | collective-permute-done | bytes 131104 | tf_op jit(solution)/shard_map/ppermute | solution.py:229
  35.1 2.1 %collective-permute-done.8.refs_2_ = bf16[2,128,256]{2,1,0:T(8,128)(2,1)S(1)} collective-permute-done((bf16[2,128,256]{2,1,0:T(8,128)(2,1)S(1)}, bf16[2,128,256]{2,1,0:T(8,128)(2,1)S(1)}, u32[]{:S(2)}, u32[]{:S(2)}) %collective-permute-start.8) | collective-permute-done | bytes 131104 | tf_op jit(solution)/shard_map/ppermute | solution.py:229
  37.2 0.1 collective-permute-done.9.refs_3_
  37.3 0.0 collective-permute-done.10.earlier.refs_1_
  37.3 0.3 far_pairs.1
  37.6 0.1 collective-permute-start.11
  37.6 0.6 %multiply_reduce_fusion = f32[2]{0:T(128)} fusion(f32[2,128]{1,0:T(2,128)S(1)} %collective-permute-done.2.before, f32[2,128]{1,0:T(2,128)S(1)} %density_terms.1.before), kind=kLoop, calls=%fused_computation | loop fusion | flops 4 | bytes 24 | tf_op jit(solution)/shard_map/div | solution.py:247
  38.3 0.2 far_turned.1.far
  38.5 0.7 %collective-permute-done.11.refs_3_ = bf16[8,128,128]{2,1,0:T(8,128)(2,1)S(1)} collective-permute-done((bf16[8,128,128]{2,1,0:T(8,128)(2,1)S(1)}, bf16[8,128,128]{2,1,0:T(8,128)(2,1)S(1)}, u32[]{:S(2)}, u32[]{:S(2)}) %collective-permute-start.11) | collective-permute-done | bytes 262176 | tf_op jit(solution)/shard_map/ppermute | solution.py:269
  39.2 6.0 %cross_terms.1 = f32[128,256,128]{2,1,0:T(8,128)} custom-call(bf16[8,256,128]{2,1,0:T(8,128)(2,1)S(1)} %get-tuple-element.30.near, bf16[8,256,128]{2,1,0:T(8,128)(2,1)S(1)} %far_turned.1.far, f32[8,128,128]{2,1,0:T(8,128)S(1)} %get-tuple-element.34.refs_0_, bf16[8,128,128]{2,1,0:T(8,128)(2,1)S(1)} %collective-permute-done.10.earlier.refs_1_, ...), custom_call_target="tpu_custom_call" | custom-call | flops 2147483648 | bytes 18874368 | tf_op jit(solution)/shard_map/cross_terms/pallas_call | solution.py:170
  (1 shorter events, 0.0 us)
Async XLA Ops:
  1.8 9.3 %collective-permute-start = (bf16[256,512]{1,0:T(8,128)(2,1)S(1)}, bf16[256,512]{1,0:T(8,128)(2,1)S(1)}, u32[]{:S(2)}, u32[]{:S(2)}) collective-permute-start(bf16[256,512]{1,0:T(8,128)(2,1)S(1)} %get-tuple-element.21), channel_id=1, source_target_pairs={{0,2},{2,0},{1,3},{3,1},{4,6},{6,4},{5,7},{7,5},{8,10},{10,8},{9,1... | collective-permute-start | bytes 786440 | tf_op jit(solution)/shard_map/ppermute | solution.py:212
  4.8 16.0 %collective-permute-start.3 = (bf16[2,512,256]{2,1,0:T(8,128)(2,1)S(1)}, bf16[2,512,256]{2,1,0:T(8,128)(2,1)S(1)}, u32[]{:S(2)}, u32[]{:S(2)}) collective-permute-start(bf16[2,512,256]{2,1,0:T(8,128)(2,1)S(1)} %get-tuple-element.22.masked), channel_id=1, source_target_pairs={{0,12},{4,8},{8,4},{12,0},{1,13},{5,9},{9,5},{13,1},{2,14},{6,10},... | collective-permute-start | bytes 1572872 | tf_op jit(solution)/shard_map/ppermute | solution.py:211
  11.1 1.5 %collective-permute-start.1 = (bf16[256,512]{1,0:T(8,128)(2,1)S(1)}, bf16[256,512]{1,0:T(8,128)(2,1)S(1)}, u32[]{:S(2)}, u32[]{:S(2)}) collective-permute-start(bf16[256,512]{1,0:T(8,128)(2,1)S(1)} %collective-permute-done.mine), channel_id=1, source_target_pairs={{0,1},{1,0},{2,3},{3,2},{4,5},{5,4},{6,7},{7,6},{8,9},{9,8},{10,11... | collective-permute-start | bytes 786440 | tf_op jit(solution)/shard_map/ppermute | solution.py:213
  13.3 18.3 %collective-permute-start.4 = (bf16[2,128,256]{2,1,0:T(8,128)(2,1)S(1)}, bf16[2,128,256]{2,1,0:T(8,128)(2,1)S(1)}, u32[]{:S(2)}, u32[]{:S(2)}) collective-permute-start(bf16[2,128,256]{2,1,0:T(8,128)(2,1)S(1)} %get-tuple-element.25.refs_1_), channel_id=1, source_target_pairs={{0,6},{2,4},{4,2},{6,0},{8,14},{10,12},{12,10},{14,8},{1,7},{3,5},... | collective-permute-start | bytes 393224 | tf_op jit(solution)/shard_map/ppermute | solution.py:229
  16.1 17.0 %collective-permute-start.5 = (bf16[2,128,256]{2,1,0:T(8,128)(2,1)S(1)}, bf16[2,128,256]{2,1,0:T(8,128)(2,1)S(1)}, u32[]{:S(2)}, u32[]{:S(2)}) collective-permute-start(bf16[2,128,256]{2,1,0:T(8,128)(2,1)S(1)} %get-tuple-element.26.refs_2_), channel_id=1, source_target_pairs={{0,4},{2,6},{4,0},{6,2},{8,12},{10,14},{12,8},{14,10},{1,5},{3,7},... | collective-permute-start | bytes 393224 | tf_op jit(solution)/shard_map/ppermute | solution.py:229
  16.6 16.5 %collective-permute-start.6 = (bf16[2,128,256]{2,1,0:T(8,128)(2,1)S(1)}, bf16[2,128,256]{2,1,0:T(8,128)(2,1)S(1)}, u32[]{:S(2)}, u32[]{:S(2)}) collective-permute-start(bf16[2,128,256]{2,1,0:T(8,128)(2,1)S(1)} %get-tuple-element.27.refs_3_), channel_id=1, source_target_pairs={{0,2},{2,0},{4,6},{6,4},{8,10},{10,8},{12,14},{14,12},{1,3},{3,1},... | collective-permute-start | bytes 393224 | tf_op jit(solution)/shard_map/ppermute | solution.py:229
  17.6 13.9 %collective-permute-start.2 = (f32[2,128]{1,0:T(2,128)S(1)}, f32[2,128]{1,0:T(2,128)S(1)}, u32[]{:S(2)}, u32[]{:S(2)}) collective-permute-start(f32[2,128]{1,0:T(2,128)S(1)} %density_terms.1.before), channel_id=1, source_target_pairs={{0,1},{1,0},{2,3},{3,2},{4,5},{5,4},{6,7},{7,6},{8,9},{9,8},{10,11... | collective-permute-start | bytes 3080 | tf_op jit(solution)/shard_map/ppermute | solution.py:246
  21.3 13.8 %collective-permute-start.7 = (bf16[2,128,256]{2,1,0:T(8,128)(2,1)S(1)}, bf16[2,128,256]{2,1,0:T(8,128)(2,1)S(1)}, u32[]{:S(2)}, u32[]{:S(2)}) collective-permute-start(bf16[2,128,256]{2,1,0:T(8,128)(2,1)S(1)} %get-tuple-element.31), channel_id=1, source_target_pairs={{0,6},{2,4},{4,2},{6,0},{8,14},{10,12},{12,10},{14,8},{1,7},{3,5},... | collective-permute-start | bytes 393224 | tf_op jit(solution)/shard_map/ppermute | solution.py:229
  31.5 5.6 %collective-permute-start.8 = (bf16[2,128,256]{2,1,0:T(8,128)(2,1)S(1)}, bf16[2,128,256]{2,1,0:T(8,128)(2,1)S(1)}, u32[]{:S(2)}, u32[]{:S(2)}) collective-permute-start(bf16[2,128,256]{2,1,0:T(8,128)(2,1)S(1)} %get-tuple-element.32), channel_id=1, source_target_pairs={{0,4},{2,6},{4,0},{6,2},{8,12},{10,14},{12,8},{14,10},{1,5},{3,7},... | collective-permute-start | bytes 393224 | tf_op jit(solution)/shard_map/ppermute | solution.py:229
  31.6 5.6 %collective-permute-start.9 = (bf16[2,128,256]{2,1,0:T(8,128)(2,1)S(1)}, bf16[2,128,256]{2,1,0:T(8,128)(2,1)S(1)}, u32[]{:S(2)}, u32[]{:S(2)}) collective-permute-start(bf16[2,128,256]{2,1,0:T(8,128)(2,1)S(1)} %get-tuple-element.33), channel_id=1, source_target_pairs={{0,2},{2,0},{4,6},{6,4},{8,10},{10,8},{12,14},{14,12},{1,3},{3,1},... | collective-permute-start | bytes 393224 | tf_op jit(solution)/shard_map/ppermute | solution.py:229
  33.4 3.9 %collective-permute-start.10 = (bf16[8,128,128]{2,1,0:T(8,128)(2,1)S(1)}, bf16[8,128,128]{2,1,0:T(8,128)(2,1)S(1)}, u32[]{:S(2)}, u32[]{:S(2)}) collective-permute-start(bf16[8,128,128]{2,1,0:T(8,128)(2,1)S(1)} %get-tuple-element.35), channel_id=1, source_target_pairs={{0,1},{1,0},{2,3},{3,2},{4,5},{5,4},{6,7},{7,6},{8,9},{9,8},{10,11... | collective-permute-start | bytes 786440 | tf_op jit(solution)/shard_map/ppermute | solution.py:262
  37.6 1.6 %collective-permute-start.11 = (bf16[8,128,128]{2,1,0:T(8,128)(2,1)S(1)}, bf16[8,128,128]{2,1,0:T(8,128)(2,1)S(1)}, u32[]{:S(2)}, u32[]{:S(2)}) collective-permute-start(bf16[8,128,128]{2,1,0:T(8,128)(2,1)S(1)} %get-tuple-element.37), channel_id=1, source_target_pairs={{0,1},{1,0},{2,3},{3,2},{4,5},{5,4},{6,7},{7,6},{8,9},{9,8},{10,11... | collective-permute-start | bytes 786440 | tf_op jit(solution)/shard_map/ppermute | solution.py:269
